TPU v7x, 32 devices: a whole 2x2x4 slice. The times are simulated.
32 devices in a mesh: seq: 2 (over core), ctx: 4 (over y, x), fsdp: 4 (over z).
Axes of the slice: x: 2, y: 2, z: 4, core: 2. Of those that a mesh axis runs over, the one named last changes fastest.
Arguments:
- tokens: bfloat16 [2, 3072, 896], P('seq', ('ctx', 'fsdp')), may hold values from -6 to 6
- out_grad: bfloat16 [2, 3072, 896], P('seq', ('ctx', 'fsdp')), may hold values from -6 to 6
- block_order: int32 [2, 4], P('seq'), may hold values from 0 to 3, each once within a row
- norm1_gain: bfloat16 [896], P('fsdp'), may hold values from 0.5 to 1.5
- q_weight: bfloat16 [896, 896], P('fsdp'), may hold values from -0.25 to 0.25
- q_bias: bfloat16 [896], P('fsdp'), may hold values from -1.25 to 1.25
- k_weight: bfloat16 [896, 128], P('fsdp'), may hold values from -0.25 to 0.25
- k_bias: bfloat16 [128], P('fsdp'), may hold values from -1.25 to 1.25
- v_weight: bfloat16 [896, 128], P('fsdp'), may hold values from -0.1875 to 0.1875
- v_bias: bfloat16 [128], P('fsdp'), may hold values from -1.25 to 1.25
- o_weight: bfloat16 [896, 896], P('fsdp'), may hold values from -0.375 to 0.375
- norm2_gain: bfloat16 [896], P('fsdp'), may hold values from 0.5 to 1.5
- gate_weight: bfloat16 [896, 4864], P('fsdp'), may hold values from -0.1875 to 0.1875
- up_weight: bfloat16 [896, 4864], P('fsdp'), may hold values from -0.1875 to 0.1875
- down_weight: bfloat16 [4864, 896], P('fsdp'), may hold values from -0.078125 to 0.078125
Outputs:
- layer_out: bfloat16 [2, 3072, 896], P('seq', ('ctx', 'fsdp'))
- tokens_grad: float32 [2, 3072, 896], P('seq', ('ctx', 'fsdp'))
- norm1_gain_grad: float32 [896], P('fsdp')
- q_weight_grad: float32 [896, 896], P('fsdp')
- q_bias_grad: float32 [896], P('fsdp')
- k_weight_grad: float32 [896, 128], P('fsdp')
- k_bias_grad: float32 [128], P('fsdp')
- v_weight_grad: float32 [896, 128], P('fsdp')
- v_bias_grad: float32 [128], P('fsdp')
- o_weight_grad: float32 [896, 896], P('fsdp')
- norm2_gain_grad: float32 [896], P('fsdp')
- gate_weight_grad: float32 [896, 4864], P('fsdp')
- up_weight_grad: float32 [896, 4864], P('fsdp')
- down_weight_grad: float32 [4864, 896], P('fsdp')
Inputs may be any that keep to these rules, and one draw needn't show every extreme that they name: `block_order`: each row is a permutation of 0 to 3.
All inputs are finite; a program needn't handle non-finite values.
Results may differ from a plain program's by a relative error of at most 0.04.
Values may be sent and summed in bfloat16 or wider, within the bound.
No kernel may reach another device: no remote copies, remote signals or barrier semaphores. Data moves between devices by JAX's collectives and lax.ppermute only.
A program may use at most 256 MiB of HBM per device.

v0:
```python
import functools
import math

import jax
import jax.numpy as jnp
from jax import lax
from jax.experimental import pallas as pl
from jax.experimental.pallas import tpu as pltpu
from jax.sharding import PartitionSpec as P

HEADS = 14
KV_HEADS = 2
HEAD = 64
GROUP = HEADS // KV_HEADS
NORM_EPS = 1e-06
ROPE_BASE = 1000000.0
MASKED = -1e30
BF16 = jnp.bfloat16
F32 = jnp.float32


def rope_tables(positions, head_dim):
    half_dim = head_dim // 2
    inverse = jnp.exp(
        jnp.arange(half_dim, dtype=jnp.float32) * (-math.log(ROPE_BASE) * 2.0 / head_dim)
    )
    angles = positions.astype(jnp.float32)[:, None] * inverse[None, :]
    return (jnp.cos(angles)[:, None, :], jnp.sin(angles)[:, None, :])


def rotate(values, cosine_table, sine_table):
    half_dim = values.shape[-1] // 2
    front_half = values[..., :half_dim]
    back_half = values[..., half_dim:]
    return jnp.concatenate(
        [
            front_half * cosine_table - back_half * sine_table,
            back_half * cosine_table + front_half * sine_table,
        ],
        -1,
    )


def matmul(left_side, right_side):
    return jnp.dot(left_side, right_side, preferred_element_type=F32)


def contract_rows(left_side, right_side):
    return lax.dot_general(
        left_side, right_side, (((0,), (0,)), ((), ())), preferred_element_type=F32
    )


def times_transposed(left_side, right_side):
    return lax.dot_general(
        left_side, right_side, (((1,), (1,)), ((), ())), preferred_element_type=F32
    )


def rms_forward(values, gain_vec):
    inv_scale = lax.rsqrt(jnp.mean(values * values, -1, keepdims=True) + NORM_EPS)
    normed = values * inv_scale
    return (normed, inv_scale, (normed * gain_vec).astype(BF16))


def rms_backward(grad_out, normed, inv_scale, gain_vec):
    scaled = grad_out * gain_vec
    grad_in = inv_scale * (scaled - normed * jnp.mean(scaled * normed, -1, keepdims=True))
    return (grad_in, grad_out * normed)


def cut_heads(ref, head):
    tile = ref[:, (head // 2) * 128 : (head // 2 + 1) * 128].astype(F32)
    group = head // GROUP
    if head % 2 != group:
        tile = jnp.concatenate([tile[:, HEAD:], tile[:, :HEAD]], 1)
    lane = lax.broadcasted_iota(jnp.int32, tile.shape, 1)
    return jnp.where((lane >= HEAD) if group else (lane < HEAD), tile, 0.0)


def split_lanes(column, shape):
    high = column.astype(BF16).astype(F32)
    mid = (column - high).astype(BF16).astype(F32)
    low = column - high - mid
    lane = lax.broadcasted_iota(jnp.int32, shape, 1)
    return jnp.where(
        lane == 0, high, jnp.where(lane == 1, mid, jnp.where(lane == 2, low, 0.0))
    ).astype(BF16)


def piece_shift(at, zed, tokens_here, keys_here):
    pieces = keys_here // tokens_here
    shift = jnp.zeros(at.shape, jnp.int32)
    for k in range(pieces):
        here = (jnp.bitwise_xor(zed, k) - k - zed) * tokens_here
        shift = jnp.where(at >= k * tokens_here, here, shift)
    return shift


def forward_kernel(by_xor, info_ref, q_ref, kv_ref, att_ref, qext_ref, top_ref, acc_ref):
    step = pl.program_id(0)
    last = pl.num_programs(0) - 1
    tokens_here = q_ref.shape[0]
    keys_here = kv_ref.shape[1]
    here = lax.axis_index("ctx")
    zed = lax.axis_index("fsdp")
    own = info_ref[here]
    block = info_ref[jnp.bitwise_xor(here, step) if by_xor else step]

    @pl.when(step == 0)
    def _():
        for h in range(HEADS):
            qext_ref[h * tokens_here : (h + 1) * tokens_here, :128] = cut_heads(q_ref, h).astype(
                BF16
            )
        top_ref[...] = jnp.full(top_ref.shape, MASKED, F32)
        acc_ref[...] = jnp.zeros(acc_ref.shape, F32)

    def attend(masked):
        keys = kv_ref[0, :, :128]
        values = jnp.concatenate(
            [kv_ref[0, :, 128:], jnp.ones((keys_here, 128), BF16)], 1
        )
        if masked:
            row = lax.broadcasted_iota(jnp.int32, (tokens_here, keys_here), 0)
            col = lax.broadcasted_iota(jnp.int32, (tokens_here, keys_here), 1)
            allowed = col + piece_shift(col, zed, tokens_here, keys_here) <= row
        for h in range(HEADS):
            rows = slice(h * tokens_here, (h + 1) * tokens_here)
            scores = times_transposed(qext_ref[rows, :128], keys)
            if masked:
                scores = jnp.where(allowed, scores, MASKED)
            old = top_ref[rows, :]
            top = jnp.maximum(old, jnp.max(scores, -1, keepdims=True))
            probs = jnp.exp(scores - top[:, :1]).astype(BF16)
            shrink = jnp.exp(old - top)
            top_ref[rows, :] = top
            acc_ref[rows, :] = acc_ref[rows, :] * jnp.concatenate([shrink, shrink], 1) + matmul(
                probs, values
            )

    @pl.when(block == own)
    def _():
        attend(True)

    @pl.when(block < own)
    def _():
        attend(False)

    @pl.when(step == last)
    def _():
        lane = lax.broadcasted_iota(jnp.int32, (tokens_here, 128), 1)
        for pair in range(HEADS // 2):
            outs = []
            for h in (2 * pair, 2 * pair + 1):
                rows = slice(h * tokens_here, (h + 1) * tokens_here)
                total = acc_ref[rows, 128:]
                out = acc_ref[rows, :128] / total
                if h // GROUP != h % 2:
                    out = jnp.concatenate([out[:, HEAD:], out[:, :HEAD]], 1)
                outs.append(out)
                log_total = top_ref[rows, :] + jnp.log(total)
                qext_ref[rows, 128:] = split_lanes(-log_total, (tokens_here, 128))
            att_ref[:, pair * 128 : (pair + 1) * 128] = jnp.where(
                lane < HEAD, outs[0], outs[1]
            ).astype(BF16)


def backward_kernel(
    by_xor, info_ref, qext_ref, do_ref, att_ref, kv_ref, dq_ref, dkv_ref, doext_ref, dqt_ref
):
    step = pl.program_id(0)
    last = pl.num_programs(0) - 1
    tokens_here = do_ref.shape[0]
    keys_here = kv_ref.shape[1]
    here = lax.axis_index("ctx")
    zed = lax.axis_index("fsdp")
    own = info_ref[here]
    block = info_ref[jnp.bitwise_xor(here, step) if by_xor else step]
    span = 2 * tokens_here

    @pl.when(step == 0)
    def _():
        for h in range(HEADS):
            rows = slice(h * tokens_here, (h + 1) * tokens_here)
            grad = cut_heads(do_ref, h)
            delta = jnp.sum(grad * cut_heads(att_ref, h), -1, keepdims=True)
            doext_ref[rows, :128] = grad.astype(BF16)
            doext_ref[rows, 128:] = split_lanes(-delta, (tokens_here, 128))
        dqt_ref[...] = jnp.zeros(dqt_ref.shape, F32)

    def attend(masked):
        lane = lax.broadcasted_iota(jnp.int32, (keys_here, 128), 1)
        ones = jnp.where(lane < 3, 1.0, 0.0).astype(BF16)
        keys = kv_ref[0, :, :128]
        keys_ext = jnp.concatenate([keys, ones], 1)
        values_ext = jnp.concatenate([kv_ref[0, :, 128:], ones], 1)
        keys_t = keys.astype(F32).T.astype(BF16)
        if masked:
            row = lax.broadcasted_iota(jnp.int32, (keys_here, tokens_here), 0)
            col = lax.broadcasted_iota(jnp.int32, (keys_here, tokens_here), 1)
            allowed = row + piece_shift(row, zed, tokens_here, keys_here) <= col
            allowed = allowed.astype(F32)
            allowed = jnp.concatenate([allowed, allowed], 1) > 0.5
        dk = jnp.zeros((keys_here, 128), F32)
        dv = jnp.zeros((keys_here, 128), F32)
        for pair in range(HEADS // 2):
            rows = slice(pair * span, (pair + 1) * span)
            probs = jnp.exp(times_transposed(keys_ext, qext_ref[rows, :]))
            if masked:
                probs = jnp.where(allowed, probs, 0.0)
            slope = (probs * times_transposed(values_ext, doext_ref[rows, :])).astype(BF16)
            dv = dv + matmul(probs.astype(BF16), doext_ref[rows, :128])
            dk = dk + matmul(slope, qext_ref[rows, :128])
            dqt_ref[pair] = dqt_ref[pair] + matmul(keys_t, slope)
        dkv_ref[0] = jnp.concatenate([dk, dv], 1).astype(BF16)

    @pl.when(block == own)
    def _():
        attend(True)

    @pl.when(block < own)
    def _():
        attend(False)

    @pl.when(block > own)
    def _():
        dkv_ref[...] = jnp.zeros(dkv_ref.shape, BF16)

    @pl.when(step == last)
    def _():
        lane = lax.broadcasted_iota(jnp.int32, (tokens_here, 128), 1)
        for pair in range(HEADS // 2):
            turned = dqt_ref[pair].T
            outs = []
            for j in range(2):
                h = 2 * pair + j
                out = turned[j * tokens_here : (j + 1) * tokens_here]
                if h // GROUP != j:
                    out = jnp.concatenate([out[:, HEAD:], out[:, :HEAD]], 1)
                outs.append(out)
            dq_ref[:, pair * 128 : (pair + 1) * 128] = (
                jnp.where(lane < HEAD, outs[0], outs[1]) * HEAD ** (-0.5)
            )


def whole_spec(shape):
    return pl.BlockSpec(shape, lambda i, info: (0,) * len(shape))


def attend_forward(info, by_xor, queries, kv):
    blocks, block_len, kv_width = kv.shape
    tokens_here, q_width = queries.shape
    rows = HEADS * tokens_here
    return pl.pallas_call(
        functools.partial(forward_kernel, by_xor),
        grid_spec=pltpu.PrefetchScalarGridSpec(
            num_scalar_prefetch=1,
            grid=(blocks,),
            in_specs=[
                whole_spec((tokens_here, q_width)),
                pl.BlockSpec((1, block_len, kv_width), lambda i, info: (i, 0, 0)),
            ],
            out_specs=[whole_spec((tokens_here, q_width)), whole_spec((rows, 256))],
            scratch_shapes=[pltpu.VMEM((rows, 128), F32), pltpu.VMEM((rows, 256), F32)],
        ),
        out_shape=[
            jax.ShapeDtypeStruct((tokens_here, q_width), BF16),
            jax.ShapeDtypeStruct((rows, 256), BF16),
        ],
        compiler_params=pltpu.CompilerParams(
            dimension_semantics=("arbitrary",), vmem_limit_bytes=40 * 2**20
        ),
        cost_estimate=pl.CostEstimate(
            flops=4 * rows * blocks * block_len * 256,
            bytes_accessed=6 * 2**20,
            transcendentals=rows * blocks * block_len,
        ),
        name="attend_forward",
    )(info, queries, kv)


def attend_backward(info, by_xor, queries_ext, grad_att, attended, kv):
    blocks, block_len, kv_width = kv.shape
    tokens_here, q_width = grad_att.shape
    rows = HEADS * tokens_here
    return pl.pallas_call(
        functools.partial(backward_kernel, by_xor),
        grid_spec=pltpu.PrefetchScalarGridSpec(
            num_scalar_prefetch=1,
            grid=(blocks,),
            in_specs=[
                whole_spec((rows, 256)),
                whole_spec((tokens_here, q_width)),
                whole_spec((tokens_here, q_width)),
                pl.BlockSpec((1, block_len, kv_width), lambda i, info: (i, 0, 0)),
            ],
            out_specs=[
                whole_spec((tokens_here, q_width)),
                pl.BlockSpec((1, block_len, kv_width), lambda i, info: (i, 0, 0)),
            ],
            scratch_shapes=[
                pltpu.VMEM((rows, 256), BF16),
                pltpu.VMEM((HEADS // 2, 128, 2 * tokens_here), F32),
            ],
        ),
        out_shape=[
            jax.ShapeDtypeStruct((tokens_here, q_width), F32),
            jax.ShapeDtypeStruct(kv.shape, BF16),
        ],
        compiler_params=pltpu.CompilerParams(
            dimension_semantics=("arbitrary",), vmem_limit_bytes=40 * 2**20
        ),
        cost_estimate=pl.CostEstimate(
            flops=10 * rows * blocks * block_len * 256,
            bytes_accessed=8 * 2**20,
            transcendentals=rows * blocks * block_len,
        ),
        name="attend_backward",
    )(info, queries_ext, grad_att, attended, kv)


def part_place(tp, j, k):
    at = jnp.bitwise_xor(lax.rem(lax.axis_index("ctx"), tp), k)
    return jnp.bitwise_xor(lax.axis_index("seq"), j) * tp + at


def spread_columns_kernel(n_z, *refs):
    pieces, outs, held = refs[:2], refs[2:-1], refs[-1]
    tp = pieces[0].shape[0]
    n_part = 2 * tp
    for j in range(2):
        for k in range(tp):
            held[part_place(tp, j, k)] = pieces[j][k].astype(F32)
    half = held.shape[2] // len(outs)
    pad = half // n_z
    for i, out in enumerate(outs):
        piece = out.shape[1] // (n_z * n_part)
        cuts = []
        for j in range(n_z):
            for e in range(n_part):
                start = i * half + j * pad
                cuts.append(held[e, :, start : start + piece])
        out[...] = jnp.concatenate(cuts, 1)


def spread_columns(pieces, n_z, ff, outs):
    tp, rows, cols = pieces[0].shape
    tile = 32
    return pl.pallas_call(
        functools.partial(spread_columns_kernel, n_z),
        grid=(rows // tile,),
        in_specs=[pl.BlockSpec((tp, tile, cols), lambda i: (0, i, 0))] * 2,
        out_specs=[pl.BlockSpec((tile, ff), lambda i: (i, 0))] * outs,
        scratch_shapes=[pltpu.VMEM((2 * tp, tile, cols), F32)],
        out_shape=[jax.ShapeDtypeStruct((rows, ff), F32)] * outs,
        compiler_params=pltpu.CompilerParams(
            dimension_semantics=("arbitrary",), vmem_limit_bytes=40 * 2**20
        ),
        cost_estimate=pl.CostEstimate(
            flops=0, bytes_accessed=rows * ff * 6 * outs, transcendentals=0
        ),
        name="spread_columns",
    )(*pieces)


def spread_rows_kernel(piece, *refs):
    pieces, out_ref = refs[:-1], refs[-1]
    room = out_ref.shape[0] // piece
    tp = pieces[0].shape[0]
    for j in range(2):
        for k in range(tp):
            place = part_place(tp, j, k)

            @pl.when(place < room)
            def _():
                start = pl.multiple_of(place * piece, 8)
                out_ref[pl.ds(start, piece), :] = pieces[j][k].astype(F32)[:piece]


def spread_rows(pieces, piece, rows_out):
    tp, rows, cols = pieces[0].shape
    tile = 128
    return pl.pallas_call(
        functools.partial(spread_rows_kernel, piece),
        grid=(cols // tile,),
        in_specs=[pl.BlockSpec((tp, rows, tile), lambda i: (0, 0, i))] * 2,
        out_specs=pl.BlockSpec((rows_out, tile), lambda i: (0, i)),
        out_shape=jax.ShapeDtypeStruct((rows_out, cols), F32),
        compiler_params=pltpu.CompilerParams(
            dimension_semantics=("arbitrary",), vmem_limit_bytes=40 * 2**20
        ),
        cost_estimate=pl.CostEstimate(
            flops=0, bytes_accessed=rows_out * cols * 6, transcendentals=0
        ),
        name="spread_rows",
    )(*pieces)


def join_weight_kernel(own_ref, sib_ref, out_ref):
    tp, n_z, part_rows = own_ref.shape[:3]
    room = out_ref.shape[1] // part_rows
    for j, ref in enumerate((own_ref, sib_ref)):
        for k in range(tp):
            place = part_place(tp, j, k)

            @pl.when(place < room)
            def _():
                start = pl.multiple_of(place * part_rows, 16)
                for z in range(n_z):
                    at = jnp.bitwise_xor(lax.axis_index("fsdp"), z)
                    out_ref[at, pl.ds(start, part_rows), :] = ref[k, z]


def join_weight(own, sib, rows_here):
    tp, n_z, part_rows, cols = own.shape
    return pl.pallas_call(
        join_weight_kernel,
        in_specs=[pl.BlockSpec(memory_space=pltpu.VMEM)] * 2,
        out_specs=pl.BlockSpec(memory_space=pltpu.VMEM),
        out_shape=jax.ShapeDtypeStruct((n_z, rows_here, cols), BF16),
        compiler_params=pltpu.CompilerParams(vmem_limit_bytes=40 * 2**20),
        cost_estimate=pl.CostEstimate(
            flops=0, bytes_accessed=4 * n_z * rows_here * cols, transcendentals=0
        ),
        name="join_weight",
    )(own, sib).reshape(n_z * rows_here, cols)


def join_kv_kernel(widths, *refs):
    pieces, (out_ref, vec_ref, held) = refs[:-3], refs[-3:]
    n_z, rows_here, cols = out_ref.shape
    for k in range(n_z):
        at = jnp.bitwise_xor(lax.axis_index("fsdp"), k)
        out_ref[at] = pieces[k][:rows_here]
        held[at] = pieces[k][rows_here:].astype(F32)
    vec_ref[...] = jnp.zeros(vec_ref.shape, F32)
    for i, size in enumerate(widths):
        row = jnp.concatenate([held[z, i : i + 1, :size] for z in range(n_z)], 1)
        vec_ref[i : i + 1, : n_z * size] = row


def join_kv(pieces, rows_here, widths):
    rows, cols = pieces[0].shape
    n_z = len(pieces)
    return pl.pallas_call(
        functools.partial(join_kv_kernel, widths),
        in_specs=[pl.BlockSpec(memory_space=pltpu.VMEM)] * n_z,
        out_specs=[pl.BlockSpec(memory_space=pltpu.VMEM)] * 2,
        out_shape=[
            jax.ShapeDtypeStruct((n_z, rows_here, cols), BF16),
            jax.ShapeDtypeStruct((8, n_z * rows_here), F32),
        ],
        scratch_shapes=[pltpu.VMEM((n_z, rows - rows_here, cols), F32)],
        compiler_params=pltpu.CompilerParams(vmem_limit_bytes=40 * 2**20),
        name="join_kv",
    )(*pieces)


def ff_kernel(tp, *refs):
    hidden, grads, weights = refs[:tp], refs[tp : 2 * tp], refs[2 * tp : 2 * tp + 4]
    act_refs, back_refs = refs[2 * tp + 4 : 2 * tp + 6], refs[2 * tp + 6 : 2 * tp + 8]
    outs = refs[2 * tp + 8 : 3 * tp + 8]
    gu_buf, down_buf, acc, sems = refs[3 * tp + 8 :]
    copies = [
        pltpu.make_async_copy(weights[i], (gu_buf if i < 2 else down_buf).at[i % 2], sems.at[i])
        for i in range(4)
    ]
    for i in (0, 2, 1, 3):
        copies[i].start()
    tokens_here = hidden[0].shape[0]
    half = down_buf.shape[1]
    step = 2 if tp % 2 == 0 else 1
    for i in range(2):
        copies[i].wait()
        for t in range(0, tp, step):
            rows = slice(t * tokens_here, (t + step) * tokens_here)
            here = jnp.concatenate([hidden[t + n][...] for n in range(step)], 0)
            grad = jnp.concatenate([grads[t + n][...] for n in range(step)], 0)
            gate = matmul(here, gu_buf[i, :, :half])
            up = matmul(here, gu_buf[i, :, half:])
            if t == 0:
                copies[2 + i].wait()
            grad_act = times_transposed(grad, down_buf[i])
            sig = 1.0 / (1.0 + jnp.exp(-gate))
            silu = gate * sig
            act_refs[i][rows, :] = (silu * up).astype(BF16)
            grad_gate = (grad_act * up * (sig + silu * (1.0 - sig))).astype(BF16)
            grad_up = (grad_act * silu).astype(BF16)
            back_refs[i][rows, :half] = grad_gate
            back_refs[i][rows, half:] = grad_up
            part = times_transposed(grad_gate, gu_buf[i, :, :half]) + times_transposed(
                grad_up, gu_buf[i, :, half:]
            )
            if i == 0:
                acc[rows, :] = part
            else:
                part = (part + acc[rows, :]).astype(BF16)
                for n in range(step):
                    outs[t + n][...] = part[n * tokens_here : (n + 1) * tokens_here]


def ff_pass(hidden, grads, gu, down):
    tp = len(hidden)
    tokens_here, width = hidden[0].shape
    half = down[0].shape[0]
    rows = tp * tokens_here
    vmem = pl.BlockSpec(memory_space=pltpu.VMEM)
    got = pl.pallas_call(
        functools.partial(ff_kernel, tp),
        in_specs=[vmem] * (2 * tp) + [pl.BlockSpec(memory_space=pl.ANY)] * 4,
        out_specs=[vmem] * (tp + 4),
        out_shape=[jax.ShapeDtypeStruct((rows, half), BF16)] * 2
        + [jax.ShapeDtypeStruct((rows, 2 * half), BF16)] * 2
        + [jax.ShapeDtypeStruct((tokens_here, width), BF16)] * tp,
        scratch_shapes=[
            pltpu.VMEM((2, width, 2 * half), BF16),
            pltpu.VMEM((2, half, width), BF16),
            pltpu.VMEM((rows, width), F32),
            pltpu.SemaphoreType.DMA((4,)),
        ],
        compiler_params=pltpu.CompilerParams(vmem_limit_bytes=56 * 2**20),
        cost_estimate=pl.CostEstimate(
            flops=20 * rows * width * half,
            bytes_accessed=20 * 2**20,
            transcendentals=2 * rows * half,
        ),
        name="ff_pass",
    )(*hidden, *grads, *gu, *down)
    return got[:2], got[2:4], got[4:]


def local(
    tokens,
    out_grad,
    block_order,
    norm1_gain,
    q_weight,
    q_bias,
    k_weight,
    k_bias,
    v_weight,
    v_bias,
    o_weight,
    norm2_gain,
    gate_weight,
    up_weight,
    down_weight,
):
    n_ctx = lax.axis_size("ctx")
    n_z = lax.axis_size("fsdp")
    tp = 4 if n_ctx % 4 == 0 else (2 if n_ctx % 2 == 0 else 1)
    here = lax.axis_index("ctx")
    zed = lax.axis_index("fsdp")
    core = lax.axis_index("seq")
    n_part = 2 * tp
    part = core * tp + lax.rem(here, tp)

    def swap(v):
        return lax.ppermute(v, "seq", [(0, 1), (1, 0)])

    def hop(v, k):
        if k == 0:
            return v
        return lax.ppermute(v, "ctx", [(i, i ^ k) for i in range(n_ctx)])

    def hop_z(v, k):
        if k == 0:
            return v
        return lax.ppermute(v, "fsdp", [(i, i ^ k) for i in range(n_z)])

    def gather_z(v):
        return lax.all_gather(v, "fsdp", axis=0, tiled=True)

    def scatter_z(v):
        return lax.psum_scatter(v, "fsdp", scatter_dimension=0, tiled=True)

    tokens_here, width = tokens.shape[1:]
    ff = gate_weight.shape[1]
    rows_here = q_weight.shape[0]
    key_width = KV_HEADS * HEAD
    block_len = tokens_here * n_z

    part_rows = -(-rows_here // (n_part * 32)) * 32

    kb = k_bias.shape[0]
    vectors = (norm1_gain, norm2_gain, q_bias, k_bias, v_bias)
    vec = sum(
        jnp.pad(v[None], ((i, 15 - i), (0, 2 * key_width - v.shape[0])))
        for i, v in enumerate(vectors)
    )
    kv_pack = jnp.concatenate([jnp.concatenate([k_weight, v_weight], 1), vec], 0)
    og_here = out_grad[0]

    def own_part(w):
        return lax.dynamic_slice_in_dim(w, part * part_rows, part_rows, 0)

    kv_pack, q_part, o_part, gate_weight, up_weight, down_weight = lax.optimization_barrier(
        (kv_pack, own_part(q_weight), own_part(o_weight), gate_weight, up_weight, down_weight)
    )
    kv_got = [hop_z(kv_pack, k) for k in range(n_z)]
    q_got = [hop_z(q_part, k) for k in range(n_z)]
    og_parts = [hop(og_here, k) for k in range(tp)]
    kv_got, q_got, og_parts, o_part = lax.optimization_barrier((kv_got, q_got, og_parts, o_part))
    w_kv, vecs = join_kv(kv_got, rows_here, tuple(v.shape[0] for v in vectors))
    w_kv = w_kv.reshape(width, 2 * key_width)
    gain_one = vecs[0:1, :width]
    gain_two = vecs[1:2, :width]
    b_query = vecs[2:3, :width]
    b_key = vecs[3:4, :key_width]
    b_value = vecs[4:5, :key_width]

    def share_pieces(mine):
        own = jnp.stack([hop(mine, k) for k in range(tp)])
        return own, swap(own)

    q_own = [hop(jnp.stack(q_got), k) for k in range(tp)]

    ff_z = ff // n_z
    piece = ff_z // n_part
    piece_pad = -(-piece // 32) * 32
    ff_half = n_z * piece_pad

    def ff_columns(w):
        cuts = []
        for j in range(n_z):
            cut = lax.dynamic_slice_in_dim(w, j * ff_z + part * piece, piece, 1)
            cuts.append(jnp.pad(cut, ((0, 0), (0, piece_pad - piece))))
        return jnp.concatenate(cuts, 1)

    gu_cut = jnp.concatenate([ff_columns(gate_weight), ff_columns(up_weight)], 1)
    down_cut = lax.dynamic_slice_in_dim(down_weight, part * piece, piece, 0)
    down_cut = jnp.pad(down_cut, ((0, piece_pad - piece), (0, 0)))
    order_row = block_order[0]
    query_pos = (
        order_row[here] * block_len
        + zed * tokens_here
        + jnp.arange(tokens_here, dtype=jnp.int32)
    )
    cosine_table, sine_table = rope_tables(query_pos, HEAD)

    inputs = tokens[0].astype(F32)
    normed_one, scale_one, hidden_one = rms_forward(inputs, gain_one)
    key_value = matmul(hidden_one, w_kv)
    key_pre = key_value[:, :key_width] + b_key
    value_pre = key_value[:, key_width:] + b_value
    key_rot = rotate(key_pre.reshape(tokens_here, KV_HEADS, HEAD), cosine_table, sine_table)
    kv_local = jnp.concatenate(
        [key_rot.astype(BF16).reshape(tokens_here, key_width), value_pre.astype(BF16)], 1
    )
    kv_local, o_part = lax.optimization_barrier((kv_local, o_part))
    kv_z = [hop_z(kv_local, k) for k in range(n_z)]
    o_got = [hop_z(o_part, k) for k in range(n_z)]
    kv_z, o_got, q_own, gu_cut, down_cut = lax.optimization_barrier(
        (kv_z, o_got, q_own, gu_cut, down_cut)
    )
    kv_block = jnp.concatenate(kv_z, 0)
    gu_own = gather_z(gu_cut)
    gu_oth = swap(gu_own)
    down_own = gather_z(down_cut)
    down_oth = swap(down_own)
    if n_ctx == tp:
        kv_blocks = [hop(kv_block, k) for k in range(n_ctx)]
    else:
        kv_blocks = lax.all_gather(kv_block, "ctx", axis=0, tiled=False)
    q_own = jnp.stack(q_own)
    w_query = join_weight(q_own, swap(q_own), rows_here)
    query_pre = matmul(hidden_one, w_query) + b_query
    queries = rotate(query_pre.reshape(tokens_here, HEADS, HEAD), cosine_table, sine_table)
    queries = queries.astype(BF16).reshape(tokens_here, HEADS * HEAD) * BF16(HEAD ** (-0.5))
    kv_blocks, o_got = lax.optimization_barrier((kv_blocks, o_got))
    o_own = [hop(jnp.stack(o_got), k) for k in range(tp)]
    kv_whole = jnp.stack(kv_blocks) if n_ctx == tp else kv_blocks
    attended, queries_ext = attend_forward(order_row, n_ctx == tp, queries, kv_whole)
    attended, o_own = lax.optimization_barrier((attended, o_own))
    o_own = jnp.stack(o_own)
    w_out = join_weight(o_own, swap(o_own), rows_here)
    resid = inputs + matmul(attended, w_out)
    normed_two, scale_two, hidden_two = rms_forward(resid, gain_two)

    h2_parts = [hop(hidden_two, k) for k in range(tp)]

    def scatter_plane(v):
        parts = v.astype(BF16).reshape(tp, tokens_here, width)
        return [hop(parts[k], k) for k in range(tp)]

    acts, ggus, dh2 = ff_pass(h2_parts, og_parts, (gu_own, gu_oth), (down_own, down_oth))
    grad_h2_parts = [hop(dh2[k], k) for k in range(tp)]
    h2_all = jnp.concatenate(h2_parts, 0)
    og_all = jnp.concatenate(og_parts, 0)

    def reduce_start(part_sum):
        cols = part_sum.shape[1]
        cut = part_sum.astype(BF16).reshape(n_z, rows_here, cols)
        cut = jnp.pad(cut, ((0, 0), (0, n_part * part_rows - rows_here), (0, 0)))
        own = lax.dynamic_slice_in_dim(cut, core * tp * part_rows, tp * part_rows, 1)
        oth = lax.dynamic_slice_in_dim(cut, (1 - core) * tp * part_rows, tp * part_rows, 1)
        both = (own.astype(F32) + swap(oth).astype(F32)).astype(BF16)
        return both.reshape(n_z, tp, part_rows, cols)

    def reduce_end(cut, z_first):
        cols = cut.shape[-1]
        total = 0.0
        if z_first:
            for k in range(n_z):
                out = lax.dynamic_index_in_dim(cut, zed ^ k, 0, keepdims=False)
                total = total + hop_z(out, k).astype(F32)
            cut = total.astype(BF16)
            total = 0.0
        for k in range(tp):
            at = lax.rem(here, tp) ^ k
            out = lax.dynamic_index_in_dim(cut, at, cut.ndim - 3, keepdims=False)
            total = total + hop(out, k).astype(F32)
        if not z_first:
            cut = total.astype(BF16)
            total = 0.0
            for k in range(n_z):
                out = lax.dynamic_index_in_dim(cut, zed ^ k, 0, keepdims=False)
                total = total + hop_z(out, k).astype(F32)
        total = ctx_groups_sum(total.astype(BF16))
        total = lax.optimization_barrier(total)
        own, sib = share_pieces(total)
        return spread_rows((own, sib), part_rows, rows_here)

    def ctx_groups_sum(v):
        if n_ctx == tp:
            return v
        groups = [[g * tp + c for g in range(n_ctx // tp)] for c in range(tp)]
        return lax.psum(v, "ctx", axis_index_groups=groups)

    def core_sum(own, oth):
        return (own + swap(oth.astype(BF16)).astype(F32)).astype(BF16)

    d_gu = core_sum(contract_rows(h2_all, ggus[0]), contract_rows(h2_all, ggus[1]))
    d_down = core_sum(contract_rows(acts[0], og_all), contract_rows(acts[1], og_all))
    ff_out = (matmul(acts[0], down_own) + matmul(acts[1], down_oth)).astype(BF16)
    grad_h2_parts, d_down, d_gu, ff_out = lax.optimization_barrier(
        (grad_h2_parts, d_down, d_gu, ff_out)
    )
    d_gu = scatter_z(d_gu)
    ff_out = scatter_plane(ff_out)
    grad_h2 = sum(v.astype(F32) for v in grad_h2_parts)

    grad_norm_two, gain_two_terms = rms_backward(grad_h2, normed_two, scale_two, gain_two)
    grad_resid = og_here.astype(F32) + grad_norm_two
    grad_proj = grad_resid.astype(BF16)
    grad_att = times_transposed(grad_proj, w_out).astype(BF16)
    grad_queries, grad_terms = attend_backward(
        order_row, n_ctx == tp, queries_ext, grad_att, attended, kv_whole
    )
    grad_terms, d_gu, ff_out, d_down = lax.optimization_barrier((grad_terms, d_gu, ff_out, d_down))
    d_down = scatter_z(d_down)
    result = resid + sum(v.astype(F32) for v in ff_out)
    layer_out = result.astype(BF16)[None]
    if n_ctx == tp:
        kv_terms = [hop(grad_terms[k], k) for k in range(n_ctx)]
        kv_terms, d_gu = lax.optimization_barrier((kv_terms, d_gu))
        kv_sum = sum(v.astype(F32) for v in kv_terms).astype(BF16)
    else:
        kv_sum = lax.psum_scatter(grad_terms, "ctx", scatter_dimension=0, tiled=False)
    d_gu = share_pieces(ctx_groups_sum(d_gu))
    kv_sum = kv_sum.reshape(n_z, tokens_here, 2 * key_width)
    grad_kv = kv_sum[0].astype(F32)
    for k in range(1, n_z):
        grad_kv = grad_kv + hop_z(kv_sum[k], k).astype(F32)

    grad_q_pre = (
        rotate(grad_queries.reshape(tokens_here, HEADS, HEAD), cosine_table, -sine_table)
        .reshape(tokens_here, HEADS * HEAD)
        .astype(BF16)
    )
    grad_k_pre = (
        rotate(
            grad_kv[:, :key_width].reshape(tokens_here, KV_HEADS, HEAD), cosine_table, -sine_table
        )
        .reshape(tokens_here, key_width)
        .astype(BF16)
    )
    grad_v_pre = grad_kv[:, key_width:].astype(BF16)

    grad_kv_pre = jnp.concatenate([grad_k_pre, grad_v_pre], 1)
    grad_hidden_one = times_transposed(grad_q_pre, w_query) + times_transposed(grad_kv_pre, w_kv)
    grad_norm_one, gain_one_terms = rms_backward(grad_hidden_one, normed_one, scale_one, gain_one)
    tokens_grad = (grad_resid + grad_norm_one)[None]

    def by_rows(v):
        share = v.shape[1] // n_z
        v = v.reshape(tokens_here, n_z, share)
        return jnp.pad(v, ((0, 0), (0, 0), (0, rows_here - share))).reshape(tokens_here, width)

    d_qo = jnp.concatenate(
        [contract_rows(hidden_one, grad_q_pre), contract_rows(attended, grad_proj)], 1
    )
    d_qo = reduce_end(reduce_start(d_qo), True)
    grad_w_query = d_qo[:, :width]
    grad_w_out = d_qo[:, width:]
    terms = (gain_one_terms, gain_two_terms, grad_q_pre, by_rows(grad_k_pre), by_rows(grad_v_pre))
    pick = jnp.arange(len(terms) * tokens_here)[:, None] // tokens_here == jnp.arange(128)[None]
    columns = contract_rows(
        jnp.concatenate([v.astype(BF16) for v in terms], 0), pick.astype(BF16)
    )
    grad_w_kv = jnp.concatenate([contract_rows(hidden_one, grad_kv_pre), columns], 1)
    grad_w_kv = reduce_end(reduce_start(grad_w_kv), False)
    sums = grad_w_kv[:, 2 * key_width :]
    grad_w_down = spread_rows(share_pieces(ctx_groups_sum(d_down)), piece, ff_z)
    grad_w_gate, grad_w_up = spread_columns(d_gu, n_z, ff, 2)

    return (
        layer_out,
        tokens_grad,
        sums[:, 0],
        grad_w_query,
        sums[:, 2],
        grad_w_kv[:, :key_width],
        sums[:kb, 3],
        grad_w_kv[:, key_width : 2 * key_width],
        sums[:kb, 4],
        grad_w_out,
        sums[:, 1],
        grad_w_gate,
        grad_w_up,
        grad_w_down,
    )


def solution(mesh):
    in_specs = (
        P("seq", ("ctx", "fsdp"), None),
        P("seq", ("ctx", "fsdp"), None),
        P("seq", None),
        P("fsdp"),
        P("fsdp", None),
        P("fsdp"),
        P("fsdp", None),
        P("fsdp"),
        P("fsdp", None),
        P("fsdp"),
        P("fsdp", None),
        P("fsdp"),
        P("fsdp", None),
        P("fsdp", None),
        P("fsdp", None),
    )
    out_specs = (
        P("seq", ("ctx", "fsdp"), None),
        P("seq", ("ctx", "fsdp"), None),
        P("fsdp"),
        P("fsdp", None),
        P("fsdp"),
        P("fsdp", None),
        P("fsdp"),
        P("fsdp", None),
        P("fsdp"),
        P("fsdp", None),
        P("fsdp"),
        P("fsdp", None),
        P("fsdp", None),
        P("fsdp", None),
    )
    return jax.shard_map(local, mesh=mesh, in_specs=in_specs, out_specs=out_specs, check_vma=False)
```

profile of v0, /device:TPU:1, one launch (start us, length us, event | category | flops | bytes accessed | tf_op | source)
XLA Modules:
  0.0 429.0 jit_solution(16949802038817279706)
XLA Ops:
  24.2 3.3 collective-permute-start.1
  28.0 4.6 %collective-permute-start.2 = (bf16[240,256]{1,0:T(8,128)(2,1)S(1)}, bf16[240,256]{1,0:T(8,128)(2,1)S(1)}, u32[]{:S(2)}, u32[]{:S(2)}) collective-permute-start(bf16[240,256]{1,0:T(8,128)(2,1)S(1)} %pad_maximum_fusion.11.refs_0_), channel_id=1, source_target_pairs={{0,3},{1,2},{2,1},{3,0},{4,7},{5,6},{6,5},{7,4},{8,11},{9,10},{10,... | collective-permute-start | bytes 368648 | tf_op jit(solution)/shard_map/ppermute | solution.py:570
  52.9 2.6 collective-permute-start.10
  62.5 6.2 %collective-permute-start.18 = (bf16[4,4,32,896]{3,2,1,0:T(8,128)(2,1)S(1)}, bf16[4,4,32,896]{3,2,1,0:T(8,128)(2,1)S(1)}, u32[]{:S(2)}, u32[]{:S(2)}) collective-permute-start(bf16[4,4,32,896]{3,2,1,0:T(8,128)(2,1)S(1)} %pad_maximum_fusion.4.own_ref), channel_id=1, source_target_pairs={{0,16},{16,0},{1,17},{17,1},{2,18},{18,2},{3,19},{19,3},{4,20},{20... | collective-permute-start | bytes 2752520 | tf_op jit(solution)/shard_map/ppermute | solution.py:560
  75.0 8.1 %collective-permute-done.19 = bf16[768,256]{1,0:T(8,128)(2,1)S(1)} collective-permute-done((bf16[768,256]{1,0:T(8,128)(2,1)S(1)}, bf16[768,256]{1,0:T(8,128)(2,1)S(1)}, u32[]{:S(2)}, u32[]{:S(2)}) %collective-permute-start.19) | collective-permute-done | bytes 393248 | tf_op jit(solution)/shard_map/ppermute | solution.py:565
  83.9 8.5 %collective-permute-done.21 = bf16[768,256]{1,0:T(8,128)(2,1)} collective-permute-done((bf16[768,256]{1,0:T(8,128)(2,1)S(1)}, bf16[768,256]{1,0:T(8,128)(2,1)}, u32[]{:S(2)}, u32[]{:S(2)}) %collective-permute-start.21) | collective-permute-done | bytes 393248 | tf_op jit(solution)/shard_map/ppermute | solution.py:565
  108.0 7.4 %all-gather.3.cloned.1.call-done.refs_8_ = bf16[896,1280]{1,0:T(8,128)(2,1)} async-done(((bf16[224,1280]{1,0:T(8,128)(2,1)}), bf16[896,1280]{1,0:T(8,128)(2,1)}) %all-gather.3.cloned.1.call-update) | async-done | bytes 2293776 | tf_op jit(solution)/shard_map/all_gather | solution.py:573
  117.1 13.0 %attend_forward.1 = (bf16[192,896]{1,0:T(8,128)(2,1)S(1)}, bf16[2688,256]{1,0:T(8,128)(2,1)S(1)}) custom-call(s32[4]{0:T(128)S(1)} %bitcast.197, bf16[192,896]{1,0:T(8,128)(2,1)S(1)} %copy-done.16, bf16[4,768,256]{2,1,0:T(8,128)(2,1)S(1)} %copy-done.6), custom_call_target="tpu_custom_call" | custom-call | flops 8455716864 | bytes 6291456 | tf_op jit(solution)/shard_map/attend_forward/pallas_call | solution.py:255
  132.6 3.6 collective-permute-start.25
  137.2 8.6 %all-gather.5.cloned.1.call-done.refs_10_ = bf16[640,896]{1,0:T(8,128)(2,1)} async-done(((bf16[160,896]{1,0:T(8,128)(2,1)}), bf16[640,896]{1,0:T(8,128)(2,1)}) %all-gather.5.cloned.1.call-update) | async-done | bytes 1146896 | tf_op jit(solution)/shard_map/all_gather | solution.py:573
  155.8 7.0 %collective-permute-done.26.refs_1_ = bf16[192,896]{1,0:T(8,128)(2,1)S(1)} collective-permute-done((bf16[192,896]{1,0:T(8,128)(2,1)S(1)}, bf16[192,896]{1,0:T(8,128)(2,1)S(1)}, u32[]{:S(2)}, u32[]{:S(2)}) %collective-permute-start.26) | collective-permute-done | bytes 344096 | tf_op jit(solution)/shard_map/ppermute | solution.py:565
  162.8 7.1 %collective-permute-done.27.refs_2_ = bf16[192,896]{1,0:T(8,128)(2,1)S(1)} collective-permute-done((bf16[192,896]{1,0:T(8,128)(2,1)S(1)}, bf16[192,896]{1,0:T(8,128)(2,1)S(1)}, u32[]{:S(2)}, u32[]{:S(2)}) %collective-permute-start.27) | collective-permute-done | bytes 344096 | tf_op jit(solution)/shard_map/ppermute | solution.py:565
  172.3 17.7 %ff_pass.1 = (bf16[768,640]{1,0:T(8,128)(2,1)}, bf16[768,640]{1,0:T(8,128)(2,1)}, bf16[768,1280]{1,0:T(8,128)(2,1)}, bf16[768,1280]{1,0:T(8,128)(2,1)}, bf16[192...) custom-call(bf16[192,896]{1,0:T(8,128)(2,1)} %copy-done.46, ...), custom_call_target="tpu_custom_call" | custom-call | flops 8808038400 | bytes 20971520 | tf_op jit(solution)/shard_map/ff_pass/pallas_call | solution.py:509
  190.0 5.6 %convolution_convert_fusion = bf16[896,1280]{1,0:T(8,128)(2,1)} fusion(bf16[768,1280]{1,0:T(8,128)(2,1)} %get-tuple-element.156, bf16[192,896]{1,0:T(8,128)(2,1)} %copy-done.80, bf16[192,896]{1,0:T(8,128)(2,1)} %copy-done.79, bf16[192,896]{1,0:T(8,128)(2,1)} %copy-done.78, bf16[192,896]{1,0:T(8,128)(2,1)} %copy-done.46), kind=kOutput, calls=%fused_computation.6 | convolution fusion | flops 1768259584 | bytes 5636096 | tf_op jit(solution)/shard_map/dot_general | solution.py:49
  208.8 2.9 fusion.65
  214.2 3.5 add_convert_fusion.3
  217.7 6.1 %add_convert_fusion = bf16[896,1280]{1,0:T(8,128)(2,1)} fusion(bf16[896,1280]{1,0:T(8,128)(2,1)} %collective-permute-done.35, bf16[768,1280]{1,0:T(8,128)(2,1)} %get-tuple-element.155, bf16[192,896]{1,0:T(8,128)(2,1)} %copy-done.80, bf16[192,896]{1,0:T(8,128)(2,1)} %copy-done.79, bf16[192,896]{1,0:T(8,128)(2,1)} %copy-done.78, bf16[192,896]{1,0:T(8,128)(2,1)} %copy-done.46), kind=kOutput, calls=%fused_computation.3 | convolution fusion | flops 1770553344 | bytes 7929856 | tf_op jit(solution)/shard_map/dot_general | solution.py:49
  233.6 21.5 %attend_backward.1 = (f32[192,896]{1,0:T(8,128)S(1)}, bf16[4,768,256]{2,1,0:T(8,128)(2,1)S(1)}) custom-call(s32[4]{0:T(128)S(1)} %bitcast.198, bf16[2688,256]{1,0:T(8,128)(2,1)S(1)} %copy-done.20, bf16[192,896]{1,0:T(8,128)(2,1)S(1)} %copy-done.15, bf16[192,896]{1,0:T(8,128)(2,1)S(1)} %get-tuple-element.137.att_ref, bf16[4,768,256]{2,1,0:T(8,128)(2,1)S(1)} %copy-done.7), custom_call_target="tpu_custom_call" | custom-call | flops 21139292160 | bytes 8388608 | tf_op jit(solution)/shard_map/attend_backward/pallas_call | solution.py:287
  265.0 7.4 %collective-permute-start.56 = (bf16[4,128,1792]{2,1,0:T(8,128)(2,1)}, bf16[4,128,1792]{2,1,0:T(8,128)(2,1)}, u32[]{:S(2)}, u32[]{:S(2)}) collective-permute-start(bf16[4,128,1792]{2,1,0:T(8,128)(2,1)} %constant_dynamic-slice_fusion), channel_id=1, source_target_pairs={{0,16},{16,0},{1,17},{17,1},{2,18},{18,2},{3,19},{19,3},{4,20},{20... | collective-permute-start | bytes 5505032 | tf_op jit(solution)/shard_map/ppermute | solution.py:560
  273.4 2.6 collective-permute-start.38
  276.1 2.5 add_convert_fusion.1
  287.1 3.0 collective-permute-done.37
  293.9 29.0 %collective-permute-done.58 = bf16[4,32,1792]{2,1,0:T(8,128)(2,1)} collective-permute-done((bf16[4,32,1792]{2,1,0:T(8,128)(2,1)}, bf16[4,32,1792]{2,1,0:T(8,128)(2,1)}, u32[]{:S(2)}, u32[]{:S(2)}) %collective-permute-start.58) | collective-permute-done | bytes 458784 | tf_op jit(solution)/shard_map/ppermute | solution.py:570
  332.6 4.2 collective-permute-done.43
  361.2 3.5 collective-permute-done.68
  364.7 2.9 collective-permute-done.67
  369.1 3.7 collective-permute-start.70
  378.2 2.5 collective-permute-done.47
  386.8 4.1 collective-permute-done.50
  396.5 3.7 collective-permute-done.72
  409.8 8.6 %spread_columns.1 = (f32[224,4864]{1,0:T(8,128)}, f32[224,4864]{1,0:T(8,128)}) custom-call(bf16[4,224,1280]{2,1,0:T(8,128)(2,1)S(1)} %copy-done.3, bf16[4,224,1280]{2,1,0:T(8,128)(2,1)} %collective-permute-done.70.refs_1_), custom_call_target="tpu_custom_call" | custom-call | bytes 13074432 | tf_op jit(solution)/shard_map/spread_columns/pallas_call | solution.py:350
  418.4 3.8 spread_rows.5
  (431 shorter events, 194.3 us)
Async XLA Ops:
  7.2 108.2 %all-gather.3.cloned.1.call-start = ((), (), s32[]{:S(2)}) async-start(), calls=%async_computation.2 | async-start | bytes 2867200 | tf_op jit(solution)/shard_map/all_gather | solution.py:573
  16.9 18.0 %collective-permute-start.6 = (bf16[192,896]{1,0:T(8,128)(2,1)}, bf16[192,896]{1,0:T(8,128)(2,1)}, u32[]{:S(2)}, u32[]{:S(2)}) collective-permute-start(bf16[192,896]{1,0:T(8,128)(2,1)} %bitcast.212), channel_id=1, source_target_pairs={{0,4},{4,0},{8,12},{12,8},{1,5},{5,1},{9,13},{13,9},{2,6},{6,2},{1... | collective-permute-start | bytes 1032200 | tf_op jit(solution)/shard_map/ppermute | solution.py:565
  18.1 16.7 %collective-permute-start.7 = (bf16[192,896]{1,0:T(8,128)(2,1)}, bf16[192,896]{1,0:T(8,128)(2,1)}, u32[]{:S(2)}, u32[]{:S(2)}) collective-permute-start(bf16[192,896]{1,0:T(8,128)(2,1)} %bitcast.213), channel_id=1, source_target_pairs={{0,8},{4,12},{8,0},{12,4},{1,9},{5,13},{9,1},{13,5},{2,10},{6,14},... | collective-permute-start | bytes 1032200 | tf_op jit(solution)/shard_map/ppermute | solution.py:565
  42.4 18.8 %collective-permute-start.15 = (bf16[4,32,896]{2,1,0:T(8,128)(2,1)S(1)}, bf16[4,32,896]{2,1,0:T(8,128)(2,1)}, u32[]{:S(2)}, u32[]{:S(2)}) collective-permute-start(bf16[4,32,896]{2,1,0:T(8,128)(2,1)S(1)} %pad_maximum_fusion.9), channel_id=1, source_target_pairs={{0,4},{4,0},{8,12},{12,8},{1,5},{5,1},{9,13},{13,9},{2,6},{6,2},{1... | collective-permute-start | bytes 688136 | tf_op jit(solution)/shard_map/ppermute | solution.py:565
  43.5 17.6 %collective-permute-start.16 = (bf16[4,32,896]{2,1,0:T(8,128)(2,1)S(1)}, bf16[4,32,896]{2,1,0:T(8,128)(2,1)}, u32[]{:S(2)}, u32[]{:S(2)}) collective-permute-start(bf16[4,32,896]{2,1,0:T(8,128)(2,1)S(1)} %pad_maximum_fusion.9), channel_id=1, source_target_pairs={{0,8},{4,12},{8,0},{12,4},{1,9},{5,13},{9,1},{13,5},{2,10},{6,14},... | collective-permute-start | bytes 688136 | tf_op jit(solution)/shard_map/ppermute | solution.py:565
  61.2 84.6 %all-gather.5.cloned.1.call-start = ((), (), s32[]{:S(2)}) async-start(), calls=%async_computation.3 | async-start | bytes 1433600 | tf_op jit(solution)/shard_map/all_gather | solution.py:573
  62.5 36.6 %collective-permute-start.18 = (bf16[4,4,32,896]{3,2,1,0:T(8,128)(2,1)S(1)}, bf16[4,4,32,896]{3,2,1,0:T(8,128)(2,1)S(1)}, u32[]{:S(2)}, u32[]{:S(2)}) collective-permute-start(bf16[4,4,32,896]{3,2,1,0:T(8,128)(2,1)S(1)} %pad_maximum_fusion.4.own_ref), channel_id=1, source_target_pairs={{0,16},{16,0},{1,17},{17,1},{2,18},{18,2},{3,19},{19,3},{4,20},{20... | collective-permute-start | bytes 2752520 | tf_op jit(solution)/shard_map/ppermute | solution.py:560
  74.6 17.8 %collective-permute-start.21 = (bf16[768,256]{1,0:T(8,128)(2,1)S(1)}, bf16[768,256]{1,0:T(8,128)(2,1)}, u32[]{:S(2)}, u32[]{:S(2)}) collective-permute-start(bf16[768,256]{1,0:T(8,128)(2,1)S(1)} %constant_dynamic-update-slice_fusion), channel_id=1, source_target_pairs={{0,12},{4,8},{8,4},{12,0},{1,13},{5,9},{9,5},{13,1},{2,14},{6,10},... | collective-permute-start | bytes 1179656 | tf_op jit(solution)/shard_map/ppermute | solution.py:565
  75.0 215.1 %reduce-scatter.3.cloned.1.call-start = ((), (), s32[]{:S(2)}) async-start(), calls=%async_computation.4 | async-start | bytes 2867200 | tf_op jit(solution)/shard_map/reduce_scatter | solution.py:576
  94.0 37.2 %collective-permute-start.22 = (bf16[4,32,896]{2,1,0:T(8,128)(2,1)}, bf16[4,32,896]{2,1,0:T(8,128)(2,1)}, u32[]{:S(2)}, u32[]{:S(2)}) collective-permute-start(bf16[4,32,896]{2,1,0:T(8,128)(2,1)} %pad_maximum_fusion.10), channel_id=1, source_target_pairs={{0,4},{4,0},{8,12},{12,8},{1,5},{5,1},{9,13},{13,9},{2,6},{6,2},{1... | collective-permute-start | bytes 688136 | tf_op jit(solution)/shard_map/ppermute | solution.py:565
  95.2 36.0 %collective-permute-start.23 = (bf16[4,32,896]{2,1,0:T(8,128)(2,1)}, bf16[4,32,896]{2,1,0:T(8,128)(2,1)}, u32[]{:S(2)}, u32[]{:S(2)}) collective-permute-start(bf16[4,32,896]{2,1,0:T(8,128)(2,1)} %pad_maximum_fusion.10), channel_id=1, source_target_pairs={{0,8},{4,12},{8,0},{12,4},{1,9},{5,13},{9,1},{13,5},{2,10},{6,14},... | collective-permute-start | bytes 688136 | tf_op jit(solution)/shard_map/ppermute | solution.py:565
  95.5 35.7 %collective-permute-start.24 = (bf16[4,32,896]{2,1,0:T(8,128)(2,1)}, bf16[4,32,896]{2,1,0:T(8,128)(2,1)}, u32[]{:S(2)}, u32[]{:S(2)}) collective-permute-start(bf16[4,32,896]{2,1,0:T(8,128)(2,1)} %pad_maximum_fusion.10), channel_id=1, source_target_pairs={{0,12},{4,8},{8,4},{12,0},{1,13},{5,9},{9,5},{13,1},{2,14},{6,10},... | collective-permute-start | bytes 688136 | tf_op jit(solution)/shard_map/ppermute | solution.py:565
  115.4 55.8 %collective-permute-start.29 = (bf16[896,1280]{1,0:T(8,128)(2,1)}, bf16[896,1280]{1,0:T(8,128)(2,1)}, u32[]{:S(2)}, u32[]{:S(2)}) collective-permute-start(bf16[896,1280]{1,0:T(8,128)(2,1)} %all-gather.3.cloned.1.call-done.refs_8_), channel_id=1, source_target_pairs={{0,16},{16,0},{1,17},{17,1},{2,18},{18,2},{3,19},{19,3},{4,20},{20... | collective-permute-start | bytes 6881288 | tf_op jit(solution)/shard_map/ppermute | solution.py:560
  145.7 25.4 %collective-permute-start.30 = (bf16[640,896]{1,0:T(8,128)(2,1)}, bf16[640,896]{1,0:T(8,128)(2,1)S(1)}, u32[]{:S(2)}, u32[]{:S(2)}) collective-permute-start(bf16[640,896]{1,0:T(8,128)(2,1)} %all-gather.5.cloned.1.call-done.refs_10_), channel_id=1, source_target_pairs={{0,16},{16,0},{1,17},{17,1},{2,18},{18,2},{3,19},{19,3},{4,20},{20... | collective-permute-start | bytes 3440648 | tf_op jit(solution)/shard_map/ppermute | solution.py:560
  195.7 22.0 %collective-permute-start.35 = (bf16[896,1280]{1,0:T(8,128)(2,1)}, bf16[896,1280]{1,0:T(8,128)(2,1)}, u32[]{:S(2)}, u32[]{:S(2)}) collective-permute-start(bf16[896,1280]{1,0:T(8,128)(2,1)} %convolution_convert_fusion), channel_id=1, source_target_pairs={{0,16},{16,0},{1,17},{17,1},{2,18},{18,2},{3,19},{19,3},{4,20},{20... | collective-permute-start | bytes 6881288 | tf_op jit(solution)/shard_map/ppermute | solution.py:560
  206.2 17.6 %collective-permute-start.31 = (bf16[192,896]{1,0:T(8,128)(2,1)}, bf16[192,896]{1,0:T(8,128)(2,1)}, u32[]{:S(2)}, u32[]{:S(2)}) collective-permute-start(bf16[192,896]{1,0:T(8,128)(2,1)} %get-tuple-element.150), channel_id=1, source_target_pairs={{0,4},{4,0},{8,12},{12,8},{1,5},{5,1},{9,13},{13,9},{2,6},{6,2},{1... | collective-permute-start | bytes 1032200 | tf_op jit(solution)/shard_map/ppermute | solution.py:565
  207.0 16.7 %collective-permute-start.32 = (bf16[192,896]{1,0:T(8,128)(2,1)}, bf16[192,896]{1,0:T(8,128)(2,1)}, u32[]{:S(2)}, u32[]{:S(2)}) collective-permute-start(bf16[192,896]{1,0:T(8,128)(2,1)} %get-tuple-element.151), channel_id=1, source_target_pairs={{0,8},{4,12},{8,0},{12,4},{1,9},{5,13},{9,1},{13,5},{2,10},{6,14},... | collective-permute-start | bytes 1032200 | tf_op jit(solution)/shard_map/ppermute | solution.py:565
  229.9 154.0 %reduce-scatter.5.cloned.1.call-start = ((), (), s32[]{:S(2)}) async-start(), calls=%async_computation.5 | async-start | bytes 1433600 | tf_op jit(solution)/shard_map/reduce_scatter | solution.py:576
  273.4 16.7 %collective-permute-start.37 = (bf16[192,896]{1,0:T(8,128)(2,1)}, bf16[192,896]{1,0:T(8,128)(2,1)}, u32[]{:S(2)}, u32[]{:S(2)}) collective-permute-start(bf16[192,896]{1,0:T(8,128)(2,1)} %get-tuple-element.206), channel_id=1, source_target_pairs={{0,8},{4,12},{8,0},{12,4},{1,9},{5,13},{9,1},{13,5},{2,10},{6,14},... | collective-permute-start | bytes 1032200 | tf_op jit(solution)/shard_map/ppermute | solution.py:565
  282.5 40.4 %collective-permute-start.58 = (bf16[4,32,1792]{2,1,0:T(8,128)(2,1)}, bf16[4,32,1792]{2,1,0:T(8,128)(2,1)}, u32[]{:S(2)}, u32[]{:S(2)}) collective-permute-start(bf16[4,32,1792]{2,1,0:T(8,128)(2,1)} %get-tuple-element.198), channel_id=1, source_target_pairs={{0,2},{1,3},{2,0},{3,1},{4,6},{5,7},{6,4},{7,5},{8,10},{9,11},{10,... | collective-permute-start | bytes 1376264 | tf_op jit(solution)/shard_map/ppermute | solution.py:570
  283.2 39.7 %collective-permute-start.57 = (bf16[4,32,1792]{2,1,0:T(8,128)(2,1)}, bf16[4,32,1792]{2,1,0:T(8,128)(2,1)}, u32[]{:S(2)}, u32[]{:S(2)}) collective-permute-start(bf16[4,32,1792]{2,1,0:T(8,128)(2,1)} %get-tuple-element.196), channel_id=1, source_target_pairs={{0,1},{1,0},{2,3},{3,2},{4,5},{5,4},{6,7},{7,6},{8,9},{9,8},{10,11... | collective-permute-start | bytes 1376264 | tf_op jit(solution)/shard_map/ppermute | solution.py:570
  290.2 34.3 %collective-permute-start.39 = (bf16[768,256]{1,0:T(8,128)(2,1)S(1)}, bf16[768,256]{1,0:T(8,128)(2,1)S(1)}, u32[]{:S(2)}, u32[]{:S(2)}) collective-permute-start(bf16[768,256]{1,0:T(8,128)(2,1)S(1)} %get-tuple-element.203), channel_id=1, source_target_pairs={{0,4},{4,0},{8,12},{12,8},{1,5},{5,1},{9,13},{13,9},{2,6},{6,2},{1... | collective-permute-start | bytes 1179656 | tf_op jit(solution)/shard_map/ppermute | solution.py:565
  291.7 32.9 %collective-permute-start.40 = (bf16[768,256]{1,0:T(8,128)(2,1)S(1)}, bf16[768,256]{1,0:T(8,128)(2,1)S(1)}, u32[]{:S(2)}, u32[]{:S(2)}) collective-permute-start(bf16[768,256]{1,0:T(8,128)(2,1)S(1)} %get-tuple-element.202), channel_id=1, source_target_pairs={{0,8},{4,12},{8,0},{12,4},{1,9},{5,13},{9,1},{13,5},{2,10},{6,14},... | collective-permute-start | bytes 1179656 | tf_op jit(solution)/shard_map/ppermute | solution.py:565
  293.8 30.7 %collective-permute-start.41 = (bf16[768,256]{1,0:T(8,128)(2,1)S(1)}, bf16[768,256]{1,0:T(8,128)(2,1)S(1)}, u32[]{:S(2)}, u32[]{:S(2)}) collective-permute-start(bf16[768,256]{1,0:T(8,128)(2,1)S(1)} %get-tuple-element.201), channel_id=1, source_target_pairs={{0,12},{4,8},{8,4},{12,0},{1,13},{5,9},{9,5},{13,1},{2,14},{6,10},... | collective-permute-start | bytes 1179656 | tf_op jit(solution)/shard_map/ppermute | solution.py:565
  329.8 23.7 %collective-permute-start.62 = (bf16[32,1792]{1,0:T(8,128)(2,1)}, bf16[32,1792]{1,0:T(8,128)(2,1)}, u32[]{:S(2)}, u32[]{:S(2)}) collective-permute-start(bf16[32,1792]{1,0:T(8,128)(2,1)} %get-tuple-element.214), channel_id=1, source_target_pairs={{0,12},{4,8},{8,4},{12,0},{1,13},{5,9},{9,5},{13,1},{2,14},{6,10},... | collective-permute-start | bytes 344072 | tf_op jit(solution)/shard_map/ppermute | solution.py:565
  329.8 25.8 %collective-permute-start.61 = (bf16[32,1792]{1,0:T(8,128)(2,1)}, bf16[32,1792]{1,0:T(8,128)(2,1)}, u32[]{:S(2)}, u32[]{:S(2)}) collective-permute-start(bf16[32,1792]{1,0:T(8,128)(2,1)} %get-tuple-element.215), channel_id=1, source_target_pairs={{0,8},{4,12},{8,0},{12,4},{1,9},{5,13},{9,1},{13,5},{2,10},{6,14},... | collective-permute-start | bytes 344072 | tf_op jit(solution)/shard_map/ppermute | solution.py:565
  331.2 25.9 %collective-permute-start.60 = (bf16[32,1792]{1,0:T(8,128)(2,1)}, bf16[32,1792]{1,0:T(8,128)(2,1)}, u32[]{:S(2)}, u32[]{:S(2)}) collective-permute-start(bf16[32,1792]{1,0:T(8,128)(2,1)} %get-tuple-element.213), channel_id=1, source_target_pairs={{0,4},{4,0},{8,12},{12,8},{1,5},{5,1},{9,13},{13,9},{2,6},{6,2},{1... | collective-permute-start | bytes 344072 | tf_op jit(solution)/shard_map/ppermute | solution.py:565
  336.9 22.7 %collective-permute-start.69 = (bf16[224,1280]{1,0:T(8,128)(2,1)}, bf16[224,1280]{1,0:T(8,128)(2,1)}, u32[]{:S(2)}, u32[]{:S(2)}) collective-permute-start(bf16[224,1280]{1,0:T(8,128)(2,1)} %reduce-scatter.3.cloned.1.call-done), channel_id=1, source_target_pairs={{0,12},{4,8},{8,4},{12,0},{1,13},{5,9},{9,5},{13,1},{2,14},{6,10},... | collective-permute-start | bytes 1720328 | tf_op jit(solution)/shard_map/ppermute | solution.py:565
  337.5 27.2 %collective-permute-start.68 = (bf16[224,1280]{1,0:T(8,128)(2,1)}, bf16[224,1280]{1,0:T(8,128)(2,1)}, u32[]{:S(2)}, u32[]{:S(2)}) collective-permute-start(bf16[224,1280]{1,0:T(8,128)(2,1)} %reduce-scatter.3.cloned.1.call-done), channel_id=1, source_target_pairs={{0,8},{4,12},{8,0},{12,4},{1,9},{5,13},{9,1},{13,5},{2,10},{6,14},... | collective-permute-start | bytes 1720328 | tf_op jit(solution)/shard_map/ppermute | solution.py:565
  358.7 17.0 %collective-permute-start.64 = (bf16[32,1792]{1,0:T(8,128)(2,1)S(1)}, bf16[32,1792]{1,0:T(8,128)(2,1)S(1)}, u32[]{:S(2)}, u32[]{:S(2)}) collective-permute-start(bf16[32,1792]{1,0:T(8,128)(2,1)S(1)} %fusion.37), channel_id=1, source_target_pairs={{0,8},{4,12},{8,0},{12,4},{1,9},{5,13},{9,1},{13,5},{2,10},{6,14},... | collective-permute-start | bytes 344072 | tf_op jit(solution)/shard_map/ppermute | solution.py:565
  369.1 40.6 %collective-permute-start.70 = (bf16[4,224,1280]{2,1,0:T(8,128)(2,1)S(1)}, bf16[4,224,1280]{2,1,0:T(8,128)(2,1)}, u32[]{:S(2)}, u32[]{:S(2)}) collective-permute-start(bf16[4,224,1280]{2,1,0:T(8,128)(2,1)S(1)} %pad_maximum_fusion.refs_0_), channel_id=1, source_target_pairs={{0,16},{16,0},{1,17},{17,1},{2,18},{18,2},{3,19},{19,3},{4,20},{20... | collective-permute-start | bytes 6881288 | tf_op jit(solution)/shard_map/ppermute | solution.py:560
  400.7 17.8 %collective-permute-start.74 = (bf16[4,160,896]{2,1,0:T(8,128)(2,1)S(1)}, bf16[4,160,896]{2,1,0:T(8,128)(2,1)S(1)}, u32[]{:S(2)}, u32[]{:S(2)}) collective-permute-start(bf16[4,160,896]{2,1,0:T(8,128)(2,1)S(1)} %pad_maximum_fusion.3.refs_0_), channel_id=1, source_target_pairs={{0,16},{16,0},{1,17},{17,1},{2,18},{18,2},{3,19},{19,3},{4,20},{20... | collective-permute-start | bytes 3440648 | tf_op jit(solution)/shard_map/ppermute | solution.py:560
  (130 other events, 972.2 us)
Sparse Core Ops, SparseCore 0:
  61.3 54.0 all-gather.2
  117.5 28.1 all-gather.4
  230.0 46.2 reduce-scatter.2
  331.1 29.8 reduce-scatter.4
where the time goes:
time: 436 us; the launch traced here: 429 us
  waiting for transfers between devices  111 us (25%)
  starting transfers between devices  93.6 us (21%)
  Pallas kernels  68.6 us (16%)
  local copies, waits for them, and re-layouts  66.6 us (15%)
  other arithmetic  39.4 us (9%)
  matrix products  33.8 us (8%)
  between operations  15.9 us (4%)
    ppermute x42, waiting for transfers between devices, hop(): return lax.ppermute(v, 'ctx', [(i, i ^ k) for i in range(n_ctx)])  50.2 us
    ppermute x21, waiting for transfers between devices, hop_z(): return lax.ppermute(v, 'fsdp', [(i, i ^ k) for i in range(n_z)])  44.7 us
    ppermute x42, starting transfers between devices, hop(): return lax.ppermute(v, 'ctx', [(i, i ^ k) for i in range(n_ctx)])  35.1 us
    ppermute x21, starting transfers between devices, hop_z(): return lax.ppermute(v, 'fsdp', [(i, i ^ k) for i in range(n_z)])  29.5 us
    ppermute x12, starting transfers between devices, swap(): return lax.ppermute(v, 'seq', [(0, 1), (1, 0)])  28.9 us
    unnamed x174, local copies, waits for them, and re-layouts  27.3 us
    pallas_call x1, Pallas kernels, attend_backward(): pl.pallas_call(functools.partial(backward_kernel, by_xor), grid_spec=pltp...  21.5 us
    dot_general x8, matrix products, contract_rows(): lax.dot_general(left_side, right_side, (((0,), (0,)), ((), ())), preferre...  21.5 us
  transfers between devices with their start and end apart: 79, of which 26 were waited for; matrix products, arithmetic and copies ran while one was open for 23% of the time, Pallas kernels for 11%

commit v1 on v0

--- a/solution.py
+++ b/solution.py
@@ -17,6 +17,7 @@
 MASKED = -1e30
 BF16 = jnp.bfloat16
 F32 = jnp.float32
+NO_COST = pl.CostEstimate(flops=0, bytes_accessed=0, transcendentals=0)
 
 
 def rope_tables(positions, head_dim):
@@ -55,12 +56,6 @@
     return lax.dot_general(
         left_side, right_side, (((1,), (1,)), ((), ())), preferred_element_type=F32
     )
-
-
-def rms_forward(values, gain_vec):
-    inv_scale = lax.rsqrt(jnp.mean(values * values, -1, keepdims=True) + NORM_EPS)
-    normed = values * inv_scale
-    return (normed, inv_scale, (normed * gain_vec).astype(BF16))
 
 
 def rms_backward(grad_out, normed, inv_scale, gain_vec):
@@ -271,11 +266,7 @@
         compiler_params=pltpu.CompilerParams(
             dimension_semantics=("arbitrary",), vmem_limit_bytes=40 * 2**20
         ),
-        cost_estimate=pl.CostEstimate(
-            flops=4 * rows * blocks * block_len * 256,
-            bytes_accessed=6 * 2**20,
-            transcendentals=rows * blocks * block_len,
-        ),
+        cost_estimate=NO_COST,
         name="attend_forward",
     )(info, queries, kv)
 
@@ -311,11 +302,7 @@
         compiler_params=pltpu.CompilerParams(
             dimension_semantics=("arbitrary",), vmem_limit_bytes=40 * 2**20
         ),
-        cost_estimate=pl.CostEstimate(
-            flops=10 * rows * blocks * block_len * 256,
-            bytes_accessed=8 * 2**20,
-            transcendentals=rows * blocks * block_len,
-        ),
+        cost_estimate=NO_COST,
         name="attend_backward",
     )(info, queries_ext, grad_att, attended, kv)
 
@@ -357,9 +344,7 @@
         compiler_params=pltpu.CompilerParams(
             dimension_semantics=("arbitrary",), vmem_limit_bytes=40 * 2**20
         ),
-        cost_estimate=pl.CostEstimate(
-            flops=0, bytes_accessed=rows * ff * 6 * outs, transcendentals=0
-        ),
+        cost_estimate=NO_COST,
         name="spread_columns",
     )(*pieces)
 
@@ -390,14 +375,12 @@
         compiler_params=pltpu.CompilerParams(
             dimension_semantics=("arbitrary",), vmem_limit_bytes=40 * 2**20
         ),
-        cost_estimate=pl.CostEstimate(
-            flops=0, bytes_accessed=rows_out * cols * 6, transcendentals=0
-        ),
+        cost_estimate=NO_COST,
         name="spread_rows",
     )(*pieces)
 
 
-def join_weight_kernel(own_ref, sib_ref, out_ref):
+def join_weight(own_ref, sib_ref, out_ref):
     tp, n_z, part_rows = own_ref.shape[:3]
     room = out_ref.shape[1] // part_rows
     for j, ref in enumerate((own_ref, sib_ref)):
@@ -412,23 +395,24 @@
                     out_ref[at, pl.ds(start, part_rows), :] = ref[k, z]
 
 
-def join_weight(own, sib, rows_here):
-    tp, n_z, part_rows, cols = own.shape
-    return pl.pallas_call(
-        join_weight_kernel,
-        in_specs=[pl.BlockSpec(memory_space=pltpu.VMEM)] * 2,
-        out_specs=pl.BlockSpec(memory_space=pltpu.VMEM),
-        out_shape=jax.ShapeDtypeStruct((n_z, rows_here, cols), BF16),
-        compiler_params=pltpu.CompilerParams(vmem_limit_bytes=40 * 2**20),
-        cost_estimate=pl.CostEstimate(
-            flops=0, bytes_accessed=4 * n_z * rows_here * cols, transcendentals=0
-        ),
-        name="join_weight",
-    )(own, sib).reshape(n_z * rows_here, cols)
-
-
-def join_kv_kernel(widths, *refs):
-    pieces, (out_ref, vec_ref, held) = refs[:-3], refs[-3:]
+def whole_weight(ref):
+    return jnp.concatenate([ref[z] for z in range(ref.shape[0])], 0)
+
+
+def turn_tile(tile, cos, sin):
+    h = HEAD // 2
+    cuts = [tile[:, h : 2 * h], tile[:, :h], tile[:, 3 * h :], tile[:, 2 * h : 3 * h]]
+    return tile * cos + jnp.concatenate(cuts, 1) * sin
+
+
+def normed_rows(values, gain):
+    inv = lax.rsqrt(jnp.mean(values * values, -1, keepdims=True) + NORM_EPS)
+    return (values * inv * gain).astype(BF16)
+
+
+def kv_kernel(widths, *refs):
+    x_ref, cos_ref, sin_ref = refs[-8:-5]
+    pieces, (out_ref, vec_ref, kv_ref, hid_ref, held) = refs[:-8], refs[-5:]
     n_z, rows_here, cols = out_ref.shape
     for k in range(n_z):
         at = jnp.bitwise_xor(lax.axis_index("fsdp"), k)
@@ -438,53 +422,163 @@
     for i, size in enumerate(widths):
         row = jnp.concatenate([held[z, i : i + 1, :size] for z in range(n_z)], 1)
         vec_ref[i : i + 1, : n_z * size] = row
-
-
-def join_kv(pieces, rows_here, widths):
+    hidden = normed_rows(x_ref[...].astype(F32), vec_ref[0:1, :])
+    hid_ref[...] = hidden
+    half = cols // 2
+    both = matmul(hidden, whole_weight(out_ref))
+    keys = both[:, :half] + vec_ref[3:4, :half]
+    kv_ref[:, :half] = turn_tile(keys, cos_ref[...], sin_ref[...]).astype(BF16)
+    kv_ref[:, half:] = (both[:, half:] + vec_ref[4:5, :half]).astype(BF16)
+
+
+def project_kv(pieces, tokens, cos, sin, rows_here, widths):
     rows, cols = pieces[0].shape
     n_z = len(pieces)
+    vmem = pl.BlockSpec(memory_space=pltpu.VMEM)
     return pl.pallas_call(
-        functools.partial(join_kv_kernel, widths),
-        in_specs=[pl.BlockSpec(memory_space=pltpu.VMEM)] * n_z,
-        out_specs=[pl.BlockSpec(memory_space=pltpu.VMEM)] * 2,
+        functools.partial(kv_kernel, widths),
+        in_specs=[vmem] * (n_z + 3),
+        out_specs=[vmem] * 4,
         out_shape=[
             jax.ShapeDtypeStruct((n_z, rows_here, cols), BF16),
             jax.ShapeDtypeStruct((8, n_z * rows_here), F32),
+            jax.ShapeDtypeStruct((tokens.shape[0], cols), BF16),
+            jax.ShapeDtypeStruct(tokens.shape, BF16),
         ],
         scratch_shapes=[pltpu.VMEM((n_z, rows - rows_here, cols), F32)],
         compiler_params=pltpu.CompilerParams(vmem_limit_bytes=40 * 2**20),
-        name="join_kv",
-    )(*pieces)
-
-
-def ff_kernel(tp, *refs):
+        cost_estimate=NO_COST,
+        name="project_kv",
+    )(*pieces, tokens, cos, sin)
+
+
+def query_kernel(own_ref, sib_ref, hid_ref, vec_ref, cos_ref, sin_ref, out_ref, q_ref):
+    join_weight(own_ref, sib_ref, out_ref)
+    whole = matmul(hid_ref[...], whole_weight(out_ref)) + vec_ref[2:3, :]
+    for pair in range(HEADS // 2):
+        lanes = slice(pair * 128, (pair + 1) * 128)
+        tile = turn_tile(whole[:, lanes], cos_ref[...], sin_ref[...]).astype(BF16)
+        q_ref[:, lanes] = (tile.astype(F32) * HEAD ** (-0.5)).astype(BF16)
+
+
+def project_query(own, sib, hidden, vecs, cos, sin, rows_here):
+    n_z, cols = own.shape[1], own.shape[3]
+    vmem = pl.BlockSpec(memory_space=pltpu.VMEM)
+    return pl.pallas_call(
+        query_kernel,
+        in_specs=[vmem] * 6,
+        out_specs=[vmem] * 2,
+        out_shape=[
+            jax.ShapeDtypeStruct((n_z, rows_here, cols), BF16),
+            jax.ShapeDtypeStruct((hidden.shape[0], cols), BF16),
+        ],
+        compiler_params=pltpu.CompilerParams(vmem_limit_bytes=40 * 2**20),
+        cost_estimate=NO_COST,
+        name="project_query",
+    )(own, sib, hidden, vecs, cos, sin)
+
+
+def out_kernel(own_ref, sib_ref, att_ref, x_ref, vec_ref, out_ref, resid_ref, hid_ref):
+    join_weight(own_ref, sib_ref, out_ref)
+    resid = x_ref[...].astype(F32) + matmul(att_ref[...], whole_weight(out_ref))
+    resid_ref[...] = resid
+    hid_ref[...] = normed_rows(resid, vec_ref[1:2, :])
+
+
+def project_out(own, sib, attended, tokens, vecs, rows_here):
+    n_z, cols = own.shape[1], own.shape[3]
+    vmem = pl.BlockSpec(memory_space=pltpu.VMEM)
+    return pl.pallas_call(
+        out_kernel,
+        in_specs=[vmem] * 5,
+        out_specs=[vmem] * 3,
+        out_shape=[
+            jax.ShapeDtypeStruct((n_z, rows_here, cols), BF16),
+            jax.ShapeDtypeStruct(tokens.shape, F32),
+            jax.ShapeDtypeStruct(tokens.shape, BF16),
+        ],
+        compiler_params=pltpu.CompilerParams(vmem_limit_bytes=40 * 2**20),
+        cost_estimate=NO_COST,
+        name="project_out",
+    )(own, sib, attended, tokens, vecs)
+
+
+def grad_weight_kernel(left_ref, right_ref, *refs):
+    total = matmul(left_ref[...], right_ref[...])
+    if len(refs) == 2:
+        total = total + refs[0][...].astype(F32)
+    refs[-1][...] = total.astype(BF16)
+
+
+def grad_weight(left, right, other=None):
+    rows, depth = left.shape
+    cols = right.shape[1]
+    tile = 128
+    by_rows = lambda width: pl.BlockSpec((tile, width), lambda i: (i, 0))
+    in_specs = [by_rows(depth), pl.BlockSpec((depth, cols), lambda i: (0, 0))]
+    args = [left, right]
+    if other is not None:
+        in_specs.append(by_rows(cols))
+        args.append(other)
+    return pl.pallas_call(
+        grad_weight_kernel,
+        grid=(rows // tile,),
+        in_specs=in_specs,
+        out_specs=by_rows(cols),
+        out_shape=jax.ShapeDtypeStruct((rows, cols), BF16),
+        compiler_params=pltpu.CompilerParams(
+            dimension_semantics=("arbitrary",), vmem_limit_bytes=40 * 2**20
+        ),
+        cost_estimate=NO_COST,
+        name="grad_weight",
+    )(*args)
+
+
+def ff_kernel(tp, n_z, *refs):
     hidden, grads, weights = refs[:tp], refs[tp : 2 * tp], refs[2 * tp : 2 * tp + 4]
-    act_refs, back_refs = refs[2 * tp + 4 : 2 * tp + 6], refs[2 * tp + 6 : 2 * tp + 8]
-    outs = refs[2 * tp + 8 : 3 * tp + 8]
-    gu_buf, down_buf, acc, sems = refs[3 * tp + 8 :]
-    copies = [
-        pltpu.make_async_copy(weights[i], (gu_buf if i < 2 else down_buf).at[i % 2], sems.at[i])
-        for i in range(4)
+    rest = refs[2 * tp + 4 :]
+    act_refs, back_refs, (hid_t, grad_all) = rest[:2], rest[2:4], rest[4:6]
+    dh_outs, outs = rest[6 : 6 + tp], rest[6 + tp : 6 + 2 * tp]
+    gu_buf, down_buf, acc, acc_out, sems = rest[6 + 2 * tp :]
+    part_rows = weights[2].shape[1]
+    gu_copies = [
+        pltpu.make_async_copy(weights[i], gu_buf.at[i], sems.at[i]) for i in range(2)
     ]
-    for i in (0, 2, 1, 3):
-        copies[i].start()
+    down_copies = []
+    for i in range(2):
+        for z in range(n_z):
+            at = jnp.bitwise_xor(lax.axis_index("fsdp"), z) * part_rows
+            to = down_buf.at[i, pl.ds(pl.multiple_of(at, 16), part_rows)]
+            sem = sems.at[2 + i * n_z + z]
+            down_copies.append(pltpu.make_async_copy(weights[2 + i].at[z], to, sem))
+    gu_copies[0].start()
+    for c in down_copies[:n_z]:
+        c.start()
+    gu_copies[1].start()
+    for c in down_copies[n_z:]:
+        c.start()
     tokens_here = hidden[0].shape[0]
     half = down_buf.shape[1]
     step = 2 if tp % 2 == 0 else 1
     for i in range(2):
-        copies[i].wait()
+        gu_copies[i].wait()
         for t in range(0, tp, step):
             rows = slice(t * tokens_here, (t + step) * tokens_here)
             here = jnp.concatenate([hidden[t + n][...] for n in range(step)], 0)
             grad = jnp.concatenate([grads[t + n][...] for n in range(step)], 0)
+            if i == 0:
+                hid_t[:, rows] = here.astype(F32).T.astype(BF16)
+                grad_all[rows, :] = grad
             gate = matmul(here, gu_buf[i, :, :half])
             up = matmul(here, gu_buf[i, :, half:])
             if t == 0:
-                copies[2 + i].wait()
+                for c in down_copies[i * n_z : (i + 1) * n_z]:
+                    c.wait()
             grad_act = times_transposed(grad, down_buf[i])
             sig = 1.0 / (1.0 + jnp.exp(-gate))
             silu = gate * sig
-            act_refs[i][rows, :] = (silu * up).astype(BF16)
+            act = silu * up
+            act_refs[i][:, rows] = act.T.astype(BF16)
             grad_gate = (grad_act * up * (sig + silu * (1.0 - sig))).astype(BF16)
             grad_up = (grad_act * silu).astype(BF16)
             back_refs[i][rows, :half] = grad_gate
@@ -492,42 +586,46 @@
             part = times_transposed(grad_gate, gu_buf[i, :, :half]) + times_transposed(
                 grad_up, gu_buf[i, :, half:]
             )
+            out = matmul(act.astype(BF16), down_buf[i])
             if i == 0:
                 acc[rows, :] = part
+                acc_out[rows, :] = out
             else:
                 part = (part + acc[rows, :]).astype(BF16)
+                out = (out + acc_out[rows, :]).astype(BF16)
                 for n in range(step):
-                    outs[t + n][...] = part[n * tokens_here : (n + 1) * tokens_here]
+                    mine = slice(n * tokens_here, (n + 1) * tokens_here)
+                    dh_outs[t + n][...] = part[mine]
+                    outs[t + n][...] = out[mine]
 
 
 def ff_pass(hidden, grads, gu, down):
     tp = len(hidden)
+    n_z, part_rows = down[0].shape[:2]
     tokens_here, width = hidden[0].shape
-    half = down[0].shape[0]
+    half = n_z * part_rows
     rows = tp * tokens_here
     vmem = pl.BlockSpec(memory_space=pltpu.VMEM)
     got = pl.pallas_call(
-        functools.partial(ff_kernel, tp),
+        functools.partial(ff_kernel, tp, n_z),
         in_specs=[vmem] * (2 * tp) + [pl.BlockSpec(memory_space=pl.ANY)] * 4,
-        out_specs=[vmem] * (tp + 4),
-        out_shape=[jax.ShapeDtypeStruct((rows, half), BF16)] * 2
+        out_specs=[vmem] * (2 * tp + 6),
+        out_shape=[jax.ShapeDtypeStruct((half, rows), BF16)] * 2
         + [jax.ShapeDtypeStruct((rows, 2 * half), BF16)] * 2
-        + [jax.ShapeDtypeStruct((tokens_here, width), BF16)] * tp,
+        + [jax.ShapeDtypeStruct((width, rows), BF16), jax.ShapeDtypeStruct((rows, width), BF16)]
+        + [jax.ShapeDtypeStruct((tokens_here, width), BF16)] * (2 * tp),
         scratch_shapes=[
             pltpu.VMEM((2, width, 2 * half), BF16),
             pltpu.VMEM((2, half, width), BF16),
             pltpu.VMEM((rows, width), F32),
-            pltpu.SemaphoreType.DMA((4,)),
+            pltpu.VMEM((rows, width), F32),
+            pltpu.SemaphoreType.DMA((2 + 2 * n_z,)),
         ],
-        compiler_params=pltpu.CompilerParams(vmem_limit_bytes=56 * 2**20),
-        cost_estimate=pl.CostEstimate(
-            flops=20 * rows * width * half,
-            bytes_accessed=20 * 2**20,
-            transcendentals=2 * rows * half,
-        ),
+        compiler_params=pltpu.CompilerParams(vmem_limit_bytes=58 * 2**20),
+        cost_estimate=NO_COST,
         name="ff_pass",
     )(*hidden, *grads, *gu, *down)
-    return got[:2], got[2:4], got[4:]
+    return got[:2], got[2:4], got[4], got[5], got[6 : 6 + tp], got[6 + tp :]
 
 
 def local(
@@ -595,31 +693,9 @@
     def own_part(w):
         return lax.dynamic_slice_in_dim(w, part * part_rows, part_rows, 0)
 
-    kv_pack, q_part, o_part, gate_weight, up_weight, down_weight = lax.optimization_barrier(
-        (kv_pack, own_part(q_weight), own_part(o_weight), gate_weight, up_weight, down_weight)
-    )
-    kv_got = [hop_z(kv_pack, k) for k in range(n_z)]
-    q_got = [hop_z(q_part, k) for k in range(n_z)]
-    og_parts = [hop(og_here, k) for k in range(tp)]
-    kv_got, q_got, og_parts, o_part = lax.optimization_barrier((kv_got, q_got, og_parts, o_part))
-    w_kv, vecs = join_kv(kv_got, rows_here, tuple(v.shape[0] for v in vectors))
-    w_kv = w_kv.reshape(width, 2 * key_width)
-    gain_one = vecs[0:1, :width]
-    gain_two = vecs[1:2, :width]
-    b_query = vecs[2:3, :width]
-    b_key = vecs[3:4, :key_width]
-    b_value = vecs[4:5, :key_width]
-
-    def share_pieces(mine):
-        own = jnp.stack([hop(mine, k) for k in range(tp)])
-        return own, swap(own)
-
-    q_own = [hop(jnp.stack(q_got), k) for k in range(tp)]
-
     ff_z = ff // n_z
     piece = ff_z // n_part
     piece_pad = -(-piece // 32) * 32
-    ff_half = n_z * piece_pad
 
     def ff_columns(w):
         cuts = []
@@ -628,66 +704,88 @@
             cuts.append(jnp.pad(cut, ((0, 0), (0, piece_pad - piece))))
         return jnp.concatenate(cuts, 1)
 
+    order_row = block_order[0]
+    x_here = tokens[0]
+    kv_pack, q_part, o_part, gate_weight, up_weight, down_weight, query_at = (
+        lax.optimization_barrier(
+            (
+                kv_pack,
+                own_part(q_weight),
+                own_part(o_weight),
+                gate_weight,
+                up_weight,
+                down_weight,
+                order_row[here] * block_len + zed * tokens_here,
+            )
+        )
+    )
+    kv_got = [hop_z(kv_pack, k) for k in range(n_z)]
+    q_got = [hop_z(q_part, k) for k in range(n_z)]
     gu_cut = jnp.concatenate([ff_columns(gate_weight), ff_columns(up_weight)], 1)
     down_cut = lax.dynamic_slice_in_dim(down_weight, part * piece, piece, 0)
     down_cut = jnp.pad(down_cut, ((0, piece_pad - piece), (0, 0)))
-    order_row = block_order[0]
-    query_pos = (
-        order_row[here] * block_len
-        + zed * tokens_here
-        + jnp.arange(tokens_here, dtype=jnp.int32)
-    )
+    query_pos = query_at + jnp.arange(tokens_here, dtype=jnp.int32)
     cosine_table, sine_table = rope_tables(query_pos, HEAD)
-
-    inputs = tokens[0].astype(F32)
-    normed_one, scale_one, hidden_one = rms_forward(inputs, gain_one)
-    key_value = matmul(hidden_one, w_kv)
-    key_pre = key_value[:, :key_width] + b_key
-    value_pre = key_value[:, key_width:] + b_value
-    key_rot = rotate(key_pre.reshape(tokens_here, KV_HEADS, HEAD), cosine_table, sine_table)
-    kv_local = jnp.concatenate(
-        [key_rot.astype(BF16).reshape(tokens_here, key_width), value_pre.astype(BF16)], 1
-    )
-    kv_local, o_part = lax.optimization_barrier((kv_local, o_part))
+    cos_wide = jnp.tile(cosine_table[:, 0], (1, 4))
+    sin_wide = jnp.tile(jnp.concatenate([-sine_table[:, 0], sine_table[:, 0]], 1), (1, 2))
+    kv_got, q_got, cos_wide, sin_wide, gu_cut, down_cut, o_part, og_here = (
+        lax.optimization_barrier(
+            (kv_got, q_got, cos_wide, sin_wide, gu_cut, down_cut, o_part, og_here)
+        )
+    )
+
+    q_own = [hop(jnp.stack(q_got), k) for k in range(tp)]
+    og_parts = [hop(og_here, k) for k in range(tp)]
+    widths = tuple(v.shape[0] for v in vectors)
+    w_kv, vecs, kv_local, hidden_one = project_kv(
+        kv_got, x_here, cos_wide, sin_wide, rows_here, widths
+    )
+    w_kv = w_kv.reshape(width, 2 * key_width)
+    gain_one = vecs[0:1, :width]
+    gain_two = vecs[1:2, :width]
     kv_z = [hop_z(kv_local, k) for k in range(n_z)]
     o_got = [hop_z(o_part, k) for k in range(n_z)]
-    kv_z, o_got, q_own, gu_cut, down_cut = lax.optimization_barrier(
-        (kv_z, o_got, q_own, gu_cut, down_cut)
-    )
+    kv_z, o_got, q_own, og_parts, gu_cut, down_cut = lax.optimization_barrier(
+        (kv_z, o_got, q_own, og_parts, gu_cut, down_cut)
+    )
+
     kv_block = jnp.concatenate(kv_z, 0)
-    gu_own = gather_z(gu_cut)
-    gu_oth = swap(gu_own)
-    down_own = gather_z(down_cut)
-    down_oth = swap(down_own)
     if n_ctx == tp:
         kv_blocks = [hop(kv_block, k) for k in range(n_ctx)]
     else:
         kv_blocks = lax.all_gather(kv_block, "ctx", axis=0, tiled=False)
+    gu_own = gather_z(gu_cut)
+    down_own = [hop_z(down_cut, k) for k in range(n_z)]
     q_own = jnp.stack(q_own)
-    w_query = join_weight(q_own, swap(q_own), rows_here)
-    query_pre = matmul(hidden_one, w_query) + b_query
-    queries = rotate(query_pre.reshape(tokens_here, HEADS, HEAD), cosine_table, sine_table)
-    queries = queries.astype(BF16).reshape(tokens_here, HEADS * HEAD) * BF16(HEAD ** (-0.5))
-    kv_blocks, o_got = lax.optimization_barrier((kv_blocks, o_got))
+    w_query, queries = project_query(
+        q_own, swap(q_own), hidden_one, vecs, cos_wide, sin_wide, rows_here
+    )
+    w_query = w_query.reshape(width, width)
+    kv_blocks, queries, o_got = lax.optimization_barrier((kv_blocks, queries, o_got))
+
     o_own = [hop(jnp.stack(o_got), k) for k in range(tp)]
     kv_whole = jnp.stack(kv_blocks) if n_ctx == tp else kv_blocks
     attended, queries_ext = attend_forward(order_row, n_ctx == tp, queries, kv_whole)
-    attended, o_own = lax.optimization_barrier((attended, o_own))
+    attended, o_own, queries_ext = lax.optimization_barrier((attended, o_own, queries_ext))
     o_own = jnp.stack(o_own)
-    w_out = join_weight(o_own, swap(o_own), rows_here)
-    resid = inputs + matmul(attended, w_out)
-    normed_two, scale_two, hidden_two = rms_forward(resid, gain_two)
-
+    w_out, resid, hidden_two = project_out(
+        o_own, swap(o_own), attended, x_here, vecs, rows_here
+    )
+    w_out = w_out.reshape(width, width)
     h2_parts = [hop(hidden_two, k) for k in range(tp)]
-
-    def scatter_plane(v):
-        parts = v.astype(BF16).reshape(tp, tokens_here, width)
-        return [hop(parts[k], k) for k in range(tp)]
-
-    acts, ggus, dh2 = ff_pass(h2_parts, og_parts, (gu_own, gu_oth), (down_own, down_oth))
+    h2_parts, gu_own, down_own = lax.optimization_barrier((h2_parts, gu_own, down_own))
+    gu_oth = swap(gu_own)
+    down_own = jnp.stack(down_own)
+    down_oth = swap(down_own)
+
+    acts, ggus, h2_turned, og_all, dh2, ff_out = ff_pass(
+        h2_parts, og_parts, (gu_own, gu_oth), (down_own, down_oth)
+    )
     grad_h2_parts = [hop(dh2[k], k) for k in range(tp)]
-    h2_all = jnp.concatenate(h2_parts, 0)
-    og_all = jnp.concatenate(og_parts, 0)
+
+    def share_pieces(mine):
+        own = jnp.stack([hop(mine, k) for k in range(tp)])
+        return own, swap(own)
 
     def reduce_start(part_sum):
         cols = part_sum.shape[1]
@@ -728,18 +826,20 @@
         groups = [[g * tp + c for g in range(n_ctx // tp)] for c in range(tp)]
         return lax.psum(v, "ctx", axis_index_groups=groups)
 
-    def core_sum(own, oth):
-        return (own + swap(oth.astype(BF16)).astype(F32)).astype(BF16)
-
-    d_gu = core_sum(contract_rows(h2_all, ggus[0]), contract_rows(h2_all, ggus[1]))
-    d_down = core_sum(contract_rows(acts[0], og_all), contract_rows(acts[1], og_all))
-    ff_out = (matmul(acts[0], down_own) + matmul(acts[1], down_oth)).astype(BF16)
-    grad_h2_parts, d_down, d_gu, ff_out = lax.optimization_barrier(
-        (grad_h2_parts, d_down, d_gu, ff_out)
+    d_gu = grad_weight(h2_turned, ggus[0], swap(grad_weight(h2_turned, ggus[1])))
+    d_down = grad_weight(acts[0], og_all, swap(grad_weight(acts[1], og_all)))
+    grad_h2_parts, d_gu, d_down, ff_out = lax.optimization_barrier(
+        (grad_h2_parts, d_gu, d_down, ff_out)
     )
     d_gu = scatter_z(d_gu)
-    ff_out = scatter_plane(ff_out)
+    ff_out = [hop(ff_out[k], k) for k in range(tp)]
+    d_down = d_down.reshape(n_z, piece_pad, width)
+    d_down = [
+        hop_z(lax.dynamic_index_in_dim(d_down, zed ^ k, 0, keepdims=False), k) for k in range(n_z)
+    ]
     grad_h2 = sum(v.astype(F32) for v in grad_h2_parts)
+    scale_two = lax.rsqrt(jnp.mean(resid * resid, -1, keepdims=True) + NORM_EPS)
+    normed_two = resid * scale_two
 
     grad_norm_two, gain_two_terms = rms_backward(grad_h2, normed_two, scale_two, gain_two)
     grad_resid = og_here.astype(F32) + grad_norm_two
@@ -748,27 +848,37 @@
     grad_queries, grad_terms = attend_backward(
         order_row, n_ctx == tp, queries_ext, grad_att, attended, kv_whole
     )
-    grad_terms, d_gu, ff_out, d_down = lax.optimization_barrier((grad_terms, d_gu, ff_out, d_down))
-    d_down = scatter_z(d_down)
-    result = resid + sum(v.astype(F32) for v in ff_out)
-    layer_out = result.astype(BF16)[None]
-    if n_ctx == tp:
-        kv_terms = [hop(grad_terms[k], k) for k in range(n_ctx)]
-        kv_terms, d_gu = lax.optimization_barrier((kv_terms, d_gu))
-        kv_sum = sum(v.astype(F32) for v in kv_terms).astype(BF16)
-    else:
-        kv_sum = lax.psum_scatter(grad_terms, "ctx", scatter_dimension=0, tiled=False)
-    d_gu = share_pieces(ctx_groups_sum(d_gu))
-    kv_sum = kv_sum.reshape(n_z, tokens_here, 2 * key_width)
-    grad_kv = kv_sum[0].astype(F32)
-    for k in range(1, n_z):
-        grad_kv = grad_kv + hop_z(kv_sum[k], k).astype(F32)
+    grad_queries, grad_terms, ff_out, grad_proj = lax.optimization_barrier(
+        (grad_queries, grad_terms, ff_out, grad_proj)
+    )
 
     grad_q_pre = (
         rotate(grad_queries.reshape(tokens_here, HEADS, HEAD), cosine_table, -sine_table)
         .reshape(tokens_here, HEADS * HEAD)
         .astype(BF16)
     )
+    d_qo = jnp.concatenate(
+        [contract_rows(hidden_one, grad_q_pre), contract_rows(attended, grad_proj)], 1
+    )
+    d_qo = reduce_start(d_qo)
+    if n_ctx == tp:
+        kv_terms = [hop(grad_terms[k], k) for k in range(n_ctx)]
+        kv_terms, d_gu, d_down, d_qo, ff_out = lax.optimization_barrier(
+            (kv_terms, d_gu, d_down, d_qo, ff_out)
+        )
+        kv_sum = sum(v.astype(F32) for v in kv_terms).astype(BF16)
+    else:
+        kv_sum = lax.psum_scatter(grad_terms, "ctx", scatter_dimension=0, tiled=False)
+    result = resid + sum(v.astype(F32) for v in ff_out)
+    layer_out = result.astype(BF16)[None]
+    d_gu = share_pieces(ctx_groups_sum(d_gu))
+    d_down = ctx_groups_sum(sum(v.astype(F32) for v in d_down).astype(BF16))
+    d_down = lax.optimization_barrier(d_down)
+    kv_sum = kv_sum.reshape(n_z, tokens_here, 2 * key_width)
+    kv_terms = [hop_z(kv_sum[k], k) for k in range(n_z)]
+    kv_terms, d_qo, d_down = lax.optimization_barrier((kv_terms, d_qo, d_down))
+    grad_kv = sum(v.astype(F32) for v in kv_terms)
+
     grad_k_pre = (
         rotate(
             grad_kv[:, :key_width].reshape(tokens_here, KV_HEADS, HEAD), cosine_table, -sine_table
@@ -780,6 +890,9 @@
 
     grad_kv_pre = jnp.concatenate([grad_k_pre, grad_v_pre], 1)
     grad_hidden_one = times_transposed(grad_q_pre, w_query) + times_transposed(grad_kv_pre, w_kv)
+    inputs = x_here.astype(F32)
+    scale_one = lax.rsqrt(jnp.mean(inputs * inputs, -1, keepdims=True) + NORM_EPS)
+    normed_one = inputs * scale_one
     grad_norm_one, gain_one_terms = rms_backward(grad_hidden_one, normed_one, scale_one, gain_one)
     tokens_grad = (grad_resid + grad_norm_one)[None]
 
@@ -788,10 +901,7 @@
         v = v.reshape(tokens_here, n_z, share)
         return jnp.pad(v, ((0, 0), (0, 0), (0, rows_here - share))).reshape(tokens_here, width)
 
-    d_qo = jnp.concatenate(
-        [contract_rows(hidden_one, grad_q_pre), contract_rows(attended, grad_proj)], 1
-    )
-    d_qo = reduce_end(reduce_start(d_qo), True)
+    d_qo = reduce_end(d_qo, True)
     grad_w_query = d_qo[:, :width]
     grad_w_out = d_qo[:, width:]
     terms = (gain_one_terms, gain_two_terms, grad_q_pre, by_rows(grad_k_pre), by_rows(grad_v_pre))
@@ -802,7 +912,7 @@
     grad_w_kv = jnp.concatenate([contract_rows(hidden_one, grad_kv_pre), columns], 1)
     grad_w_kv = reduce_end(reduce_start(grad_w_kv), False)
     sums = grad_w_kv[:, 2 * key_width :]
-    grad_w_down = spread_rows(share_pieces(ctx_groups_sum(d_down)), piece, ff_z)
+    grad_w_down = spread_rows(share_pieces(d_down), piece, ff_z)
     grad_w_gate, grad_w_up = spread_columns(d_gu, n_z, ff, 2)
 
     return (

time: 436 us -> 440 us (level)
  Pallas kernels: 68.6 us -> 98 us
  waiting for transfers between devices: 111 us -> 138 us
  matrix products: 33.8 us -> 8.21 us
  local copies, waits for them, and re-layouts: 66.6 us -> 45.6 us
  other arithmetic: 39.4 us -> 25.6 us
  starting transfers between devices: 93.6 us -> 103 us
    ppermute x21 -> x27, waiting for transfers between devices: 44.7 us -> 73.9 us  [hop_z(): return lax.ppermute(v, 'fsdp', [(i, i ^ k) for i in range(n_z)])]
    pallas_call x4 -> x8, Pallas kernels: 20 us -> 42 us  [the longest x1 21.4 us: ff_pass(): pl.pallas_call(functools.partial(ff_kernel, tp, n_z), in_specs=[vmem] * (...]
    dot_general x8 -> x4, matrix products: 21.5 us -> 4.94 us  [contract_rows(): lax.dot_general(left_side, right_side, (((0,), (0,)), ((), ())), preferre...]
    all_gather x2 -> x1, waiting for transfers between devices: 16 us -> 0.01 us  [gather_z(): return lax.all_gather(v, 'fsdp', axis=0, tiled=True)]
    ppermute x21 -> x27, starting transfers between devices: 29.5 us -> 41.9 us  [hop_z(): return lax.ppermute(v, 'fsdp', [(i, i ^ k) for i in range(n_z)])]
    ppermute x42, waiting for transfers between devices: 50.2 us -> 59.4 us  [hop(): return lax.ppermute(v, 'ctx', [(i, i ^ k) for i in range(n_ctx)])]
    dot_general x5 -> x0, matrix products: 8.64 us -> none  [matmul(): return jnp.dot(left_side, right_side, preferred_element_type=F32)]
    ppermute x12, starting transfers between devices: 28.9 us -> 22.5 us  [swap(): return lax.ppermute(v, 'seq', [(0, 1), (1, 0)])]
  transfers between devices with their start and end apart: 79 -> 83, of which waited for: 26 -> 26; matrix products, arithmetic and copies ran while one was open for 23% -> 11% of each run, Pallas kernels for 11% -> 15%
where the time goes in v1:
time: 440 us; the launch traced here: 435 us
  waiting for transfers between devices  138 us (31%)
  starting transfers between devices  103 us (23%)
  Pallas kernels  98 us (22%)
  local copies, waits for them, and re-layouts  45.6 us (10%)
  other arithmetic  25.6 us (6%)
  between operations  16.1 us (4%)
  matrix products  8.21 us (2%)
    ppermute x27, waiting for transfers between devices, hop_z(): return lax.ppermute(v, 'fsdp', [(i, i ^ k) for i in range(n_z)])  73.9 us
    ppermute x42, waiting for transfers between devices, hop(): return lax.ppermute(v, 'ctx', [(i, i ^ k) for i in range(n_ctx)])  59.4 us
    ppermute x27, starting transfers between devices, hop_z(): return lax.ppermute(v, 'fsdp', [(i, i ^ k) for i in range(n_z)])  41.9 us
    ppermute x42, starting transfers between devices, hop(): return lax.ppermute(v, 'ctx', [(i, i ^ k) for i in range(n_ctx)])  39 us
    pallas_call x1, Pallas kernels, attend_backward(): pl.pallas_call(functools.partial(backward_kernel, by_xor), grid_spec=pltp...  27.4 us
    unnamed x133, local copies, waits for them, and re-layouts  23.3 us
    ppermute x12, starting transfers between devices, swap(): return lax.ppermute(v, 'seq', [(0, 1), (1, 0)])  22.5 us
    pallas_call x1, Pallas kernels, ff_pass(): pl.pallas_call(functools.partial(ff_kernel, tp, n_z), in_specs=[vmem] * (...  21.4 us
  transfers between devices with their start and end apart: 83, of which 26 were waited for; matrix products, arithmetic and copies ran while one was open for 11% of the time, Pallas kernels for 15%

profile of v1, /device:TPU:1, one launch (start us, length us, event | category | flops | bytes accessed | tf_op | source)
XLA Modules:
  0.0 435.3 jit_solution(7900643444027748239)
XLA Ops:
  19.1 3.2 collective-permute-start.4
  28.2 3.3 collective-permute-done.4
  39.8 2.9 collective-permute-start.7
  51.9 3.1 collective-permute-done.8
  57.4 14.9 %collective-permute-done.13 = bf16[4,32,896]{2,1,0:T(8,128)(2,1)S(1)} collective-permute-done((bf16[4,32,896]{2,1,0:T(8,128)(2,1)S(1)}, bf16[4,32,896]{2,1,0:T(8,128)(2,1)S(1)}, u32[]{:S(2)}, u32[]{:S(2)}) %collective-permute-start.13) | collective-permute-done | bytes 229408 | tf_op jit(solution)/shard_map/ppermute | solution.py:663
  74.3 3.7 collective-permute-start.21
  81.9 7.0 %collective-permute-done.18 = bf16[768,256]{1,0:T(8,128)(2,1)S(1)} collective-permute-done((bf16[768,256]{1,0:T(8,128)(2,1)S(1)}, bf16[768,256]{1,0:T(8,128)(2,1)S(1)}, u32[]{:S(2)}, u32[]{:S(2)}) %collective-permute-start.18) | collective-permute-done | bytes 393248 | tf_op jit(solution)/shard_map/ppermute | solution.py:663
  88.9 9.4 %collective-permute-done.20 = bf16[768,256]{1,0:T(8,128)(2,1)S(1)} collective-permute-done((bf16[768,256]{1,0:T(8,128)(2,1)S(1)}, bf16[768,256]{1,0:T(8,128)(2,1)S(1)}, u32[]{:S(2)}, u32[]{:S(2)}) %collective-permute-start.20) | collective-permute-done | bytes 393248 | tf_op jit(solution)/shard_map/ppermute | solution.py:663
  101.3 16.5 %attend_forward.1 = (bf16[192,896]{1,0:T(8,128)(2,1)S(1)}, bf16[2688,256]{1,0:T(8,128)(2,1)S(1)}) custom-call(s32[4]{0:T(128)S(1)} %bitcast.149, bf16[192,896]{1,0:T(8,128)(2,1)S(1)} %get-tuple-element.180.q_ref, bf16[4,768,256]{2,1,0:T(8,128)(2,1)S(1)} %pad_maximum_fusion.1.kv_ref), custom_call_target="tpu_custom_call" | custom-call | tf_op jit(solution)/shard_map/attend_forward/pallas_call | solution.py:250
  126.0 3.4 collective-permute-start.30
  132.1 15.8 %collective-permute-done.30 = bf16[160,896]{1,0:T(8,128)(2,1)S(1)} collective-permute-done((bf16[160,896]{1,0:T(8,128)(2,1)S(1)}, bf16[160,896]{1,0:T(8,128)(2,1)S(1)}, u32[]{:S(2)}, u32[]{:S(2)}) %collective-permute-start.30) | collective-permute-done | bytes 286752 | tf_op jit(solution)/shard_map/ppermute | solution.py:668
  149.6 2.6 collective-permute-start.32
  153.7 4.2 collective-permute-done.33.refs_11_
  158.9 21.4 %ff_pass.1 = (bf16[640,768]{1,0:T(8,128)(2,1)}, bf16[640,768]{1,0:T(8,128)(2,1)}, bf16[768,1280]{1,0:T(8,128)(2,1)}, bf16[768,1280]{1,0:T(8,128)(2,1)}, bf16[896...) custom-call(bf16[192,896]{1,0:T(8,128)(2,1)} %copy-done.23, ...), custom_call_target="tpu_custom_call" | custom-call | tf_op jit(solution)/shard_map/ff_pass/pallas_call | solution.py:609
  183.3 4.6 %grad_weight.4 = bf16[896,1280]{1,0:T(8,128)(2,1)} custom-call(bf16[896,768]{1,0:T(8,128)(2,1)S(1)} %copy-done.6, bf16[768,1280]{1,0:T(8,128)(2,1)S(1)} %copy-done.11), custom_call_target="tpu_custom_call" | custom-call | tf_op jit(solution)/shard_map/grad_weight/pallas_call | solution.py:523
  188.3 3.3 grad_weight.6
  198.5 4.2 grad_weight.7
  203.7 5.7 %grad_weight.5 = bf16[896,1280]{1,0:T(8,128)(2,1)S(1)} custom-call(bf16[896,768]{1,0:T(8,128)(2,1)S(1)} %copy-done.7, bf16[768,1280]{1,0:T(8,128)(2,1)S(1)} %copy-done.10, bf16[896,1280]{1,0:T(8,128)(2,1)} %collective-permute-done.37.refs_0_), custom_call_target="tpu_custom_call" | custom-call | tf_op jit(solution)/shard_map/grad_weight/pallas_call | solution.py:523
  215.7 2.7 fusion.40
  219.8 27.4 %attend_backward.1 = (f32[192,896]{1,0:T(8,128)S(1)}, bf16[4,768,256]{2,1,0:T(8,128)(2,1)S(1)}) custom-call(s32[4]{0:T(128)S(1)} %bitcast.150, bf16[2688,256]{1,0:T(8,128)(2,1)S(1)} %copy-done.17, bf16[192,896]{1,0:T(8,128)(2,1)S(1)} %convolution_convert_fusion.3.do_ref, bf16[192,896]{1,0:T(8,128)(2,1)S(1)} %get-tuple-element.195.att_ref, ...), custom_call_target="tpu_custom_call" | custom-call | tf_op jit(solution)/shard_map/attend_backward/pallas_call | solution.py:278
  257.4 4.9 %collective-permute-start.45 = (bf16[160,896]{1,0:T(8,128)(2,1)}, bf16[160,896]{1,0:T(8,128)(2,1)}, u32[]{:S(2)}, u32[]{:S(2)}) collective-permute-start(bf16[160,896]{1,0:T(8,128)(2,1)} %get-tuple-element.300), channel_id=1, source_target_pairs={{0,1},{1,0},{2,3},{3,2},{4,5},{5,4},{6,7},{7,6},{8,9},{9,8},{10,11... | collective-permute-start | bytes 860168 | tf_op jit(solution)/shard_map/ppermute | solution.py:668
  267.8 9.7 %collective-permute-done.45 = bf16[160,896]{1,0:T(8,128)(2,1)} collective-permute-done((bf16[160,896]{1,0:T(8,128)(2,1)}, bf16[160,896]{1,0:T(8,128)(2,1)}, u32[]{:S(2)}, u32[]{:S(2)}) %collective-permute-start.45) | collective-permute-done | bytes 286752 | tf_op jit(solution)/shard_map/ppermute | solution.py:668
  279.4 3.7 add_convert_fusion
  285.5 10.8 %collective-permute-done.43 = bf16[768,256]{1,0:T(8,128)(2,1)} collective-permute-done((bf16[768,256]{1,0:T(8,128)(2,1)}, bf16[768,256]{1,0:T(8,128)(2,1)}, u32[]{:S(2)}, u32[]{:S(2)}) %collective-permute-start.43) | collective-permute-done | bytes 393248 | tf_op jit(solution)/shard_map/ppermute | solution.py:663
  305.3 3.4 collective-permute-start.79
  321.4 3.9 collective-permute-start.52
  332.9 6.6 %collective-permute-done.65 = bf16[4,32,1792]{2,1,0:T(8,128)(2,1)S(1)} collective-permute-done((bf16[4,32,1792]{2,1,0:T(8,128)(2,1)S(1)}, bf16[4,32,1792]{2,1,0:T(8,128)(2,1)S(1)}, u32[]{:S(2)}, u32[]{:S(2)}) %collective-permute-start.65) | collective-permute-done | bytes 458784 | tf_op jit(solution)/shard_map/ppermute | solution.py:668
  340.5 27.7 %collective-permute-done.64 = bf16[4,32,1792]{2,1,0:T(8,128)(2,1)S(1)} collective-permute-done((bf16[4,32,1792]{2,1,0:T(8,128)(2,1)S(1)}, bf16[4,32,1792]{2,1,0:T(8,128)(2,1)S(1)}, u32[]{:S(2)}, u32[]{:S(2)}) %collective-permute-start.64) | collective-permute-done | bytes 458784 | tf_op jit(solution)/shard_map/ppermute | solution.py:668
  374.9 9.1 %collective-permute-done.53 = bf16[4,32,384]{2,1,0:T(8,128)(2,1)S(1)} collective-permute-done((bf16[4,32,384]{2,1,0:T(8,128)(2,1)S(1)}, bf16[4,32,384]{2,1,0:T(8,128)(2,1)S(1)}, u32[]{:S(2)}, u32[]{:S(2)}) %collective-permute-start.53) | collective-permute-done | bytes 98336 | tf_op jit(solution)/shard_map/ppermute | solution.py:663
  398.9 4.4 %collective-permute-start.62 = (bf16[4,32,384]{2,1,0:T(8,128)(2,1)S(1)}, bf16[4,32,384]{2,1,0:T(8,128)(2,1)S(1)}, u32[]{:S(2)}, u32[]{:S(2)}) collective-permute-start(bf16[4,32,384]{2,1,0:T(8,128)(2,1)S(1)} %pad_maximum_fusion.11.refs_0_), channel_id=1, source_target_pairs={{0,16},{16,0},{1,17},{17,1},{2,18},{18,2},{3,19},{19,3},{4,20},{20... | collective-permute-start | bytes 294920 | tf_op jit(solution)/shard_map/ppermute | solution.py:658
  417.7 3.8 spread_rows.5
  421.5 6.7 %spread_columns.1 = (f32[224,4864]{1,0:T(8,128)}, f32[224,4864]{1,0:T(8,128)}) custom-call(bf16[4,224,1280]{2,1,0:T(8,128)(2,1)S(1)} %pad_maximum_fusion.refs_0_, bf16[4,224,1280]{2,1,0:T(8,128)(2,1)S(1)} %collective-permute-done.76.refs_1_), custom_call_target="tpu_custom_call" | custom-call | tf_op jit(solution)/shard_map/spread_columns/pallas_call | solution.py:337
  (384 shorter events, 165.2 us)
Async XLA Ops:
  7.2 142.4 %all-gather.2.cloned.1.call-start = ((), (), s32[]{:S(2)}) async-start(), calls=%async_computation.1 | async-start | bytes 2867200 | tf_op jit(solution)/shard_map/all_gather | solution.py:671
  33.8 22.5 %collective-permute-start.12 = (bf16[4,32,896]{2,1,0:T(8,128)(2,1)S(1)}, bf16[4,32,896]{2,1,0:T(8,128)(2,1)S(1)}, u32[]{:S(2)}, u32[]{:S(2)}) collective-permute-start(bf16[4,32,896]{2,1,0:T(8,128)(2,1)S(1)} %pad_maximum_fusion.7), channel_id=1, source_target_pairs={{0,4},{4,0},{8,12},{12,8},{1,5},{5,1},{9,13},{13,9},{2,6},{6,2},{1... | collective-permute-start | bytes 688136 | tf_op jit(solution)/shard_map/ppermute | solution.py:663
  46.9 25.3 %collective-permute-start.15 = (bf16[192,896]{1,0:T(8,128)(2,1)S(1)}, bf16[192,896]{1,0:T(8,128)(2,1)S(1)}, u32[]{:S(2)}, u32[]{:S(2)}) collective-permute-start(bf16[192,896]{1,0:T(8,128)(2,1)S(1)} %bitcast.164), channel_id=1, source_target_pairs={{0,4},{4,0},{8,12},{12,8},{1,5},{5,1},{9,13},{13,9},{2,6},{6,2},{1... | collective-permute-start | bytes 1032200 | tf_op jit(solution)/shard_map/ppermute | solution.py:663
  48.2 24.1 %collective-permute-start.16 = (bf16[192,896]{1,0:T(8,128)(2,1)S(1)}, bf16[192,896]{1,0:T(8,128)(2,1)S(1)}, u32[]{:S(2)}, u32[]{:S(2)}) collective-permute-start(bf16[192,896]{1,0:T(8,128)(2,1)S(1)} %bitcast.165), channel_id=1, source_target_pairs={{0,8},{4,12},{8,0},{12,4},{1,9},{5,13},{9,1},{13,5},{2,10},{6,14},... | collective-permute-start | bytes 1032200 | tf_op jit(solution)/shard_map/ppermute | solution.py:663
  49.4 23.5 %collective-permute-start.17 = (bf16[192,896]{1,0:T(8,128)(2,1)S(1)}, bf16[192,896]{1,0:T(8,128)(2,1)S(1)}, u32[]{:S(2)}, u32[]{:S(2)}) collective-permute-start(bf16[192,896]{1,0:T(8,128)(2,1)S(1)} %bitcast.166), channel_id=1, source_target_pairs={{0,12},{4,8},{8,4},{12,0},{1,13},{5,9},{9,5},{13,1},{2,14},{6,10},... | collective-permute-start | bytes 1032200 | tf_op jit(solution)/shard_map/ppermute | solution.py:663
  73.0 223.4 %reduce-scatter.2.cloned.1.call-start = ((), (), s32[]{:S(2)}) async-start(), calls=%async_computation.2 | async-start | bytes 2867200 | tf_op jit(solution)/shard_map/reduce_scatter | solution.py:674
  79.6 18.7 %collective-permute-start.20 = (bf16[768,256]{1,0:T(8,128)(2,1)S(1)}, bf16[768,256]{1,0:T(8,128)(2,1)S(1)}, u32[]{:S(2)}, u32[]{:S(2)}) collective-permute-start(bf16[768,256]{1,0:T(8,128)(2,1)S(1)} %constant_dynamic-update-slice_fusion), channel_id=1, source_target_pairs={{0,12},{4,8},{8,4},{12,0},{1,13},{5,9},{9,5},{13,1},{2,14},{6,10},... | collective-permute-start | bytes 1179656 | tf_op jit(solution)/shard_map/ppermute | solution.py:663
  98.4 19.5 %collective-permute-start.22 = (bf16[4,32,896]{2,1,0:T(8,128)(2,1)S(1)}, bf16[4,32,896]{2,1,0:T(8,128)(2,1)S(1)}, u32[]{:S(2)}, u32[]{:S(2)}) collective-permute-start(bf16[4,32,896]{2,1,0:T(8,128)(2,1)S(1)} %pad_maximum_fusion.8), channel_id=1, source_target_pairs={{0,4},{4,0},{8,12},{12,8},{1,5},{5,1},{9,13},{13,9},{2,6},{6,2},{1... | collective-permute-start | bytes 688136 | tf_op jit(solution)/shard_map/ppermute | solution.py:663
  98.8 19.1 %collective-permute-start.23 = (bf16[4,32,896]{2,1,0:T(8,128)(2,1)S(1)}, bf16[4,32,896]{2,1,0:T(8,128)(2,1)S(1)}, u32[]{:S(2)}, u32[]{:S(2)}) collective-permute-start(bf16[4,32,896]{2,1,0:T(8,128)(2,1)S(1)} %pad_maximum_fusion.8), channel_id=1, source_target_pairs={{0,8},{4,12},{8,0},{12,4},{1,9},{5,13},{9,1},{13,5},{2,10},{6,14},... | collective-permute-start | bytes 688136 | tf_op jit(solution)/shard_map/ppermute | solution.py:663
  123.1 24.9 %collective-permute-start.26 = (bf16[192,896]{1,0:T(8,128)(2,1)S(1)}, bf16[192,896]{1,0:T(8,128)(2,1)S(1)}, u32[]{:S(2)}, u32[]{:S(2)}) collective-permute-start(bf16[192,896]{1,0:T(8,128)(2,1)S(1)} %get-tuple-element.201.refs_0_), channel_id=1, source_target_pairs={{0,4},{4,0},{8,12},{12,8},{1,5},{5,1},{9,13},{13,9},{2,6},{6,2},{1... | collective-permute-start | bytes 1032200 | tf_op jit(solution)/shard_map/ppermute | solution.py:663
  123.1 24.9 %collective-permute-start.27 = (bf16[192,896]{1,0:T(8,128)(2,1)S(1)}, bf16[192,896]{1,0:T(8,128)(2,1)S(1)}, u32[]{:S(2)}, u32[]{:S(2)}) collective-permute-start(bf16[192,896]{1,0:T(8,128)(2,1)S(1)} %get-tuple-element.201.refs_0_), channel_id=1, source_target_pairs={{0,8},{4,12},{8,0},{12,4},{1,9},{5,13},{9,1},{13,5},{2,10},{6,14},... | collective-permute-start | bytes 1032200 | tf_op jit(solution)/shard_map/ppermute | solution.py:663
  124.8 24.8 %collective-permute-start.28 = (bf16[192,896]{1,0:T(8,128)(2,1)S(1)}, bf16[192,896]{1,0:T(8,128)(2,1)}, u32[]{:S(2)}, u32[]{:S(2)}) collective-permute-start(bf16[192,896]{1,0:T(8,128)(2,1)S(1)} %get-tuple-element.201.refs_0_), channel_id=1, source_target_pairs={{0,12},{4,8},{8,4},{12,0},{1,13},{5,9},{9,5},{13,1},{2,14},{6,10},... | collective-permute-start | bytes 1032200 | tf_op jit(solution)/shard_map/ppermute | solution.py:663
  126.0 22.0 %collective-permute-start.30 = (bf16[160,896]{1,0:T(8,128)(2,1)S(1)}, bf16[160,896]{1,0:T(8,128)(2,1)S(1)}, u32[]{:S(2)}, u32[]{:S(2)}) collective-permute-start(bf16[160,896]{1,0:T(8,128)(2,1)S(1)} %copy-done.42), channel_id=1, source_target_pairs={{0,2},{1,3},{2,0},{3,1},{4,6},{5,7},{6,4},{7,5},{8,10},{9,11},{10,... | collective-permute-start | bytes 860168 | tf_op jit(solution)/shard_map/ppermute | solution.py:668
  212.9 36.3 %collective-permute-start.39 = (bf16[192,896]{1,0:T(8,128)(2,1)}, bf16[192,896]{1,0:T(8,128)(2,1)}, u32[]{:S(2)}, u32[]{:S(2)}) collective-permute-start(bf16[192,896]{1,0:T(8,128)(2,1)} %get-tuple-element.236), channel_id=1, source_target_pairs={{0,4},{4,0},{8,12},{12,8},{1,5},{5,1},{9,13},{13,9},{2,6},{6,2},{1... | collective-permute-start | bytes 1032200 | tf_op jit(solution)/shard_map/ppermute | solution.py:663
  213.4 35.9 %collective-permute-start.40 = (bf16[192,896]{1,0:T(8,128)(2,1)}, bf16[192,896]{1,0:T(8,128)(2,1)}, u32[]{:S(2)}, u32[]{:S(2)}) collective-permute-start(bf16[192,896]{1,0:T(8,128)(2,1)} %get-tuple-element.237), channel_id=1, source_target_pairs={{0,8},{4,12},{8,0},{12,4},{1,9},{5,13},{9,1},{13,5},{2,10},{6,14},... | collective-permute-start | bytes 1032200 | tf_op jit(solution)/shard_map/ppermute | solution.py:663
  214.4 34.8 %collective-permute-start.41 = (bf16[192,896]{1,0:T(8,128)(2,1)}, bf16[192,896]{1,0:T(8,128)(2,1)}, u32[]{:S(2)}, u32[]{:S(2)}) collective-permute-start(bf16[192,896]{1,0:T(8,128)(2,1)} %get-tuple-element.238), channel_id=1, source_target_pairs={{0,12},{4,8},{8,4},{12,0},{1,13},{5,9},{9,5},{13,1},{2,14},{6,10},... | collective-permute-start | bytes 1032200 | tf_op jit(solution)/shard_map/ppermute | solution.py:663
  256.1 22.3 %collective-permute-start.48 = (bf16[4,128,1792]{2,1,0:T(8,128)(2,1)}, bf16[4,128,1792]{2,1,0:T(8,128)(2,1)}, u32[]{:S(2)}, u32[]{:S(2)}) collective-permute-start(bf16[4,128,1792]{2,1,0:T(8,128)(2,1)} %constant_dynamic-slice_fusion.1), channel_id=1, source_target_pairs={{0,16},{16,0},{1,17},{17,1},{2,18},{18,2},{3,19},{19,3},{4,20},{20... | collective-permute-start | bytes 5505032 | tf_op jit(solution)/shard_map/ppermute | solution.py:658
  257.4 20.1 %collective-permute-start.45 = (bf16[160,896]{1,0:T(8,128)(2,1)}, bf16[160,896]{1,0:T(8,128)(2,1)}, u32[]{:S(2)}, u32[]{:S(2)}) collective-permute-start(bf16[160,896]{1,0:T(8,128)(2,1)} %get-tuple-element.300), channel_id=1, source_target_pairs={{0,1},{1,0},{2,3},{3,2},{4,5},{5,4},{6,7},{7,6},{8,9},{9,8},{10,11... | collective-permute-start | bytes 860168 | tf_op jit(solution)/shard_map/ppermute | solution.py:668
  262.4 20.8 %collective-permute-start.46 = (bf16[160,896]{1,0:T(8,128)(2,1)}, bf16[160,896]{1,0:T(8,128)(2,1)}, u32[]{:S(2)}, u32[]{:S(2)}) collective-permute-start(bf16[160,896]{1,0:T(8,128)(2,1)} %get-tuple-element.299), channel_id=1, source_target_pairs={{0,2},{1,3},{2,0},{3,1},{4,6},{5,7},{6,4},{7,5},{8,10},{9,11},{10,... | collective-permute-start | bytes 860168 | tf_op jit(solution)/shard_map/ppermute | solution.py:668
  262.7 22.8 %collective-permute-start.47 = (bf16[160,896]{1,0:T(8,128)(2,1)}, bf16[160,896]{1,0:T(8,128)(2,1)}, u32[]{:S(2)}, u32[]{:S(2)}) collective-permute-start(bf16[160,896]{1,0:T(8,128)(2,1)} %get-tuple-element.298), channel_id=1, source_target_pairs={{0,3},{1,2},{2,1},{3,0},{4,7},{5,6},{6,5},{7,4},{8,11},{9,10},{10,... | collective-permute-start | bytes 860168 | tf_op jit(solution)/shard_map/ppermute | solution.py:668
  277.5 18.8 %collective-permute-start.43 = (bf16[768,256]{1,0:T(8,128)(2,1)}, bf16[768,256]{1,0:T(8,128)(2,1)}, u32[]{:S(2)}, u32[]{:S(2)}) collective-permute-start(bf16[768,256]{1,0:T(8,128)(2,1)} %get-tuple-element.295), channel_id=1, source_target_pairs={{0,8},{4,12},{8,0},{12,4},{1,9},{5,13},{9,1},{13,5},{2,10},{6,14},... | collective-permute-start | bytes 1179656 | tf_op jit(solution)/shard_map/ppermute | solution.py:663
  305.3 21.7 %collective-permute-start.79 = (bf16[160,896]{1,0:T(8,128)(2,1)S(1)}, bf16[160,896]{1,0:T(8,128)(2,1)S(1)}, u32[]{:S(2)}, u32[]{:S(2)}) collective-permute-start(bf16[160,896]{1,0:T(8,128)(2,1)S(1)} %add_convert_fusion.4), channel_id=1, source_target_pairs={{0,12},{4,8},{8,4},{12,0},{1,13},{5,9},{9,5},{13,1},{2,14},{6,10},... | collective-permute-start | bytes 860168 | tf_op jit(solution)/shard_map/ppermute | solution.py:663
  308.8 20.5 %collective-permute-start.78 = (bf16[160,896]{1,0:T(8,128)(2,1)S(1)}, bf16[160,896]{1,0:T(8,128)(2,1)}, u32[]{:S(2)}, u32[]{:S(2)}) collective-permute-start(bf16[160,896]{1,0:T(8,128)(2,1)S(1)} %add_convert_fusion.4), channel_id=1, source_target_pairs={{0,8},{4,12},{8,0},{12,4},{1,9},{5,13},{9,1},{13,5},{2,10},{6,14},... | collective-permute-start | bytes 860168 | tf_op jit(solution)/shard_map/ppermute | solution.py:663
  308.8 22.6 %collective-permute-start.77 = (bf16[160,896]{1,0:T(8,128)(2,1)S(1)}, bf16[160,896]{1,0:T(8,128)(2,1)}, u32[]{:S(2)}, u32[]{:S(2)}) collective-permute-start(bf16[160,896]{1,0:T(8,128)(2,1)S(1)} %add_convert_fusion.4), channel_id=1, source_target_pairs={{0,4},{4,0},{8,12},{12,8},{1,5},{5,1},{9,13},{13,9},{2,6},{6,2},{1... | collective-permute-start | bytes 860168 | tf_op jit(solution)/shard_map/ppermute | solution.py:663
  327.1 41.1 %collective-permute-start.64 = (bf16[4,32,1792]{2,1,0:T(8,128)(2,1)S(1)}, bf16[4,32,1792]{2,1,0:T(8,128)(2,1)S(1)}, u32[]{:S(2)}, u32[]{:S(2)}) collective-permute-start(bf16[4,32,1792]{2,1,0:T(8,128)(2,1)S(1)} %get-tuple-element.291), channel_id=1, source_target_pairs={{0,2},{1,3},{2,0},{3,1},{4,6},{5,7},{6,4},{7,5},{8,10},{9,11},{10,... | collective-permute-start | bytes 1376264 | tf_op jit(solution)/shard_map/ppermute | solution.py:668
  328.1 41.1 %collective-permute-start.63 = (bf16[4,32,1792]{2,1,0:T(8,128)(2,1)S(1)}, bf16[4,32,1792]{2,1,0:T(8,128)(2,1)S(1)}, u32[]{:S(2)}, u32[]{:S(2)}) collective-permute-start(bf16[4,32,1792]{2,1,0:T(8,128)(2,1)S(1)} %get-tuple-element.289), channel_id=1, source_target_pairs={{0,1},{1,0},{2,3},{3,2},{4,5},{5,4},{6,7},{7,6},{8,9},{9,8},{10,11... | collective-permute-start | bytes 1376264 | tf_op jit(solution)/shard_map/ppermute | solution.py:668
  329.3 56.8 %collective-permute-start.75 = (bf16[224,1280]{1,0:T(8,128)(2,1)S(1)}, bf16[224,1280]{1,0:T(8,128)(2,1)S(1)}, u32[]{:S(2)}, u32[]{:S(2)}) collective-permute-start(bf16[224,1280]{1,0:T(8,128)(2,1)S(1)} %copy-done.43), channel_id=1, source_target_pairs={{0,12},{4,8},{8,4},{12,0},{1,13},{5,9},{9,5},{13,1},{2,14},{6,10},... | collective-permute-start | bytes 1720328 | tf_op jit(solution)/shard_map/ppermute | solution.py:663
  331.4 39.1 %collective-permute-start.55 = (bf16[4,32,384]{2,1,0:T(8,128)(2,1)S(1)}, bf16[4,32,384]{2,1,0:T(8,128)(2,1)S(1)}, u32[]{:S(2)}, u32[]{:S(2)}) collective-permute-start(bf16[4,32,384]{2,1,0:T(8,128)(2,1)S(1)} %get-tuple-element.308), channel_id=1, source_target_pairs={{0,12},{4,8},{8,4},{12,0},{1,13},{5,9},{9,5},{13,1},{2,14},{6,10},... | collective-permute-start | bytes 294920 | tf_op jit(solution)/shard_map/ppermute | solution.py:663
  339.5 46.5 %collective-permute-start.74 = (bf16[224,1280]{1,0:T(8,128)(2,1)S(1)}, bf16[224,1280]{1,0:T(8,128)(2,1)S(1)}, u32[]{:S(2)}, u32[]{:S(2)}) collective-permute-start(bf16[224,1280]{1,0:T(8,128)(2,1)S(1)} %copy-done.43), channel_id=1, source_target_pairs={{0,8},{4,12},{8,0},{12,4},{1,9},{5,13},{9,1},{13,5},{2,10},{6,14},... | collective-permute-start | bytes 1720328 | tf_op jit(solution)/shard_map/ppermute | solution.py:663
  368.2 19.5 %collective-permute-start.73 = (bf16[224,1280]{1,0:T(8,128)(2,1)S(1)}, bf16[224,1280]{1,0:T(8,128)(2,1)S(1)}, u32[]{:S(2)}, u32[]{:S(2)}) collective-permute-start(bf16[224,1280]{1,0:T(8,128)(2,1)S(1)} %copy-done.43), channel_id=1, source_target_pairs={{0,4},{4,0},{8,12},{12,8},{1,5},{5,1},{9,13},{13,9},{2,6},{6,2},{1... | collective-permute-start | bytes 1720328 | tf_op jit(solution)/shard_map/ppermute | solution.py:663
  373.0 44.7 %collective-permute-start.80 = (bf16[4,160,896]{2,1,0:T(8,128)(2,1)S(1)}, bf16[4,160,896]{2,1,0:T(8,128)(2,1)S(1)}, u32[]{:S(2)}, u32[]{:S(2)}) collective-permute-start(bf16[4,160,896]{2,1,0:T(8,128)(2,1)S(1)} %pad_maximum_fusion.3.refs_0_), channel_id=1, source_target_pairs={{0,16},{16,0},{1,17},{17,1},{2,18},{18,2},{3,19},{19,3},{4,20},{20... | collective-permute-start | bytes 3440648 | tf_op jit(solution)/shard_map/ppermute | solution.py:658
  388.0 33.6 %collective-permute-start.76 = (bf16[4,224,1280]{2,1,0:T(8,128)(2,1)S(1)}, bf16[4,224,1280]{2,1,0:T(8,128)(2,1)S(1)}, u32[]{:S(2)}, u32[]{:S(2)}) collective-permute-start(bf16[4,224,1280]{2,1,0:T(8,128)(2,1)S(1)} %pad_maximum_fusion.refs_0_), channel_id=1, source_target_pairs={{0,16},{16,0},{1,17},{17,1},{2,18},{18,2},{3,19},{19,3},{4,20},{20... | collective-permute-start | bytes 6881288 | tf_op jit(solution)/shard_map/ppermute | solution.py:658
  (115 other events, 871.3 us)
Sparse Core Ops, SparseCore 0:
  73.1 52.6 all-gather.1
  215.8 50.6 reduce-scatter.1

commit v2 on v1

--- a/solution.py
+++ b/solution.py
@@ -513,7 +513,7 @@
 def grad_weight(left, right, other=None):
     rows, depth = left.shape
     cols = right.shape[1]
-    tile = 128
+    tile = rows // 2 if rows % 32 == 0 else rows
     by_rows = lambda width: pl.BlockSpec((tile, width), lambda i: (i, 0))
     in_specs = [by_rows(depth), pl.BlockSpec((depth, cols), lambda i: (0, 0))]
     args = [left, right]
@@ -735,7 +735,6 @@
     )
 
     q_own = [hop(jnp.stack(q_got), k) for k in range(tp)]
-    og_parts = [hop(og_here, k) for k in range(tp)]
     widths = tuple(v.shape[0] for v in vectors)
     w_kv, vecs, kv_local, hidden_one = project_kv(
         kv_got, x_here, cos_wide, sin_wide, rows_here, widths
@@ -744,10 +743,7 @@
     gain_one = vecs[0:1, :width]
     gain_two = vecs[1:2, :width]
     kv_z = [hop_z(kv_local, k) for k in range(n_z)]
-    o_got = [hop_z(o_part, k) for k in range(n_z)]
-    kv_z, o_got, q_own, og_parts, gu_cut, down_cut = lax.optimization_barrier(
-        (kv_z, o_got, q_own, og_parts, gu_cut, down_cut)
-    )
+    kv_z, gu_cut, down_cut, o_part = lax.optimization_barrier((kv_z, gu_cut, down_cut, o_part))
 
     kv_block = jnp.concatenate(kv_z, 0)
     if n_ctx == tp:
@@ -756,24 +752,29 @@
         kv_blocks = lax.all_gather(kv_block, "ctx", axis=0, tiled=False)
     gu_own = gather_z(gu_cut)
     down_own = [hop_z(down_cut, k) for k in range(n_z)]
+    o_got = [hop_z(o_part, k) for k in range(n_z)]
     q_own = jnp.stack(q_own)
     w_query, queries = project_query(
         q_own, swap(q_own), hidden_one, vecs, cos_wide, sin_wide, rows_here
     )
     w_query = w_query.reshape(width, width)
-    kv_blocks, queries, o_got = lax.optimization_barrier((kv_blocks, queries, o_got))
+    kv_blocks, queries, o_got, og_here = lax.optimization_barrier(
+        (kv_blocks, queries, o_got, og_here)
+    )
 
     o_own = [hop(jnp.stack(o_got), k) for k in range(tp)]
+    og_parts = [hop(og_here, k) for k in range(tp)]
     kv_whole = jnp.stack(kv_blocks) if n_ctx == tp else kv_blocks
     attended, queries_ext = attend_forward(order_row, n_ctx == tp, queries, kv_whole)
-    attended, o_own, queries_ext = lax.optimization_barrier((attended, o_own, queries_ext))
+    attended, o_own, queries_ext, og_parts, down_own = lax.optimization_barrier(
+        (attended, o_own, queries_ext, og_parts, down_own)
+    )
     o_own = jnp.stack(o_own)
     w_out, resid, hidden_two = project_out(
         o_own, swap(o_own), attended, x_here, vecs, rows_here
     )
     w_out = w_out.reshape(width, width)
     h2_parts = [hop(hidden_two, k) for k in range(tp)]
-    h2_parts, gu_own, down_own = lax.optimization_barrier((h2_parts, gu_own, down_own))
     gu_oth = swap(gu_own)
     down_own = jnp.stack(down_own)
     down_oth = swap(down_own)
@@ -787,38 +788,22 @@
         own = jnp.stack([hop(mine, k) for k in range(tp)])
         return own, swap(own)
 
-    def reduce_start(part_sum):
+    def core_halves(part_sum):
         cols = part_sum.shape[1]
         cut = part_sum.astype(BF16).reshape(n_z, rows_here, cols)
         cut = jnp.pad(cut, ((0, 0), (0, n_part * part_rows - rows_here), (0, 0)))
         own = lax.dynamic_slice_in_dim(cut, core * tp * part_rows, tp * part_rows, 1)
         oth = lax.dynamic_slice_in_dim(cut, (1 - core) * tp * part_rows, tp * part_rows, 1)
-        both = (own.astype(F32) + swap(oth).astype(F32)).astype(BF16)
-        return both.reshape(n_z, tp, part_rows, cols)
-
-    def reduce_end(cut, z_first):
-        cols = cut.shape[-1]
-        total = 0.0
-        if z_first:
-            for k in range(n_z):
-                out = lax.dynamic_index_in_dim(cut, zed ^ k, 0, keepdims=False)
-                total = total + hop_z(out, k).astype(F32)
-            cut = total.astype(BF16)
-            total = 0.0
-        for k in range(tp):
-            at = lax.rem(here, tp) ^ k
-            out = lax.dynamic_index_in_dim(cut, at, cut.ndim - 3, keepdims=False)
-            total = total + hop(out, k).astype(F32)
-        if not z_first:
-            cut = total.astype(BF16)
-            total = 0.0
-            for k in range(n_z):
-                out = lax.dynamic_index_in_dim(cut, zed ^ k, 0, keepdims=False)
-                total = total + hop_z(out, k).astype(F32)
-        total = ctx_groups_sum(total.astype(BF16))
-        total = lax.optimization_barrier(total)
-        own, sib = share_pieces(total)
-        return spread_rows((own, sib), part_rows, rows_here)
+        return own, oth
+
+    def core_total(own, sib):
+        return (own.astype(F32) + sib.astype(F32)).astype(BF16)
+
+    def scatter_hops(cut):
+        return [
+            hop_z(lax.dynamic_index_in_dim(cut, zed ^ k, 0, keepdims=False), k)
+            for k in range(n_z)
+        ]
 
     def ctx_groups_sum(v):
         if n_ctx == tp:
@@ -857,28 +842,34 @@
         .reshape(tokens_here, HEADS * HEAD)
         .astype(BF16)
     )
-    d_qo = jnp.concatenate(
-        [contract_rows(hidden_one, grad_q_pre), contract_rows(attended, grad_proj)], 1
-    )
-    d_qo = reduce_start(d_qo)
+    qo_own, qo_oth = core_halves(
+        jnp.concatenate(
+            [contract_rows(hidden_one, grad_q_pre), contract_rows(attended, grad_proj)], 1
+        )
+    )
     if n_ctx == tp:
         kv_terms = [hop(grad_terms[k], k) for k in range(n_ctx)]
-        kv_terms, d_gu, d_down, d_qo, ff_out = lax.optimization_barrier(
-            (kv_terms, d_gu, d_down, d_qo, ff_out)
-        )
-        kv_sum = sum(v.astype(F32) for v in kv_terms).astype(BF16)
     else:
-        kv_sum = lax.psum_scatter(grad_terms, "ctx", scatter_dimension=0, tiled=False)
+        kv_terms = [lax.psum_scatter(grad_terms, "ctx", scatter_dimension=0, tiled=False)]
+    kv_terms, d_gu, d_down, qo_own, qo_oth, ff_out = lax.optimization_barrier(
+        (kv_terms, d_gu, d_down, qo_own, qo_oth, ff_out)
+    )
+
+    kv_sum = sum(v.astype(F32) for v in kv_terms).astype(BF16)
+    kv_sum = kv_sum.reshape(n_z, tokens_here, 2 * key_width)
+    kv_terms = [hop_z(kv_sum[k], k) for k in range(n_z)]
+    d_gu = ctx_groups_sum(d_gu)
+    gu_pieces = [hop(d_gu, k) for k in range(tp)]
+    qo_sib = swap(qo_oth)
     result = resid + sum(v.astype(F32) for v in ff_out)
     layer_out = result.astype(BF16)[None]
-    d_gu = share_pieces(ctx_groups_sum(d_gu))
-    d_down = ctx_groups_sum(sum(v.astype(F32) for v in d_down).astype(BF16))
-    d_down = lax.optimization_barrier(d_down)
-    kv_sum = kv_sum.reshape(n_z, tokens_here, 2 * key_width)
-    kv_terms = [hop_z(kv_sum[k], k) for k in range(n_z)]
-    kv_terms, d_qo, d_down = lax.optimization_barrier((kv_terms, d_qo, d_down))
+    kv_terms, qo_own, qo_sib, d_down = lax.optimization_barrier(
+        (kv_terms, qo_own, qo_sib, d_down)
+    )
+
+    qo_cut = core_total(qo_own, qo_sib)
+    qo_terms = scatter_hops(qo_cut)
     grad_kv = sum(v.astype(F32) for v in kv_terms)
-
     grad_k_pre = (
         rotate(
             grad_kv[:, :key_width].reshape(tokens_here, KV_HEADS, HEAD), cosine_table, -sine_table
@@ -887,7 +878,6 @@
         .astype(BF16)
     )
     grad_v_pre = grad_kv[:, key_width:].astype(BF16)
-
     grad_kv_pre = jnp.concatenate([grad_k_pre, grad_v_pre], 1)
     grad_hidden_one = times_transposed(grad_q_pre, w_query) + times_transposed(grad_kv_pre, w_kv)
     inputs = x_here.astype(F32)
@@ -901,19 +891,50 @@
         v = v.reshape(tokens_here, n_z, share)
         return jnp.pad(v, ((0, 0), (0, 0), (0, rows_here - share))).reshape(tokens_here, width)
 
-    d_qo = reduce_end(d_qo, True)
-    grad_w_query = d_qo[:, :width]
-    grad_w_out = d_qo[:, width:]
     terms = (gain_one_terms, gain_two_terms, grad_q_pre, by_rows(grad_k_pre), by_rows(grad_v_pre))
     pick = jnp.arange(len(terms) * tokens_here)[:, None] // tokens_here == jnp.arange(128)[None]
     columns = contract_rows(
         jnp.concatenate([v.astype(BF16) for v in terms], 0), pick.astype(BF16)
     )
-    grad_w_kv = jnp.concatenate([contract_rows(hidden_one, grad_kv_pre), columns], 1)
-    grad_w_kv = reduce_end(reduce_start(grad_w_kv), False)
+    kv_own, kv_oth = core_halves(
+        jnp.concatenate([contract_rows(hidden_one, grad_kv_pre), columns], 1)
+    )
+    kv_sib = swap(kv_oth)
+    kv_own, kv_sib, gu_pieces, d_down = lax.optimization_barrier(
+        (kv_own, kv_sib, gu_pieces, d_down)
+    )
+
+    kv_terms = scatter_hops(core_total(kv_own, kv_sib))
+    d_down = ctx_groups_sum(sum(v.astype(F32) for v in d_down).astype(BF16))
+    d_down = lax.optimization_barrier(d_down)
+    down_pieces = [hop(d_down, k) for k in range(tp)]
+    gu_pieces = jnp.stack(gu_pieces)
+    gu_sib = swap(gu_pieces)
+    qo_terms, kv_terms, down_pieces, gu_sib, gu_pieces = lax.optimization_barrier(
+        (qo_terms, kv_terms, down_pieces, gu_sib, gu_pieces)
+    )
+
+    last = jnp.concatenate(
+        [sum(v.astype(F32) for v in qo_terms), sum(v.astype(F32) for v in kv_terms)], 1
+    ).astype(BF16)
+    last = last.reshape(tp, part_rows, -1)
+    at = lax.rem(here, tp)
+    last = [hop(lax.dynamic_index_in_dim(last, at ^ k, 0, keepdims=False), k) for k in range(tp)]
+    down_pieces = jnp.stack(down_pieces)
+    down_sib = swap(down_pieces)
+    grad_w_gate, grad_w_up = spread_columns((gu_pieces, gu_sib), n_z, ff, 2)
+    last, down_sib, down_pieces, grad_w_gate, grad_w_up = lax.optimization_barrier(
+        (last, down_sib, down_pieces, grad_w_gate, grad_w_up)
+    )
+
+    last = ctx_groups_sum(sum(v.astype(F32) for v in last).astype(BF16))
+    last = lax.optimization_barrier(last)
+    grad_w_down = spread_rows((down_pieces, down_sib), piece, ff_z)
+    last = spread_rows(share_pieces(last), part_rows, rows_here)
+    grad_w_query = last[:, :width]
+    grad_w_out = last[:, width : 2 * width]
+    grad_w_kv = last[:, 2 * width :]
     sums = grad_w_kv[:, 2 * key_width :]
-    grad_w_down = spread_rows(share_pieces(d_down), piece, ff_z)
-    grad_w_gate, grad_w_up = spread_columns(d_gu, n_z, ff, 2)
 
     return (
         layer_out,

time: 440 us -> 444 us (level)
  Pallas kernels: 98 us -> 60.9 us
  starting transfers between devices: 103 us -> 130 us
  waiting for transfers between devices: 138 us -> 155 us
    pallas_call x1, Pallas kernels: 27.4 us -> 8.9 us  [attend_backward(): pl.pallas_call(functools.partial(backward_kernel, by_xor), grid_spec=pltp...]
    ppermute x27, waiting for transfers between devices: 73.9 us -> 90.8 us  [hop_z(): return lax.ppermute(v, 'fsdp', [(i, i ^ k) for i in range(n_z)])]
    ppermute x42 -> x36, waiting for transfers between devices: 59.4 us -> 45.6 us  [hop(): return lax.ppermute(v, 'ctx', [(i, i ^ k) for i in range(n_ctx)])]
    ppermute x42 -> x36, starting transfers between devices: 39 us -> 52.6 us  [hop(): return lax.ppermute(v, 'ctx', [(i, i ^ k) for i in range(n_ctx)])]
    ppermute x27, starting transfers between devices: 41.9 us -> 55.5 us  [hop_z(): return lax.ppermute(v, 'fsdp', [(i, i ^ k) for i in range(n_z)])]
    all_gather x1, waiting for transfers between devices: 0.01 us -> 12.1 us  [gather_z(): return lax.all_gather(v, 'fsdp', axis=0, tiled=True)]
    pallas_call x4, Pallas kernels: 17.7 us -> 7.02 us  [grad_weight(): pl.pallas_call(grad_weight_kernel, grid=(rows // tile,), in_specs=in_spec...]
    pallas_call x1, Pallas kernels: 16.5 us -> 5.85 us  [attend_forward(): pl.pallas_call(functools.partial(forward_kernel, by_xor), grid_spec=pltpu...]
  transfers between devices with their start and end apart: 83 -> 76, of which waited for: 26 -> 31; matrix products, arithmetic and copies ran while one was open for 11% -> 11% of each run, Pallas kernels for 15% -> 8%
where the time goes in v2:
time: 444 us; the launch traced here: 439 us
  waiting for transfers between devices  155 us (35%)
  starting transfers between devices  130 us (29%)
  Pallas kernels  60.9 us (14%)
  local copies, waits for them, and re-layouts  42.5 us (10%)
  other arithmetic  26.4 us (6%)
  between operations  16.3 us (4%)
  matrix products  8.09 us (2%)
    ppermute x27, waiting for transfers between devices, hop_z(): return lax.ppermute(v, 'fsdp', [(i, i ^ k) for i in range(n_z)])  90.8 us
    ppermute x27, starting transfers between devices, hop_z(): return lax.ppermute(v, 'fsdp', [(i, i ^ k) for i in range(n_z)])  55.5 us
    ppermute x36, starting transfers between devices, hop(): return lax.ppermute(v, 'ctx', [(i, i ^ k) for i in range(n_ctx)])  52.6 us
    ppermute x36, waiting for transfers between devices, hop(): return lax.ppermute(v, 'ctx', [(i, i ^ k) for i in range(n_ctx)])  45.6 us
    ppermute x11, starting transfers between devices, swap(): return lax.ppermute(v, 'seq', [(0, 1), (1, 0)])  21.8 us
    pallas_call x1, Pallas kernels, ff_pass(): pl.pallas_call(functools.partial(ff_kernel, tp, n_z), in_specs=[vmem] * (...  21.7 us
    unnamed x157, local copies, waits for them, and re-layouts  17.1 us
    all_gather x1, waiting for transfers between devices, gather_z(): return lax.all_gather(v, 'fsdp', axis=0, tiled=True)  12.1 us
  transfers between devices with their start and end apart: 76, of which 31 were waited for; matrix products, arithmetic and copies ran while one was open for 11% of the time, Pallas kernels for 8%

profile of v2, /device:TPU:1, one launch (start us, length us, event | category | flops | bytes accessed | tf_op | source)
XLA Modules:
  0.0 438.9 jit_solution(2393472309005329993)
XLA Ops:
  19.1 3.2 collective-permute-start.4
  27.5 4.0 collective-permute-done.4
  42.1 3.8 collective-permute-done.8
  49.7 3.2 collective-permute-done.14
  55.8 5.4 %collective-permute-start.15 = (bf16[4,4,32,896]{3,2,1,0:T(8,128)(2,1)S(1)}, bf16[4,4,32,896]{3,2,1,0:T(8,128)(2,1)S(1)}, u32[]{:S(2)}, u32[]{:S(2)}) collective-permute-start(bf16[4,4,32,896]{3,2,1,0:T(8,128)(2,1)S(1)} %pad_maximum_fusion.4.own_ref), channel_id=1, source_target_pairs={{0,16},{16,0},{1,17},{17,1},{2,18},{18,2},{3,19},{19,3},{4,20},{20... | collective-permute-start | bytes 2752520 | tf_op jit(solution)/shard_map/ppermute | solution.py:658
  67.3 3.3 collective-permute-start.16
  70.6 5.5 %collective-permute-done.16 = bf16[32,896]{1,0:T(8,128)(2,1)S(1)} collective-permute-done((bf16[32,896]{1,0:T(8,128)(2,1)S(1)}, bf16[32,896]{1,0:T(8,128)(2,1)S(1)}, u32[]{:S(2)}, u32[]{:S(2)}) %collective-permute-start.16) | collective-permute-done | bytes 57376 | tf_op jit(solution)/shard_map/ppermute | solution.py:668
  77.0 8.5 %collective-permute-done.17 = bf16[32,896]{1,0:T(8,128)(2,1)S(1)} collective-permute-done((bf16[32,896]{1,0:T(8,128)(2,1)S(1)}, bf16[32,896]{1,0:T(8,128)(2,1)S(1)}, u32[]{:S(2)}, u32[]{:S(2)}) %collective-permute-start.17) | collective-permute-done | bytes 57376 | tf_op jit(solution)/shard_map/ppermute | solution.py:668
  85.5 3.3 collective-permute-start.18
  91.7 12.1 %all-gather.2.cloned.1.call-done.refs_8_ = bf16[896,1280]{1,0:T(8,128)(2,1)} async-done(((bf16[224,1280]{1,0:T(8,128)(2,1)}), bf16[896,1280]{1,0:T(8,128)(2,1)}) %all-gather.2.cloned.1.call-update) | async-done | bytes 2293776 | tf_op jit(solution)/shard_map/all_gather | solution.py:671
  110.6 6.0 %collective-permute-done.25 = bf16[160,896]{1,0:T(8,128)(2,1)S(1)} collective-permute-done((bf16[160,896]{1,0:T(8,128)(2,1)S(1)}, bf16[160,896]{1,0:T(8,128)(2,1)S(1)}, u32[]{:S(2)}, u32[]{:S(2)}) %collective-permute-start.25) | collective-permute-done | bytes 286752 | tf_op jit(solution)/shard_map/ppermute | solution.py:668
  117.8 9.6 %collective-permute-done.26 = bf16[160,896]{1,0:T(8,128)(2,1)S(1)} collective-permute-done((bf16[160,896]{1,0:T(8,128)(2,1)S(1)}, bf16[160,896]{1,0:T(8,128)(2,1)S(1)}, u32[]{:S(2)}, u32[]{:S(2)}) %collective-permute-start.26) | collective-permute-done | bytes 286752 | tf_op jit(solution)/shard_map/ppermute | solution.py:668
  133.8 5.9 %attend_forward.1 = (bf16[192,896]{1,0:T(8,128)(2,1)S(1)}, bf16[2688,256]{1,0:T(8,128)(2,1)S(1)}) custom-call(s32[4]{0:T(128)S(1)} %bitcast.132, bf16[192,896]{1,0:T(8,128)(2,1)S(1)} %get-tuple-element.199.q_ref, bf16[4,768,256]{2,1,0:T(8,128)(2,1)S(1)} %pad_maximum_fusion.1.kv_ref), custom_call_target="tpu_custom_call" | custom-call | tf_op jit(solution)/shard_map/attend_forward/pallas_call | solution.py:250
  139.7 9.6 %collective-permute-done.21 = bf16[4,32,896]{2,1,0:T(8,128)(2,1)S(1)} collective-permute-done((bf16[4,32,896]{2,1,0:T(8,128)(2,1)S(1)}, bf16[4,32,896]{2,1,0:T(8,128)(2,1)S(1)}, u32[]{:S(2)}, u32[]{:S(2)}) %collective-permute-start.21) | collective-permute-done | bytes 229408 | tf_op jit(solution)/shard_map/ppermute | solution.py:663
  159.1 6.6 %collective-permute-done.29.refs_1_ = bf16[192,896]{1,0:T(8,128)(2,1)S(1)} collective-permute-done((bf16[192,896]{1,0:T(8,128)(2,1)S(1)}, bf16[192,896]{1,0:T(8,128)(2,1)S(1)}, u32[]{:S(2)}, u32[]{:S(2)}) %collective-permute-start.29) | collective-permute-done | bytes 344096 | tf_op jit(solution)/shard_map/ppermute | solution.py:663
  166.4 7.7 %collective-permute-done.31.refs_3_ = bf16[192,896]{1,0:T(8,128)(2,1)S(1)} collective-permute-done((bf16[192,896]{1,0:T(8,128)(2,1)S(1)}, bf16[192,896]{1,0:T(8,128)(2,1)S(1)}, u32[]{:S(2)}, u32[]{:S(2)}) %collective-permute-start.31) | collective-permute-done | bytes 344096 | tf_op jit(solution)/shard_map/ppermute | solution.py:663
  174.8 21.7 %ff_pass.1 = (bf16[640,768]{1,0:T(8,128)(2,1)}, bf16[640,768]{1,0:T(8,128)(2,1)}, bf16[768,1280]{1,0:T(8,128)(2,1)}, bf16[768,1280]{1,0:T(8,128)(2,1)}, bf16[896...) custom-call(bf16[192,896]{1,0:T(8,128)(2,1)} %copy-done.21, ...), custom_call_target="tpu_custom_call" | custom-call | tf_op jit(solution)/shard_map/ff_pass/pallas_call | solution.py:609
  214.8 7.5 %collective-permute-done.36 = bf16[192,896]{1,0:T(8,128)(2,1)} collective-permute-done((bf16[192,896]{1,0:T(8,128)(2,1)}, bf16[192,896]{1,0:T(8,128)(2,1)}, u32[]{:S(2)}, u32[]{:S(2)}) %collective-permute-start.36) | collective-permute-done | bytes 344096 | tf_op jit(solution)/shard_map/ppermute | solution.py:663
  231.7 6.0 %collective-permute-start.45 = (bf16[160,896]{1,0:T(8,128)(2,1)}, bf16[160,896]{1,0:T(8,128)(2,1)}, u32[]{:S(2)}, u32[]{:S(2)}) collective-permute-start(bf16[160,896]{1,0:T(8,128)(2,1)} %get-tuple-element.357), channel_id=1, source_target_pairs={{0,1},{1,0},{2,3},{3,2},{4,5},{5,4},{6,7},{7,6},{8,9},{9,8},{10,11... | collective-permute-start | bytes 860168 | tf_op jit(solution)/shard_map/ppermute | solution.py:668
  238.5 8.9 %attend_backward.1 = (f32[192,896]{1,0:T(8,128)S(1)}, bf16[4,768,256]{2,1,0:T(8,128)(2,1)S(1)}) custom-call(s32[4]{0:T(128)S(1)} %bitcast.133, bf16[2688,256]{1,0:T(8,128)(2,1)S(1)} %copy-done.15, bf16[192,896]{1,0:T(8,128)(2,1)S(1)} %convolution_convert_fusion.3.do_ref, bf16[192,896]{1,0:T(8,128)(2,1)S(1)} %get-tuple-element.216.att_ref, ...), custom_call_target="tpu_custom_call" | custom-call | tf_op jit(solution)/shard_map/attend_backward/pallas_call | solution.py:278
  248.8 12.6 %collective-permute-start.42 = (bf16[768,256]{1,0:T(8,128)(2,1)}, bf16[768,256]{1,0:T(8,128)(2,1)}, u32[]{:S(2)}, u32[]{:S(2)}) collective-permute-start(bf16[768,256]{1,0:T(8,128)(2,1)} %get-tuple-element.353), channel_id=1, source_target_pairs={{0,4},{4,0},{8,12},{12,8},{1,5},{5,1},{9,13},{13,9},{2,6},{6,2},{1... | collective-permute-start | bytes 1179656 | tf_op jit(solution)/shard_map/ppermute | solution.py:663
  261.4 6.0 %collective-permute-start.43 = (bf16[768,256]{1,0:T(8,128)(2,1)}, bf16[768,256]{1,0:T(8,128)(2,1)}, u32[]{:S(2)}, u32[]{:S(2)}) collective-permute-start(bf16[768,256]{1,0:T(8,128)(2,1)} %get-tuple-element.352), channel_id=1, source_target_pairs={{0,8},{4,12},{8,0},{12,4},{1,9},{5,13},{9,1},{13,5},{2,10},{6,14},... | collective-permute-start | bytes 1179656 | tf_op jit(solution)/shard_map/ppermute | solution.py:663
  276.0 11.1 %collective-permute-done.47 = bf16[160,896]{1,0:T(8,128)(2,1)S(1)} collective-permute-done((bf16[160,896]{1,0:T(8,128)(2,1)S(1)}, bf16[160,896]{1,0:T(8,128)(2,1)S(1)}, u32[]{:S(2)}, u32[]{:S(2)}) %collective-permute-start.47) | collective-permute-done | bytes 286752 | tf_op jit(solution)/shard_map/ppermute | solution.py:668
  294.7 5.4 %collective-permute-start.48 = (bf16[192,256]{1,0:T(8,128)(2,1)}, bf16[192,256]{1,0:T(8,128)(2,1)S(1)}, u32[]{:S(2)}, u32[]{:S(2)}) collective-permute-start(bf16[192,256]{1,0:T(8,128)(2,1)} %get-tuple-element.373), channel_id=1, source_target_pairs={{0,1},{1,0},{2,3},{3,2},{4,5},{5,4},{6,7},{7,6},{8,9},{9,8},{10,11... | collective-permute-start | bytes 294920 | tf_op jit(solution)/shard_map/ppermute | solution.py:668
  304.8 4.8 %collective-permute-done.49 = bf16[192,256]{1,0:T(8,128)(2,1)S(1)} collective-permute-done((bf16[192,256]{1,0:T(8,128)(2,1)}, bf16[192,256]{1,0:T(8,128)(2,1)S(1)}, u32[]{:S(2)}, u32[]{:S(2)}) %collective-permute-start.49) | collective-permute-done | bytes 98336 | tf_op jit(solution)/shard_map/ppermute | solution.py:668
  330.0 3.2 pad_maximum_fusion.refs_0_
  342.9 15.7 %collective-permute-done.52 = bf16[128,1792]{1,0:T(8,128)(2,1)S(1)} collective-permute-done((bf16[128,1792]{1,0:T(8,128)(2,1)S(1)}, bf16[128,1792]{1,0:T(8,128)(2,1)S(1)}, u32[]{:S(2)}, u32[]{:S(2)}) %collective-permute-start.52) | collective-permute-done | bytes 458784 | tf_op jit(solution)/shard_map/ppermute | solution.py:668
  359.5 11.7 %collective-permute-done.53 = bf16[128,1792]{1,0:T(8,128)(2,1)S(1)} collective-permute-done((bf16[128,1792]{1,0:T(8,128)(2,1)S(1)}, bf16[128,1792]{1,0:T(8,128)(2,1)S(1)}, u32[]{:S(2)}, u32[]{:S(2)}) %collective-permute-start.53) | collective-permute-done | bytes 458784 | tf_op jit(solution)/shard_map/ppermute | solution.py:668
  373.7 9.8 %collective-permute-start.60 = (bf16[128,384]{1,0:T(8,128)(2,1)S(1)}, bf16[128,384]{1,0:T(8,128)(2,1)S(1)}, u32[]{:S(2)}, u32[]{:S(2)}) collective-permute-start(bf16[128,384]{1,0:T(8,128)(2,1)S(1)} %get-tuple-element.368), channel_id=1, source_target_pairs={{0,2},{1,3},{2,0},{3,1},{4,6},{5,7},{6,4},{7,5},{8,10},{9,11},{10,... | collective-permute-start | bytes 294920 | tf_op jit(solution)/shard_map/ppermute | solution.py:668
  393.1 4.6 %collective-permute-start.69 = (bf16[4,160,896]{2,1,0:T(8,128)(2,1)S(1)}, bf16[4,160,896]{2,1,0:T(8,128)(2,1)S(1)}, u32[]{:S(2)}, u32[]{:S(2)}) collective-permute-start(bf16[4,160,896]{2,1,0:T(8,128)(2,1)S(1)} %pad_maximum_fusion.3.refs_0_), channel_id=1, source_target_pairs={{0,16},{16,0},{1,17},{17,1},{2,18},{18,2},{3,19},{19,3},{4,20},{20... | collective-permute-start | bytes 3440648 | tf_op jit(solution)/shard_map/ppermute | solution.py:658
  401.8 9.1 %spread_columns.1 = (f32[224,4864]{1,0:T(8,128)}, f32[224,4864]{1,0:T(8,128)}) custom-call(bf16[4,224,1280]{2,1,0:T(8,128)(2,1)} %pad_maximum_fusion.refs_0_, bf16[4,224,1280]{2,1,0:T(8,128)(2,1)} %collective-permute-done.65.refs_1_), custom_call_target="tpu_custom_call" | custom-call | tf_op jit(solution)/shard_map/spread_columns/pallas_call | solution.py:337
  422.8 3.8 spread_rows.3
  (390 shorter events, 182.9 us)
Async XLA Ops:
  7.2 96.6 %all-gather.2.cloned.1.call-start = ((), (), s32[]{:S(2)}) async-start(), calls=%async_computation.1 | async-start | bytes 2867200 | tf_op jit(solution)/shard_map/all_gather | solution.py:671
  46.0 244.3 %reduce-scatter.2.cloned.1.call-start = ((), (), s32[]{:S(2)}) async-start(), calls=%async_computation.2 | async-start | bytes 2867200 | tf_op jit(solution)/shard_map/reduce_scatter | solution.py:674
  55.8 48.7 %collective-permute-start.15 = (bf16[4,4,32,896]{3,2,1,0:T(8,128)(2,1)S(1)}, bf16[4,4,32,896]{3,2,1,0:T(8,128)(2,1)S(1)}, u32[]{:S(2)}, u32[]{:S(2)}) collective-permute-start(bf16[4,4,32,896]{3,2,1,0:T(8,128)(2,1)S(1)} %pad_maximum_fusion.4.own_ref), channel_id=1, source_target_pairs={{0,16},{16,0},{1,17},{17,1},{2,18},{18,2},{3,19},{19,3},{4,20},{20... | collective-permute-start | bytes 2752520 | tf_op jit(solution)/shard_map/ppermute | solution.py:658
  64.7 41.0 %collective-permute-start.9 = (bf16[768,256]{1,0:T(8,128)(2,1)}, bf16[768,256]{1,0:T(8,128)(2,1)}, u32[]{:S(2)}, u32[]{:S(2)}) collective-permute-start(bf16[768,256]{1,0:T(8,128)(2,1)} %constant_dynamic-update-slice_fusion), channel_id=1, source_target_pairs={{0,4},{4,0},{8,12},{12,8},{1,5},{5,1},{9,13},{13,9},{2,6},{6,2},{1... | collective-permute-start | bytes 1179656 | tf_op jit(solution)/shard_map/ppermute | solution.py:663
  65.9 40.7 %collective-permute-start.10 = (bf16[768,256]{1,0:T(8,128)(2,1)}, bf16[768,256]{1,0:T(8,128)(2,1)}, u32[]{:S(2)}, u32[]{:S(2)}) collective-permute-start(bf16[768,256]{1,0:T(8,128)(2,1)} %constant_dynamic-update-slice_fusion), channel_id=1, source_target_pairs={{0,8},{4,12},{8,0},{12,4},{1,9},{5,13},{9,1},{13,5},{2,10},{6,14},... | collective-permute-start | bytes 1179656 | tf_op jit(solution)/shard_map/ppermute | solution.py:663
  66.6 42.7 %collective-permute-start.11 = (bf16[768,256]{1,0:T(8,128)(2,1)}, bf16[768,256]{1,0:T(8,128)(2,1)}, u32[]{:S(2)}, u32[]{:S(2)}) collective-permute-start(bf16[768,256]{1,0:T(8,128)(2,1)} %constant_dynamic-update-slice_fusion), channel_id=1, source_target_pairs={{0,12},{4,8},{8,4},{12,0},{1,13},{5,9},{9,5},{13,1},{2,14},{6,10},... | collective-permute-start | bytes 1179656 | tf_op jit(solution)/shard_map/ppermute | solution.py:663
  103.8 71.0 %collective-permute-start.32 = (bf16[896,1280]{1,0:T(8,128)(2,1)}, bf16[896,1280]{1,0:T(8,128)(2,1)}, u32[]{:S(2)}, u32[]{:S(2)}) collective-permute-start(bf16[896,1280]{1,0:T(8,128)(2,1)} %all-gather.2.cloned.1.call-done.refs_8_), channel_id=1, source_target_pairs={{0,16},{16,0},{1,17},{17,1},{2,18},{18,2},{3,19},{19,3},{4,20},{20... | collective-permute-start | bytes 6881288 | tf_op jit(solution)/shard_map/ppermute | solution.py:658
  105.7 21.7 %collective-permute-start.26 = (bf16[160,896]{1,0:T(8,128)(2,1)S(1)}, bf16[160,896]{1,0:T(8,128)(2,1)S(1)}, u32[]{:S(2)}, u32[]{:S(2)}) collective-permute-start(bf16[160,896]{1,0:T(8,128)(2,1)S(1)} %pad.77), channel_id=1, source_target_pairs={{0,2},{1,3},{2,0},{3,1},{4,6},{5,7},{6,4},{7,5},{8,10},{9,11},{10,... | collective-permute-start | bytes 860168 | tf_op jit(solution)/shard_map/ppermute | solution.py:668
  106.6 22.0 %collective-permute-start.27 = (bf16[160,896]{1,0:T(8,128)(2,1)S(1)}, bf16[160,896]{1,0:T(8,128)(2,1)S(1)}, u32[]{:S(2)}, u32[]{:S(2)}) collective-permute-start(bf16[160,896]{1,0:T(8,128)(2,1)S(1)} %pad.77), channel_id=1, source_target_pairs={{0,3},{1,2},{2,1},{3,0},{4,7},{5,6},{6,5},{7,4},{8,11},{9,10},{10,... | collective-permute-start | bytes 860168 | tf_op jit(solution)/shard_map/ppermute | solution.py:668
  109.4 20.5 %collective-permute-start.19 = (bf16[4,32,896]{2,1,0:T(8,128)(2,1)S(1)}, bf16[4,32,896]{2,1,0:T(8,128)(2,1)S(1)}, u32[]{:S(2)}, u32[]{:S(2)}) collective-permute-start(bf16[4,32,896]{2,1,0:T(8,128)(2,1)S(1)} %pad_maximum_fusion.8), channel_id=1, source_target_pairs={{0,4},{4,0},{8,12},{12,8},{1,5},{5,1},{9,13},{13,9},{2,6},{6,2},{1... | collective-permute-start | bytes 688136 | tf_op jit(solution)/shard_map/ppermute | solution.py:663
  127.4 21.8 %collective-permute-start.22 = (bf16[192,896]{1,0:T(8,128)(2,1)}, bf16[192,896]{1,0:T(8,128)(2,1)S(1)}, u32[]{:S(2)}, u32[]{:S(2)}) collective-permute-start(bf16[192,896]{1,0:T(8,128)(2,1)} %bitcast.6.refs_4_), channel_id=1, source_target_pairs={{0,4},{4,0},{8,12},{12,8},{1,5},{5,1},{9,13},{13,9},{2,6},{6,2},{1... | collective-permute-start | bytes 1032200 | tf_op jit(solution)/shard_map/ppermute | solution.py:663
  128.6 20.6 %collective-permute-start.23 = (bf16[192,896]{1,0:T(8,128)(2,1)}, bf16[192,896]{1,0:T(8,128)(2,1)S(1)}, u32[]{:S(2)}, u32[]{:S(2)}) collective-permute-start(bf16[192,896]{1,0:T(8,128)(2,1)} %bitcast.6.refs_4_), channel_id=1, source_target_pairs={{0,8},{4,12},{8,0},{12,4},{1,9},{5,13},{9,1},{13,5},{2,10},{6,14},... | collective-permute-start | bytes 1032200 | tf_op jit(solution)/shard_map/ppermute | solution.py:663
  129.8 19.4 %collective-permute-start.24 = (bf16[192,896]{1,0:T(8,128)(2,1)}, bf16[192,896]{1,0:T(8,128)(2,1)S(1)}, u32[]{:S(2)}, u32[]{:S(2)}) collective-permute-start(bf16[192,896]{1,0:T(8,128)(2,1)} %bitcast.6.refs_4_), channel_id=1, source_target_pairs={{0,12},{4,8},{8,4},{12,0},{1,13},{5,9},{9,5},{13,1},{2,14},{6,10},... | collective-permute-start | bytes 1032200 | tf_op jit(solution)/shard_map/ppermute | solution.py:663
  223.7 23.7 %collective-permute-start.39 = (bf16[192,896]{1,0:T(8,128)(2,1)}, bf16[192,896]{1,0:T(8,128)(2,1)S(1)}, u32[]{:S(2)}, u32[]{:S(2)}) collective-permute-start(bf16[192,896]{1,0:T(8,128)(2,1)} %get-tuple-element.251), channel_id=1, source_target_pairs={{0,4},{4,0},{8,12},{12,8},{1,5},{5,1},{9,13},{13,9},{2,6},{6,2},{1... | collective-permute-start | bytes 1032200 | tf_op jit(solution)/shard_map/ppermute | solution.py:663
  224.8 22.7 %collective-permute-start.40 = (bf16[192,896]{1,0:T(8,128)(2,1)}, bf16[192,896]{1,0:T(8,128)(2,1)S(1)}, u32[]{:S(2)}, u32[]{:S(2)}) collective-permute-start(bf16[192,896]{1,0:T(8,128)(2,1)} %get-tuple-element.252), channel_id=1, source_target_pairs={{0,8},{4,12},{8,0},{12,4},{1,9},{5,13},{9,1},{13,5},{2,10},{6,14},... | collective-permute-start | bytes 1032200 | tf_op jit(solution)/shard_map/ppermute | solution.py:663
  224.8 22.7 %collective-permute-start.41 = (bf16[192,896]{1,0:T(8,128)(2,1)}, bf16[192,896]{1,0:T(8,128)(2,1)S(1)}, u32[]{:S(2)}, u32[]{:S(2)}) collective-permute-start(bf16[192,896]{1,0:T(8,128)(2,1)} %get-tuple-element.253), channel_id=1, source_target_pairs={{0,12},{4,8},{8,4},{12,0},{1,13},{5,9},{9,5},{13,1},{2,14},{6,10},... | collective-permute-start | bytes 1032200 | tf_op jit(solution)/shard_map/ppermute | solution.py:663
  231.7 39.5 %collective-permute-start.45 = (bf16[160,896]{1,0:T(8,128)(2,1)}, bf16[160,896]{1,0:T(8,128)(2,1)}, u32[]{:S(2)}, u32[]{:S(2)}) collective-permute-start(bf16[160,896]{1,0:T(8,128)(2,1)} %get-tuple-element.357), channel_id=1, source_target_pairs={{0,1},{1,0},{2,3},{3,2},{4,5},{5,4},{6,7},{7,6},{8,9},{9,8},{10,11... | collective-permute-start | bytes 860168 | tf_op jit(solution)/shard_map/ppermute | solution.py:668
  237.7 38.3 %collective-permute-start.46 = (bf16[160,896]{1,0:T(8,128)(2,1)}, bf16[160,896]{1,0:T(8,128)(2,1)}, u32[]{:S(2)}, u32[]{:S(2)}) collective-permute-start(bf16[160,896]{1,0:T(8,128)(2,1)} %get-tuple-element.356), channel_id=1, source_target_pairs={{0,2},{1,3},{2,0},{3,1},{4,6},{5,7},{6,4},{7,5},{8,10},{9,11},{10,... | collective-permute-start | bytes 860168 | tf_op jit(solution)/shard_map/ppermute | solution.py:668
  248.8 38.3 %collective-permute-start.42 = (bf16[768,256]{1,0:T(8,128)(2,1)}, bf16[768,256]{1,0:T(8,128)(2,1)}, u32[]{:S(2)}, u32[]{:S(2)}) collective-permute-start(bf16[768,256]{1,0:T(8,128)(2,1)} %get-tuple-element.353), channel_id=1, source_target_pairs={{0,4},{4,0},{8,12},{12,8},{1,5},{5,1},{9,13},{13,9},{2,6},{6,2},{1... | collective-permute-start | bytes 1179656 | tf_op jit(solution)/shard_map/ppermute | solution.py:663
  261.4 25.7 %collective-permute-start.43 = (bf16[768,256]{1,0:T(8,128)(2,1)}, bf16[768,256]{1,0:T(8,128)(2,1)}, u32[]{:S(2)}, u32[]{:S(2)}) collective-permute-start(bf16[768,256]{1,0:T(8,128)(2,1)} %get-tuple-element.352), channel_id=1, source_target_pairs={{0,8},{4,12},{8,0},{12,4},{1,9},{5,13},{9,1},{13,5},{2,10},{6,14},... | collective-permute-start | bytes 1179656 | tf_op jit(solution)/shard_map/ppermute | solution.py:663
  267.5 19.7 %collective-permute-start.44 = (bf16[768,256]{1,0:T(8,128)(2,1)}, bf16[768,256]{1,0:T(8,128)(2,1)}, u32[]{:S(2)}, u32[]{:S(2)}) collective-permute-start(bf16[768,256]{1,0:T(8,128)(2,1)} %get-tuple-element.351), channel_id=1, source_target_pairs={{0,12},{4,8},{8,4},{12,0},{1,13},{5,9},{9,5},{13,1},{2,14},{6,10},... | collective-permute-start | bytes 1179656 | tf_op jit(solution)/shard_map/ppermute | solution.py:663
  290.2 21.5 %collective-permute-start.51 = (bf16[4,128,1792]{2,1,0:T(8,128)(2,1)}, bf16[4,128,1792]{2,1,0:T(8,128)(2,1)}, u32[]{:S(2)}, u32[]{:S(2)}) collective-permute-start(bf16[4,128,1792]{2,1,0:T(8,128)(2,1)} %get-tuple-element.273), channel_id=1, source_target_pairs={{0,16},{16,0},{1,17},{17,1},{2,18},{18,2},{3,19},{19,3},{4,20},{20... | collective-permute-start | bytes 5505032 | tf_op jit(solution)/shard_map/ppermute | solution.py:658
  302.4 26.2 %collective-permute-start.56 = (bf16[224,1280]{1,0:T(8,128)(2,1)}, bf16[224,1280]{1,0:T(8,128)(2,1)}, u32[]{:S(2)}, u32[]{:S(2)}) collective-permute-start(bf16[224,1280]{1,0:T(8,128)(2,1)} %reduce-scatter.2.cloned.1.call-done), channel_id=1, source_target_pairs={{0,4},{4,0},{8,12},{12,8},{1,5},{5,1},{9,13},{13,9},{2,6},{6,2},{1... | collective-permute-start | bytes 1720328 | tf_op jit(solution)/shard_map/ppermute | solution.py:663
  303.6 24.9 %collective-permute-start.57 = (bf16[224,1280]{1,0:T(8,128)(2,1)}, bf16[224,1280]{1,0:T(8,128)(2,1)}, u32[]{:S(2)}, u32[]{:S(2)}) collective-permute-start(bf16[224,1280]{1,0:T(8,128)(2,1)} %reduce-scatter.2.cloned.1.call-done), channel_id=1, source_target_pairs={{0,8},{4,12},{8,0},{12,4},{1,9},{5,13},{9,1},{13,5},{2,10},{6,14},... | collective-permute-start | bytes 1720328 | tf_op jit(solution)/shard_map/ppermute | solution.py:663
  309.6 20.3 %collective-permute-start.58 = (bf16[224,1280]{1,0:T(8,128)(2,1)}, bf16[224,1280]{1,0:T(8,128)(2,1)}, u32[]{:S(2)}, u32[]{:S(2)}) collective-permute-start(bf16[224,1280]{1,0:T(8,128)(2,1)} %reduce-scatter.2.cloned.1.call-done), channel_id=1, source_target_pairs={{0,12},{4,8},{8,4},{12,0},{1,13},{5,9},{9,5},{13,1},{2,14},{6,10},... | collective-permute-start | bytes 1720328 | tf_op jit(solution)/shard_map/ppermute | solution.py:663
  333.2 57.7 %collective-permute-start.65 = (bf16[4,224,1280]{2,1,0:T(8,128)(2,1)}, bf16[4,224,1280]{2,1,0:T(8,128)(2,1)}, u32[]{:S(2)}, u32[]{:S(2)}) collective-permute-start(bf16[4,224,1280]{2,1,0:T(8,128)(2,1)} %pad_maximum_fusion.refs_0_), channel_id=1, source_target_pairs={{0,16},{16,0},{1,17},{17,1},{2,18},{18,2},{3,19},{19,3},{4,20},{20... | collective-permute-start | bytes 6881288 | tf_op jit(solution)/shard_map/ppermute | solution.py:658
  337.7 20.8 %collective-permute-start.52 = (bf16[128,1792]{1,0:T(8,128)(2,1)S(1)}, bf16[128,1792]{1,0:T(8,128)(2,1)S(1)}, u32[]{:S(2)}, u32[]{:S(2)}) collective-permute-start(bf16[128,1792]{1,0:T(8,128)(2,1)S(1)} %get-tuple-element.349), channel_id=1, source_target_pairs={{0,1},{1,0},{2,3},{3,2},{4,5},{5,4},{6,7},{7,6},{8,9},{9,8},{10,11... | collective-permute-start | bytes 1376264 | tf_op jit(solution)/shard_map/ppermute | solution.py:668
  338.8 32.5 %collective-permute-start.53 = (bf16[128,1792]{1,0:T(8,128)(2,1)S(1)}, bf16[128,1792]{1,0:T(8,128)(2,1)S(1)}, u32[]{:S(2)}, u32[]{:S(2)}) collective-permute-start(bf16[128,1792]{1,0:T(8,128)(2,1)S(1)} %get-tuple-element.348), channel_id=1, source_target_pairs={{0,2},{1,3},{2,0},{3,1},{4,6},{5,7},{6,4},{7,5},{8,10},{9,11},{10,... | collective-permute-start | bytes 1376264 | tf_op jit(solution)/shard_map/ppermute | solution.py:668
  339.2 33.3 %collective-permute-start.54 = (bf16[128,1792]{1,0:T(8,128)(2,1)S(1)}, bf16[128,1792]{1,0:T(8,128)(2,1)S(1)}, u32[]{:S(2)}, u32[]{:S(2)}) collective-permute-start(bf16[128,1792]{1,0:T(8,128)(2,1)S(1)} %get-tuple-element.347), channel_id=1, source_target_pairs={{0,3},{1,2},{2,1},{3,0},{4,7},{5,6},{6,5},{7,4},{8,11},{9,10},{10,... | collective-permute-start | bytes 1376264 | tf_op jit(solution)/shard_map/ppermute | solution.py:668
  341.5 32.2 %collective-permute-start.59 = (bf16[128,384]{1,0:T(8,128)(2,1)S(1)}, bf16[128,384]{1,0:T(8,128)(2,1)S(1)}, u32[]{:S(2)}, u32[]{:S(2)}) collective-permute-start(bf16[128,384]{1,0:T(8,128)(2,1)S(1)} %get-tuple-element.369), channel_id=1, source_target_pairs={{0,1},{1,0},{2,3},{3,2},{4,5},{5,4},{6,7},{7,6},{8,9},{9,8},{10,11... | collective-permute-start | bytes 294920 | tf_op jit(solution)/shard_map/ppermute | solution.py:668
  358.6 32.2 %collective-permute-start.62 = (bf16[160,896]{1,0:T(8,128)(2,1)S(1)}, bf16[160,896]{1,0:T(8,128)(2,1)S(1)}, u32[]{:S(2)}, u32[]{:S(2)}) collective-permute-start(bf16[160,896]{1,0:T(8,128)(2,1)S(1)} %add_convert_fusion.5), channel_id=1, source_target_pairs={{0,4},{4,0},{8,12},{12,8},{1,5},{5,1},{9,13},{13,9},{2,6},{6,2},{1... | collective-permute-start | bytes 860168 | tf_op jit(solution)/shard_map/ppermute | solution.py:663
  371.3 19.5 %collective-permute-start.63 = (bf16[160,896]{1,0:T(8,128)(2,1)S(1)}, bf16[160,896]{1,0:T(8,128)(2,1)S(1)}, u32[]{:S(2)}, u32[]{:S(2)}) collective-permute-start(bf16[160,896]{1,0:T(8,128)(2,1)S(1)} %add_convert_fusion.5), channel_id=1, source_target_pairs={{0,8},{4,12},{8,0},{12,4},{1,9},{5,13},{9,1},{13,5},{2,10},{6,14},... | collective-permute-start | bytes 860168 | tf_op jit(solution)/shard_map/ppermute | solution.py:663
  (120 other events, 1064.6 us)
Sparse Core Ops, SparseCore 0:
  46.1 57.6 all-gather.1
  222.5 67.6 reduce-scatter.1

commit v3 on v2

--- a/solution.py
+++ b/solution.py
@@ -266,7 +266,9 @@
         compiler_params=pltpu.CompilerParams(
             dimension_semantics=("arbitrary",), vmem_limit_bytes=40 * 2**20
         ),
-        cost_estimate=NO_COST,
+        cost_estimate=pl.CostEstimate(
+            flops=3 * 10**10, bytes_accessed=2**23, transcendentals=0
+        ),
         name="attend_forward",
     )(info, queries, kv)
 
@@ -302,7 +304,9 @@
         compiler_params=pltpu.CompilerParams(
             dimension_semantics=("arbitrary",), vmem_limit_bytes=40 * 2**20
         ),
-        cost_estimate=NO_COST,
+        cost_estimate=pl.CostEstimate(
+            flops=5 * 10**10, bytes_accessed=2**23, transcendentals=0
+        ),
         name="attend_backward",
     )(info, queries_ext, grad_att, attended, kv)
 
@@ -721,6 +725,7 @@
     )
     kv_got = [hop_z(kv_pack, k) for k in range(n_z)]
     q_got = [hop_z(q_part, k) for k in range(n_z)]
+    o_got = [hop_z(o_part, k) for k in range(n_z)]
     gu_cut = jnp.concatenate([ff_columns(gate_weight), ff_columns(up_weight)], 1)
     down_cut = lax.dynamic_slice_in_dim(down_weight, part * piece, piece, 0)
     down_cut = jnp.pad(down_cut, ((0, piece_pad - piece), (0, 0)))
@@ -728,9 +733,9 @@
     cosine_table, sine_table = rope_tables(query_pos, HEAD)
     cos_wide = jnp.tile(cosine_table[:, 0], (1, 4))
     sin_wide = jnp.tile(jnp.concatenate([-sine_table[:, 0], sine_table[:, 0]], 1), (1, 2))
-    kv_got, q_got, cos_wide, sin_wide, gu_cut, down_cut, o_part, og_here = (
+    kv_got, q_got, cos_wide, sin_wide, gu_cut, down_cut, o_got, og_here = (
         lax.optimization_barrier(
-            (kv_got, q_got, cos_wide, sin_wide, gu_cut, down_cut, o_part, og_here)
+            (kv_got, q_got, cos_wide, sin_wide, gu_cut, down_cut, o_got, og_here)
         )
     )
 
@@ -743,7 +748,7 @@
     gain_one = vecs[0:1, :width]
     gain_two = vecs[1:2, :width]
     kv_z = [hop_z(kv_local, k) for k in range(n_z)]
-    kv_z, gu_cut, down_cut, o_part = lax.optimization_barrier((kv_z, gu_cut, down_cut, o_part))
+    kv_z, q_own, gu_cut, down_cut = lax.optimization_barrier((kv_z, q_own, gu_cut, down_cut))
 
     kv_block = jnp.concatenate(kv_z, 0)
     if n_ctx == tp:
@@ -751,19 +756,18 @@
     else:
         kv_blocks = lax.all_gather(kv_block, "ctx", axis=0, tiled=False)
     gu_own = gather_z(gu_cut)
-    down_own = [hop_z(down_cut, k) for k in range(n_z)]
-    o_got = [hop_z(o_part, k) for k in range(n_z)]
     q_own = jnp.stack(q_own)
     w_query, queries = project_query(
         q_own, swap(q_own), hidden_one, vecs, cos_wide, sin_wide, rows_here
     )
     w_query = w_query.reshape(width, width)
-    kv_blocks, queries, o_got, og_here = lax.optimization_barrier(
-        (kv_blocks, queries, o_got, og_here)
+    kv_blocks, queries, o_got, og_here, down_cut = lax.optimization_barrier(
+        (kv_blocks, queries, o_got, og_here, down_cut)
     )
 
     o_own = [hop(jnp.stack(o_got), k) for k in range(tp)]
     og_parts = [hop(og_here, k) for k in range(tp)]
+    down_own = [hop_z(down_cut, k) for k in range(n_z)]
     kv_whole = jnp.stack(kv_blocks) if n_ctx == tp else kv_blocks
     attended, queries_ext = attend_forward(order_row, n_ctx == tp, queries, kv_whole)
     attended, o_own, queries_ext, og_parts, down_own = lax.optimization_barrier(
@@ -799,10 +803,11 @@
     def core_total(own, sib):
         return (own.astype(F32) + sib.astype(F32)).astype(BF16)
 
-    def scatter_hops(cut):
+    def scatter_parts(cut):
+        cut = cut.reshape(n_z, tp, part_rows, -1)
+        at = lax.rem(here, tp)
         return [
-            hop_z(lax.dynamic_index_in_dim(cut, zed ^ k, 0, keepdims=False), k)
-            for k in range(n_z)
+            hop(lax.dynamic_index_in_dim(cut, at ^ k, 1, keepdims=False), k) for k in range(tp)
         ]
 
     def ctx_groups_sum(v):
@@ -817,11 +822,7 @@
         (grad_h2_parts, d_gu, d_down, ff_out)
     )
     d_gu = scatter_z(d_gu)
-    ff_out = [hop(ff_out[k], k) for k in range(tp)]
     d_down = d_down.reshape(n_z, piece_pad, width)
-    d_down = [
-        hop_z(lax.dynamic_index_in_dim(d_down, zed ^ k, 0, keepdims=False), k) for k in range(n_z)
-    ]
     grad_h2 = sum(v.astype(F32) for v in grad_h2_parts)
     scale_two = lax.rsqrt(jnp.mean(resid * resid, -1, keepdims=True) + NORM_EPS)
     normed_two = resid * scale_two
@@ -830,11 +831,17 @@
     grad_resid = og_here.astype(F32) + grad_norm_two
     grad_proj = grad_resid.astype(BF16)
     grad_att = times_transposed(grad_proj, w_out).astype(BF16)
+    o_own, o_oth = core_halves(contract_rows(attended, grad_proj))
+    o_own, o_sib, grad_att, ff_out = lax.optimization_barrier(
+        (o_own, swap(o_oth), grad_att, ff_out)
+    )
+    ff_out = [hop(ff_out[k], k) for k in range(tp)]
+    o_terms = scatter_parts(core_total(o_own, o_sib))
     grad_queries, grad_terms = attend_backward(
         order_row, n_ctx == tp, queries_ext, grad_att, attended, kv_whole
     )
-    grad_queries, grad_terms, ff_out, grad_proj = lax.optimization_barrier(
-        (grad_queries, grad_terms, ff_out, grad_proj)
+    grad_queries, grad_terms, ff_out, o_terms, d_down = lax.optimization_barrier(
+        (grad_queries, grad_terms, ff_out, o_terms, d_down)
     )
 
     grad_q_pre = (
@@ -842,17 +849,13 @@
         .reshape(tokens_here, HEADS * HEAD)
         .astype(BF16)
     )
-    qo_own, qo_oth = core_halves(
-        jnp.concatenate(
-            [contract_rows(hidden_one, grad_q_pre), contract_rows(attended, grad_proj)], 1
-        )
-    )
+    q_own, q_oth = core_halves(contract_rows(hidden_one, grad_q_pre))
     if n_ctx == tp:
         kv_terms = [hop(grad_terms[k], k) for k in range(n_ctx)]
     else:
         kv_terms = [lax.psum_scatter(grad_terms, "ctx", scatter_dimension=0, tiled=False)]
-    kv_terms, d_gu, d_down, qo_own, qo_oth, ff_out = lax.optimization_barrier(
-        (kv_terms, d_gu, d_down, qo_own, qo_oth, ff_out)
+    kv_terms, d_gu, d_down, q_own, q_oth, ff_out, o_terms = lax.optimization_barrier(
+        (kv_terms, d_gu, d_down, q_own, q_oth, ff_out, o_terms)
     )
 
     kv_sum = sum(v.astype(F32) for v in kv_terms).astype(BF16)
@@ -860,15 +863,15 @@
     kv_terms = [hop_z(kv_sum[k], k) for k in range(n_z)]
     d_gu = ctx_groups_sum(d_gu)
     gu_pieces = [hop(d_gu, k) for k in range(tp)]
-    qo_sib = swap(qo_oth)
+    q_sib = swap(q_oth)
     result = resid + sum(v.astype(F32) for v in ff_out)
     layer_out = result.astype(BF16)[None]
-    kv_terms, qo_own, qo_sib, d_down = lax.optimization_barrier(
-        (kv_terms, qo_own, qo_sib, d_down)
-    )
-
-    qo_cut = core_total(qo_own, qo_sib)
-    qo_terms = scatter_hops(qo_cut)
+    kv_terms, q_own, q_sib, d_down = lax.optimization_barrier((kv_terms, q_own, q_sib, d_down))
+
+    q_terms = scatter_parts(core_total(q_own, q_sib))
+    d_down = [
+        hop_z(lax.dynamic_index_in_dim(d_down, zed ^ k, 0, keepdims=False), k) for k in range(n_z)
+    ]
     grad_kv = sum(v.astype(F32) for v in kv_terms)
     grad_k_pre = (
         rotate(
@@ -900,37 +903,38 @@
         jnp.concatenate([contract_rows(hidden_one, grad_kv_pre), columns], 1)
     )
     kv_sib = swap(kv_oth)
-    kv_own, kv_sib, gu_pieces, d_down = lax.optimization_barrier(
-        (kv_own, kv_sib, gu_pieces, d_down)
-    )
-
-    kv_terms = scatter_hops(core_total(kv_own, kv_sib))
+    kv_own, kv_sib, gu_pieces, q_terms = lax.optimization_barrier(
+        (kv_own, kv_sib, gu_pieces, q_terms)
+    )
+
+    kv_terms = scatter_parts(core_total(kv_own, kv_sib))
+    gu_pieces = jnp.stack(gu_pieces)
+    gu_sib = swap(gu_pieces)
+    kv_terms, d_down = lax.optimization_barrier((kv_terms, d_down))
+
+    last = jnp.concatenate(
+        [sum(v.astype(F32) for v in t).astype(BF16) for t in (q_terms, o_terms, kv_terms)], 2
+    )
+    last = [
+        hop_z(lax.dynamic_index_in_dim(last, zed ^ k, 0, keepdims=False), k) for k in range(n_z)
+    ]
     d_down = ctx_groups_sum(sum(v.astype(F32) for v in d_down).astype(BF16))
     d_down = lax.optimization_barrier(d_down)
     down_pieces = [hop(d_down, k) for k in range(tp)]
-    gu_pieces = jnp.stack(gu_pieces)
-    gu_sib = swap(gu_pieces)
-    qo_terms, kv_terms, down_pieces, gu_sib, gu_pieces = lax.optimization_barrier(
-        (qo_terms, kv_terms, down_pieces, gu_sib, gu_pieces)
-    )
-
-    last = jnp.concatenate(
-        [sum(v.astype(F32) for v in qo_terms), sum(v.astype(F32) for v in kv_terms)], 1
-    ).astype(BF16)
-    last = last.reshape(tp, part_rows, -1)
-    at = lax.rem(here, tp)
-    last = [hop(lax.dynamic_index_in_dim(last, at ^ k, 0, keepdims=False), k) for k in range(tp)]
+    grad_w_gate, grad_w_up = spread_columns((gu_pieces, gu_sib), n_z, ff, 2)
+    last, down_pieces, grad_w_gate, grad_w_up = lax.optimization_barrier(
+        (last, down_pieces, grad_w_gate, grad_w_up)
+    )
+
+    last = ctx_groups_sum(sum(v.astype(F32) for v in last).astype(BF16))
+    last = lax.optimization_barrier(last)
+    last = [hop(last, k) for k in range(tp)]
     down_pieces = jnp.stack(down_pieces)
     down_sib = swap(down_pieces)
-    grad_w_gate, grad_w_up = spread_columns((gu_pieces, gu_sib), n_z, ff, 2)
-    last, down_sib, down_pieces, grad_w_gate, grad_w_up = lax.optimization_barrier(
-        (last, down_sib, down_pieces, grad_w_gate, grad_w_up)
-    )
-
-    last = ctx_groups_sum(sum(v.astype(F32) for v in last).astype(BF16))
-    last = lax.optimization_barrier(last)
+    last, down_pieces, down_sib = lax.optimization_barrier((last, down_pieces, down_sib))
+    last = jnp.stack(last)
     grad_w_down = spread_rows((down_pieces, down_sib), piece, ff_z)
-    last = spread_rows(share_pieces(last), part_rows, rows_here)
+    last = spread_rows((last, swap(last)), part_rows, rows_here)
     grad_w_query = last[:, :width]
     grad_w_out = last[:, width : 2 * width]
     grad_w_kv = last[:, 2 * width :]

time: 444 us -> 442 us (level)
  starting transfers between devices: 130 us -> 103 us
  Pallas kernels: 60.9 us -> 81.7 us
  local copies, waits for them, and re-layouts: 42.5 us -> 56.1 us
  waiting for transfers between devices: 155 us -> 142 us
    ppermute x27 -> x24, waiting for transfers between devices: 90.8 us -> 50.4 us  [hop_z(): return lax.ppermute(v, 'fsdp', [(i, i ^ k) for i in range(n_z)])]
    ppermute x36 -> x42, waiting for transfers between devices: 45.6 us -> 72.9 us  [hop(): return lax.ppermute(v, 'ctx', [(i, i ^ k) for i in range(n_ctx)])]
    ppermute x27 -> x24, starting transfers between devices: 55.5 us -> 30.3 us  [hop_z(): return lax.ppermute(v, 'fsdp', [(i, i ^ k) for i in range(n_z)])]
    pallas_call x1, Pallas kernels: 8.9 us -> 21.1 us  [attend_backward(): pl.pallas_call(functools.partial(backward_kernel, by_xor), grid_spec=pltp...]
    pallas_call x1, Pallas kernels: 5.85 us -> 12.8 us  [attend_forward(): pl.pallas_call(functools.partial(forward_kernel, by_xor), grid_spec=pltpu...]
    all_gather x1, waiting for transfers between devices: 12.1 us -> 18.1 us  [gather_z(): return lax.all_gather(v, 'fsdp', axis=0, tiled=True)]
    unnamed x157 -> x191, local copies, waits for them, and re-layouts: 17.1 us -> 22.1 us
    ppermute x36 -> x42, starting transfers between devices: 52.6 us -> 50.1 us  [hop(): return lax.ppermute(v, 'ctx', [(i, i ^ k) for i in range(n_ctx)])]
  transfers between devices with their start and end apart: 76 -> 80, of which waited for: 31 -> 32; matrix products, arithmetic and copies ran while one was open for 11% -> 13% of each run, Pallas kernels for 8% -> 13%
where the time goes in v3:
time: 442 us; the launch traced here: 437 us
  waiting for transfers between devices  142 us (32%)
  starting transfers between devices  103 us (23%)
  Pallas kernels  81.7 us (18%)
  local copies, waits for them, and re-layouts  56.1 us (13%)
  other arithmetic  28.2 us (6%)
  between operations  16.3 us (4%)
  matrix products  9.82 us (2%)
    ppermute x42, waiting for transfers between devices, hop(): return lax.ppermute(v, 'ctx', [(i, i ^ k) for i in range(n_ctx)])  72.9 us
    ppermute x24, waiting for transfers between devices, hop_z(): return lax.ppermute(v, 'fsdp', [(i, i ^ k) for i in range(n_z)])  50.4 us
    ppermute x42, starting transfers between devices, hop(): return lax.ppermute(v, 'ctx', [(i, i ^ k) for i in range(n_ctx)])  50.1 us
    ppermute x24, starting transfers between devices, hop_z(): return lax.ppermute(v, 'fsdp', [(i, i ^ k) for i in range(n_z)])  30.3 us
    ppermute x12, starting transfers between devices, swap(): return lax.ppermute(v, 'seq', [(0, 1), (1, 0)])  22.8 us
    unnamed x191, local copies, waits for them, and re-layouts  22.1 us
    pallas_call x1, Pallas kernels, ff_pass(): pl.pallas_call(functools.partial(ff_kernel, tp, n_z), in_specs=[vmem] * (...  21.9 us
    pallas_call x1, Pallas kernels, attend_backward(): pl.pallas_call(functools.partial(backward_kernel, by_xor), grid_spec=pltp...  21.1 us
  transfers between devices with their start and end apart: 80, of which 32 were waited for; matrix products, arithmetic and copies ran while one was open for 13% of the time, Pallas kernels for 13%

profile of v3, /device:TPU:1, one launch (start us, length us, event | category | flops | bytes accessed | tf_op | source)
XLA Modules:
  0.0 437.3 jit_solution(9480514344235179163)
XLA Ops:
  18.5 3.2 collective-permute-start.4
  26.6 4.9 %collective-permute-done.4 = bf16[32,896]{1,0:T(8,128)(2,1)S(1)} collective-permute-done((bf16[32,896]{1,0:T(8,128)(2,1)S(1)}, bf16[32,896]{1,0:T(8,128)(2,1)S(1)}, u32[]{:S(2)}, u32[]{:S(2)}) %collective-permute-start.4) | collective-permute-done | bytes 57376 | tf_op jit(solution)/shard_map/ppermute | solution.py:672
  42.1 2.8 collective-permute-done.8
  51.4 3.9 collective-permute-done.9
  55.3 5.5 %collective-permute-done.11 = bf16[192,256]{1,0:T(8,128)(2,1)S(1)} collective-permute-done((bf16[192,256]{1,0:T(8,128)(2,1)S(1)}, bf16[192,256]{1,0:T(8,128)(2,1)S(1)}, u32[]{:S(2)}, u32[]{:S(2)}) %collective-permute-start.11) | collective-permute-done | bytes 98336 | tf_op jit(solution)/shard_map/ppermute | solution.py:672
  62.8 7.2 %collective-permute-start.18 = (bf16[4,4,32,896]{3,2,1,0:T(8,128)(2,1)S(1)}, bf16[4,4,32,896]{3,2,1,0:T(8,128)(2,1)S(1)}, u32[]{:S(2)}, u32[]{:S(2)}) collective-permute-start(bf16[4,4,32,896]{3,2,1,0:T(8,128)(2,1)S(1)} %pad_maximum_fusion.4.own_ref), channel_id=1, source_target_pairs={{0,16},{16,0},{1,17},{17,1},{2,18},{18,2},{3,19},{19,3},{4,20},{20... | collective-permute-start | bytes 2752520 | tf_op jit(solution)/shard_map/ppermute | solution.py:662
  73.9 7.1 %collective-permute-done.15 = bf16[768,256]{1,0:T(8,128)(2,1)S(1)} collective-permute-done((bf16[768,256]{1,0:T(8,128)(2,1)S(1)}, bf16[768,256]{1,0:T(8,128)(2,1)S(1)}, u32[]{:S(2)}, u32[]{:S(2)}) %collective-permute-start.15) | collective-permute-done | bytes 393248 | tf_op jit(solution)/shard_map/ppermute | solution.py:667
  81.0 8.1 %collective-permute-done.16 = bf16[768,256]{1,0:T(8,128)(2,1)S(1)} collective-permute-done((bf16[768,256]{1,0:T(8,128)(2,1)S(1)}, bf16[768,256]{1,0:T(8,128)(2,1)S(1)}, u32[]{:S(2)}, u32[]{:S(2)}) %collective-permute-start.16) | collective-permute-done | bytes 393248 | tf_op jit(solution)/shard_map/ppermute | solution.py:667
  95.4 2.9 collective-permute-done.19
  99.8 4.2 collective-permute-done.21
  105.5 11.9 %collective-permute-done.25 = bf16[160,896]{1,0:T(8,128)(2,1)S(1)} collective-permute-done((bf16[160,896]{1,0:T(8,128)(2,1)S(1)}, bf16[160,896]{1,0:T(8,128)(2,1)S(1)}, u32[]{:S(2)}, u32[]{:S(2)}) %collective-permute-start.25) | collective-permute-done | bytes 286752 | tf_op jit(solution)/shard_map/ppermute | solution.py:672
  120.5 18.1 %all-gather.2.cloned.1.call-done.refs_8_ = bf16[896,1280]{1,0:T(8,128)(2,1)} async-done(((bf16[224,1280]{1,0:T(8,128)(2,1)}), bf16[896,1280]{1,0:T(8,128)(2,1)}) %all-gather.2.cloned.1.call-update) | async-done | bytes 2293776 | tf_op jit(solution)/shard_map/all_gather | solution.py:675
  139.7 12.8 %attend_forward.1 = (bf16[192,896]{1,0:T(8,128)(2,1)S(1)}, bf16[2688,256]{1,0:T(8,128)(2,1)S(1)}) custom-call(s32[4]{0:T(128)S(1)} %bitcast.158, bf16[192,896]{1,0:T(8,128)(2,1)S(1)} %get-tuple-element.224.q_ref, bf16[4,768,256]{2,1,0:T(8,128)(2,1)S(1)} %pad_maximum_fusion.1.kv_ref), custom_call_target="tpu_custom_call" | custom-call | flops 30000001024 | bytes 8388608 | tf_op jit(solution)/shard_map/attend_forward/pallas_call | solution.py:250
  157.6 4.6 %collective-permute-start.29 = (bf16[192,896]{1,0:T(8,128)(2,1)S(1)}, bf16[192,896]{1,0:T(8,128)(2,1)S(1)}, u32[]{:S(2)}, u32[]{:S(2)}) collective-permute-start(bf16[192,896]{1,0:T(8,128)(2,1)S(1)} %get-tuple-element.244.refs_0_), channel_id=1, source_target_pairs={{0,4},{4,0},{8,12},{12,8},{1,5},{5,1},{9,13},{13,9},{2,6},{6,2},{1... | collective-permute-start | bytes 1032200 | tf_op jit(solution)/shard_map/ppermute | solution.py:667
  163.5 6.9 %collective-permute-done.29.refs_1_ = bf16[192,896]{1,0:T(8,128)(2,1)S(1)} collective-permute-done((bf16[192,896]{1,0:T(8,128)(2,1)S(1)}, bf16[192,896]{1,0:T(8,128)(2,1)S(1)}, u32[]{:S(2)}, u32[]{:S(2)}) %collective-permute-start.29) | collective-permute-done | bytes 344096 | tf_op jit(solution)/shard_map/ppermute | solution.py:667
  171.2 7.6 %collective-permute-done.31.refs_3_ = bf16[192,896]{1,0:T(8,128)(2,1)S(1)} collective-permute-done((bf16[192,896]{1,0:T(8,128)(2,1)S(1)}, bf16[192,896]{1,0:T(8,128)(2,1)S(1)}, u32[]{:S(2)}, u32[]{:S(2)}) %collective-permute-start.31) | collective-permute-done | bytes 344096 | tf_op jit(solution)/shard_map/ppermute | solution.py:667
  179.6 21.9 %ff_pass.1 = (bf16[640,768]{1,0:T(8,128)(2,1)}, bf16[640,768]{1,0:T(8,128)(2,1)}, bf16[768,1280]{1,0:T(8,128)(2,1)}, bf16[768,1280]{1,0:T(8,128)(2,1)}, bf16[896...) custom-call(bf16[192,896]{1,0:T(8,128)(2,1)} %copy-done.23, ...), custom_call_target="tpu_custom_call" | custom-call | tf_op jit(solution)/shard_map/ff_pass/pallas_call | solution.py:613
  204.3 3.1 grad_weight.4
  221.1 4.5 %grad_weight.5 = bf16[896,1280]{1,0:T(8,128)(2,1)} custom-call(bf16[896,768]{1,0:T(8,128)(2,1)S(1)} %copy-done.5, bf16[768,1280]{1,0:T(8,128)(2,1)S(1)} %copy-done.6, bf16[896,1280]{1,0:T(8,128)(2,1)} %collective-permute-done.37.refs_0_), custom_call_target="tpu_custom_call" | custom-call | tf_op jit(solution)/shard_map/grad_weight/pallas_call | solution.py:527
  225.6 3.6 collective-permute-done.36
  253.1 21.1 %attend_backward.1 = (f32[192,896]{1,0:T(8,128)S(1)}, bf16[4,768,256]{2,1,0:T(8,128)(2,1)S(1)}) custom-call(s32[4]{0:T(128)S(1)} %bitcast.159, bf16[2688,256]{1,0:T(8,128)(2,1)S(1)} %copy-done.28, bf16[192,896]{1,0:T(8,128)(2,1)S(1)} %convolution_convert_fusion.3.do_ref, bf16[192,896]{1,0:T(8,128)(2,1)S(1)} %copy-done.16, bf16[4,768,256]{2,1,0:T(8,128)(2,1)S(1)} %copy-done.12), custom_call_target="tpu_custom_call" | custom-call | flops 49999998976 | bytes 8388608 | tf_op jit(solution)/shard_map/attend_backward/pallas_call | solution.py:280
  275.5 7.2 %collective-permute-start.47 = (bf16[768,256]{1,0:T(8,128)(2,1)}, bf16[768,256]{1,0:T(8,128)(2,1)}, u32[]{:S(2)}, u32[]{:S(2)}) collective-permute-start(bf16[768,256]{1,0:T(8,128)(2,1)} %get-tuple-element.384), channel_id=1, source_target_pairs={{0,8},{4,12},{8,0},{12,4},{1,9},{5,13},{9,1},{13,5},{2,10},{6,14},... | collective-permute-start | bytes 1179656 | tf_op jit(solution)/shard_map/ppermute | solution.py:667
  288.8 9.9 %collective-permute-done.47 = bf16[768,256]{1,0:T(8,128)(2,1)} collective-permute-done((bf16[768,256]{1,0:T(8,128)(2,1)}, bf16[768,256]{1,0:T(8,128)(2,1)}, u32[]{:S(2)}, u32[]{:S(2)}) %collective-permute-start.47) | collective-permute-done | bytes 393248 | tf_op jit(solution)/shard_map/ppermute | solution.py:667
  298.8 3.3 collective-permute-start.52
  346.5 4.5 %collective-permute-done.57 = bf16[4,32,896]{2,1,0:T(8,128)(2,1)} collective-permute-done((bf16[4,32,896]{2,1,0:T(8,128)(2,1)}, bf16[4,32,896]{2,1,0:T(8,128)(2,1)}, u32[]{:S(2)}, u32[]{:S(2)}) %collective-permute-start.57) | collective-permute-done | bytes 229408 | tf_op jit(solution)/shard_map/ppermute | solution.py:667
  351.0 4.7 %collective-permute-done.59 = bf16[4,32,896]{2,1,0:T(8,128)(2,1)} collective-permute-done((bf16[4,32,896]{2,1,0:T(8,128)(2,1)}, bf16[4,32,896]{2,1,0:T(8,128)(2,1)}, u32[]{:S(2)}, u32[]{:S(2)}) %collective-permute-start.59) | collective-permute-done | bytes 229408 | tf_op jit(solution)/shard_map/ppermute | solution.py:667
  365.7 7.2 %collective-permute-done.63 = bf16[160,896]{1,0:T(8,128)(2,1)S(1)} collective-permute-done((bf16[160,896]{1,0:T(8,128)(2,1)S(1)}, bf16[160,896]{1,0:T(8,128)(2,1)S(1)}, u32[]{:S(2)}, u32[]{:S(2)}) %collective-permute-start.63) | collective-permute-done | bytes 286752 | tf_op jit(solution)/shard_map/ppermute | solution.py:672
  374.1 7.3 %collective-permute-done.64 = bf16[160,896]{1,0:T(8,128)(2,1)S(1)} collective-permute-done((bf16[160,896]{1,0:T(8,128)(2,1)S(1)}, bf16[160,896]{1,0:T(8,128)(2,1)S(1)}, u32[]{:S(2)}, u32[]{:S(2)}) %collective-permute-start.64) | collective-permute-done | bytes 286752 | tf_op jit(solution)/shard_map/ppermute | solution.py:672
  397.2 6.7 %spread_columns.1 = (f32[224,4864]{1,0:T(8,128)}, f32[224,4864]{1,0:T(8,128)}) custom-call(bf16[4,224,1280]{2,1,0:T(8,128)(2,1)S(1)} %pad_maximum_fusion.refs_0_, bf16[4,224,1280]{2,1,0:T(8,128)(2,1)S(1)} %collective-permute-done.72.refs_1_), custom_call_target="tpu_custom_call" | custom-call | tf_op jit(solution)/shard_map/spread_columns/pallas_call | solution.py:341
  404.1 4.5 %collective-permute-start.76 = (bf16[4,160,896]{2,1,0:T(8,128)(2,1)S(1)}, bf16[4,160,896]{2,1,0:T(8,128)(2,1)S(1)}, u32[]{:S(2)}, u32[]{:S(2)}) collective-permute-start(bf16[4,160,896]{2,1,0:T(8,128)(2,1)S(1)} %pad_maximum_fusion.3.refs_0_), channel_id=1, source_target_pairs={{0,16},{16,0},{1,17},{17,1},{2,18},{18,2},{3,19},{19,3},{4,20},{20... | collective-permute-start | bytes 3440648 | tf_op jit(solution)/shard_map/ppermute | solution.py:662
  414.9 3.3 collective-permute-done.75
  421.3 3.8 spread_rows.3
  (435 shorter events, 193.0 us)
Async XLA Ops:
  7.2 131.4 %all-gather.2.cloned.1.call-start = ((), (), s32[]{:S(2)}) async-start(), calls=%async_computation.1 | async-start | bytes 2867200 | tf_op jit(solution)/shard_map/all_gather | solution.py:675
  13.7 31.2 %collective-permute-start = (bf16[240,256]{1,0:T(8,128)(2,1)S(1)}, bf16[240,256]{1,0:T(8,128)(2,1)S(1)}, u32[]{:S(2)}, u32[]{:S(2)}) collective-permute-start(bf16[240,256]{1,0:T(8,128)(2,1)S(1)} %pad_maximum_fusion.10.refs_0_), channel_id=1, source_target_pairs={{0,1},{1,0},{2,3},{3,2},{4,5},{5,4},{6,7},{7,6},{8,9},{9,8},{10,11... | collective-permute-start | bytes 368648 | tf_op jit(solution)/shard_map/ppermute | solution.py:672
  15.9 29.0 %collective-permute-start.1 = (bf16[240,256]{1,0:T(8,128)(2,1)S(1)}, bf16[240,256]{1,0:T(8,128)(2,1)S(1)}, u32[]{:S(2)}, u32[]{:S(2)}) collective-permute-start(bf16[240,256]{1,0:T(8,128)(2,1)S(1)} %pad_maximum_fusion.10.refs_0_), channel_id=1, source_target_pairs={{0,2},{1,3},{2,0},{3,1},{4,6},{5,7},{6,4},{7,5},{8,10},{9,11},{10,... | collective-permute-start | bytes 368648 | tf_op jit(solution)/shard_map/ppermute | solution.py:672
  18.2 26.7 %collective-permute-start.2 = (bf16[240,256]{1,0:T(8,128)(2,1)S(1)}, bf16[240,256]{1,0:T(8,128)(2,1)S(1)}, u32[]{:S(2)}, u32[]{:S(2)}) collective-permute-start(bf16[240,256]{1,0:T(8,128)(2,1)S(1)} %pad_maximum_fusion.10.refs_0_), channel_id=1, source_target_pairs={{0,3},{1,2},{2,1},{3,0},{4,7},{5,6},{6,5},{7,4},{8,11},{9,10},{10,... | collective-permute-start | bytes 368648 | tf_op jit(solution)/shard_map/ppermute | solution.py:672
  60.8 237.9 %reduce-scatter.2.cloned.1.call-start = ((), (), s32[]{:S(2)}) async-start(), calls=%async_computation.2 | async-start | bytes 2867200 | tf_op jit(solution)/shard_map/reduce_scatter | solution.py:678
  71.4 17.7 %collective-permute-start.16 = (bf16[768,256]{1,0:T(8,128)(2,1)S(1)}, bf16[768,256]{1,0:T(8,128)(2,1)S(1)}, u32[]{:S(2)}, u32[]{:S(2)}) collective-permute-start(bf16[768,256]{1,0:T(8,128)(2,1)S(1)} %constant_dynamic-update-slice_fusion), channel_id=1, source_target_pairs={{0,8},{4,12},{8,0},{12,4},{1,9},{5,13},{9,1},{13,5},{2,10},{6,14},... | collective-permute-start | bytes 1179656 | tf_op jit(solution)/shard_map/ppermute | solution.py:667
  72.6 17.8 %collective-permute-start.17 = (bf16[768,256]{1,0:T(8,128)(2,1)S(1)}, bf16[768,256]{1,0:T(8,128)(2,1)S(1)}, u32[]{:S(2)}, u32[]{:S(2)}) collective-permute-start(bf16[768,256]{1,0:T(8,128)(2,1)S(1)} %constant_dynamic-update-slice_fusion), channel_id=1, source_target_pairs={{0,12},{4,8},{8,4},{12,0},{1,13},{5,9},{9,5},{13,1},{2,14},{6,10},... | collective-permute-start | bytes 1179656 | tf_op jit(solution)/shard_map/ppermute | solution.py:667
  90.4 27.0 %collective-permute-start.25 = (bf16[160,896]{1,0:T(8,128)(2,1)S(1)}, bf16[160,896]{1,0:T(8,128)(2,1)S(1)}, u32[]{:S(2)}, u32[]{:S(2)}) collective-permute-start(bf16[160,896]{1,0:T(8,128)(2,1)S(1)} %pad.80), channel_id=1, source_target_pairs={{0,1},{1,0},{2,3},{3,2},{4,5},{5,4},{6,7},{7,6},{8,9},{9,8},{10,11... | collective-permute-start | bytes 860168 | tf_op jit(solution)/shard_map/ppermute | solution.py:672
  90.4 30.1 %collective-permute-start.26 = (bf16[160,896]{1,0:T(8,128)(2,1)S(1)}, bf16[160,896]{1,0:T(8,128)(2,1)}, u32[]{:S(2)}, u32[]{:S(2)}) collective-permute-start(bf16[160,896]{1,0:T(8,128)(2,1)S(1)} %pad.80), channel_id=1, source_target_pairs={{0,2},{1,3},{2,0},{3,1},{4,6},{5,7},{6,4},{7,5},{8,10},{9,11},{10,... | collective-permute-start | bytes 860168 | tf_op jit(solution)/shard_map/ppermute | solution.py:672
  98.3 54.2 %collective-permute-start.22 = (bf16[192,896]{1,0:T(8,128)(2,1)S(1)}, bf16[192,896]{1,0:T(8,128)(2,1)}, u32[]{:S(2)}, u32[]{:S(2)}) collective-permute-start(bf16[192,896]{1,0:T(8,128)(2,1)S(1)} %bitcast.173), channel_id=1, source_target_pairs={{0,4},{4,0},{8,12},{12,8},{1,5},{5,1},{9,13},{13,9},{2,6},{6,2},{1... | collective-permute-start | bytes 1032200 | tf_op jit(solution)/shard_map/ppermute | solution.py:667
  99.8 52.8 %collective-permute-start.23 = (bf16[192,896]{1,0:T(8,128)(2,1)S(1)}, bf16[192,896]{1,0:T(8,128)(2,1)}, u32[]{:S(2)}, u32[]{:S(2)}) collective-permute-start(bf16[192,896]{1,0:T(8,128)(2,1)S(1)} %bitcast.174), channel_id=1, source_target_pairs={{0,8},{4,12},{8,0},{12,4},{1,9},{5,13},{9,1},{13,5},{2,10},{6,14},... | collective-permute-start | bytes 1032200 | tf_op jit(solution)/shard_map/ppermute | solution.py:667
  104.0 48.6 %collective-permute-start.24 = (bf16[192,896]{1,0:T(8,128)(2,1)S(1)}, bf16[192,896]{1,0:T(8,128)(2,1)}, u32[]{:S(2)}, u32[]{:S(2)}) collective-permute-start(bf16[192,896]{1,0:T(8,128)(2,1)S(1)} %bitcast.175), channel_id=1, source_target_pairs={{0,12},{4,8},{8,4},{12,0},{1,13},{5,9},{9,5},{13,1},{2,14},{6,10},... | collective-permute-start | bytes 1032200 | tf_op jit(solution)/shard_map/ppermute | solution.py:667
  118.2 34.4 %collective-permute-start.27 = (bf16[160,896]{1,0:T(8,128)(2,1)S(1)}, bf16[160,896]{1,0:T(8,128)(2,1)}, u32[]{:S(2)}, u32[]{:S(2)}) collective-permute-start(bf16[160,896]{1,0:T(8,128)(2,1)S(1)} %pad.80), channel_id=1, source_target_pairs={{0,3},{1,2},{2,1},{3,0},{4,7},{5,6},{6,5},{7,4},{8,11},{9,10},{10,... | collective-permute-start | bytes 860168 | tf_op jit(solution)/shard_map/ppermute | solution.py:672
  138.6 40.3 %collective-permute-start.32 = (bf16[896,1280]{1,0:T(8,128)(2,1)}, bf16[896,1280]{1,0:T(8,128)(2,1)}, u32[]{:S(2)}, u32[]{:S(2)}) collective-permute-start(bf16[896,1280]{1,0:T(8,128)(2,1)} %all-gather.2.cloned.1.call-done.refs_8_), channel_id=1, source_target_pairs={{0,16},{16,0},{1,17},{17,1},{2,18},{18,2},{3,19},{19,3},{4,20},{20... | collective-permute-start | bytes 6881288 | tf_op jit(solution)/shard_map/ppermute | solution.py:662
  162.3 16.5 %collective-permute-start.31 = (bf16[192,896]{1,0:T(8,128)(2,1)S(1)}, bf16[192,896]{1,0:T(8,128)(2,1)S(1)}, u32[]{:S(2)}, u32[]{:S(2)}) collective-permute-start(bf16[192,896]{1,0:T(8,128)(2,1)S(1)} %get-tuple-element.244.refs_0_), channel_id=1, source_target_pairs={{0,12},{4,8},{8,4},{12,0},{1,13},{5,9},{9,5},{13,1},{2,14},{6,10},... | collective-permute-start | bytes 1032200 | tf_op jit(solution)/shard_map/ppermute | solution.py:667
  242.1 32.1 %collective-permute-start.40 = (bf16[192,896]{1,0:T(8,128)(2,1)}, bf16[192,896]{1,0:T(8,128)(2,1)S(1)}, u32[]{:S(2)}, u32[]{:S(2)}) collective-permute-start(bf16[192,896]{1,0:T(8,128)(2,1)} %get-tuple-element.281), channel_id=1, source_target_pairs={{0,4},{4,0},{8,12},{12,8},{1,5},{5,1},{9,13},{13,9},{2,6},{6,2},{1... | collective-permute-start | bytes 1032200 | tf_op jit(solution)/shard_map/ppermute | solution.py:667
  242.5 31.8 %collective-permute-start.41 = (bf16[192,896]{1,0:T(8,128)(2,1)}, bf16[192,896]{1,0:T(8,128)(2,1)S(1)}, u32[]{:S(2)}, u32[]{:S(2)}) collective-permute-start(bf16[192,896]{1,0:T(8,128)(2,1)} %get-tuple-element.282), channel_id=1, source_target_pairs={{0,8},{4,12},{8,0},{12,4},{1,9},{5,13},{9,1},{13,5},{2,10},{6,14},... | collective-permute-start | bytes 1032200 | tf_op jit(solution)/shard_map/ppermute | solution.py:667
  244.0 30.3 %collective-permute-start.42 = (bf16[192,896]{1,0:T(8,128)(2,1)}, bf16[192,896]{1,0:T(8,128)(2,1)S(1)}, u32[]{:S(2)}, u32[]{:S(2)}) collective-permute-start(bf16[192,896]{1,0:T(8,128)(2,1)} %get-tuple-element.283), channel_id=1, source_target_pairs={{0,12},{4,8},{8,4},{12,0},{1,13},{5,9},{9,5},{13,1},{2,14},{6,10},... | collective-permute-start | bytes 1032200 | tf_op jit(solution)/shard_map/ppermute | solution.py:667
  244.9 29.3 %collective-permute-start.44 = (bf16[4,32,896]{2,1,0:T(8,128)(2,1)}, bf16[4,32,896]{2,1,0:T(8,128)(2,1)S(1)}, u32[]{:S(2)}, u32[]{:S(2)}) collective-permute-start(bf16[4,32,896]{2,1,0:T(8,128)(2,1)} %get-tuple-element.398), channel_id=1, source_target_pairs={{0,8},{4,12},{8,0},{12,4},{1,9},{5,13},{9,1},{13,5},{2,10},{6,14},... | collective-permute-start | bytes 688136 | tf_op jit(solution)/shard_map/ppermute | solution.py:667
  248.5 25.8 %collective-permute-start.45 = (bf16[4,32,896]{2,1,0:T(8,128)(2,1)}, bf16[4,32,896]{2,1,0:T(8,128)(2,1)S(1)}, u32[]{:S(2)}, u32[]{:S(2)}) collective-permute-start(bf16[4,32,896]{2,1,0:T(8,128)(2,1)} %get-tuple-element.397), channel_id=1, source_target_pairs={{0,12},{4,8},{8,4},{12,0},{1,13},{5,9},{9,5},{13,1},{2,14},{6,10},... | collective-permute-start | bytes 688136 | tf_op jit(solution)/shard_map/ppermute | solution.py:667
  275.5 23.2 %collective-permute-start.47 = (bf16[768,256]{1,0:T(8,128)(2,1)}, bf16[768,256]{1,0:T(8,128)(2,1)}, u32[]{:S(2)}, u32[]{:S(2)}) collective-permute-start(bf16[768,256]{1,0:T(8,128)(2,1)} %get-tuple-element.384), channel_id=1, source_target_pairs={{0,8},{4,12},{8,0},{12,4},{1,9},{5,13},{9,1},{13,5},{2,10},{6,14},... | collective-permute-start | bytes 1179656 | tf_op jit(solution)/shard_map/ppermute | solution.py:667
  298.8 18.2 %collective-permute-start.52 = (bf16[4,128,896]{2,1,0:T(8,128)(2,1)}, bf16[4,128,896]{2,1,0:T(8,128)(2,1)}, u32[]{:S(2)}, u32[]{:S(2)}) collective-permute-start(bf16[4,128,896]{2,1,0:T(8,128)(2,1)} %get-tuple-element.309), channel_id=1, source_target_pairs={{0,16},{16,0},{1,17},{17,1},{2,18},{18,2},{3,19},{19,3},{4,20},{20... | collective-permute-start | bytes 2752520 | tf_op jit(solution)/shard_map/ppermute | solution.py:662
  310.0 33.8 %collective-permute-start.54 = (bf16[224,1280]{1,0:T(8,128)(2,1)}, bf16[224,1280]{1,0:T(8,128)(2,1)}, u32[]{:S(2)}, u32[]{:S(2)}) collective-permute-start(bf16[224,1280]{1,0:T(8,128)(2,1)} %reduce-scatter.2.cloned.1.call-done), channel_id=1, source_target_pairs={{0,4},{4,0},{8,12},{12,8},{1,5},{5,1},{9,13},{13,9},{2,6},{6,2},{1... | collective-permute-start | bytes 1720328 | tf_op jit(solution)/shard_map/ppermute | solution.py:667
  311.0 33.4 %collective-permute-start.55 = (bf16[224,1280]{1,0:T(8,128)(2,1)}, bf16[224,1280]{1,0:T(8,128)(2,1)}, u32[]{:S(2)}, u32[]{:S(2)}) collective-permute-start(bf16[224,1280]{1,0:T(8,128)(2,1)} %reduce-scatter.2.cloned.1.call-done), channel_id=1, source_target_pairs={{0,8},{4,12},{8,0},{12,4},{1,9},{5,13},{9,1},{13,5},{2,10},{6,14},... | collective-permute-start | bytes 1720328 | tf_op jit(solution)/shard_map/ppermute | solution.py:667
  314.9 31.6 %collective-permute-start.56 = (bf16[224,1280]{1,0:T(8,128)(2,1)}, bf16[224,1280]{1,0:T(8,128)(2,1)}, u32[]{:S(2)}, u32[]{:S(2)}) collective-permute-start(bf16[224,1280]{1,0:T(8,128)(2,1)} %reduce-scatter.2.cloned.1.call-done), channel_id=1, source_target_pairs={{0,12},{4,8},{8,4},{12,0},{1,13},{5,9},{9,5},{13,1},{2,14},{6,10},... | collective-permute-start | bytes 1720328 | tf_op jit(solution)/shard_map/ppermute | solution.py:667
  357.6 37.5 %collective-permute-start.72 = (bf16[4,224,1280]{2,1,0:T(8,128)(2,1)S(1)}, bf16[4,224,1280]{2,1,0:T(8,128)(2,1)S(1)}, u32[]{:S(2)}, u32[]{:S(2)}) collective-permute-start(bf16[4,224,1280]{2,1,0:T(8,128)(2,1)S(1)} %pad_maximum_fusion.refs_0_), channel_id=1, source_target_pairs={{0,16},{16,0},{1,17},{17,1},{2,18},{18,2},{3,19},{19,3},{4,20},{20... | collective-permute-start | bytes 6881288 | tf_op jit(solution)/shard_map/ppermute | solution.py:662
  360.0 21.3 %collective-permute-start.64 = (bf16[160,896]{1,0:T(8,128)(2,1)S(1)}, bf16[160,896]{1,0:T(8,128)(2,1)S(1)}, u32[]{:S(2)}, u32[]{:S(2)}) collective-permute-start(bf16[160,896]{1,0:T(8,128)(2,1)S(1)} %get-tuple-element.388), channel_id=1, source_target_pairs={{0,2},{1,3},{2,0},{3,1},{4,6},{5,7},{6,4},{7,5},{8,10},{9,11},{10,... | collective-permute-start | bytes 860168 | tf_op jit(solution)/shard_map/ppermute | solution.py:672
  360.9 22.9 %collective-permute-start.65 = (bf16[160,896]{1,0:T(8,128)(2,1)S(1)}, bf16[160,896]{1,0:T(8,128)(2,1)S(1)}, u32[]{:S(2)}, u32[]{:S(2)}) collective-permute-start(bf16[160,896]{1,0:T(8,128)(2,1)S(1)} %get-tuple-element.387), channel_id=1, source_target_pairs={{0,3},{1,2},{2,1},{3,0},{4,7},{5,6},{6,5},{7,4},{8,11},{9,10},{10,... | collective-permute-start | bytes 860168 | tf_op jit(solution)/shard_map/ppermute | solution.py:672
  364.2 19.6 %collective-permute-start.60 = (bf16[4,32,384]{2,1,0:T(8,128)(2,1)S(1)}, bf16[4,32,384]{2,1,0:T(8,128)(2,1)S(1)}, u32[]{:S(2)}, u32[]{:S(2)}) collective-permute-start(bf16[4,32,384]{2,1,0:T(8,128)(2,1)S(1)} %get-tuple-element.409), channel_id=1, source_target_pairs={{0,4},{4,0},{8,12},{12,8},{1,5},{5,1},{9,13},{13,9},{2,6},{6,2},{1... | collective-permute-start | bytes 294920 | tf_op jit(solution)/shard_map/ppermute | solution.py:667
  385.9 18.0 %collective-permute-start.69 = (bf16[160,896]{1,0:T(8,128)(2,1)S(1)}, bf16[160,896]{1,0:T(8,128)(2,1)S(1)}, u32[]{:S(2)}, u32[]{:S(2)}) collective-permute-start(bf16[160,896]{1,0:T(8,128)(2,1)S(1)} %add_convert_fusion.5), channel_id=1, source_target_pairs={{0,4},{4,0},{8,12},{12,8},{1,5},{5,1},{9,13},{13,9},{2,6},{6,2},{1... | collective-permute-start | bytes 860168 | tf_op jit(solution)/shard_map/ppermute | solution.py:667
  387.1 16.8 %collective-permute-start.70 = (bf16[160,896]{1,0:T(8,128)(2,1)S(1)}, bf16[160,896]{1,0:T(8,128)(2,1)S(1)}, u32[]{:S(2)}, u32[]{:S(2)}) collective-permute-start(bf16[160,896]{1,0:T(8,128)(2,1)S(1)} %add_convert_fusion.5), channel_id=1, source_target_pairs={{0,8},{4,12},{8,0},{12,4},{1,9},{5,13},{9,1},{13,5},{2,10},{6,14},... | collective-permute-start | bytes 860168 | tf_op jit(solution)/shard_map/ppermute | solution.py:667
  387.5 16.4 %collective-permute-start.71 = (bf16[160,896]{1,0:T(8,128)(2,1)S(1)}, bf16[160,896]{1,0:T(8,128)(2,1)S(1)}, u32[]{:S(2)}, u32[]{:S(2)}) collective-permute-start(bf16[160,896]{1,0:T(8,128)(2,1)S(1)} %add_convert_fusion.5), channel_id=1, source_target_pairs={{0,12},{4,8},{8,4},{12,0},{1,13},{5,9},{9,5},{13,1},{2,14},{6,10},... | collective-permute-start | bytes 860168 | tf_op jit(solution)/shard_map/ppermute | solution.py:667
  (141 other events, 1408.4 us)
Sparse Core Ops, SparseCore 0:
  61.0 77.5 all-gather.1
  242.3 44.6 reduce-scatter.1

commit v4 on v3

--- a/solution.py
+++ b/solution.py
@@ -27,19 +27,6 @@
     )
     angles = positions.astype(jnp.float32)[:, None] * inverse[None, :]
     return (jnp.cos(angles)[:, None, :], jnp.sin(angles)[:, None, :])
-
-
-def rotate(values, cosine_table, sine_table):
-    half_dim = values.shape[-1] // 2
-    front_half = values[..., :half_dim]
-    back_half = values[..., half_dim:]
-    return jnp.concatenate(
-        [
-            front_half * cosine_table - back_half * sine_table,
-            back_half * cosine_table + front_half * sine_table,
-        ],
-        -1,
-    )
 
 
 def matmul(left_side, right_side):
@@ -162,7 +149,8 @@
 
 
 def backward_kernel(
-    by_xor, info_ref, qext_ref, do_ref, att_ref, kv_ref, dq_ref, dkv_ref, doext_ref, dqt_ref
+    by_xor, info_ref, qext_ref, do_ref, att_ref, cos_ref, sin_ref, kv_ref, dq_ref, dkv_ref,
+    doext_ref, dqt_ref
 ):
     step = pl.program_id(0)
     last = pl.num_programs(0) - 1
@@ -234,9 +222,10 @@
                 if h // GROUP != j:
                     out = jnp.concatenate([out[:, HEAD:], out[:, :HEAD]], 1)
                 outs.append(out)
-            dq_ref[:, pair * 128 : (pair + 1) * 128] = (
-                jnp.where(lane < HEAD, outs[0], outs[1]) * HEAD ** (-0.5)
-            )
+            out = jnp.where(lane < HEAD, outs[0], outs[1]) * HEAD ** (-0.5)
+            dq_ref[:, pair * 128 : (pair + 1) * 128] = turn_tile(
+                out, cos_ref[...], -sin_ref[...]
+            ).astype(BF16)
 
 
 def whole_spec(shape):
@@ -273,7 +262,7 @@
     )(info, queries, kv)
 
 
-def attend_backward(info, by_xor, queries_ext, grad_att, attended, kv):
+def attend_backward(info, by_xor, queries_ext, grad_att, attended, cos, sin, kv):
     blocks, block_len, kv_width = kv.shape
     tokens_here, q_width = grad_att.shape
     rows = HEADS * tokens_here
@@ -286,6 +275,8 @@
                 whole_spec((rows, 256)),
                 whole_spec((tokens_here, q_width)),
                 whole_spec((tokens_here, q_width)),
+                whole_spec(cos.shape),
+                whole_spec(sin.shape),
                 pl.BlockSpec((1, block_len, kv_width), lambda i, info: (i, 0, 0)),
             ],
             out_specs=[
@@ -298,7 +289,7 @@
             ],
         ),
         out_shape=[
-            jax.ShapeDtypeStruct((tokens_here, q_width), F32),
+            jax.ShapeDtypeStruct((tokens_here, q_width), BF16),
             jax.ShapeDtypeStruct(kv.shape, BF16),
         ],
         compiler_params=pltpu.CompilerParams(
@@ -308,7 +299,7 @@
             flops=5 * 10**10, bytes_accessed=2**23, transcendentals=0
         ),
         name="attend_backward",
-    )(info, queries_ext, grad_att, attended, kv)
+    )(info, queries_ext, grad_att, attended, cos, sin, kv)
 
 
 def part_place(tp, j, k):
@@ -384,8 +375,8 @@
     )(*pieces)
 
 
-def join_weight(own_ref, sib_ref, out_ref):
-    tp, n_z, part_rows = own_ref.shape[:3]
+def join_weight(own_ref, sib_ref, first, part_rows, out_ref):
+    tp, n_z = own_ref.shape[:2]
     room = out_ref.shape[1] // part_rows
     for j, ref in enumerate((own_ref, sib_ref)):
         for k in range(tp):
@@ -396,7 +387,7 @@
                 start = pl.multiple_of(place * part_rows, 16)
                 for z in range(n_z):
                     at = jnp.bitwise_xor(lax.axis_index("fsdp"), z)
-                    out_ref[at, pl.ds(start, part_rows), :] = ref[k, z]
+                    out_ref[at, pl.ds(start, part_rows), :] = ref[k, z, first : first + part_rows]
 
 
 def whole_weight(ref):
@@ -457,7 +448,8 @@
 
 
 def query_kernel(own_ref, sib_ref, hid_ref, vec_ref, cos_ref, sin_ref, out_ref, q_ref):
-    join_weight(own_ref, sib_ref, out_ref)
+    part_rows = own_ref.shape[2] // 2
+    join_weight(own_ref, sib_ref, 0, part_rows, out_ref)
     whole = matmul(hid_ref[...], whole_weight(out_ref)) + vec_ref[2:3, :]
     for pair in range(HEADS // 2):
         lanes = slice(pair * 128, (pair + 1) * 128)
@@ -483,7 +475,8 @@
 
 
 def out_kernel(own_ref, sib_ref, att_ref, x_ref, vec_ref, out_ref, resid_ref, hid_ref):
-    join_weight(own_ref, sib_ref, out_ref)
+    part_rows = own_ref.shape[2] // 2
+    join_weight(own_ref, sib_ref, part_rows, part_rows, out_ref)
     resid = x_ref[...].astype(F32) + matmul(att_ref[...], whole_weight(out_ref))
     resid_ref[...] = resid
     hid_ref[...] = normed_rows(resid, vec_ref[1:2, :])
@@ -505,6 +498,66 @@
         cost_estimate=NO_COST,
         name="project_out",
     )(own, sib, attended, tokens, vecs)
+
+
+def kv_back_kernel(n_z, *refs):
+    terms, rest = refs[:n_z], refs[n_z:]
+    cos_ref, sin_ref, gq_ref, hid_ref, wq_ref, wkv_ref, x_ref, res_ref, vec_ref, two_ref = rest[:10]
+    tokens_ref, part_ref = rest[10:]
+    rows_here, width = x_ref.shape
+    total = sum(t[...].astype(F32) for t in terms)
+    half = total.shape[1] // 2
+    keys = turn_tile(total[:, :half], cos_ref[...], -sin_ref[...]).astype(BF16)
+    both = jnp.concatenate([keys, total[:, half:].astype(BF16)], 1)
+    grad = times_transposed(gq_ref[...], wq_ref[...]) + times_transposed(both, wkv_ref[...])
+    x = x_ref[...].astype(F32)
+    inv = lax.rsqrt(jnp.mean(x * x, -1, keepdims=True) + NORM_EPS)
+    normed = x * inv
+    scaled = grad * vec_ref[0:1, :]
+    tokens_ref[...] = res_ref[...] + inv * (
+        scaled - normed * jnp.mean(scaled * normed, -1, keepdims=True)
+    )
+    sums = jnp.sum(both.astype(F32), 0, keepdims=True)
+    share = half // n_z
+    gap = jnp.zeros((1, width // n_z - share), F32)
+    spread = []
+    for i in range(2):
+        cuts = []
+        for z in range(n_z):
+            at = i * half + z * share
+            cuts += [sums[:, at : at + share], gap]
+        spread.append(jnp.concatenate(cuts, 1))
+    columns = [
+        jnp.sum(grad * normed, 0, keepdims=True),
+        two_ref[...],
+        jnp.sum(gq_ref[...].astype(F32), 0, keepdims=True),
+    ] + spread
+    row = lax.broadcasted_iota(jnp.int32, (128, width), 0)
+    table = jnp.zeros((128, width), F32)
+    for i, v in enumerate(columns):
+        table = jnp.where(row == i, v, table)
+    part_ref[:, 2 * half :] = table.T.astype(BF16)
+    pad = -rows_here % 128
+    left = jnp.concatenate([hid_ref[...].astype(F32), jnp.zeros((pad, width), F32)], 0)
+    right = jnp.concatenate([both, jnp.zeros((pad, 2 * half), BF16)], 0)
+    part_ref[:, : 2 * half] = matmul(left.T.astype(BF16), right).astype(BF16)
+
+
+def kv_back(terms, cos, sin, gq, hidden, wq, wkv, tokens, resid_grad, vecs, two_sum):
+    vmem = pl.BlockSpec(memory_space=pltpu.VMEM)
+    width = tokens.shape[1]
+    return pl.pallas_call(
+        functools.partial(kv_back_kernel, len(terms)),
+        in_specs=[vmem] * (len(terms) + 10),
+        out_specs=[vmem] * 2,
+        out_shape=[
+            jax.ShapeDtypeStruct(tokens.shape, F32),
+            jax.ShapeDtypeStruct((width, wkv.shape[1] + 128), BF16),
+        ],
+        compiler_params=pltpu.CompilerParams(vmem_limit_bytes=40 * 2**20),
+        cost_estimate=NO_COST,
+        name="kv_back",
+    )(*terms, cos, sin, gq, hidden, wq, wkv, tokens, resid_grad, vecs, two_sum)
 
 
 def grad_weight_kernel(left_ref, right_ref, *refs):
@@ -723,9 +776,10 @@
             )
         )
     )
-    kv_got = [hop_z(kv_pack, k) for k in range(n_z)]
-    q_got = [hop_z(q_part, k) for k in range(n_z)]
-    o_got = [hop_z(o_part, k) for k in range(n_z)]
+    pack_rows = kv_pack.shape[0]
+    qo_part = jnp.concatenate([q_part, o_part], 0)
+    pack = jnp.concatenate([kv_pack, qo_part.reshape(-1, 2 * key_width)], 0)
+    got = [hop_z(pack, k) for k in range(n_z)]
     gu_cut = jnp.concatenate([ff_columns(gate_weight), ff_columns(up_weight)], 1)
     down_cut = lax.dynamic_slice_in_dim(down_weight, part * piece, piece, 0)
     down_cut = jnp.pad(down_cut, ((0, piece_pad - piece), (0, 0)))
@@ -733,13 +787,13 @@
     cosine_table, sine_table = rope_tables(query_pos, HEAD)
     cos_wide = jnp.tile(cosine_table[:, 0], (1, 4))
     sin_wide = jnp.tile(jnp.concatenate([-sine_table[:, 0], sine_table[:, 0]], 1), (1, 2))
-    kv_got, q_got, cos_wide, sin_wide, gu_cut, down_cut, o_got, og_here = (
-        lax.optimization_barrier(
-            (kv_got, q_got, cos_wide, sin_wide, gu_cut, down_cut, o_got, og_here)
-        )
-    )
-
-    q_own = [hop(jnp.stack(q_got), k) for k in range(tp)]
+    got, cos_wide, sin_wide, gu_cut, down_cut, og_here = lax.optimization_barrier(
+        (got, cos_wide, sin_wide, gu_cut, down_cut, og_here)
+    )
+    kv_got = [v[:pack_rows] for v in got]
+
+    qo_got = jnp.stack([v[pack_rows:].reshape(2 * part_rows, width) for v in got])
+    qo_own = [hop(qo_got, k) for k in range(tp)]
     widths = tuple(v.shape[0] for v in vectors)
     w_kv, vecs, kv_local, hidden_one = project_kv(
         kv_got, x_here, cos_wide, sin_wide, rows_here, widths
@@ -748,7 +802,7 @@
     gain_one = vecs[0:1, :width]
     gain_two = vecs[1:2, :width]
     kv_z = [hop_z(kv_local, k) for k in range(n_z)]
-    kv_z, q_own, gu_cut, down_cut = lax.optimization_barrier((kv_z, q_own, gu_cut, down_cut))
+    kv_z, qo_own, gu_cut, down_cut = lax.optimization_barrier((kv_z, qo_own, gu_cut, down_cut))
 
     kv_block = jnp.concatenate(kv_z, 0)
     if n_ctx == tp:
@@ -756,26 +810,25 @@
     else:
         kv_blocks = lax.all_gather(kv_block, "ctx", axis=0, tiled=False)
     gu_own = gather_z(gu_cut)
-    q_own = jnp.stack(q_own)
+    qo_own = jnp.stack(qo_own)
+    qo_sib = swap(qo_own)
     w_query, queries = project_query(
-        q_own, swap(q_own), hidden_one, vecs, cos_wide, sin_wide, rows_here
+        qo_own, qo_sib, hidden_one, vecs, cos_wide, sin_wide, rows_here
     )
     w_query = w_query.reshape(width, width)
-    kv_blocks, queries, o_got, og_here, down_cut = lax.optimization_barrier(
-        (kv_blocks, queries, o_got, og_here, down_cut)
-    )
-
-    o_own = [hop(jnp.stack(o_got), k) for k in range(tp)]
+    kv_blocks, queries, og_here, down_cut = lax.optimization_barrier(
+        (kv_blocks, queries, og_here, down_cut)
+    )
+
     og_parts = [hop(og_here, k) for k in range(tp)]
     down_own = [hop_z(down_cut, k) for k in range(n_z)]
     kv_whole = jnp.stack(kv_blocks) if n_ctx == tp else kv_blocks
     attended, queries_ext = attend_forward(order_row, n_ctx == tp, queries, kv_whole)
-    attended, o_own, queries_ext, og_parts, down_own = lax.optimization_barrier(
-        (attended, o_own, queries_ext, og_parts, down_own)
-    )
-    o_own = jnp.stack(o_own)
+    attended, queries_ext, og_parts, down_own, gu_own = lax.optimization_barrier(
+        (attended, queries_ext, og_parts, down_own, gu_own)
+    )
     w_out, resid, hidden_two = project_out(
-        o_own, swap(o_own), attended, x_here, vecs, rows_here
+        qo_own, qo_sib, attended, x_here, vecs, rows_here
     )
     w_out = w_out.reshape(width, width)
     h2_parts = [hop(hidden_two, k) for k in range(tp)]
@@ -818,10 +871,6 @@
 
     d_gu = grad_weight(h2_turned, ggus[0], swap(grad_weight(h2_turned, ggus[1])))
     d_down = grad_weight(acts[0], og_all, swap(grad_weight(acts[1], og_all)))
-    grad_h2_parts, d_gu, d_down, ff_out = lax.optimization_barrier(
-        (grad_h2_parts, d_gu, d_down, ff_out)
-    )
-    d_gu = scatter_z(d_gu)
     d_down = d_down.reshape(n_z, piece_pad, width)
     grad_h2 = sum(v.astype(F32) for v in grad_h2_parts)
     scale_two = lax.rsqrt(jnp.mean(resid * resid, -1, keepdims=True) + NORM_EPS)
@@ -831,31 +880,27 @@
     grad_resid = og_here.astype(F32) + grad_norm_two
     grad_proj = grad_resid.astype(BF16)
     grad_att = times_transposed(grad_proj, w_out).astype(BF16)
-    o_own, o_oth = core_halves(contract_rows(attended, grad_proj))
-    o_own, o_sib, grad_att, ff_out = lax.optimization_barrier(
-        (o_own, swap(o_oth), grad_att, ff_out)
-    )
+    grad_att, d_gu, ff_out = lax.optimization_barrier((grad_att, d_gu, ff_out))
+    d_gu = scatter_z(d_gu)
     ff_out = [hop(ff_out[k], k) for k in range(tp)]
-    o_terms = scatter_parts(core_total(o_own, o_sib))
-    grad_queries, grad_terms = attend_backward(
-        order_row, n_ctx == tp, queries_ext, grad_att, attended, kv_whole
-    )
-    grad_queries, grad_terms, ff_out, o_terms, d_down = lax.optimization_barrier(
-        (grad_queries, grad_terms, ff_out, o_terms, d_down)
-    )
-
-    grad_q_pre = (
-        rotate(grad_queries.reshape(tokens_here, HEADS, HEAD), cosine_table, -sine_table)
-        .reshape(tokens_here, HEADS * HEAD)
-        .astype(BF16)
-    )
-    q_own, q_oth = core_halves(contract_rows(hidden_one, grad_q_pre))
+    grad_q_pre, grad_terms = attend_backward(
+        order_row, n_ctx == tp, queries_ext, grad_att, attended, cos_wide, sin_wide, kv_whole
+    )
+    grad_q_pre, grad_terms, ff_out, d_down, grad_proj = lax.optimization_barrier(
+        (grad_q_pre, grad_terms, ff_out, d_down, grad_proj)
+    )
+
+    qo_own, qo_oth = core_halves(
+        jnp.concatenate(
+            [contract_rows(hidden_one, grad_q_pre), contract_rows(attended, grad_proj)], 1
+        )
+    )
     if n_ctx == tp:
         kv_terms = [hop(grad_terms[k], k) for k in range(n_ctx)]
     else:
         kv_terms = [lax.psum_scatter(grad_terms, "ctx", scatter_dimension=0, tiled=False)]
-    kv_terms, d_gu, d_down, q_own, q_oth, ff_out, o_terms = lax.optimization_barrier(
-        (kv_terms, d_gu, d_down, q_own, q_oth, ff_out, o_terms)
+    kv_terms, d_gu, d_down, qo_own, qo_oth, ff_out = lax.optimization_barrier(
+        (kv_terms, d_gu, d_down, qo_own, qo_oth, ff_out)
     )
 
     kv_sum = sum(v.astype(F32) for v in kv_terms).astype(BF16)
@@ -863,58 +908,42 @@
     kv_terms = [hop_z(kv_sum[k], k) for k in range(n_z)]
     d_gu = ctx_groups_sum(d_gu)
     gu_pieces = [hop(d_gu, k) for k in range(tp)]
-    q_sib = swap(q_oth)
+    qo_sib = swap(qo_oth)
     result = resid + sum(v.astype(F32) for v in ff_out)
     layer_out = result.astype(BF16)[None]
-    kv_terms, q_own, q_sib, d_down = lax.optimization_barrier((kv_terms, q_own, q_sib, d_down))
-
-    q_terms = scatter_parts(core_total(q_own, q_sib))
+    kv_terms, qo_own, qo_sib, d_down = lax.optimization_barrier(
+        (kv_terms, qo_own, qo_sib, d_down)
+    )
+
+    tokens_grad, kv_part = kv_back(
+        kv_terms,
+        cos_wide,
+        sin_wide,
+        grad_q_pre,
+        hidden_one,
+        w_query,
+        w_kv,
+        x_here,
+        grad_resid,
+        vecs,
+        jnp.sum(gain_two_terms, 0, keepdims=True),
+    )
+    tokens_grad = tokens_grad[None]
+    kv_own, kv_oth = core_halves(kv_part)
+    last = core_total(qo_own, qo_sib)
+    kv_own, kv_sib, gu_pieces, d_down, last = lax.optimization_barrier(
+        (kv_own, swap(kv_oth), gu_pieces, d_down, last)
+    )
+
+    last = scatter_parts(jnp.concatenate([last, core_total(kv_own, kv_sib)], 2))
     d_down = [
         hop_z(lax.dynamic_index_in_dim(d_down, zed ^ k, 0, keepdims=False), k) for k in range(n_z)
     ]
-    grad_kv = sum(v.astype(F32) for v in kv_terms)
-    grad_k_pre = (
-        rotate(
-            grad_kv[:, :key_width].reshape(tokens_here, KV_HEADS, HEAD), cosine_table, -sine_table
-        )
-        .reshape(tokens_here, key_width)
-        .astype(BF16)
-    )
-    grad_v_pre = grad_kv[:, key_width:].astype(BF16)
-    grad_kv_pre = jnp.concatenate([grad_k_pre, grad_v_pre], 1)
-    grad_hidden_one = times_transposed(grad_q_pre, w_query) + times_transposed(grad_kv_pre, w_kv)
-    inputs = x_here.astype(F32)
-    scale_one = lax.rsqrt(jnp.mean(inputs * inputs, -1, keepdims=True) + NORM_EPS)
-    normed_one = inputs * scale_one
-    grad_norm_one, gain_one_terms = rms_backward(grad_hidden_one, normed_one, scale_one, gain_one)
-    tokens_grad = (grad_resid + grad_norm_one)[None]
-
-    def by_rows(v):
-        share = v.shape[1] // n_z
-        v = v.reshape(tokens_here, n_z, share)
-        return jnp.pad(v, ((0, 0), (0, 0), (0, rows_here - share))).reshape(tokens_here, width)
-
-    terms = (gain_one_terms, gain_two_terms, grad_q_pre, by_rows(grad_k_pre), by_rows(grad_v_pre))
-    pick = jnp.arange(len(terms) * tokens_here)[:, None] // tokens_here == jnp.arange(128)[None]
-    columns = contract_rows(
-        jnp.concatenate([v.astype(BF16) for v in terms], 0), pick.astype(BF16)
-    )
-    kv_own, kv_oth = core_halves(
-        jnp.concatenate([contract_rows(hidden_one, grad_kv_pre), columns], 1)
-    )
-    kv_sib = swap(kv_oth)
-    kv_own, kv_sib, gu_pieces, q_terms = lax.optimization_barrier(
-        (kv_own, kv_sib, gu_pieces, q_terms)
-    )
-
-    kv_terms = scatter_parts(core_total(kv_own, kv_sib))
     gu_pieces = jnp.stack(gu_pieces)
     gu_sib = swap(gu_pieces)
-    kv_terms, d_down = lax.optimization_barrier((kv_terms, d_down))
-
-    last = jnp.concatenate(
-        [sum(v.astype(F32) for v in t).astype(BF16) for t in (q_terms, o_terms, kv_terms)], 2
-    )
+    last, d_down, gu_pieces, gu_sib = lax.optimization_barrier((last, d_down, gu_pieces, gu_sib))
+
+    last = sum(v.astype(F32) for v in last).astype(BF16)
     last = [
         hop_z(lax.dynamic_index_in_dim(last, zed ^ k, 0, keepdims=False), k) for k in range(n_z)
     ]

time: 442 us -> 406 us (0.919)
  starting transfers between devices: 103 us -> 81.3 us
  Pallas kernels: 81.7 us -> 98.7 us
  local copies, waits for them, and re-layouts: 56.1 us -> 42.4 us
  other arithmetic: 28.2 us -> 17.6 us
  matrix products: 9.82 us -> 2.76 us
    ppermute x42 -> x33, starting transfers between devices: 50.1 us -> 29.2 us  [hop(): return lax.ppermute(v, 'ctx', [(i, i ^ k) for i in range(n_ctx)])]
    all_gather x1, waiting for transfers between devices: 18.1 us -> 3.78 us  [gather_z(): return lax.all_gather(v, 'fsdp', axis=0, tiled=True)]
    ppermute x24 -> x18, waiting for transfers between devices: 50.4 us -> 63.9 us  [hop_z(): return lax.ppermute(v, 'fsdp', [(i, i ^ k) for i in range(n_z)])]
    pallas_call x1, Pallas kernels: 21.1 us -> 28.1 us  [attend_backward(): pl.pallas_call(functools.partial(backward_kernel, by_xor), grid_spec=pltp...]
    ppermute x12 -> x10, starting transfers between devices: 22.8 us -> 20 us  [swap(): return lax.ppermute(v, 'seq', [(0, 1), (1, 0)])]
    unnamed x191 -> x119, local copies, waits for them, and re-layouts: 22.1 us -> 19.7 us
    ppermute x42 -> x33, waiting for transfers between devices: 72.9 us -> 75.2 us  [hop(): return lax.ppermute(v, 'ctx', [(i, i ^ k) for i in range(n_ctx)])]
    ppermute x24 -> x18, starting transfers between devices: 30.3 us -> 32 us  [hop_z(): return lax.ppermute(v, 'fsdp', [(i, i ^ k) for i in range(n_z)])]
  transfers between devices with their start and end apart: 80 -> 63, of which waited for: 32 -> 29; matrix products, arithmetic and copies ran while one was open for 13% -> 7% of each run, Pallas kernels for 13% -> 17%
where the time goes in v4:
time: 406 us; the launch traced here: 402 us
  waiting for transfers between devices  143 us (35%)
  Pallas kernels  98.7 us (24%)
  starting transfers between devices  81.3 us (20%)
  local copies, waits for them, and re-layouts  42.4 us (10%)
  other arithmetic  17.6 us (4%)
  between operations  15.9 us (4%)
    ppermute x33, waiting for transfers between devices, hop(): return lax.ppermute(v, 'ctx', [(i, i ^ k) for i in range(n_ctx)])  75.2 us
    ppermute x18, waiting for transfers between devices, hop_z(): return lax.ppermute(v, 'fsdp', [(i, i ^ k) for i in range(n_z)])  63.9 us
    ppermute x18, starting transfers between devices, hop_z(): return lax.ppermute(v, 'fsdp', [(i, i ^ k) for i in range(n_z)])  32 us
    ppermute x33, starting transfers between devices, hop(): return lax.ppermute(v, 'ctx', [(i, i ^ k) for i in range(n_ctx)])  29.2 us
    pallas_call x1, Pallas kernels, attend_backward(): pl.pallas_call(functools.partial(backward_kernel, by_xor), grid_spec=pltp...  28.1 us
    pallas_call x1, Pallas kernels, ff_pass(): pl.pallas_call(functools.partial(ff_kernel, tp, n_z), in_specs=[vmem] * (...  21.4 us
    ppermute x10, starting transfers between devices, swap(): return lax.ppermute(v, 'seq', [(0, 1), (1, 0)])  20 us
    unnamed x119, local copies, waits for them, and re-layouts  19.7 us
  transfers between devices with their start and end apart: 63, of which 29 were waited for; matrix products, arithmetic and copies ran while one was open for 7% of the time, Pallas kernels for 17%

profile of v4, /device:TPU:1, one launch (start us, length us, event | category | flops | bytes accessed | tf_op | source)
XLA Modules:
  0.0 401.6 jit_solution(16209606924573803907)
XLA Ops:
  26.0 7.8 %collective-permute-done.2 = bf16[464,256]{1,0:T(8,128)(2,1)} collective-permute-done((bf16[464,256]{1,0:T(8,128)(2,1)S(1)}, bf16[464,256]{1,0:T(8,128)(2,1)}, u32[]{:S(2)}, u32[]{:S(2)}) %collective-permute-start.2) | collective-permute-done | bytes 237600 | tf_op jit(solution)/shard_map/ppermute | solution.py:725
  43.5 5.3 %collective-permute-start.3 = (bf16[192,256]{1,0:T(8,128)(2,1)S(1)}, bf16[192,256]{1,0:T(8,128)(2,1)S(1)}, u32[]{:S(2)}, u32[]{:S(2)}) collective-permute-start(bf16[192,256]{1,0:T(8,128)(2,1)S(1)} %get-tuple-element.176), channel_id=1, source_target_pairs={{0,1},{1,0},{2,3},{3,2},{4,5},{5,4},{6,7},{7,6},{8,9},{9,8},{10,11... | collective-permute-start | bytes 294920 | tf_op jit(solution)/shard_map/ppermute | solution.py:725
  54.2 3.2 collective-permute-done.5
  59.9 4.0 collective-permute-start.9
  69.3 2.6 project_query.1
  71.9 5.6 %collective-permute-done.10 = bf16[768,256]{1,0:T(8,128)(2,1)} collective-permute-done((bf16[768,256]{1,0:T(8,128)(2,1)}, bf16[768,256]{1,0:T(8,128)(2,1)}, u32[]{:S(2)}, u32[]{:S(2)}) %collective-permute-start.10) | collective-permute-done | bytes 393248 | tf_op jit(solution)/shard_map/ppermute | solution.py:720
  77.6 8.2 %collective-permute-done.11 = bf16[768,256]{1,0:T(8,128)(2,1)} collective-permute-done((bf16[768,256]{1,0:T(8,128)(2,1)}, bf16[768,256]{1,0:T(8,128)(2,1)}, u32[]{:S(2)}, u32[]{:S(2)}) %collective-permute-start.11) | collective-permute-done | bytes 393248 | tf_op jit(solution)/shard_map/ppermute | solution.py:720
  87.0 4.6 %collective-permute-start.16 = (bf16[160,896]{1,0:T(8,128)(2,1)S(1)}, bf16[160,896]{1,0:T(8,128)(2,1)S(1)}, u32[]{:S(2)}, u32[]{:S(2)}) collective-permute-start(bf16[160,896]{1,0:T(8,128)(2,1)S(1)} %pad.70), channel_id=1, source_target_pairs={{0,1},{1,0},{2,3},{3,2},{4,5},{5,4},{6,7},{7,6},{8,9},{9,8},{10,11... | collective-permute-start | bytes 860168 | tf_op jit(solution)/shard_map/ppermute | solution.py:725
  96.8 21.9 %collective-permute-done.16 = bf16[160,896]{1,0:T(8,128)(2,1)S(1)} collective-permute-done((bf16[160,896]{1,0:T(8,128)(2,1)S(1)}, bf16[160,896]{1,0:T(8,128)(2,1)S(1)}, u32[]{:S(2)}, u32[]{:S(2)}) %collective-permute-start.16) | collective-permute-done | bytes 286752 | tf_op jit(solution)/shard_map/ppermute | solution.py:725
  119.4 17.1 %attend_forward.1 = (bf16[192,896]{1,0:T(8,128)(2,1)S(1)}, bf16[2688,256]{1,0:T(8,128)(2,1)S(1)}) custom-call(s32[4]{0:T(128)S(1)} %bitcast.97, bf16[192,896]{1,0:T(8,128)(2,1)S(1)} %get-tuple-element.185.q_ref, bf16[4,768,256]{2,1,0:T(8,128)(2,1)S(1)} %pad_maximum_fusion.3.kv_ref), custom_call_target="tpu_custom_call" | custom-call | flops 30000001024 | bytes 8388608 | tf_op jit(solution)/shard_map/attend_forward/pallas_call | solution.py:239
  140.1 3.8 all-gather.2.cloned.1.call-done.refs_8_
  146.4 3.1 project_out.1
  153.7 7.0 %collective-permute-done.19.refs_1_ = bf16[192,896]{1,0:T(8,128)(2,1)S(1)} collective-permute-done((bf16[192,896]{1,0:T(8,128)(2,1)S(1)}, bf16[192,896]{1,0:T(8,128)(2,1)S(1)}, u32[]{:S(2)}, u32[]{:S(2)}) %collective-permute-start.19) | collective-permute-done | bytes 344096 | tf_op jit(solution)/shard_map/ppermute | solution.py:720
  160.7 7.2 %collective-permute-done.20.refs_2_ = bf16[192,896]{1,0:T(8,128)(2,1)S(1)} collective-permute-done((bf16[192,896]{1,0:T(8,128)(2,1)S(1)}, bf16[192,896]{1,0:T(8,128)(2,1)S(1)}, u32[]{:S(2)}, u32[]{:S(2)}) %collective-permute-start.20) | collective-permute-done | bytes 344096 | tf_op jit(solution)/shard_map/ppermute | solution.py:720
  170.2 21.4 %ff_pass.1 = (bf16[640,768]{1,0:T(8,128)(2,1)}, bf16[640,768]{1,0:T(8,128)(2,1)}, bf16[768,1280]{1,0:T(8,128)(2,1)}, bf16[768,1280]{1,0:T(8,128)(2,1)}, bf16[896...) custom-call(bf16[192,896]{1,0:T(8,128)(2,1)} %copy-done.27, ...), custom_call_target="tpu_custom_call" | custom-call | tf_op jit(solution)/shard_map/ff_pass/pallas_call | solution.py:666
  194.5 3.1 grad_weight.4
  205.3 3.6 collective-permute-done.24
  209.5 7.8 %collective-permute-done.26 = bf16[192,896]{1,0:T(8,128)(2,1)S(1)} collective-permute-done((bf16[192,896]{1,0:T(8,128)(2,1)S(1)}, bf16[192,896]{1,0:T(8,128)(2,1)S(1)}, u32[]{:S(2)}, u32[]{:S(2)}) %collective-permute-start.26) | collective-permute-done | bytes 344096 | tf_op jit(solution)/shard_map/ppermute | solution.py:720
  223.3 3.4 grad_weight.5
  234.1 28.1 %attend_backward.1 = (bf16[192,896]{1,0:T(8,128)(2,1)S(1)}, bf16[4,768,256]{2,1,0:T(8,128)(2,1)S(1)}) custom-call(s32[4]{0:T(128)S(1)} %bitcast.98, bf16[2688,256]{1,0:T(8,128)(2,1)S(1)} %copy-done.31, bf16[192,896]{1,0:T(8,128)(2,1)S(1)} %copy-done.28, bf16[192,896]{1,0:T(8,128)(2,1)S(1)} %copy-done.20, f32[192,128]{1,0:T(8,128)S(1)} %copy.33.refs_5_.cos_ref.refs_4_, ...), custom_call_target="tpu_custom_call" | custom-call | flops 49999998976 | bytes 8388608 | tf_op jit(solution)/shard_map/attend_backward/pallas_call | solution.py:269
  272.2 9.1 %collective-permute-done.33 = bf16[768,256]{1,0:T(8,128)(2,1)S(1)} collective-permute-done((bf16[768,256]{1,0:T(8,128)(2,1)S(1)}, bf16[768,256]{1,0:T(8,128)(2,1)S(1)}, u32[]{:S(2)}, u32[]{:S(2)}) %collective-permute-start.33) | collective-permute-done | bytes 393248 | tf_op jit(solution)/shard_map/ppermute | solution.py:720
  291.5 5.9 %collective-permute-done.36.refs_2_ = bf16[192,256]{1,0:T(8,128)(2,1)S(1)} collective-permute-done((bf16[192,256]{1,0:T(8,128)(2,1)S(1)}, bf16[192,256]{1,0:T(8,128)(2,1)S(1)}, u32[]{:S(2)}, u32[]{:S(2)}) %collective-permute-start.36) | collective-permute-done | bytes 98336 | tf_op jit(solution)/shard_map/ppermute | solution.py:725
  306.1 10.5 %collective-permute-done.42 = bf16[224,1280]{1,0:T(8,128)(2,1)S(1)} collective-permute-done((bf16[224,1280]{1,0:T(8,128)(2,1)}, bf16[224,1280]{1,0:T(8,128)(2,1)S(1)}, u32[]{:S(2)}, u32[]{:S(2)}) %collective-permute-start.42) | collective-permute-done | bytes 573472 | tf_op jit(solution)/shard_map/ppermute | solution.py:720
  318.3 2.8 collective-permute-start.49
  324.4 10.0 %collective-permute-done.46 = bf16[160,896]{1,0:T(8,128)(2,1)S(1)} collective-permute-done((bf16[160,896]{1,0:T(8,128)(2,1)S(1)}, bf16[160,896]{1,0:T(8,128)(2,1)S(1)}, u32[]{:S(2)}, u32[]{:S(2)}) %collective-permute-start.46) | collective-permute-done | bytes 286752 | tf_op jit(solution)/shard_map/ppermute | solution.py:725
  337.9 8.4 %collective-permute-done.48 = bf16[160,896]{1,0:T(8,128)(2,1)S(1)} collective-permute-done((bf16[160,896]{1,0:T(8,128)(2,1)S(1)}, bf16[160,896]{1,0:T(8,128)(2,1)S(1)}, u32[]{:S(2)}, u32[]{:S(2)}) %collective-permute-start.48) | collective-permute-done | bytes 286752 | tf_op jit(solution)/shard_map/ppermute | solution.py:725
  356.2 2.7 collective-permute-start.52
  358.9 9.1 %spread_columns.1 = (f32[224,4864]{1,0:T(8,128)}, f32[224,4864]{1,0:T(8,128)}) custom-call(bf16[4,224,1280]{2,1,0:T(8,128)(2,1)} %pad_maximum_fusion.refs_0_, bf16[4,224,1280]{2,1,0:T(8,128)(2,1)} %collective-permute-done.49.refs_1_), custom_call_target="tpu_custom_call" | custom-call | tf_op jit(solution)/shard_map/spread_columns/pallas_call | solution.py:332
  368.3 5.3 %collective-permute-start.59 = (bf16[4,160,896]{2,1,0:T(8,128)(2,1)S(1)}, bf16[4,160,896]{2,1,0:T(8,128)(2,1)S(1)}, u32[]{:S(2)}, u32[]{:S(2)}) collective-permute-start(bf16[4,160,896]{2,1,0:T(8,128)(2,1)S(1)} %pad_maximum_fusion.5.refs_0_), channel_id=1, source_target_pairs={{0,16},{16,0},{1,17},{17,1},{2,18},{18,2},{3,19},{19,3},{4,20},{20... | collective-permute-start | bytes 3440648 | tf_op jit(solution)/shard_map/ppermute | solution.py:715
  376.4 2.6 collective-permute-done.56
  379.0 3.2 collective-permute-done.57
  385.6 3.8 spread_rows.3
  (310 shorter events, 143.2 us)
Async XLA Ops:
  7.2 136.6 %all-gather.2.cloned.1.call-start = ((), (), s32[]{:S(2)}) async-start(), calls=%async_computation.1 | async-start | bytes 2867200 | tf_op jit(solution)/shard_map/all_gather | solution.py:728
  37.3 20.1 %collective-permute-start.6 = (bf16[4,64,896]{2,1,0:T(8,128)(2,1)S(1)}, bf16[4,64,896]{2,1,0:T(8,128)(2,1)S(1)}, u32[]{:S(2)}, u32[]{:S(2)}) collective-permute-start(bf16[4,64,896]{2,1,0:T(8,128)(2,1)S(1)} %constant_dynamic-update-slice_fusion.2), channel_id=1, source_target_pairs={{0,4},{4,0},{8,12},{12,8},{1,5},{5,1},{9,13},{13,9},{2,6},{6,2},{1... | collective-permute-start | bytes 1376264 | tf_op jit(solution)/shard_map/ppermute | solution.py:720
  38.6 18.8 %collective-permute-start.7 = (bf16[4,64,896]{2,1,0:T(8,128)(2,1)S(1)}, bf16[4,64,896]{2,1,0:T(8,128)(2,1)}, u32[]{:S(2)}, u32[]{:S(2)}) collective-permute-start(bf16[4,64,896]{2,1,0:T(8,128)(2,1)S(1)} %constant_dynamic-update-slice_fusion.2), channel_id=1, source_target_pairs={{0,8},{4,12},{8,0},{12,4},{1,9},{5,13},{9,1},{13,5},{2,10},{6,14},... | collective-permute-start | bytes 1376264 | tf_op jit(solution)/shard_map/ppermute | solution.py:720
  39.9 17.6 %collective-permute-start.8 = (bf16[4,64,896]{2,1,0:T(8,128)(2,1)S(1)}, bf16[4,64,896]{2,1,0:T(8,128)(2,1)}, u32[]{:S(2)}, u32[]{:S(2)}) collective-permute-start(bf16[4,64,896]{2,1,0:T(8,128)(2,1)S(1)} %constant_dynamic-update-slice_fusion.2), channel_id=1, source_target_pairs={{0,12},{4,8},{8,4},{12,0},{1,13},{5,9},{9,5},{13,1},{2,14},{6,10},... | collective-permute-start | bytes 1376264 | tf_op jit(solution)/shard_map/ppermute | solution.py:720
  67.7 18.1 %collective-permute-start.11 = (bf16[768,256]{1,0:T(8,128)(2,1)}, bf16[768,256]{1,0:T(8,128)(2,1)}, u32[]{:S(2)}, u32[]{:S(2)}) collective-permute-start(bf16[768,256]{1,0:T(8,128)(2,1)} %constant_dynamic-update-slice_fusion.6), channel_id=1, source_target_pairs={{0,8},{4,12},{8,0},{12,4},{1,9},{5,13},{9,1},{13,5},{2,10},{6,14},... | collective-permute-start | bytes 1179656 | tf_op jit(solution)/shard_map/ppermute | solution.py:720
  69.0 18.0 %collective-permute-start.12 = (bf16[768,256]{1,0:T(8,128)(2,1)}, bf16[768,256]{1,0:T(8,128)(2,1)}, u32[]{:S(2)}, u32[]{:S(2)}) collective-permute-start(bf16[768,256]{1,0:T(8,128)(2,1)} %constant_dynamic-update-slice_fusion.6), channel_id=1, source_target_pairs={{0,12},{4,8},{8,4},{12,0},{1,13},{5,9},{9,5},{13,1},{2,14},{6,10},... | collective-permute-start | bytes 1179656 | tf_op jit(solution)/shard_map/ppermute | solution.py:720
  69.2 212.9 %reduce-scatter.2.cloned.1.call-start = ((), (), s32[]{:S(2)}) async-start(), calls=%async_computation.2 | async-start | bytes 2867200 | tf_op jit(solution)/shard_map/reduce_scatter | solution.py:731
  87.0 31.7 %collective-permute-start.16 = (bf16[160,896]{1,0:T(8,128)(2,1)S(1)}, bf16[160,896]{1,0:T(8,128)(2,1)S(1)}, u32[]{:S(2)}, u32[]{:S(2)}) collective-permute-start(bf16[160,896]{1,0:T(8,128)(2,1)S(1)} %pad.70), channel_id=1, source_target_pairs={{0,1},{1,0},{2,3},{3,2},{4,5},{5,4},{6,7},{7,6},{8,9},{9,8},{10,11... | collective-permute-start | bytes 860168 | tf_op jit(solution)/shard_map/ppermute | solution.py:725
  91.6 46.8 %collective-permute-start.13 = (bf16[192,896]{1,0:T(8,128)(2,1)S(1)}, bf16[192,896]{1,0:T(8,128)(2,1)S(1)}, u32[]{:S(2)}, u32[]{:S(2)}) collective-permute-start(bf16[192,896]{1,0:T(8,128)(2,1)S(1)} %bitcast.103), channel_id=1, source_target_pairs={{0,4},{4,0},{8,12},{12,8},{1,5},{5,1},{9,13},{13,9},{2,6},{6,2},{1... | collective-permute-start | bytes 1032200 | tf_op jit(solution)/shard_map/ppermute | solution.py:720
  91.9 46.5 %collective-permute-start.14 = (bf16[192,896]{1,0:T(8,128)(2,1)S(1)}, bf16[192,896]{1,0:T(8,128)(2,1)S(1)}, u32[]{:S(2)}, u32[]{:S(2)}) collective-permute-start(bf16[192,896]{1,0:T(8,128)(2,1)S(1)} %bitcast.104), channel_id=1, source_target_pairs={{0,8},{4,12},{8,0},{12,4},{1,9},{5,13},{9,1},{13,5},{2,10},{6,14},... | collective-permute-start | bytes 1032200 | tf_op jit(solution)/shard_map/ppermute | solution.py:720
  92.8 47.2 %collective-permute-start.15 = (bf16[192,896]{1,0:T(8,128)(2,1)S(1)}, bf16[192,896]{1,0:T(8,128)(2,1)}, u32[]{:S(2)}, u32[]{:S(2)}) collective-permute-start(bf16[192,896]{1,0:T(8,128)(2,1)S(1)} %bitcast.105), channel_id=1, source_target_pairs={{0,12},{4,8},{8,4},{12,0},{1,13},{5,9},{9,5},{13,1},{2,14},{6,10},... | collective-permute-start | bytes 1032200 | tf_op jit(solution)/shard_map/ppermute | solution.py:720
  94.2 44.2 %collective-permute-start.17 = (bf16[160,896]{1,0:T(8,128)(2,1)S(1)}, bf16[160,896]{1,0:T(8,128)(2,1)S(1)}, u32[]{:S(2)}, u32[]{:S(2)}) collective-permute-start(bf16[160,896]{1,0:T(8,128)(2,1)S(1)} %pad.70), channel_id=1, source_target_pairs={{0,2},{1,3},{2,0},{3,1},{4,6},{5,7},{6,4},{7,5},{8,10},{9,11},{10,... | collective-permute-start | bytes 860168 | tf_op jit(solution)/shard_map/ppermute | solution.py:725
  118.7 19.7 %collective-permute-start.18 = (bf16[160,896]{1,0:T(8,128)(2,1)S(1)}, bf16[160,896]{1,0:T(8,128)(2,1)S(1)}, u32[]{:S(2)}, u32[]{:S(2)}) collective-permute-start(bf16[160,896]{1,0:T(8,128)(2,1)S(1)} %pad.70), channel_id=1, source_target_pairs={{0,3},{1,2},{2,1},{3,0},{4,7},{5,6},{6,5},{7,4},{8,11},{9,10},{10,... | collective-permute-start | bytes 860168 | tf_op jit(solution)/shard_map/ppermute | solution.py:725
  143.8 25.2 %collective-permute-start.22 = (bf16[896,1280]{1,0:T(8,128)(2,1)}, bf16[896,1280]{1,0:T(8,128)(2,1)}, u32[]{:S(2)}, u32[]{:S(2)}) collective-permute-start(bf16[896,1280]{1,0:T(8,128)(2,1)} %all-gather.2.cloned.1.call-done.refs_8_), channel_id=1, source_target_pairs={{0,16},{16,0},{1,17},{17,1},{2,18},{18,2},{3,19},{19,3},{4,20},{20... | collective-permute-start | bytes 6881288 | tf_op jit(solution)/shard_map/ppermute | solution.py:715
  146.3 22.8 %collective-permute-start.23 = (bf16[4,160,896]{2,1,0:T(8,128)(2,1)S(1)}, bf16[4,160,896]{2,1,0:T(8,128)(2,1)S(1)}, u32[]{:S(2)}, u32[]{:S(2)}) collective-permute-start(bf16[4,160,896]{2,1,0:T(8,128)(2,1)S(1)} %pad_maximum_fusion.4.refs_10_), channel_id=1, source_target_pairs={{0,16},{16,0},{1,17},{17,1},{2,18},{18,2},{3,19},{19,3},{4,20},{20... | collective-permute-start | bytes 3440648 | tf_op jit(solution)/shard_map/ppermute | solution.py:715
  197.7 25.6 %collective-permute-start.27 = (bf16[896,1280]{1,0:T(8,128)(2,1)}, bf16[896,1280]{1,0:T(8,128)(2,1)}, u32[]{:S(2)}, u32[]{:S(2)}) collective-permute-start(bf16[896,1280]{1,0:T(8,128)(2,1)} %grad_weight.4), channel_id=1, source_target_pairs={{0,16},{16,0},{1,17},{17,1},{2,18},{18,2},{3,19},{19,3},{4,20},{20... | collective-permute-start | bytes 6881288 | tf_op jit(solution)/shard_map/ppermute | solution.py:715
  200.5 16.8 %collective-permute-start.26 = (bf16[192,896]{1,0:T(8,128)(2,1)S(1)}, bf16[192,896]{1,0:T(8,128)(2,1)S(1)}, u32[]{:S(2)}, u32[]{:S(2)}) collective-permute-start(bf16[192,896]{1,0:T(8,128)(2,1)S(1)} %copy-done.55), channel_id=1, source_target_pairs={{0,12},{4,8},{8,4},{12,0},{1,13},{5,9},{9,5},{13,1},{2,14},{6,10},... | collective-permute-start | bytes 1032200 | tf_op jit(solution)/shard_map/ppermute | solution.py:720
  204.4 16.4 %collective-permute-start.31 = (bf16[640,896]{1,0:T(8,128)(2,1)S(1)}, bf16[640,896]{1,0:T(8,128)(2,1)S(1)}, u32[]{:S(2)}, u32[]{:S(2)}) collective-permute-start(bf16[640,896]{1,0:T(8,128)(2,1)S(1)} %grad_weight.6), channel_id=1, source_target_pairs={{0,16},{16,0},{1,17},{17,1},{2,18},{18,2},{3,19},{19,3},{4,20},{20... | collective-permute-start | bytes 3440648 | tf_op jit(solution)/shard_map/ppermute | solution.py:715
  228.1 34.1 %collective-permute-start.28 = (bf16[192,896]{1,0:T(8,128)(2,1)}, bf16[192,896]{1,0:T(8,128)(2,1)}, u32[]{:S(2)}, u32[]{:S(2)}) collective-permute-start(bf16[192,896]{1,0:T(8,128)(2,1)} %get-tuple-element.224), channel_id=1, source_target_pairs={{0,4},{4,0},{8,12},{12,8},{1,5},{5,1},{9,13},{13,9},{2,6},{6,2},{1... | collective-permute-start | bytes 1032200 | tf_op jit(solution)/shard_map/ppermute | solution.py:720
  228.4 33.9 %collective-permute-start.29 = (bf16[192,896]{1,0:T(8,128)(2,1)}, bf16[192,896]{1,0:T(8,128)(2,1)}, u32[]{:S(2)}, u32[]{:S(2)}) collective-permute-start(bf16[192,896]{1,0:T(8,128)(2,1)} %get-tuple-element.225), channel_id=1, source_target_pairs={{0,8},{4,12},{8,0},{12,4},{1,9},{5,13},{9,1},{13,5},{2,10},{6,14},... | collective-permute-start | bytes 1032200 | tf_op jit(solution)/shard_map/ppermute | solution.py:720
  229.2 33.0 %collective-permute-start.30 = (bf16[192,896]{1,0:T(8,128)(2,1)}, bf16[192,896]{1,0:T(8,128)(2,1)}, u32[]{:S(2)}, u32[]{:S(2)}) collective-permute-start(bf16[192,896]{1,0:T(8,128)(2,1)} %get-tuple-element.226), channel_id=1, source_target_pairs={{0,12},{4,8},{8,4},{12,0},{1,13},{5,9},{9,5},{13,1},{2,14},{6,10},... | collective-permute-start | bytes 1032200 | tf_op jit(solution)/shard_map/ppermute | solution.py:720
  263.1 18.2 %collective-permute-start.33 = (bf16[768,256]{1,0:T(8,128)(2,1)S(1)}, bf16[768,256]{1,0:T(8,128)(2,1)S(1)}, u32[]{:S(2)}, u32[]{:S(2)}) collective-permute-start(bf16[768,256]{1,0:T(8,128)(2,1)S(1)} %get-tuple-element.326), channel_id=1, source_target_pairs={{0,8},{4,12},{8,0},{12,4},{1,9},{5,13},{9,1},{13,5},{2,10},{6,14},... | collective-permute-start | bytes 1179656 | tf_op jit(solution)/shard_map/ppermute | solution.py:720
  263.1 19.0 %collective-permute-start.34 = (bf16[768,256]{1,0:T(8,128)(2,1)S(1)}, bf16[768,256]{1,0:T(8,128)(2,1)}, u32[]{:S(2)}, u32[]{:S(2)}) collective-permute-start(bf16[768,256]{1,0:T(8,128)(2,1)S(1)} %get-tuple-element.325), channel_id=1, source_target_pairs={{0,12},{4,8},{8,4},{12,0},{1,13},{5,9},{9,5},{13,1},{2,14},{6,10},... | collective-permute-start | bytes 1179656 | tf_op jit(solution)/shard_map/ppermute | solution.py:720
  282.1 16.5 %collective-permute-start.38 = (bf16[4,128,1792]{2,1,0:T(8,128)(2,1)}, bf16[4,128,1792]{2,1,0:T(8,128)(2,1)S(1)}, u32[]{:S(2)}, u32[]{:S(2)}) collective-permute-start(bf16[4,128,1792]{2,1,0:T(8,128)(2,1)} %get-tuple-element.248), channel_id=1, source_target_pairs={{0,16},{16,0},{1,17},{17,1},{2,18},{18,2},{3,19},{19,3},{4,20},{20... | collective-permute-start | bytes 5505032 | tf_op jit(solution)/shard_map/ppermute | solution.py:715
  297.4 19.3 %collective-permute-start.42 = (bf16[224,1280]{1,0:T(8,128)(2,1)}, bf16[224,1280]{1,0:T(8,128)(2,1)S(1)}, u32[]{:S(2)}, u32[]{:S(2)}) collective-permute-start(bf16[224,1280]{1,0:T(8,128)(2,1)} %reduce-scatter.2.cloned.1.call-done), channel_id=1, source_target_pairs={{0,12},{4,8},{8,4},{12,0},{1,13},{5,9},{9,5},{13,1},{2,14},{6,10},... | collective-permute-start | bytes 1720328 | tf_op jit(solution)/shard_map/ppermute | solution.py:720
  300.7 15.9 %collective-permute-start.39 = (bf16[4,128,384]{2,1,0:T(8,128)(2,1)S(1)}, bf16[4,128,384]{2,1,0:T(8,128)(2,1)S(1)}, u32[]{:S(2)}, u32[]{:S(2)}) collective-permute-start(bf16[4,128,384]{2,1,0:T(8,128)(2,1)S(1)} %get-tuple-element.333), channel_id=1, source_target_pairs={{0,16},{16,0},{1,17},{17,1},{2,18},{18,2},{3,19},{19,3},{4,20},{20... | collective-permute-start | bytes 1179656 | tf_op jit(solution)/shard_map/ppermute | solution.py:715
  318.3 30.4 %collective-permute-start.49 = (bf16[4,224,1280]{2,1,0:T(8,128)(2,1)}, bf16[4,224,1280]{2,1,0:T(8,128)(2,1)}, u32[]{:S(2)}, u32[]{:S(2)}) collective-permute-start(bf16[4,224,1280]{2,1,0:T(8,128)(2,1)} %pad_maximum_fusion.refs_0_), channel_id=1, source_target_pairs={{0,16},{16,0},{1,17},{17,1},{2,18},{18,2},{3,19},{19,3},{4,20},{20... | collective-permute-start | bytes 6881288 | tf_op jit(solution)/shard_map/ppermute | solution.py:715
  323.1 23.1 %collective-permute-start.43 = (bf16[4,32,2176]{2,1,0:T(8,128)(2,1)S(1)}, bf16[4,32,2176]{2,1,0:T(8,128)(2,1)S(1)}, u32[]{:S(2)}, u32[]{:S(2)}) collective-permute-start(bf16[4,32,2176]{2,1,0:T(8,128)(2,1)S(1)} %get-tuple-element.311), channel_id=1, source_target_pairs={{0,4},{4,0},{8,12},{12,8},{1,5},{5,1},{9,13},{13,9},{2,6},{6,2},{1... | collective-permute-start | bytes 1671176 | tf_op jit(solution)/shard_map/ppermute | solution.py:720
  323.9 22.3 %collective-permute-start.44 = (bf16[4,32,2176]{2,1,0:T(8,128)(2,1)S(1)}, bf16[4,32,2176]{2,1,0:T(8,128)(2,1)S(1)}, u32[]{:S(2)}, u32[]{:S(2)}) collective-permute-start(bf16[4,32,2176]{2,1,0:T(8,128)(2,1)S(1)} %get-tuple-element.310), channel_id=1, source_target_pairs={{0,8},{4,12},{8,0},{12,4},{1,9},{5,13},{9,1},{13,5},{2,10},{6,14},... | collective-permute-start | bytes 1671176 | tf_op jit(solution)/shard_map/ppermute | solution.py:720
  348.9 19.2 %collective-permute-start.53 = (bf16[160,896]{1,0:T(8,128)(2,1)S(1)}, bf16[160,896]{1,0:T(8,128)(2,1)S(1)}, u32[]{:S(2)}, u32[]{:S(2)}) collective-permute-start(bf16[160,896]{1,0:T(8,128)(2,1)S(1)} %add_convert_fusion.5), channel_id=1, source_target_pairs={{0,4},{4,0},{8,12},{12,8},{1,5},{5,1},{9,13},{13,9},{2,6},{6,2},{1... | collective-permute-start | bytes 860168 | tf_op jit(solution)/shard_map/ppermute | solution.py:720
  349.8 18.3 %collective-permute-start.54 = (bf16[160,896]{1,0:T(8,128)(2,1)S(1)}, bf16[160,896]{1,0:T(8,128)(2,1)S(1)}, u32[]{:S(2)}, u32[]{:S(2)}) collective-permute-start(bf16[160,896]{1,0:T(8,128)(2,1)S(1)} %add_convert_fusion.5), channel_id=1, source_target_pairs={{0,8},{4,12},{8,0},{12,4},{1,9},{5,13},{9,1},{13,5},{2,10},{6,14},... | collective-permute-start | bytes 860168 | tf_op jit(solution)/shard_map/ppermute | solution.py:720
  351.2 16.9 %collective-permute-start.55 = (bf16[160,896]{1,0:T(8,128)(2,1)S(1)}, bf16[160,896]{1,0:T(8,128)(2,1)S(1)}, u32[]{:S(2)}, u32[]{:S(2)}) collective-permute-start(bf16[160,896]{1,0:T(8,128)(2,1)S(1)} %add_convert_fusion.5), channel_id=1, source_target_pairs={{0,12},{4,8},{8,4},{12,0},{1,13},{5,9},{9,5},{13,1},{2,14},{6,10},... | collective-permute-start | bytes 860168 | tf_op jit(solution)/shard_map/ppermute | solution.py:720
  (87 other events, 840.0 us)
Sparse Core Ops, SparseCore 0:
  69.3 74.4 all-gather.1
  230.9 47.4 reduce-scatter.1

commit v5 on v4

--- a/solution.py
+++ b/solution.py
@@ -604,8 +604,7 @@
     down_copies = []
     for i in range(2):
         for z in range(n_z):
-            at = jnp.bitwise_xor(lax.axis_index("fsdp"), z) * part_rows
-            to = down_buf.at[i, pl.ds(pl.multiple_of(at, 16), part_rows)]
+            to = down_buf.at[i, pl.ds(z * part_rows, part_rows)]
             sem = sems.at[2 + i * n_z + z]
             down_copies.append(pltpu.make_async_copy(weights[2 + i].at[z], to, sem))
     gu_copies[0].start()
@@ -821,11 +820,10 @@
     )
 
     og_parts = [hop(og_here, k) for k in range(tp)]
-    down_own = [hop_z(down_cut, k) for k in range(n_z)]
     kv_whole = jnp.stack(kv_blocks) if n_ctx == tp else kv_blocks
     attended, queries_ext = attend_forward(order_row, n_ctx == tp, queries, kv_whole)
-    attended, queries_ext, og_parts, down_own, gu_own = lax.optimization_barrier(
-        (attended, queries_ext, og_parts, down_own, gu_own)
+    attended, queries_ext, og_parts, down_cut, gu_own = lax.optimization_barrier(
+        (attended, queries_ext, og_parts, down_cut, gu_own)
     )
     w_out, resid, hidden_two = project_out(
         qo_own, qo_sib, attended, x_here, vecs, rows_here
@@ -833,7 +831,7 @@
     w_out = w_out.reshape(width, width)
     h2_parts = [hop(hidden_two, k) for k in range(tp)]
     gu_oth = swap(gu_own)
-    down_own = jnp.stack(down_own)
+    down_own = gather_z(down_cut).reshape(n_z, piece_pad, width)
     down_oth = swap(down_own)
 
     acts, ggus, h2_turned, og_all, dh2, ff_out = ff_pass(
@@ -869,9 +867,11 @@
         groups = [[g * tp + c for g in range(n_ctx // tp)] for c in range(tp)]
         return lax.psum(v, "ctx", axis_index_groups=groups)
 
+    if tp > 1:
+        grad_h2_parts[1], h2_turned, ggus = lax.optimization_barrier(
+            (grad_h2_parts[1], h2_turned, ggus)
+        )
     d_gu = grad_weight(h2_turned, ggus[0], swap(grad_weight(h2_turned, ggus[1])))
-    d_down = grad_weight(acts[0], og_all, swap(grad_weight(acts[1], og_all)))
-    d_down = d_down.reshape(n_z, piece_pad, width)
     grad_h2 = sum(v.astype(F32) for v in grad_h2_parts)
     scale_two = lax.rsqrt(jnp.mean(resid * resid, -1, keepdims=True) + NORM_EPS)
     normed_two = resid * scale_two
@@ -886,9 +886,10 @@
     grad_q_pre, grad_terms = attend_backward(
         order_row, n_ctx == tp, queries_ext, grad_att, attended, cos_wide, sin_wide, kv_whole
     )
-    grad_q_pre, grad_terms, ff_out, d_down, grad_proj = lax.optimization_barrier(
-        (grad_q_pre, grad_terms, ff_out, d_down, grad_proj)
-    )
+    grad_q_pre, grad_terms, ff_out, acts, grad_proj = lax.optimization_barrier(
+        (grad_q_pre, grad_terms, ff_out, acts, grad_proj)
+    )
+    d_down = grad_weight(acts[0], og_all, swap(grad_weight(acts[1], og_all)))
 
     qo_own, qo_oth = core_halves(
         jnp.concatenate(
@@ -911,9 +912,8 @@
     qo_sib = swap(qo_oth)
     result = resid + sum(v.astype(F32) for v in ff_out)
     layer_out = result.astype(BF16)[None]
-    kv_terms, qo_own, qo_sib, d_down = lax.optimization_barrier(
-        (kv_terms, qo_own, qo_sib, d_down)
-    )
+    d_down = scatter_z(d_down)
+    kv_terms, qo_own, qo_sib = lax.optimization_barrier((kv_terms, qo_own, qo_sib))
 
     tokens_grad, kv_part = kv_back(
         kv_terms,
@@ -931,28 +931,21 @@
     tokens_grad = tokens_grad[None]
     kv_own, kv_oth = core_halves(kv_part)
     last = core_total(qo_own, qo_sib)
-    kv_own, kv_sib, gu_pieces, d_down, last = lax.optimization_barrier(
-        (kv_own, swap(kv_oth), gu_pieces, d_down, last)
-    )
+    kv_own, kv_sib, last = lax.optimization_barrier((kv_own, swap(kv_oth), last))
 
     last = scatter_parts(jnp.concatenate([last, core_total(kv_own, kv_sib)], 2))
-    d_down = [
-        hop_z(lax.dynamic_index_in_dim(d_down, zed ^ k, 0, keepdims=False), k) for k in range(n_z)
-    ]
-    gu_pieces = jnp.stack(gu_pieces)
-    gu_sib = swap(gu_pieces)
-    last, d_down, gu_pieces, gu_sib = lax.optimization_barrier((last, d_down, gu_pieces, gu_sib))
+    last, d_down, gu_pieces = lax.optimization_barrier((last, d_down, gu_pieces))
 
     last = sum(v.astype(F32) for v in last).astype(BF16)
     last = [
         hop_z(lax.dynamic_index_in_dim(last, zed ^ k, 0, keepdims=False), k) for k in range(n_z)
     ]
-    d_down = ctx_groups_sum(sum(v.astype(F32) for v in d_down).astype(BF16))
-    d_down = lax.optimization_barrier(d_down)
+    d_down = ctx_groups_sum(d_down)
+    gu_pieces = jnp.stack(gu_pieces)
+    gu_sib = swap(gu_pieces)
     down_pieces = [hop(d_down, k) for k in range(tp)]
-    grad_w_gate, grad_w_up = spread_columns((gu_pieces, gu_sib), n_z, ff, 2)
-    last, down_pieces, grad_w_gate, grad_w_up = lax.optimization_barrier(
-        (last, down_pieces, grad_w_gate, grad_w_up)
+    last, down_pieces, gu_pieces, gu_sib = lax.optimization_barrier(
+        (last, down_pieces, gu_pieces, gu_sib)
     )
 
     last = ctx_groups_sum(sum(v.astype(F32) for v in last).astype(BF16))
@@ -960,7 +953,10 @@
     last = [hop(last, k) for k in range(tp)]
     down_pieces = jnp.stack(down_pieces)
     down_sib = swap(down_pieces)
-    last, down_pieces, down_sib = lax.optimization_barrier((last, down_pieces, down_sib))
+    grad_w_gate, grad_w_up = spread_columns((gu_pieces, gu_sib), n_z, ff, 2)
+    last, down_pieces, down_sib, grad_w_gate, grad_w_up = lax.optimization_barrier(
+        (last, down_pieces, down_sib, grad_w_gate, grad_w_up)
+    )
     last = jnp.stack(last)
     grad_w_down = spread_rows((down_pieces, down_sib), piece, ff_z)
     last = spread_rows((last, swap(last)), part_rows, rows_here)

time: 406 us -> 417 us (1.027)
  waiting for transfers between devices: 143 us -> 179 us
  Pallas kernels: 98.7 us -> 69.3 us
  starting transfers between devices: 81.3 us -> 86.3 us
    all_gather x1 -> x2, waiting for transfers between devices: 3.78 us -> 43.4 us  [gather_z(): return lax.all_gather(v, 'fsdp', axis=0, tiled=True)]
    ppermute x18 -> x12, waiting for transfers between devices: 63.9 us -> 32.8 us  [hop_z(): return lax.ppermute(v, 'fsdp', [(i, i ^ k) for i in range(n_z)])]
    ppermute x33, waiting for transfers between devices: 75.2 us -> 101 us  [hop(): return lax.ppermute(v, 'ctx', [(i, i ^ k) for i in range(n_ctx)])]
    pallas_call x1, Pallas kernels: 28.1 us -> 9.86 us  [attend_backward(): pl.pallas_call(functools.partial(backward_kernel, by_xor), grid_spec=pltp...]
    ppermute x18 -> x12, starting transfers between devices: 32 us -> 20.1 us  [hop_z(): return lax.ppermute(v, 'fsdp', [(i, i ^ k) for i in range(n_z)])]
    pallas_call x1, Pallas kernels: 17.1 us -> 6 us  [attend_forward(): pl.pallas_call(functools.partial(forward_kernel, by_xor), grid_spec=pltpu...]
    ppermute x10, starting transfers between devices: 20 us -> 30 us  [swap(): return lax.ppermute(v, 'seq', [(0, 1), (1, 0)])]
    ppermute x33, starting transfers between devices: 29.2 us -> 36 us  [hop(): return lax.ppermute(v, 'ctx', [(i, i ^ k) for i in range(n_ctx)])]
  transfers between devices with their start and end apart: 63 -> 59, of which waited for: 29 -> 30; matrix products, arithmetic and copies ran while one was open for 7% -> 6% of each run, Pallas kernels for 17% -> 10%
where the time goes in v5:
time: 417 us; the launch traced here: 412 us
  waiting for transfers between devices  179 us (43%)
  starting transfers between devices  86.3 us (21%)
  Pallas kernels  69.3 us (17%)
  local copies, waits for them, and re-layouts  41.7 us (10%)
  other arithmetic  17.5 us (4%)
  between operations  15.6 us (4%)
    ppermute x33, waiting for transfers between devices, hop(): return lax.ppermute(v, 'ctx', [(i, i ^ k) for i in range(n_ctx)])  101 us
    all_gather x2, waiting for transfers between devices, gather_z(): return lax.all_gather(v, 'fsdp', axis=0, tiled=True)  43.4 us
    ppermute x33, starting transfers between devices, hop(): return lax.ppermute(v, 'ctx', [(i, i ^ k) for i in range(n_ctx)])  36 us
    ppermute x12, waiting for transfers between devices, hop_z(): return lax.ppermute(v, 'fsdp', [(i, i ^ k) for i in range(n_z)])  32.8 us
    ppermute x10, starting transfers between devices, swap(): return lax.ppermute(v, 'seq', [(0, 1), (1, 0)])  30 us
    pallas_call x1, Pallas kernels, ff_pass(): pl.pallas_call(functools.partial(ff_kernel, tp, n_z), in_specs=[vmem] * (...  20.9 us
    ppermute x12, starting transfers between devices, hop_z(): return lax.ppermute(v, 'fsdp', [(i, i ^ k) for i in range(n_z)])  20.1 us
    unnamed x103, local copies, waits for them, and re-layouts  17.5 us
  transfers between devices with their start and end apart: 59, of which 30 were waited for; matrix products, arithmetic and copies ran while one was open for 6% of the time, Pallas kernels for 10%

profile of v5, /device:TPU:1, one launch (start us, length us, event | category | flops | bytes accessed | tf_op | source)
XLA Modules:
  0.0 412.3 jit_solution(12688054266888198945)
XLA Ops:
  26.0 7.8 %collective-permute-done.2 = bf16[464,256]{1,0:T(8,128)(2,1)} collective-permute-done((bf16[464,256]{1,0:T(8,128)(2,1)S(1)}, bf16[464,256]{1,0:T(8,128)(2,1)}, u32[]{:S(2)}, u32[]{:S(2)}) %collective-permute-start.2) | collective-permute-done | bytes 237600 | tf_op jit(solution)/shard_map/ppermute | solution.py:724
  43.5 5.3 %collective-permute-start.3 = (bf16[192,256]{1,0:T(8,128)(2,1)S(1)}, bf16[192,256]{1,0:T(8,128)(2,1)S(1)}, u32[]{:S(2)}, u32[]{:S(2)}) collective-permute-start(bf16[192,256]{1,0:T(8,128)(2,1)S(1)} %get-tuple-element.173), channel_id=1, source_target_pairs={{0,1},{1,0},{2,3},{3,2},{4,5},{5,4},{6,7},{7,6},{8,9},{9,8},{10,11... | collective-permute-start | bytes 294920 | tf_op jit(solution)/shard_map/ppermute | solution.py:724
  54.2 3.3 collective-permute-done.5
  60.1 3.9 collective-permute-start.9
  70.3 5.4 %collective-permute-done.10 = bf16[768,256]{1,0:T(8,128)(2,1)S(1)} collective-permute-done((bf16[768,256]{1,0:T(8,128)(2,1)S(1)}, bf16[768,256]{1,0:T(8,128)(2,1)S(1)}, u32[]{:S(2)}, u32[]{:S(2)}) %collective-permute-start.10) | collective-permute-done | bytes 393248 | tf_op jit(solution)/shard_map/ppermute | solution.py:719
  75.7 8.2 %collective-permute-done.11 = bf16[768,256]{1,0:T(8,128)(2,1)S(1)} collective-permute-done((bf16[768,256]{1,0:T(8,128)(2,1)S(1)}, bf16[768,256]{1,0:T(8,128)(2,1)S(1)}, u32[]{:S(2)}, u32[]{:S(2)}) %collective-permute-start.11) | collective-permute-done | bytes 393248 | tf_op jit(solution)/shard_map/ppermute | solution.py:719
  88.1 6.0 %attend_forward.1 = (bf16[192,896]{1,0:T(8,128)(2,1)S(1)}, bf16[2688,256]{1,0:T(8,128)(2,1)S(1)}) custom-call(s32[4]{0:T(128)S(1)} %bitcast.84, bf16[192,896]{1,0:T(8,128)(2,1)S(1)} %get-tuple-element.182.q_ref, bf16[4,768,256]{2,1,0:T(8,128)(2,1)S(1)} %pad_maximum_fusion.3.kv_ref), custom_call_target="tpu_custom_call" | custom-call | flops 30000001024 | bytes 8388608 | tf_op jit(solution)/shard_map/attend_forward/pallas_call | solution.py:239
  96.8 5.4 %collective-permute-done.15.refs_7_ = bf16[192,896]{1,0:T(8,128)(2,1)} collective-permute-done((bf16[192,896]{1,0:T(8,128)(2,1)S(1)}, bf16[192,896]{1,0:T(8,128)(2,1)}, u32[]{:S(2)}, u32[]{:S(2)}) %collective-permute-start.15) | collective-permute-done | bytes 344096 | tf_op jit(solution)/shard_map/ppermute | solution.py:719
  102.2 13.9 %all-gather.3.cloned.1.call-done.refs_8_ = bf16[896,1280]{1,0:T(8,128)(2,1)} async-done(((bf16[224,1280]{1,0:T(8,128)(2,1)}), bf16[896,1280]{1,0:T(8,128)(2,1)}) %all-gather.3.cloned.1.call-update) | async-done | bytes 2293776 | tf_op jit(solution)/shard_map/all_gather | solution.py:727
  117.0 29.5 %all-gather.5.cloned.1.call-done = bf16[640,896]{1,0:T(8,128)(2,1)} async-done(((bf16[160,896]{1,0:T(8,128)(2,1)}), bf16[640,896]{1,0:T(8,128)(2,1)}) %all-gather.5.cloned.1.call-update) | async-done | bytes 1146896 | tf_op jit(solution)/shard_map/all_gather | solution.py:727
  148.3 2.8 project_out.1
  154.9 7.0 %collective-permute-done.16.refs_1_ = bf16[192,896]{1,0:T(8,128)(2,1)S(1)} collective-permute-done((bf16[192,896]{1,0:T(8,128)(2,1)S(1)}, bf16[192,896]{1,0:T(8,128)(2,1)S(1)}, u32[]{:S(2)}, u32[]{:S(2)}) %collective-permute-start.16) | collective-permute-done | bytes 344096 | tf_op jit(solution)/shard_map/ppermute | solution.py:719
  162.0 7.1 %collective-permute-done.17.refs_2_ = bf16[192,896]{1,0:T(8,128)(2,1)S(1)} collective-permute-done((bf16[192,896]{1,0:T(8,128)(2,1)S(1)}, bf16[192,896]{1,0:T(8,128)(2,1)S(1)}, u32[]{:S(2)}, u32[]{:S(2)}) %collective-permute-start.17) | collective-permute-done | bytes 344096 | tf_op jit(solution)/shard_map/ppermute | solution.py:719
  172.1 20.9 %ff_pass.1 = (bf16[640,768]{1,0:T(8,128)(2,1)}, bf16[640,768]{1,0:T(8,128)(2,1)}, bf16[768,1280]{1,0:T(8,128)(2,1)}, bf16[768,1280]{1,0:T(8,128)(2,1)}, bf16[896...) custom-call(bf16[192,896]{1,0:T(8,128)(2,1)} %copy-done.25, ...), custom_call_target="tpu_custom_call" | custom-call | tf_op jit(solution)/shard_map/ff_pass/pallas_call | solution.py:665
  194.1 7.5 %collective-permute-done.21 = bf16[192,896]{1,0:T(8,128)(2,1)S(1)} collective-permute-done((bf16[192,896]{1,0:T(8,128)(2,1)}, bf16[192,896]{1,0:T(8,128)(2,1)S(1)}, u32[]{:S(2)}, u32[]{:S(2)}) %collective-permute-start.21) | collective-permute-done | bytes 344096 | tf_op jit(solution)/shard_map/ppermute | solution.py:719
  204.6 3.1 grad_weight.4
  212.3 14.8 %collective-permute-done.22 = bf16[192,896]{1,0:T(8,128)(2,1)S(1)} collective-permute-done((bf16[192,896]{1,0:T(8,128)(2,1)}, bf16[192,896]{1,0:T(8,128)(2,1)S(1)}, u32[]{:S(2)}, u32[]{:S(2)}) %collective-permute-start.22) | collective-permute-done | bytes 344096 | tf_op jit(solution)/shard_map/ppermute | solution.py:719
  230.5 3.4 grad_weight.5
  241.9 9.9 %attend_backward.1 = (bf16[192,896]{1,0:T(8,128)(2,1)S(1)}, bf16[4,768,256]{2,1,0:T(8,128)(2,1)S(1)}) custom-call(s32[4]{0:T(128)S(1)} %bitcast.85, bf16[2688,256]{1,0:T(8,128)(2,1)S(1)} %copy-done.29, bf16[192,896]{1,0:T(8,128)(2,1)S(1)} %copy-done.26, bf16[192,896]{1,0:T(8,128)(2,1)S(1)} %copy-done.18, f32[192,128]{1,0:T(8,128)S(1)} %copy.33.refs_5_.cos_ref.refs_4_, ...), custom_call_target="tpu_custom_call" | custom-call | flops 49999998976 | bytes 8388608 | tf_op jit(solution)/shard_map/attend_backward/pallas_call | solution.py:269
  254.2 12.9 %collective-permute-start.31 = (bf16[640,896]{1,0:T(8,128)(2,1)S(1)}, bf16[640,896]{1,0:T(8,128)(2,1)S(1)}, u32[]{:S(2)}, u32[]{:S(2)}) collective-permute-start(bf16[640,896]{1,0:T(8,128)(2,1)S(1)} %grad_weight.6), channel_id=1, source_target_pairs={{0,16},{16,0},{1,17},{17,1},{2,18},{18,2},{3,19},{19,3},{4,20},{20... | collective-permute-start | bytes 3440648 | tf_op jit(solution)/shard_map/ppermute | solution.py:714
  269.0 5.6 %collective-permute-start.28 = (bf16[768,256]{1,0:T(8,128)(2,1)}, bf16[768,256]{1,0:T(8,128)(2,1)}, u32[]{:S(2)}, u32[]{:S(2)}) collective-permute-start(bf16[768,256]{1,0:T(8,128)(2,1)} %get-tuple-element.321), channel_id=1, source_target_pairs={{0,4},{4,0},{8,12},{12,8},{1,5},{5,1},{9,13},{13,9},{2,6},{6,2},{1... | collective-permute-start | bytes 1179656 | tf_op jit(solution)/shard_map/ppermute | solution.py:719
  284.0 9.6 %collective-permute-done.29 = bf16[768,256]{1,0:T(8,128)(2,1)} collective-permute-done((bf16[768,256]{1,0:T(8,128)(2,1)}, bf16[768,256]{1,0:T(8,128)(2,1)}, u32[]{:S(2)}, u32[]{:S(2)}) %collective-permute-start.29) | collective-permute-done | bytes 393248 | tf_op jit(solution)/shard_map/ppermute | solution.py:719
  311.5 3.8 collective-permute-start.36
  321.4 7.2 %collective-permute-done.42 = bf16[224,1280]{1,0:T(8,128)(2,1)} collective-permute-done((bf16[224,1280]{1,0:T(8,128)(2,1)}, bf16[224,1280]{1,0:T(8,128)(2,1)}, u32[]{:S(2)}, u32[]{:S(2)}) %collective-permute-start.42) | collective-permute-done | bytes 573472 | tf_op jit(solution)/shard_map/ppermute | solution.py:719
  330.5 8.8 %collective-permute-done.37 = bf16[4,32,2176]{2,1,0:T(8,128)(2,1)S(1)} collective-permute-done((bf16[4,32,2176]{2,1,0:T(8,128)(2,1)}, bf16[4,32,2176]{2,1,0:T(8,128)(2,1)S(1)}, u32[]{:S(2)}, u32[]{:S(2)}) %collective-permute-start.37) | collective-permute-done | bytes 557088 | tf_op jit(solution)/shard_map/ppermute | solution.py:719
  339.3 4.2 %collective-permute-done.38 = bf16[4,32,2176]{2,1,0:T(8,128)(2,1)S(1)} collective-permute-done((bf16[4,32,2176]{2,1,0:T(8,128)(2,1)}, bf16[4,32,2176]{2,1,0:T(8,128)(2,1)S(1)}, u32[]{:S(2)}, u32[]{:S(2)}) %collective-permute-start.38) | collective-permute-done | bytes 557088 | tf_op jit(solution)/shard_map/ppermute | solution.py:719
  343.5 9.0 %collective-permute-done.39 = bf16[4,32,2176]{2,1,0:T(8,128)(2,1)} collective-permute-done((bf16[4,32,2176]{2,1,0:T(8,128)(2,1)}, bf16[4,32,2176]{2,1,0:T(8,128)(2,1)}, u32[]{:S(2)}, u32[]{:S(2)}) %collective-permute-start.39) | collective-permute-done | bytes 557088 | tf_op jit(solution)/shard_map/ppermute | solution.py:719
  352.6 3.1 pad_maximum_fusion.refs_0_
  365.6 7.8 %collective-permute-done.44 = bf16[32,2176]{1,0:T(8,128)(2,1)S(1)} collective-permute-done((bf16[32,2176]{1,0:T(8,128)(2,1)S(1)}, bf16[32,2176]{1,0:T(8,128)(2,1)S(1)}, u32[]{:S(2)}, u32[]{:S(2)}) %collective-permute-start.44) | collective-permute-done | bytes 139296 | tf_op jit(solution)/shard_map/ppermute | solution.py:724
  374.8 4.6 %collective-permute-done.45 = bf16[32,2176]{1,0:T(8,128)(2,1)S(1)} collective-permute-done((bf16[32,2176]{1,0:T(8,128)(2,1)S(1)}, bf16[32,2176]{1,0:T(8,128)(2,1)S(1)}, u32[]{:S(2)}, u32[]{:S(2)}) %collective-permute-start.45) | collective-permute-done | bytes 139296 | tf_op jit(solution)/shard_map/ppermute | solution.py:724
  384.3 9.1 %spread_columns.1 = (f32[224,4864]{1,0:T(8,128)}, f32[224,4864]{1,0:T(8,128)}) custom-call(bf16[4,224,1280]{2,1,0:T(8,128)(2,1)} %pad_maximum_fusion.refs_0_, bf16[4,224,1280]{2,1,0:T(8,128)(2,1)} %collective-permute-done.49.refs_1_), custom_call_target="tpu_custom_call" | custom-call | tf_op jit(solution)/shard_map/spread_columns/pallas_call | solution.py:332
  396.6 3.8 spread_rows.3
  (285 shorter events, 141.8 us)
Async XLA Ops:
  7.2 108.9 %all-gather.3.cloned.1.call-start = ((), (), s32[]{:S(2)}) async-start(), calls=%async_computation.2 | async-start | bytes 2867200 | tf_op jit(solution)/shard_map/all_gather | solution.py:727
  37.3 20.2 %collective-permute-start.6 = (bf16[4,64,896]{2,1,0:T(8,128)(2,1)S(1)}, bf16[4,64,896]{2,1,0:T(8,128)(2,1)S(1)}, u32[]{:S(2)}, u32[]{:S(2)}) collective-permute-start(bf16[4,64,896]{2,1,0:T(8,128)(2,1)S(1)} %constant_dynamic-update-slice_fusion.2), channel_id=1, source_target_pairs={{0,4},{4,0},{8,12},{12,8},{1,5},{5,1},{9,13},{13,9},{2,6},{6,2},{1... | collective-permute-start | bytes 1376264 | tf_op jit(solution)/shard_map/ppermute | solution.py:719
  38.6 18.9 %collective-permute-start.7 = (bf16[4,64,896]{2,1,0:T(8,128)(2,1)S(1)}, bf16[4,64,896]{2,1,0:T(8,128)(2,1)S(1)}, u32[]{:S(2)}, u32[]{:S(2)}) collective-permute-start(bf16[4,64,896]{2,1,0:T(8,128)(2,1)S(1)} %constant_dynamic-update-slice_fusion.2), channel_id=1, source_target_pairs={{0,8},{4,12},{8,0},{12,4},{1,9},{5,13},{9,1},{13,5},{2,10},{6,14},... | collective-permute-start | bytes 1376264 | tf_op jit(solution)/shard_map/ppermute | solution.py:719
  39.8 17.7 %collective-permute-start.8 = (bf16[4,64,896]{2,1,0:T(8,128)(2,1)S(1)}, bf16[4,64,896]{2,1,0:T(8,128)(2,1)}, u32[]{:S(2)}, u32[]{:S(2)}) collective-permute-start(bf16[4,64,896]{2,1,0:T(8,128)(2,1)S(1)} %constant_dynamic-update-slice_fusion.2), channel_id=1, source_target_pairs={{0,12},{4,8},{8,4},{12,0},{1,13},{5,9},{9,5},{13,1},{2,14},{6,10},... | collective-permute-start | bytes 1376264 | tf_op jit(solution)/shard_map/ppermute | solution.py:719
  64.0 82.5 %all-gather.5.cloned.1.call-start = ((), (), s32[]{:S(2)}) async-start(), calls=%async_computation.3 | async-start | bytes 1433600 | tf_op jit(solution)/shard_map/all_gather | solution.py:727
  66.2 17.7 %collective-permute-start.11 = (bf16[768,256]{1,0:T(8,128)(2,1)S(1)}, bf16[768,256]{1,0:T(8,128)(2,1)S(1)}, u32[]{:S(2)}, u32[]{:S(2)}) collective-permute-start(bf16[768,256]{1,0:T(8,128)(2,1)S(1)} %constant_dynamic-update-slice_fusion.6), channel_id=1, source_target_pairs={{0,8},{4,12},{8,0},{12,4},{1,9},{5,13},{9,1},{13,5},{2,10},{6,14},... | collective-permute-start | bytes 1179656 | tf_op jit(solution)/shard_map/ppermute | solution.py:719
  67.4 17.8 %collective-permute-start.12 = (bf16[768,256]{1,0:T(8,128)(2,1)S(1)}, bf16[768,256]{1,0:T(8,128)(2,1)S(1)}, u32[]{:S(2)}, u32[]{:S(2)}) collective-permute-start(bf16[768,256]{1,0:T(8,128)(2,1)S(1)} %constant_dynamic-update-slice_fusion.6), channel_id=1, source_target_pairs={{0,12},{4,8},{8,4},{12,0},{1,13},{5,9},{9,5},{13,1},{2,14},{6,10},... | collective-permute-start | bytes 1179656 | tf_op jit(solution)/shard_map/ppermute | solution.py:719
  86.7 15.5 %collective-permute-start.15 = (bf16[192,896]{1,0:T(8,128)(2,1)S(1)}, bf16[192,896]{1,0:T(8,128)(2,1)}, u32[]{:S(2)}, u32[]{:S(2)}) collective-permute-start(bf16[192,896]{1,0:T(8,128)(2,1)S(1)} %bitcast.92), channel_id=1, source_target_pairs={{0,12},{4,8},{8,4},{12,0},{1,13},{5,9},{9,5},{13,1},{2,14},{6,10},... | collective-permute-start | bytes 1032200 | tf_op jit(solution)/shard_map/ppermute | solution.py:719
  116.1 178.4 %reduce-scatter.3.cloned.1.call-start = ((), (), s32[]{:S(2)}) async-start(), calls=%async_computation.4 | async-start | bytes 2867200 | tf_op jit(solution)/shard_map/reduce_scatter | solution.py:730
  116.2 54.2 %collective-permute-start.19 = (bf16[896,1280]{1,0:T(8,128)(2,1)}, bf16[896,1280]{1,0:T(8,128)(2,1)}, u32[]{:S(2)}, u32[]{:S(2)}) collective-permute-start(bf16[896,1280]{1,0:T(8,128)(2,1)} %all-gather.3.cloned.1.call-done.refs_8_), channel_id=1, source_target_pairs={{0,16},{16,0},{1,17},{17,1},{2,18},{18,2},{3,19},{19,3},{4,20},{20... | collective-permute-start | bytes 6881288 | tf_op jit(solution)/shard_map/ppermute | solution.py:714
  146.5 23.9 %collective-permute-start.20 = (bf16[4,160,896]{2,1,0:T(8,128)(2,1)}, bf16[4,160,896]{2,1,0:T(8,128)(2,1)S(1)}, u32[]{:S(2)}, u32[]{:S(2)}) collective-permute-start(bf16[4,160,896]{2,1,0:T(8,128)(2,1)} %bitcast.94), channel_id=1, source_target_pairs={{0,16},{16,0},{1,17},{17,1},{2,18},{18,2},{3,19},{19,3},{4,20},{20... | collective-permute-start | bytes 3440648 | tf_op jit(solution)/shard_map/ppermute | solution.py:714
  153.5 15.6 %collective-permute-start.17 = (bf16[192,896]{1,0:T(8,128)(2,1)S(1)}, bf16[192,896]{1,0:T(8,128)(2,1)S(1)}, u32[]{:S(2)}, u32[]{:S(2)}) collective-permute-start(bf16[192,896]{1,0:T(8,128)(2,1)S(1)} %get-tuple-element.195.refs_0_), channel_id=1, source_target_pairs={{0,8},{4,12},{8,0},{12,4},{1,9},{5,13},{9,1},{13,5},{2,10},{6,14},... | collective-permute-start | bytes 1032200 | tf_op jit(solution)/shard_map/ppermute | solution.py:719
  154.7 15.7 %collective-permute-start.18 = (bf16[192,896]{1,0:T(8,128)(2,1)S(1)}, bf16[192,896]{1,0:T(8,128)(2,1)S(1)}, u32[]{:S(2)}, u32[]{:S(2)}) collective-permute-start(bf16[192,896]{1,0:T(8,128)(2,1)S(1)} %get-tuple-element.195.refs_0_), channel_id=1, source_target_pairs={{0,12},{4,8},{8,4},{12,0},{1,13},{5,9},{9,5},{13,1},{2,14},{6,10},... | collective-permute-start | bytes 1032200 | tf_op jit(solution)/shard_map/ppermute | solution.py:719
  207.7 22.8 %collective-permute-start.24 = (bf16[896,1280]{1,0:T(8,128)(2,1)}, bf16[896,1280]{1,0:T(8,128)(2,1)}, u32[]{:S(2)}, u32[]{:S(2)}) collective-permute-start(bf16[896,1280]{1,0:T(8,128)(2,1)} %grad_weight.4), channel_id=1, source_target_pairs={{0,16},{16,0},{1,17},{17,1},{2,18},{18,2},{3,19},{19,3},{4,20},{20... | collective-permute-start | bytes 6881288 | tf_op jit(solution)/shard_map/ppermute | solution.py:714
  209.8 17.3 %collective-permute-start.22 = (bf16[192,896]{1,0:T(8,128)(2,1)}, bf16[192,896]{1,0:T(8,128)(2,1)S(1)}, u32[]{:S(2)}, u32[]{:S(2)}) collective-permute-start(bf16[192,896]{1,0:T(8,128)(2,1)} %get-tuple-element.208), channel_id=1, source_target_pairs={{0,8},{4,12},{8,0},{12,4},{1,9},{5,13},{9,1},{13,5},{2,10},{6,14},... | collective-permute-start | bytes 1032200 | tf_op jit(solution)/shard_map/ppermute | solution.py:719
  211.0 16.1 %collective-permute-start.23 = (bf16[192,896]{1,0:T(8,128)(2,1)}, bf16[192,896]{1,0:T(8,128)(2,1)S(1)}, u32[]{:S(2)}, u32[]{:S(2)}) collective-permute-start(bf16[192,896]{1,0:T(8,128)(2,1)} %get-tuple-element.209), channel_id=1, source_target_pairs={{0,12},{4,8},{8,4},{12,0},{1,13},{5,9},{9,5},{13,1},{2,14},{6,10},... | collective-permute-start | bytes 1032200 | tf_op jit(solution)/shard_map/ppermute | solution.py:719
  235.4 16.5 %collective-permute-start.25 = (bf16[192,896]{1,0:T(8,128)(2,1)}, bf16[192,896]{1,0:T(8,128)(2,1)}, u32[]{:S(2)}, u32[]{:S(2)}) collective-permute-start(bf16[192,896]{1,0:T(8,128)(2,1)} %get-tuple-element.222), channel_id=1, source_target_pairs={{0,4},{4,0},{8,12},{12,8},{1,5},{5,1},{9,13},{13,9},{2,6},{6,2},{1... | collective-permute-start | bytes 1032200 | tf_op jit(solution)/shard_map/ppermute | solution.py:719
  236.8 16.0 %collective-permute-start.27 = (bf16[192,896]{1,0:T(8,128)(2,1)}, bf16[192,896]{1,0:T(8,128)(2,1)}, u32[]{:S(2)}, u32[]{:S(2)}) collective-permute-start(bf16[192,896]{1,0:T(8,128)(2,1)} %get-tuple-element.224), channel_id=1, source_target_pairs={{0,12},{4,8},{8,4},{12,0},{1,13},{5,9},{9,5},{13,1},{2,14},{6,10},... | collective-permute-start | bytes 1032200 | tf_op jit(solution)/shard_map/ppermute | solution.py:719
  238.0 92.5 %reduce-scatter.5.cloned.1.call-start = ((), (), s32[]{:S(2)}) async-start(), calls=%async_computation.5 | async-start | bytes 1433600 | tf_op jit(solution)/shard_map/reduce_scatter | solution.py:730
  254.2 25.4 %collective-permute-start.31 = (bf16[640,896]{1,0:T(8,128)(2,1)S(1)}, bf16[640,896]{1,0:T(8,128)(2,1)S(1)}, u32[]{:S(2)}, u32[]{:S(2)}) collective-permute-start(bf16[640,896]{1,0:T(8,128)(2,1)S(1)} %grad_weight.6), channel_id=1, source_target_pairs={{0,16},{16,0},{1,17},{17,1},{2,18},{18,2},{3,19},{19,3},{4,20},{20... | collective-permute-start | bytes 3440648 | tf_op jit(solution)/shard_map/ppermute | solution.py:714
  274.6 18.9 %collective-permute-start.29 = (bf16[768,256]{1,0:T(8,128)(2,1)}, bf16[768,256]{1,0:T(8,128)(2,1)}, u32[]{:S(2)}, u32[]{:S(2)}) collective-permute-start(bf16[768,256]{1,0:T(8,128)(2,1)} %get-tuple-element.320), channel_id=1, source_target_pairs={{0,8},{4,12},{8,0},{12,4},{1,9},{5,13},{9,1},{13,5},{2,10},{6,14},... | collective-permute-start | bytes 1179656 | tf_op jit(solution)/shard_map/ppermute | solution.py:719
  276.5 18.0 %collective-permute-start.30 = (bf16[768,256]{1,0:T(8,128)(2,1)}, bf16[768,256]{1,0:T(8,128)(2,1)}, u32[]{:S(2)}, u32[]{:S(2)}) collective-permute-start(bf16[768,256]{1,0:T(8,128)(2,1)} %get-tuple-element.319), channel_id=1, source_target_pairs={{0,12},{4,8},{8,4},{12,0},{1,13},{5,9},{9,5},{13,1},{2,14},{6,10},... | collective-permute-start | bytes 1179656 | tf_op jit(solution)/shard_map/ppermute | solution.py:719
  301.3 19.0 %collective-permute-start.40 = (bf16[224,1280]{1,0:T(8,128)(2,1)}, bf16[224,1280]{1,0:T(8,128)(2,1)}, u32[]{:S(2)}, u32[]{:S(2)}) collective-permute-start(bf16[224,1280]{1,0:T(8,128)(2,1)} %reduce-scatter.3.cloned.1.call-done), channel_id=1, source_target_pairs={{0,4},{4,0},{8,12},{12,8},{1,5},{5,1},{9,13},{13,9},{2,6},{6,2},{1... | collective-permute-start | bytes 1720328 | tf_op jit(solution)/shard_map/ppermute | solution.py:719
  302.5 18.9 %collective-permute-start.41 = (bf16[224,1280]{1,0:T(8,128)(2,1)}, bf16[224,1280]{1,0:T(8,128)(2,1)}, u32[]{:S(2)}, u32[]{:S(2)}) collective-permute-start(bf16[224,1280]{1,0:T(8,128)(2,1)} %reduce-scatter.3.cloned.1.call-done), channel_id=1, source_target_pairs={{0,8},{4,12},{8,0},{12,4},{1,9},{5,13},{9,1},{13,5},{2,10},{6,14},... | collective-permute-start | bytes 1720328 | tf_op jit(solution)/shard_map/ppermute | solution.py:719
  304.3 24.4 %collective-permute-start.42 = (bf16[224,1280]{1,0:T(8,128)(2,1)}, bf16[224,1280]{1,0:T(8,128)(2,1)}, u32[]{:S(2)}, u32[]{:S(2)}) collective-permute-start(bf16[224,1280]{1,0:T(8,128)(2,1)} %reduce-scatter.3.cloned.1.call-done), channel_id=1, source_target_pairs={{0,12},{4,8},{8,4},{12,0},{1,13},{5,9},{9,5},{13,1},{2,14},{6,10},... | collective-permute-start | bytes 1720328 | tf_op jit(solution)/shard_map/ppermute | solution.py:719
  318.8 20.6 %collective-permute-start.37 = (bf16[4,32,2176]{2,1,0:T(8,128)(2,1)}, bf16[4,32,2176]{2,1,0:T(8,128)(2,1)S(1)}, u32[]{:S(2)}, u32[]{:S(2)}) collective-permute-start(bf16[4,32,2176]{2,1,0:T(8,128)(2,1)} %get-tuple-element.305), channel_id=1, source_target_pairs={{0,4},{4,0},{8,12},{12,8},{1,5},{5,1},{9,13},{13,9},{2,6},{6,2},{1... | collective-permute-start | bytes 1671176 | tf_op jit(solution)/shard_map/ppermute | solution.py:719
  320.2 23.3 %collective-permute-start.38 = (bf16[4,32,2176]{2,1,0:T(8,128)(2,1)}, bf16[4,32,2176]{2,1,0:T(8,128)(2,1)S(1)}, u32[]{:S(2)}, u32[]{:S(2)}) collective-permute-start(bf16[4,32,2176]{2,1,0:T(8,128)(2,1)} %get-tuple-element.304), channel_id=1, source_target_pairs={{0,8},{4,12},{8,0},{12,4},{1,9},{5,13},{9,1},{13,5},{2,10},{6,14},... | collective-permute-start | bytes 1671176 | tf_op jit(solution)/shard_map/ppermute | solution.py:719
  320.3 32.3 %collective-permute-start.39 = (bf16[4,32,2176]{2,1,0:T(8,128)(2,1)}, bf16[4,32,2176]{2,1,0:T(8,128)(2,1)}, u32[]{:S(2)}, u32[]{:S(2)}) collective-permute-start(bf16[4,32,2176]{2,1,0:T(8,128)(2,1)} %get-tuple-element.303), channel_id=1, source_target_pairs={{0,12},{4,8},{8,4},{12,0},{1,13},{5,9},{9,5},{13,1},{2,14},{6,10},... | collective-permute-start | bytes 1671176 | tf_op jit(solution)/shard_map/ppermute | solution.py:719
  355.6 23.8 %collective-permute-start.49 = (bf16[4,224,1280]{2,1,0:T(8,128)(2,1)}, bf16[4,224,1280]{2,1,0:T(8,128)(2,1)}, u32[]{:S(2)}, u32[]{:S(2)}) collective-permute-start(bf16[4,224,1280]{2,1,0:T(8,128)(2,1)} %pad_maximum_fusion.refs_0_), channel_id=1, source_target_pairs={{0,16},{16,0},{1,17},{17,1},{2,18},{18,2},{3,19},{19,3},{4,20},{20... | collective-permute-start | bytes 6881288 | tf_op jit(solution)/shard_map/ppermute | solution.py:714
  359.7 19.7 %collective-permute-start.46 = (bf16[160,896]{1,0:T(8,128)(2,1)S(1)}, bf16[160,896]{1,0:T(8,128)(2,1)S(1)}, u32[]{:S(2)}, u32[]{:S(2)}) collective-permute-start(bf16[160,896]{1,0:T(8,128)(2,1)S(1)} %copy-done.46), channel_id=1, source_target_pairs={{0,4},{4,0},{8,12},{12,8},{1,5},{5,1},{9,13},{13,9},{2,6},{6,2},{1... | collective-permute-start | bytes 860168 | tf_op jit(solution)/shard_map/ppermute | solution.py:719
  360.9 18.5 %collective-permute-start.47 = (bf16[160,896]{1,0:T(8,128)(2,1)S(1)}, bf16[160,896]{1,0:T(8,128)(2,1)S(1)}, u32[]{:S(2)}, u32[]{:S(2)}) collective-permute-start(bf16[160,896]{1,0:T(8,128)(2,1)S(1)} %copy-done.46), channel_id=1, source_target_pairs={{0,8},{4,12},{8,0},{12,4},{1,9},{5,13},{9,1},{13,5},{2,10},{6,14},... | collective-permute-start | bytes 860168 | tf_op jit(solution)/shard_map/ppermute | solution.py:719
  361.2 18.2 %collective-permute-start.48 = (bf16[160,896]{1,0:T(8,128)(2,1)S(1)}, bf16[160,896]{1,0:T(8,128)(2,1)S(1)}, u32[]{:S(2)}, u32[]{:S(2)}) collective-permute-start(bf16[160,896]{1,0:T(8,128)(2,1)S(1)} %copy-done.46), channel_id=1, source_target_pairs={{0,12},{4,8},{8,4},{12,0},{1,13},{5,9},{9,5},{13,1},{2,14},{6,10},... | collective-permute-start | bytes 860168 | tf_op jit(solution)/shard_map/ppermute | solution.py:719
  (75 other events, 664.6 us)
Sparse Core Ops, SparseCore 0:
  64.1 51.9 all-gather.2
  118.2 28.1 all-gather.4
  238.1 46.3 reduce-scatter.2
  302.6 27.8 reduce-scatter.4

commit v6 on v5

--- a/solution.py
+++ b/solution.py
@@ -801,37 +801,37 @@
     gain_one = vecs[0:1, :width]
     gain_two = vecs[1:2, :width]
     kv_z = [hop_z(kv_local, k) for k in range(n_z)]
-    kv_z, qo_own, gu_cut, down_cut = lax.optimization_barrier((kv_z, qo_own, gu_cut, down_cut))
+    gu_own = gather_z(gu_cut)
+    kv_z, qo_own = lax.optimization_barrier((kv_z, qo_own))
 
     kv_block = jnp.concatenate(kv_z, 0)
     if n_ctx == tp:
         kv_blocks = [hop(kv_block, k) for k in range(n_ctx)]
     else:
         kv_blocks = lax.all_gather(kv_block, "ctx", axis=0, tiled=False)
-    gu_own = gather_z(gu_cut)
     qo_own = jnp.stack(qo_own)
     qo_sib = swap(qo_own)
     w_query, queries = project_query(
         qo_own, qo_sib, hidden_one, vecs, cos_wide, sin_wide, rows_here
     )
     w_query = w_query.reshape(width, width)
-    kv_blocks, queries, og_here, down_cut = lax.optimization_barrier(
-        (kv_blocks, queries, og_here, down_cut)
+    kv_blocks, queries, og_here, down_cut, gu_own = lax.optimization_barrier(
+        (kv_blocks, queries, og_here, down_cut, gu_own)
     )
 
     og_parts = [hop(og_here, k) for k in range(tp)]
     kv_whole = jnp.stack(kv_blocks) if n_ctx == tp else kv_blocks
     attended, queries_ext = attend_forward(order_row, n_ctx == tp, queries, kv_whole)
-    attended, queries_ext, og_parts, down_cut, gu_own = lax.optimization_barrier(
-        (attended, queries_ext, og_parts, down_cut, gu_own)
-    )
+    down_own = gather_z(down_cut)
+    attended, queries_ext, og_parts = lax.optimization_barrier((attended, queries_ext, og_parts))
     w_out, resid, hidden_two = project_out(
         qo_own, qo_sib, attended, x_here, vecs, rows_here
     )
     w_out = w_out.reshape(width, width)
     h2_parts = [hop(hidden_two, k) for k in range(tp)]
     gu_oth = swap(gu_own)
-    down_own = gather_z(down_cut).reshape(n_z, piece_pad, width)
+    h2_parts, down_own = lax.optimization_barrier((h2_parts, down_own))
+    down_own = down_own.reshape(n_z, piece_pad, width)
     down_oth = swap(down_own)
 
     acts, ggus, h2_turned, og_all, dh2, ff_out = ff_pass(
@@ -867,11 +867,8 @@
         groups = [[g * tp + c for g in range(n_ctx // tp)] for c in range(tp)]
         return lax.psum(v, "ctx", axis_index_groups=groups)
 
-    if tp > 1:
-        grad_h2_parts[1], h2_turned, ggus = lax.optimization_barrier(
-            (grad_h2_parts[1], h2_turned, ggus)
-        )
     d_gu = grad_weight(h2_turned, ggus[0], swap(grad_weight(h2_turned, ggus[1])))
+    grad_h2_parts, d_gu = lax.optimization_barrier((grad_h2_parts, d_gu))
     grad_h2 = sum(v.astype(F32) for v in grad_h2_parts)
     scale_two = lax.rsqrt(jnp.mean(resid * resid, -1, keepdims=True) + NORM_EPS)
     normed_two = resid * scale_two
@@ -943,14 +940,14 @@
     d_down = ctx_groups_sum(d_down)
     gu_pieces = jnp.stack(gu_pieces)
     gu_sib = swap(gu_pieces)
-    down_pieces = [hop(d_down, k) for k in range(tp)]
-    last, down_pieces, gu_pieces, gu_sib = lax.optimization_barrier(
-        (last, down_pieces, gu_pieces, gu_sib)
+    last, d_down, gu_pieces, gu_sib = lax.optimization_barrier(
+        (last, d_down, gu_pieces, gu_sib)
     )
 
     last = ctx_groups_sum(sum(v.astype(F32) for v in last).astype(BF16))
     last = lax.optimization_barrier(last)
     last = [hop(last, k) for k in range(tp)]
+    down_pieces = [hop(d_down, k) for k in range(tp)]
     down_pieces = jnp.stack(down_pieces)
     down_sib = swap(down_pieces)
     grad_w_gate, grad_w_up = spread_columns((gu_pieces, gu_sib), n_z, ff, 2)

time: 417 us -> 387 us (0.928)
  waiting for transfers between devices: 179 us -> 137 us
  Pallas kernels: 69.3 us -> 85.7 us
  starting transfers between devices: 86.3 us -> 78.6 us
    all_gather x2, waiting for transfers between devices: 43.4 us -> 5.17 us  [gather_z(): return lax.all_gather(v, 'fsdp', axis=0, tiled=True)]
    ppermute x10, starting transfers between devices: 30 us -> 15.5 us  [swap(): return lax.ppermute(v, 'seq', [(0, 1), (1, 0)])]
    ppermute x33, waiting for transfers between devices: 101 us -> 88.2 us  [hop(): return lax.ppermute(v, 'ctx', [(i, i ^ k) for i in range(n_ctx)])]
    pallas_call x1, Pallas kernels: 9.86 us -> 22.1 us  [attend_backward(): pl.pallas_call(functools.partial(backward_kernel, by_xor), grid_spec=pltp...]
    pallas_call x1, Pallas kernels: 6 us -> 13.4 us  [attend_forward(): pl.pallas_call(functools.partial(forward_kernel, by_xor), grid_spec=pltpu...]
    ppermute x33, starting transfers between devices: 36 us -> 41.1 us  [hop(): return lax.ppermute(v, 'ctx', [(i, i ^ k) for i in range(n_ctx)])]
    ppermute x10, waiting for transfers between devices: 0.03 us -> 4.83 us  [swap(): return lax.ppermute(v, 'seq', [(0, 1), (1, 0)])]
    unnamed x103 -> x105, local copies, waits for them, and re-layouts: 17.5 us -> 16.5 us
  transfers between devices with their start and end apart: 59 -> 59, of which waited for: 30 -> 28; matrix products, arithmetic and copies ran while one was open for 6% -> 8% of each run, Pallas kernels for 10% -> 16%
where the time goes in v6:
time: 387 us; the launch traced here: 381 us
  waiting for transfers between devices  137 us (35%)
  Pallas kernels  85.7 us (22%)
  starting transfers between devices  78.6 us (20%)
  local copies, waits for them, and re-layouts  39.8 us (10%)
  other arithmetic  21.3 us (6%)
  between operations  15.6 us (4%)
    ppermute x33, waiting for transfers between devices, hop(): return lax.ppermute(v, 'ctx', [(i, i ^ k) for i in range(n_ctx)])  88.2 us
    ppermute x33, starting transfers between devices, hop(): return lax.ppermute(v, 'ctx', [(i, i ^ k) for i in range(n_ctx)])  41.1 us
    ppermute x12, waiting for transfers between devices, hop_z(): return lax.ppermute(v, 'fsdp', [(i, i ^ k) for i in range(n_z)])  36.8 us
    pallas_call x1, Pallas kernels, attend_backward(): pl.pallas_call(functools.partial(backward_kernel, by_xor), grid_spec=pltp...  22.1 us
    ppermute x12, starting transfers between devices, hop_z(): return lax.ppermute(v, 'fsdp', [(i, i ^ k) for i in range(n_z)])  21.8 us
    pallas_call x1, Pallas kernels, ff_pass(): pl.pallas_call(functools.partial(ff_kernel, tp, n_z), in_specs=[vmem] * (...  20.9 us
    unnamed x105, local copies, waits for them, and re-layouts  16.5 us
    ppermute x10, starting transfers between devices, swap(): return lax.ppermute(v, 'seq', [(0, 1), (1, 0)])  15.5 us
  transfers between devices with their start and end apart: 59, of which 28 were waited for; matrix products, arithmetic and copies ran while one was open for 8% of the time, Pallas kernels for 16%

profile of v6, /device:TPU:1, one launch (start us, length us, event | category | flops | bytes accessed | tf_op | source)
XLA Modules:
  0.0 380.8 jit_solution(53082810161528557)
XLA Ops:
  26.0 7.8 %collective-permute-done.2 = bf16[464,256]{1,0:T(8,128)(2,1)} collective-permute-done((bf16[464,256]{1,0:T(8,128)(2,1)S(1)}, bf16[464,256]{1,0:T(8,128)(2,1)}, u32[]{:S(2)}, u32[]{:S(2)}) %collective-permute-start.2) | collective-permute-done | bytes 237600 | tf_op jit(solution)/shard_map/ppermute | solution.py:724
  43.5 5.3 %collective-permute-start.3 = (bf16[192,256]{1,0:T(8,128)(2,1)S(1)}, bf16[192,256]{1,0:T(8,128)(2,1)S(1)}, u32[]{:S(2)}, u32[]{:S(2)}) collective-permute-start(bf16[192,256]{1,0:T(8,128)(2,1)S(1)} %get-tuple-element.171), channel_id=1, source_target_pairs={{0,1},{1,0},{2,3},{3,2},{4,5},{5,4},{6,7},{7,6},{8,9},{9,8},{10,11... | collective-permute-start | bytes 294920 | tf_op jit(solution)/shard_map/ppermute | solution.py:724
  50.0 7.3 %collective-permute-done.3 = bf16[192,256]{1,0:T(8,128)(2,1)S(1)} collective-permute-done((bf16[192,256]{1,0:T(8,128)(2,1)S(1)}, bf16[192,256]{1,0:T(8,128)(2,1)S(1)}, u32[]{:S(2)}, u32[]{:S(2)}) %collective-permute-start.3) | collective-permute-done | bytes 98336 | tf_op jit(solution)/shard_map/ppermute | solution.py:724
  60.3 5.0 %collective-permute-done.5 = bf16[192,256]{1,0:T(8,128)(2,1)S(1)} collective-permute-done((bf16[192,256]{1,0:T(8,128)(2,1)S(1)}, bf16[192,256]{1,0:T(8,128)(2,1)S(1)}, u32[]{:S(2)}, u32[]{:S(2)}) %collective-permute-start.5) | collective-permute-done | bytes 98336 | tf_op jit(solution)/shard_map/ppermute | solution.py:724
  67.8 3.5 collective-permute-start.9
  77.2 5.2 %collective-permute-done.10 = bf16[768,256]{1,0:T(8,128)(2,1)S(1)} collective-permute-done((bf16[768,256]{1,0:T(8,128)(2,1)S(1)}, bf16[768,256]{1,0:T(8,128)(2,1)S(1)}, u32[]{:S(2)}, u32[]{:S(2)}) %collective-permute-start.10) | collective-permute-done | bytes 393248 | tf_op jit(solution)/shard_map/ppermute | solution.py:719
  82.3 8.1 %collective-permute-done.11 = bf16[768,256]{1,0:T(8,128)(2,1)S(1)} collective-permute-done((bf16[768,256]{1,0:T(8,128)(2,1)S(1)}, bf16[768,256]{1,0:T(8,128)(2,1)S(1)}, u32[]{:S(2)}, u32[]{:S(2)}) %collective-permute-start.11) | collective-permute-done | bytes 393248 | tf_op jit(solution)/shard_map/ppermute | solution.py:719
  91.7 5.2 %all-gather.3.cloned.1.call-done.refs_8_ = bf16[896,1280]{1,0:T(8,128)(2,1)} async-done(((bf16[224,1280]{1,0:T(8,128)(2,1)}), bf16[896,1280]{1,0:T(8,128)(2,1)}) %all-gather.3.cloned.1.call-update) | async-done | bytes 2293776 | tf_op jit(solution)/shard_map/all_gather | solution.py:727
  103.0 13.4 %attend_forward.1 = (bf16[192,896]{1,0:T(8,128)(2,1)S(1)}, bf16[2688,256]{1,0:T(8,128)(2,1)S(1)}) custom-call(s32[4]{0:T(128)S(1)} %bitcast.84, bf16[192,896]{1,0:T(8,128)(2,1)S(1)} %get-tuple-element.181.q_ref, bf16[4,768,256]{2,1,0:T(8,128)(2,1)S(1)} %pad_maximum_fusion.3.kv_ref), custom_call_target="tpu_custom_call" | custom-call | flops 30000001024 | bytes 8388608 | tf_op jit(solution)/shard_map/attend_forward/pallas_call | solution.py:239
  118.9 4.9 %collective-permute-start.17 = (bf16[192,896]{1,0:T(8,128)(2,1)S(1)}, bf16[192,896]{1,0:T(8,128)(2,1)S(1)}, u32[]{:S(2)}, u32[]{:S(2)}) collective-permute-start(bf16[192,896]{1,0:T(8,128)(2,1)S(1)} %get-tuple-element.194.refs_0_), channel_id=1, source_target_pairs={{0,8},{4,12},{8,0},{12,4},{1,9},{5,13},{9,1},{13,5},{2,10},{6,14},... | collective-permute-start | bytes 1032200 | tf_op jit(solution)/shard_map/ppermute | solution.py:719
  125.0 4.1 %collective-permute-done.16.refs_1_ = bf16[192,896]{1,0:T(8,128)(2,1)S(1)} collective-permute-done((bf16[192,896]{1,0:T(8,128)(2,1)S(1)}, bf16[192,896]{1,0:T(8,128)(2,1)S(1)}, u32[]{:S(2)}, u32[]{:S(2)}) %collective-permute-start.16) | collective-permute-done | bytes 344096 | tf_op jit(solution)/shard_map/ppermute | solution.py:719
  129.1 9.6 %collective-permute-done.17.refs_2_ = bf16[192,896]{1,0:T(8,128)(2,1)S(1)} collective-permute-done((bf16[192,896]{1,0:T(8,128)(2,1)S(1)}, bf16[192,896]{1,0:T(8,128)(2,1)S(1)}, u32[]{:S(2)}, u32[]{:S(2)}) %collective-permute-start.17) | collective-permute-done | bytes 344096 | tf_op jit(solution)/shard_map/ppermute | solution.py:719
  145.1 20.9 %ff_pass.1 = (bf16[640,768]{1,0:T(8,128)(2,1)}, bf16[640,768]{1,0:T(8,128)(2,1)}, bf16[768,1280]{1,0:T(8,128)(2,1)}, bf16[768,1280]{1,0:T(8,128)(2,1)}, bf16[896...) custom-call(bf16[192,896]{1,0:T(8,128)(2,1)} %copy-done.26, ...), custom_call_target="tpu_custom_call" | custom-call | tf_op jit(solution)/shard_map/ff_pass/pallas_call | solution.py:665
  168.8 3.1 grad_weight.4
  178.3 3.5 grad_weight.5
  183.2 6.6 %collective-permute-done.23 = bf16[192,896]{1,0:T(8,128)(2,1)} collective-permute-done((bf16[192,896]{1,0:T(8,128)(2,1)}, bf16[192,896]{1,0:T(8,128)(2,1)}, u32[]{:S(2)}, u32[]{:S(2)}) %collective-permute-start.23) | collective-permute-done | bytes 344096 | tf_op jit(solution)/shard_map/ppermute | solution.py:719
  201.8 22.1 %attend_backward.1 = (bf16[192,896]{1,0:T(8,128)(2,1)S(1)}, bf16[4,768,256]{2,1,0:T(8,128)(2,1)S(1)}) custom-call(s32[4]{0:T(128)S(1)} %bitcast.85, bf16[2688,256]{1,0:T(8,128)(2,1)S(1)} %copy-done.30, bf16[192,896]{1,0:T(8,128)(2,1)S(1)} %copy-done.27, bf16[192,896]{1,0:T(8,128)(2,1)S(1)} %copy-done.19, f32[192,128]{1,0:T(8,128)S(1)} %copy.33.refs_5_.cos_ref.refs_4_, ...), custom_call_target="tpu_custom_call" | custom-call | flops 49999998976 | bytes 8388608 | tf_op jit(solution)/shard_map/attend_backward/pallas_call | solution.py:269
  227.3 3.2 collective-permute-start.28
  230.5 6.4 %collective-permute-start.29 = (bf16[768,256]{1,0:T(8,128)(2,1)}, bf16[768,256]{1,0:T(8,128)(2,1)}, u32[]{:S(2)}, u32[]{:S(2)}) collective-permute-start(bf16[768,256]{1,0:T(8,128)(2,1)} %get-tuple-element.320), channel_id=1, source_target_pairs={{0,8},{4,12},{8,0},{12,4},{1,9},{5,13},{9,1},{13,5},{2,10},{6,14},... | collective-permute-start | bytes 1179656 | tf_op jit(solution)/shard_map/ppermute | solution.py:719
  243.3 10.8 %collective-permute-done.29 = bf16[768,256]{1,0:T(8,128)(2,1)} collective-permute-done((bf16[768,256]{1,0:T(8,128)(2,1)}, bf16[768,256]{1,0:T(8,128)(2,1)}, u32[]{:S(2)}, u32[]{:S(2)}) %collective-permute-start.29) | collective-permute-done | bytes 393248 | tf_op jit(solution)/shard_map/ppermute | solution.py:719
  267.6 3.1 collective-permute-done.34.refs_3_
  274.2 3.4 collective-permute-start.36
  283.8 6.0 %collective-permute-done.42 = bf16[224,1280]{1,0:T(8,128)(2,1)} collective-permute-done((bf16[224,1280]{1,0:T(8,128)(2,1)}, bf16[224,1280]{1,0:T(8,128)(2,1)}, u32[]{:S(2)}, u32[]{:S(2)}) %collective-permute-start.42) | collective-permute-done | bytes 573472 | tf_op jit(solution)/shard_map/ppermute | solution.py:719
  291.8 9.8 %collective-permute-done.37 = bf16[4,32,2176]{2,1,0:T(8,128)(2,1)S(1)} collective-permute-done((bf16[4,32,2176]{2,1,0:T(8,128)(2,1)}, bf16[4,32,2176]{2,1,0:T(8,128)(2,1)S(1)}, u32[]{:S(2)}, u32[]{:S(2)}) %collective-permute-start.37) | collective-permute-done | bytes 557088 | tf_op jit(solution)/shard_map/ppermute | solution.py:719
  301.6 13.2 %collective-permute-done.38 = bf16[4,32,2176]{2,1,0:T(8,128)(2,1)S(1)} collective-permute-done((bf16[4,32,2176]{2,1,0:T(8,128)(2,1)}, bf16[4,32,2176]{2,1,0:T(8,128)(2,1)S(1)}, u32[]{:S(2)}, u32[]{:S(2)}) %collective-permute-start.38) | collective-permute-done | bytes 557088 | tf_op jit(solution)/shard_map/ppermute | solution.py:719
  314.9 3.1 pad_maximum_fusion.refs_0_
  324.2 4.1 %collective-permute-done.43 = bf16[32,2176]{1,0:T(8,128)(2,1)S(1)} collective-permute-done((bf16[32,2176]{1,0:T(8,128)(2,1)S(1)}, bf16[32,2176]{1,0:T(8,128)(2,1)S(1)}, u32[]{:S(2)}, u32[]{:S(2)}) %collective-permute-start.43) | collective-permute-done | bytes 139296 | tf_op jit(solution)/shard_map/ppermute | solution.py:724
  328.3 5.8 %collective-permute-done.45 = bf16[32,2176]{1,0:T(8,128)(2,1)S(1)} collective-permute-done((bf16[32,2176]{1,0:T(8,128)(2,1)S(1)}, bf16[32,2176]{1,0:T(8,128)(2,1)S(1)}, u32[]{:S(2)}, u32[]{:S(2)}) %collective-permute-start.45) | collective-permute-done | bytes 139296 | tf_op jit(solution)/shard_map/ppermute | solution.py:724
  336.7 4.1 %collective-permute-done.50 = bf16[160,896]{1,0:T(8,128)(2,1)S(1)} collective-permute-done((bf16[160,896]{1,0:T(8,128)(2,1)S(1)}, bf16[160,896]{1,0:T(8,128)(2,1)S(1)}, u32[]{:S(2)}, u32[]{:S(2)}) %collective-permute-start.50) | collective-permute-done | bytes 286752 | tf_op jit(solution)/shard_map/ppermute | solution.py:719
  340.8 6.2 %collective-permute-done.52 = bf16[160,896]{1,0:T(8,128)(2,1)S(1)} collective-permute-done((bf16[160,896]{1,0:T(8,128)(2,1)S(1)}, bf16[160,896]{1,0:T(8,128)(2,1)S(1)}, u32[]{:S(2)}, u32[]{:S(2)}) %collective-permute-start.52) | collective-permute-done | bytes 286752 | tf_op jit(solution)/shard_map/ppermute | solution.py:719
  352.8 9.1 %spread_columns.1 = (f32[224,4864]{1,0:T(8,128)}, f32[224,4864]{1,0:T(8,128)}) custom-call(bf16[4,224,1280]{2,1,0:T(8,128)(2,1)} %pad_maximum_fusion.refs_0_, bf16[4,224,1280]{2,1,0:T(8,128)(2,1)} %collective-permute-done.46.refs_1_), custom_call_target="tpu_custom_call" | custom-call | tf_op jit(solution)/shard_map/spread_columns/pallas_call | solution.py:332
  365.1 3.8 %spread_rows.3 = f32[1216,896]{1,0:T(8,128)} custom-call(bf16[4,160,896]{2,1,0:T(8,128)(2,1)S(1)} %pad_maximum_fusion.4.refs_0_, bf16[4,160,896]{2,1,0:T(8,128)(2,1)S(1)} %collective-permute-done.53.refs_1_), custom_call_target="tpu_custom_call" | custom-call | tf_op jit(solution)/shard_map/spread_rows/pallas_call | solution.py:364
  (287 shorter events, 137.6 us)
Async XLA Ops:
  7.2 89.7 %all-gather.3.cloned.1.call-start = ((), (), s32[]{:S(2)}) async-start(), calls=%async_computation.2 | async-start | bytes 2867200 | tf_op jit(solution)/shard_map/all_gather | solution.py:727
  18.4 15.4 %collective-permute-start.2 = (bf16[464,256]{1,0:T(8,128)(2,1)S(1)}, bf16[464,256]{1,0:T(8,128)(2,1)}, u32[]{:S(2)}, u32[]{:S(2)}) collective-permute-start(bf16[464,256]{1,0:T(8,128)(2,1)S(1)} %constant_dynamic-update-slice_fusion), channel_id=1, source_target_pairs={{0,3},{1,2},{2,1},{3,0},{4,7},{5,6},{6,5},{7,4},{8,11},{9,10},{10,... | collective-permute-start | bytes 712712 | tf_op jit(solution)/shard_map/ppermute | solution.py:724
  33.8 106.8 %all-gather.5.cloned.1.call-start = ((), (), s32[]{:S(2)}) async-start(), calls=%async_computation.3 | async-start | bytes 1433600 | tf_op jit(solution)/shard_map/all_gather | solution.py:727
  37.4 27.9 %collective-permute-start.6 = (bf16[4,64,896]{2,1,0:T(8,128)(2,1)S(1)}, bf16[4,64,896]{2,1,0:T(8,128)(2,1)S(1)}, u32[]{:S(2)}, u32[]{:S(2)}) collective-permute-start(bf16[4,64,896]{2,1,0:T(8,128)(2,1)S(1)} %constant_dynamic-update-slice_fusion.2), channel_id=1, source_target_pairs={{0,4},{4,0},{8,12},{12,8},{1,5},{5,1},{9,13},{13,9},{2,6},{6,2},{1... | collective-permute-start | bytes 1376264 | tf_op jit(solution)/shard_map/ppermute | solution.py:719
  38.7 26.6 %collective-permute-start.7 = (bf16[4,64,896]{2,1,0:T(8,128)(2,1)S(1)}, bf16[4,64,896]{2,1,0:T(8,128)(2,1)S(1)}, u32[]{:S(2)}, u32[]{:S(2)}) collective-permute-start(bf16[4,64,896]{2,1,0:T(8,128)(2,1)S(1)} %constant_dynamic-update-slice_fusion.2), channel_id=1, source_target_pairs={{0,8},{4,12},{8,0},{12,4},{1,9},{5,13},{9,1},{13,5},{2,10},{6,14},... | collective-permute-start | bytes 1376264 | tf_op jit(solution)/shard_map/ppermute | solution.py:719
  39.9 25.4 %collective-permute-start.8 = (bf16[4,64,896]{2,1,0:T(8,128)(2,1)S(1)}, bf16[4,64,896]{2,1,0:T(8,128)(2,1)}, u32[]{:S(2)}, u32[]{:S(2)}) collective-permute-start(bf16[4,64,896]{2,1,0:T(8,128)(2,1)S(1)} %constant_dynamic-update-slice_fusion.2), channel_id=1, source_target_pairs={{0,12},{4,8},{8,4},{12,0},{1,13},{5,9},{9,5},{13,1},{2,14},{6,10},... | collective-permute-start | bytes 1376264 | tf_op jit(solution)/shard_map/ppermute | solution.py:719
  72.7 17.7 %collective-permute-start.11 = (bf16[768,256]{1,0:T(8,128)(2,1)S(1)}, bf16[768,256]{1,0:T(8,128)(2,1)S(1)}, u32[]{:S(2)}, u32[]{:S(2)}) collective-permute-start(bf16[768,256]{1,0:T(8,128)(2,1)S(1)} %constant_dynamic-update-slice_fusion.6), channel_id=1, source_target_pairs={{0,8},{4,12},{8,0},{12,4},{1,9},{5,13},{9,1},{13,5},{2,10},{6,14},... | collective-permute-start | bytes 1179656 | tf_op jit(solution)/shard_map/ppermute | solution.py:719
  73.9 17.8 %collective-permute-start.12 = (bf16[768,256]{1,0:T(8,128)(2,1)S(1)}, bf16[768,256]{1,0:T(8,128)(2,1)}, u32[]{:S(2)}, u32[]{:S(2)}) collective-permute-start(bf16[768,256]{1,0:T(8,128)(2,1)S(1)} %constant_dynamic-update-slice_fusion.6), channel_id=1, source_target_pairs={{0,12},{4,8},{8,4},{12,0},{1,13},{5,9},{9,5},{13,1},{2,14},{6,10},... | collective-permute-start | bytes 1179656 | tf_op jit(solution)/shard_map/ppermute | solution.py:719
  96.9 19.5 %collective-permute-start.13 = (bf16[192,896]{1,0:T(8,128)(2,1)S(1)}, bf16[192,896]{1,0:T(8,128)(2,1)}, u32[]{:S(2)}, u32[]{:S(2)}) collective-permute-start(bf16[192,896]{1,0:T(8,128)(2,1)S(1)} %bitcast.90), channel_id=1, source_target_pairs={{0,4},{4,0},{8,12},{12,8},{1,5},{5,1},{9,13},{13,9},{2,6},{6,2},{1... | collective-permute-start | bytes 1032200 | tf_op jit(solution)/shard_map/ppermute | solution.py:719
  98.1 18.3 %collective-permute-start.14 = (bf16[192,896]{1,0:T(8,128)(2,1)S(1)}, bf16[192,896]{1,0:T(8,128)(2,1)}, u32[]{:S(2)}, u32[]{:S(2)}) collective-permute-start(bf16[192,896]{1,0:T(8,128)(2,1)S(1)} %bitcast.91), channel_id=1, source_target_pairs={{0,8},{4,12},{8,0},{12,4},{1,9},{5,13},{9,1},{13,5},{2,10},{6,14},... | collective-permute-start | bytes 1032200 | tf_op jit(solution)/shard_map/ppermute | solution.py:719
  99.3 17.2 %collective-permute-start.15 = (bf16[192,896]{1,0:T(8,128)(2,1)S(1)}, bf16[192,896]{1,0:T(8,128)(2,1)}, u32[]{:S(2)}, u32[]{:S(2)}) collective-permute-start(bf16[192,896]{1,0:T(8,128)(2,1)S(1)} %bitcast.92), channel_id=1, source_target_pairs={{0,12},{4,8},{8,4},{12,0},{1,13},{5,9},{9,5},{13,1},{2,14},{6,10},... | collective-permute-start | bytes 1032200 | tf_op jit(solution)/shard_map/ppermute | solution.py:719
  99.6 156.5 %reduce-scatter.3.cloned.1.call-start = ((), (), s32[]{:S(2)}) async-start(), calls=%async_computation.4 | async-start | bytes 2867200 | tf_op jit(solution)/shard_map/reduce_scatter | solution.py:730
  99.8 41.6 %collective-permute-start.19 = (bf16[896,1280]{1,0:T(8,128)(2,1)}, bf16[896,1280]{1,0:T(8,128)(2,1)}, u32[]{:S(2)}, u32[]{:S(2)}) collective-permute-start(bf16[896,1280]{1,0:T(8,128)(2,1)} %all-gather.3.cloned.1.call-done.refs_8_), channel_id=1, source_target_pairs={{0,16},{16,0},{1,17},{17,1},{2,18},{18,2},{3,19},{19,3},{4,20},{20... | collective-permute-start | bytes 6881288 | tf_op jit(solution)/shard_map/ppermute | solution.py:714
  118.9 19.7 %collective-permute-start.17 = (bf16[192,896]{1,0:T(8,128)(2,1)S(1)}, bf16[192,896]{1,0:T(8,128)(2,1)S(1)}, u32[]{:S(2)}, u32[]{:S(2)}) collective-permute-start(bf16[192,896]{1,0:T(8,128)(2,1)S(1)} %get-tuple-element.194.refs_0_), channel_id=1, source_target_pairs={{0,8},{4,12},{8,0},{12,4},{1,9},{5,13},{9,1},{13,5},{2,10},{6,14},... | collective-permute-start | bytes 1032200 | tf_op jit(solution)/shard_map/ppermute | solution.py:719
  123.8 16.8 %collective-permute-start.18 = (bf16[192,896]{1,0:T(8,128)(2,1)S(1)}, bf16[192,896]{1,0:T(8,128)(2,1)S(1)}, u32[]{:S(2)}, u32[]{:S(2)}) collective-permute-start(bf16[192,896]{1,0:T(8,128)(2,1)S(1)} %get-tuple-element.194.refs_0_), channel_id=1, source_target_pairs={{0,12},{4,8},{8,4},{12,0},{1,13},{5,9},{9,5},{13,1},{2,14},{6,10},... | collective-permute-start | bytes 1032200 | tf_op jit(solution)/shard_map/ppermute | solution.py:719
  174.2 15.5 %collective-permute-start.23 = (bf16[192,896]{1,0:T(8,128)(2,1)}, bf16[192,896]{1,0:T(8,128)(2,1)}, u32[]{:S(2)}, u32[]{:S(2)}) collective-permute-start(bf16[192,896]{1,0:T(8,128)(2,1)} %get-tuple-element.207), channel_id=1, source_target_pairs={{0,12},{4,8},{8,4},{12,0},{1,13},{5,9},{9,5},{13,1},{2,14},{6,10},... | collective-permute-start | bytes 1032200 | tf_op jit(solution)/shard_map/ppermute | solution.py:719
  195.3 28.6 %collective-permute-start.25 = (bf16[192,896]{1,0:T(8,128)(2,1)}, bf16[192,896]{1,0:T(8,128)(2,1)}, u32[]{:S(2)}, u32[]{:S(2)}) collective-permute-start(bf16[192,896]{1,0:T(8,128)(2,1)} %get-tuple-element.225), channel_id=1, source_target_pairs={{0,4},{4,0},{8,12},{12,8},{1,5},{5,1},{9,13},{13,9},{2,6},{6,2},{1... | collective-permute-start | bytes 1032200 | tf_op jit(solution)/shard_map/ppermute | solution.py:719
  196.7 27.2 %collective-permute-start.26 = (bf16[192,896]{1,0:T(8,128)(2,1)}, bf16[192,896]{1,0:T(8,128)(2,1)}, u32[]{:S(2)}, u32[]{:S(2)}) collective-permute-start(bf16[192,896]{1,0:T(8,128)(2,1)} %get-tuple-element.226), channel_id=1, source_target_pairs={{0,8},{4,12},{8,0},{12,4},{1,9},{5,13},{9,1},{13,5},{2,10},{6,14},... | collective-permute-start | bytes 1032200 | tf_op jit(solution)/shard_map/ppermute | solution.py:719
  196.7 27.2 %collective-permute-start.27 = (bf16[192,896]{1,0:T(8,128)(2,1)}, bf16[192,896]{1,0:T(8,128)(2,1)}, u32[]{:S(2)}, u32[]{:S(2)}) collective-permute-start(bf16[192,896]{1,0:T(8,128)(2,1)} %get-tuple-element.227), channel_id=1, source_target_pairs={{0,12},{4,8},{8,4},{12,0},{1,13},{5,9},{9,5},{13,1},{2,14},{6,10},... | collective-permute-start | bytes 1032200 | tf_op jit(solution)/shard_map/ppermute | solution.py:719
  198.0 93.9 %reduce-scatter.5.cloned.1.call-start = ((), (), s32[]{:S(2)}) async-start(), calls=%async_computation.5 | async-start | bytes 1433600 | tf_op jit(solution)/shard_map/reduce_scatter | solution.py:730
  225.4 15.8 %collective-permute-start.31 = (bf16[640,896]{1,0:T(8,128)(2,1)S(1)}, bf16[640,896]{1,0:T(8,128)(2,1)S(1)}, u32[]{:S(2)}, u32[]{:S(2)}) collective-permute-start(bf16[640,896]{1,0:T(8,128)(2,1)S(1)} %grad_weight.6), channel_id=1, source_target_pairs={{0,16},{16,0},{1,17},{17,1},{2,18},{18,2},{3,19},{19,3},{4,20},{20... | collective-permute-start | bytes 3440648 | tf_op jit(solution)/shard_map/ppermute | solution.py:714
  227.3 16.0 %collective-permute-start.28 = (bf16[768,256]{1,0:T(8,128)(2,1)}, bf16[768,256]{1,0:T(8,128)(2,1)}, u32[]{:S(2)}, u32[]{:S(2)}) collective-permute-start(bf16[768,256]{1,0:T(8,128)(2,1)} %get-tuple-element.321), channel_id=1, source_target_pairs={{0,4},{4,0},{8,12},{12,8},{1,5},{5,1},{9,13},{13,9},{2,6},{6,2},{1... | collective-permute-start | bytes 1179656 | tf_op jit(solution)/shard_map/ppermute | solution.py:719
  230.5 23.7 %collective-permute-start.29 = (bf16[768,256]{1,0:T(8,128)(2,1)}, bf16[768,256]{1,0:T(8,128)(2,1)}, u32[]{:S(2)}, u32[]{:S(2)}) collective-permute-start(bf16[768,256]{1,0:T(8,128)(2,1)} %get-tuple-element.320), channel_id=1, source_target_pairs={{0,8},{4,12},{8,0},{12,4},{1,9},{5,13},{9,1},{13,5},{2,10},{6,14},... | collective-permute-start | bytes 1179656 | tf_op jit(solution)/shard_map/ppermute | solution.py:719
  236.9 19.2 %collective-permute-start.30 = (bf16[768,256]{1,0:T(8,128)(2,1)}, bf16[768,256]{1,0:T(8,128)(2,1)}, u32[]{:S(2)}, u32[]{:S(2)}) collective-permute-start(bf16[768,256]{1,0:T(8,128)(2,1)} %get-tuple-element.319), channel_id=1, source_target_pairs={{0,12},{4,8},{8,4},{12,0},{1,13},{5,9},{9,5},{13,1},{2,14},{6,10},... | collective-permute-start | bytes 1179656 | tf_op jit(solution)/shard_map/ppermute | solution.py:719
  263.3 19.0 %collective-permute-start.40 = (bf16[224,1280]{1,0:T(8,128)(2,1)}, bf16[224,1280]{1,0:T(8,128)(2,1)}, u32[]{:S(2)}, u32[]{:S(2)}) collective-permute-start(bf16[224,1280]{1,0:T(8,128)(2,1)} %reduce-scatter.3.cloned.1.call-done), channel_id=1, source_target_pairs={{0,4},{4,0},{8,12},{12,8},{1,5},{5,1},{9,13},{13,9},{2,6},{6,2},{1... | collective-permute-start | bytes 1720328 | tf_op jit(solution)/shard_map/ppermute | solution.py:719
  264.1 19.6 %collective-permute-start.41 = (bf16[224,1280]{1,0:T(8,128)(2,1)}, bf16[224,1280]{1,0:T(8,128)(2,1)}, u32[]{:S(2)}, u32[]{:S(2)}) collective-permute-start(bf16[224,1280]{1,0:T(8,128)(2,1)} %reduce-scatter.3.cloned.1.call-done), channel_id=1, source_target_pairs={{0,8},{4,12},{8,0},{12,4},{1,9},{5,13},{9,1},{13,5},{2,10},{6,14},... | collective-permute-start | bytes 1720328 | tf_op jit(solution)/shard_map/ppermute | solution.py:719
  266.1 23.8 %collective-permute-start.42 = (bf16[224,1280]{1,0:T(8,128)(2,1)}, bf16[224,1280]{1,0:T(8,128)(2,1)}, u32[]{:S(2)}, u32[]{:S(2)}) collective-permute-start(bf16[224,1280]{1,0:T(8,128)(2,1)} %reduce-scatter.3.cloned.1.call-done), channel_id=1, source_target_pairs={{0,12},{4,8},{8,4},{12,0},{1,13},{5,9},{9,5},{13,1},{2,14},{6,10},... | collective-permute-start | bytes 1720328 | tf_op jit(solution)/shard_map/ppermute | solution.py:719
  281.1 20.5 %collective-permute-start.37 = (bf16[4,32,2176]{2,1,0:T(8,128)(2,1)}, bf16[4,32,2176]{2,1,0:T(8,128)(2,1)S(1)}, u32[]{:S(2)}, u32[]{:S(2)}) collective-permute-start(bf16[4,32,2176]{2,1,0:T(8,128)(2,1)} %get-tuple-element.305), channel_id=1, source_target_pairs={{0,4},{4,0},{8,12},{12,8},{1,5},{5,1},{9,13},{13,9},{2,6},{6,2},{1... | collective-permute-start | bytes 1671176 | tf_op jit(solution)/shard_map/ppermute | solution.py:719
  281.1 33.7 %collective-permute-start.38 = (bf16[4,32,2176]{2,1,0:T(8,128)(2,1)}, bf16[4,32,2176]{2,1,0:T(8,128)(2,1)S(1)}, u32[]{:S(2)}, u32[]{:S(2)}) collective-permute-start(bf16[4,32,2176]{2,1,0:T(8,128)(2,1)} %get-tuple-element.304), channel_id=1, source_target_pairs={{0,8},{4,12},{8,0},{12,4},{1,9},{5,13},{9,1},{13,5},{2,10},{6,14},... | collective-permute-start | bytes 1671176 | tf_op jit(solution)/shard_map/ppermute | solution.py:719
  282.3 32.6 %collective-permute-start.39 = (bf16[4,32,2176]{2,1,0:T(8,128)(2,1)}, bf16[4,32,2176]{2,1,0:T(8,128)(2,1)}, u32[]{:S(2)}, u32[]{:S(2)}) collective-permute-start(bf16[4,32,2176]{2,1,0:T(8,128)(2,1)} %get-tuple-element.303), channel_id=1, source_target_pairs={{0,12},{4,8},{8,4},{12,0},{1,13},{5,9},{9,5},{13,1},{2,14},{6,10},... | collective-permute-start | bytes 1671176 | tf_op jit(solution)/shard_map/ppermute | solution.py:719
  317.9 16.1 %collective-permute-start.46 = (bf16[4,224,1280]{2,1,0:T(8,128)(2,1)}, bf16[4,224,1280]{2,1,0:T(8,128)(2,1)}, u32[]{:S(2)}, u32[]{:S(2)}) collective-permute-start(bf16[4,224,1280]{2,1,0:T(8,128)(2,1)} %pad_maximum_fusion.refs_0_), channel_id=1, source_target_pairs={{0,16},{16,0},{1,17},{17,1},{2,18},{18,2},{3,19},{19,3},{4,20},{20... | collective-permute-start | bytes 6881288 | tf_op jit(solution)/shard_map/ppermute | solution.py:714
  347.1 14.8 %collective-permute-start.53 = (bf16[4,160,896]{2,1,0:T(8,128)(2,1)S(1)}, bf16[4,160,896]{2,1,0:T(8,128)(2,1)S(1)}, u32[]{:S(2)}, u32[]{:S(2)}) collective-permute-start(bf16[4,160,896]{2,1,0:T(8,128)(2,1)S(1)} %pad_maximum_fusion.4.refs_0_), channel_id=1, source_target_pairs={{0,16},{16,0},{1,17},{17,1},{2,18},{18,2},{3,19},{19,3},{4,20},{20... | collective-permute-start | bytes 3440648 | tf_op jit(solution)/shard_map/ppermute | solution.py:714
  (76 other events, 641.7 us)
Sparse Core Ops, SparseCore 0:
  34.0 62.8 all-gather.2
  99.7 30.0 all-gather.4
  198.1 48.2 reduce-scatter.2
  263.7 28.0 reduce-scatter.4

commit v7 on v6

--- a/solution.py
+++ b/solution.py
@@ -339,7 +339,9 @@
         compiler_params=pltpu.CompilerParams(
             dimension_semantics=("arbitrary",), vmem_limit_bytes=40 * 2**20
         ),
-        cost_estimate=NO_COST,
+        cost_estimate=pl.CostEstimate(
+            flops=10**10, bytes_accessed=2**23, transcendentals=0
+        ),
         name="spread_columns",
     )(*pieces)
 
@@ -412,7 +414,7 @@
     for k in range(n_z):
         at = jnp.bitwise_xor(lax.axis_index("fsdp"), k)
         out_ref[at] = pieces[k][:rows_here]
-        held[at] = pieces[k][rows_here:].astype(F32)
+        held[at] = pieces[k][rows_here : rows_here + held.shape[1]].astype(F32)
     vec_ref[...] = jnp.zeros(vec_ref.shape, F32)
     for i, size in enumerate(widths):
         row = jnp.concatenate([held[z, i : i + 1, :size] for z in range(n_z)], 1)
@@ -426,8 +428,8 @@
     kv_ref[:, half:] = (both[:, half:] + vec_ref[4:5, :half]).astype(BF16)
 
 
-def project_kv(pieces, tokens, cos, sin, rows_here, widths):
-    rows, cols = pieces[0].shape
+def project_kv(pieces, tokens, cos, sin, rows_here, vec_rows, widths):
+    cols = pieces[0].shape[1]
     n_z = len(pieces)
     vmem = pl.BlockSpec(memory_space=pltpu.VMEM)
     return pl.pallas_call(
@@ -440,7 +442,7 @@
             jax.ShapeDtypeStruct((tokens.shape[0], cols), BF16),
             jax.ShapeDtypeStruct(tokens.shape, BF16),
         ],
-        scratch_shapes=[pltpu.VMEM((n_z, rows - rows_here, cols), F32)],
+        scratch_shapes=[pltpu.VMEM((n_z, vec_rows, cols), F32)],
         compiler_params=pltpu.CompilerParams(vmem_limit_bytes=40 * 2**20),
         cost_estimate=NO_COST,
         name="project_kv",
@@ -789,13 +791,12 @@
     got, cos_wide, sin_wide, gu_cut, down_cut, og_here = lax.optimization_barrier(
         (got, cos_wide, sin_wide, gu_cut, down_cut, og_here)
     )
-    kv_got = [v[:pack_rows] for v in got]
 
     qo_got = jnp.stack([v[pack_rows:].reshape(2 * part_rows, width) for v in got])
     qo_own = [hop(qo_got, k) for k in range(tp)]
     widths = tuple(v.shape[0] for v in vectors)
     w_kv, vecs, kv_local, hidden_one = project_kv(
-        kv_got, x_here, cos_wide, sin_wide, rows_here, widths
+        got, x_here, cos_wide, sin_wide, rows_here, pack_rows - rows_here, widths
     )
     w_kv = w_kv.reshape(width, 2 * key_width)
     gain_one = vecs[0:1, :width]
@@ -946,14 +947,15 @@
 
     last = ctx_groups_sum(sum(v.astype(F32) for v in last).astype(BF16))
     last = lax.optimization_barrier(last)
+    down_pieces = [hop(d_down, k) for k in range(tp)]
+    grad_w_gate, grad_w_up = spread_columns((gu_pieces, gu_sib), n_z, ff, 2)
+    last, down_pieces, grad_w_gate, grad_w_up = lax.optimization_barrier(
+        (last, down_pieces, grad_w_gate, grad_w_up)
+    )
     last = [hop(last, k) for k in range(tp)]
-    down_pieces = [hop(d_down, k) for k in range(tp)]
     down_pieces = jnp.stack(down_pieces)
     down_sib = swap(down_pieces)
-    grad_w_gate, grad_w_up = spread_columns((gu_pieces, gu_sib), n_z, ff, 2)
-    last, down_pieces, down_sib, grad_w_gate, grad_w_up = lax.optimization_barrier(
-        (last, down_pieces, down_sib, grad_w_gate, grad_w_up)
-    )
+    last, down_pieces, down_sib = lax.optimization_barrier((last, down_pieces, down_sib))
     last = jnp.stack(last)
     grad_w_down = spread_rows((down_pieces, down_sib), piece, ff_z)
     last = spread_rows((last, swap(last)), part_rows, rows_here)

time: 387 us -> 386 us (level)
  Pallas kernels: 85.7 us -> 67.1 us
  starting transfers between devices: 78.6 us -> 96.6 us
  waiting for transfers between devices: 137 us -> 131 us
  local copies, waits for them, and re-layouts: 39.8 us -> 44.3 us
    ppermute x10, starting transfers between devices: 15.5 us -> 35.9 us  [swap(): return lax.ppermute(v, 'seq', [(0, 1), (1, 0)])]
    pallas_call x1, Pallas kernels: 22.1 us -> 9.86 us  [attend_backward(): pl.pallas_call(functools.partial(backward_kernel, by_xor), grid_spec=pltp...]
    pallas_call x1, Pallas kernels: 13.4 us -> 6.01 us  [attend_forward(): pl.pallas_call(functools.partial(forward_kernel, by_xor), grid_spec=pltpu...]
    ppermute x12, waiting for transfers between devices: 36.8 us -> 31.1 us  [hop_z(): return lax.ppermute(v, 'fsdp', [(i, i ^ k) for i in range(n_z)])]
    ppermute x33, starting transfers between devices: 41.1 us -> 36 us  [hop(): return lax.ppermute(v, 'ctx', [(i, i ^ k) for i in range(n_ctx)])]
    unnamed x105 -> x117, local copies, waits for them, and re-layouts: 16.5 us -> 19.3 us
  transfers between devices with their start and end apart: 59 -> 59, of which waited for: 28 -> 26; matrix products, arithmetic and copies ran while one was open for 8% -> 8% of each run, Pallas kernels for 16% -> 11%
where the time goes in v7:
time: 386 us; the launch traced here: 379 us
  waiting for transfers between devices  131 us (34%)
  starting transfers between devices  96.6 us (25%)
  Pallas kernels  67.1 us (17%)
  local copies, waits for them, and re-layouts  44.3 us (11%)
  other arithmetic  21.5 us (6%)
  between operations  15.6 us (4%)
    ppermute x33, waiting for transfers between devices, hop(): return lax.ppermute(v, 'ctx', [(i, i ^ k) for i in range(n_ctx)])  90.6 us
    ppermute x33, starting transfers between devices, hop(): return lax.ppermute(v, 'ctx', [(i, i ^ k) for i in range(n_ctx)])  36 us
    ppermute x10, starting transfers between devices, swap(): return lax.ppermute(v, 'seq', [(0, 1), (1, 0)])  35.9 us
    ppermute x12, waiting for transfers between devices, hop_z(): return lax.ppermute(v, 'fsdp', [(i, i ^ k) for i in range(n_z)])  31.1 us
    ppermute x12, starting transfers between devices, hop_z(): return lax.ppermute(v, 'fsdp', [(i, i ^ k) for i in range(n_z)])  24.3 us
    pallas_call x1, Pallas kernels, ff_pass(): pl.pallas_call(functools.partial(ff_kernel, tp, n_z), in_specs=[vmem] * (...  20.9 us
    unnamed x117, local copies, waits for them, and re-layouts  19.3 us
    pallas_call x4, Pallas kernels, grad_weight(): pl.pallas_call(grad_weight_kernel, grid=(rows // tile,), in_specs=in_spec...  10.2 us
  transfers between devices with their start and end apart: 59, of which 26 were waited for; matrix products, arithmetic and copies ran while one was open for 8% of the time, Pallas kernels for 11%

profile of v7, /device:TPU:1, one launch (start us, length us, event | category | flops | bytes accessed | tf_op | source)
XLA Modules:
  0.0 378.8 jit_solution(5208011499326791566)
XLA Ops:
  28.4 5.4 %collective-permute-done.2.refs_3_ = bf16[464,256]{1,0:T(8,128)(2,1)} collective-permute-done((bf16[464,256]{1,0:T(8,128)(2,1)S(1)}, bf16[464,256]{1,0:T(8,128)(2,1)}, u32[]{:S(2)}, u32[]{:S(2)}) %collective-permute-start.2) | collective-permute-done | bytes 237600 | tf_op jit(solution)/shard_map/ppermute | solution.py:726
  44.2 5.3 %collective-permute-start.3 = (bf16[192,256]{1,0:T(8,128)(2,1)S(1)}, bf16[192,256]{1,0:T(8,128)(2,1)S(1)}, u32[]{:S(2)}, u32[]{:S(2)}) collective-permute-start(bf16[192,256]{1,0:T(8,128)(2,1)S(1)} %get-tuple-element.176), channel_id=1, source_target_pairs={{0,1},{1,0},{2,3},{3,2},{4,5},{5,4},{6,7},{7,6},{8,9},{9,8},{10,11... | collective-permute-start | bytes 294920 | tf_op jit(solution)/shard_map/ppermute | solution.py:726
  50.5 6.9 %collective-permute-done.3 = bf16[192,256]{1,0:T(8,128)(2,1)S(1)} collective-permute-done((bf16[192,256]{1,0:T(8,128)(2,1)S(1)}, bf16[192,256]{1,0:T(8,128)(2,1)S(1)}, u32[]{:S(2)}, u32[]{:S(2)}) %collective-permute-start.3) | collective-permute-done | bytes 98336 | tf_op jit(solution)/shard_map/ppermute | solution.py:726
  57.4 4.1 %collective-permute-start.5 = (bf16[192,256]{1,0:T(8,128)(2,1)S(1)}, bf16[192,256]{1,0:T(8,128)(2,1)S(1)}, u32[]{:S(2)}, u32[]{:S(2)}) collective-permute-start(bf16[192,256]{1,0:T(8,128)(2,1)S(1)} %get-tuple-element.176), channel_id=1, source_target_pairs={{0,3},{1,2},{2,1},{3,0},{4,7},{5,6},{6,5},{7,4},{8,11},{9,10},{10,... | collective-permute-start | bytes 294920 | tf_op jit(solution)/shard_map/ppermute | solution.py:726
  61.5 4.3 %collective-permute-done.5 = bf16[192,256]{1,0:T(8,128)(2,1)S(1)} collective-permute-done((bf16[192,256]{1,0:T(8,128)(2,1)S(1)}, bf16[192,256]{1,0:T(8,128)(2,1)S(1)}, u32[]{:S(2)}, u32[]{:S(2)}) %collective-permute-start.5) | collective-permute-done | bytes 98336 | tf_op jit(solution)/shard_map/ppermute | solution.py:726
  68.6 4.1 %collective-permute-start.9 = (bf16[4,4,64,896]{3,2,1,0:T(8,128)(2,1)S(1)}, bf16[4,4,64,896]{3,2,1,0:T(8,128)(2,1)S(1)}, u32[]{:S(2)}, u32[]{:S(2)}) collective-permute-start(bf16[4,4,64,896]{3,2,1,0:T(8,128)(2,1)S(1)} %pad_maximum_fusion.2.own_ref), channel_id=1, source_target_pairs={{0,16},{16,0},{1,17},{17,1},{2,18},{18,2},{3,19},{19,3},{4,20},{20... | collective-permute-start | bytes 5505032 | tf_op jit(solution)/shard_map/ppermute | solution.py:716
  78.5 5.1 %collective-permute-done.10 = bf16[768,256]{1,0:T(8,128)(2,1)S(1)} collective-permute-done((bf16[768,256]{1,0:T(8,128)(2,1)S(1)}, bf16[768,256]{1,0:T(8,128)(2,1)S(1)}, u32[]{:S(2)}, u32[]{:S(2)}) %collective-permute-start.10) | collective-permute-done | bytes 393248 | tf_op jit(solution)/shard_map/ppermute | solution.py:721
  83.7 8.1 %collective-permute-done.11 = bf16[768,256]{1,0:T(8,128)(2,1)S(1)} collective-permute-done((bf16[768,256]{1,0:T(8,128)(2,1)S(1)}, bf16[768,256]{1,0:T(8,128)(2,1)S(1)}, u32[]{:S(2)}, u32[]{:S(2)}) %collective-permute-start.11) | collective-permute-done | bytes 393248 | tf_op jit(solution)/shard_map/ppermute | solution.py:721
  93.1 3.7 all-gather.3.cloned.1.call-done.refs_8_
  103.0 6.0 %attend_forward.1 = (bf16[192,896]{1,0:T(8,128)(2,1)S(1)}, bf16[2688,256]{1,0:T(8,128)(2,1)S(1)}) custom-call(s32[4]{0:T(128)S(1)} %bitcast.84, bf16[192,896]{1,0:T(8,128)(2,1)S(1)} %get-tuple-element.186.q_ref, bf16[4,768,256]{2,1,0:T(8,128)(2,1)S(1)} %pad_maximum_fusion.3.kv_ref), custom_call_target="tpu_custom_call" | custom-call | flops 30000001024 | bytes 8388608 | tf_op jit(solution)/shard_map/attend_forward/pallas_call | solution.py:239
  109.0 5.1 %collective-permute-done.15.refs_7_ = bf16[192,896]{1,0:T(8,128)(2,1)} collective-permute-done((bf16[192,896]{1,0:T(8,128)(2,1)S(1)}, bf16[192,896]{1,0:T(8,128)(2,1)}, u32[]{:S(2)}, u32[]{:S(2)}) %collective-permute-start.15) | collective-permute-done | bytes 344096 | tf_op jit(solution)/shard_map/ppermute | solution.py:721
  116.7 3.4 collective-permute-start.16
  120.1 3.7 collective-permute-start.17
  125.2 13.9 %collective-permute-done.17.refs_2_ = bf16[192,896]{1,0:T(8,128)(2,1)S(1)} collective-permute-done((bf16[192,896]{1,0:T(8,128)(2,1)S(1)}, bf16[192,896]{1,0:T(8,128)(2,1)S(1)}, u32[]{:S(2)}, u32[]{:S(2)}) %collective-permute-start.17) | collective-permute-done | bytes 344096 | tf_op jit(solution)/shard_map/ppermute | solution.py:721
  144.0 20.9 %ff_pass.1 = (bf16[640,768]{1,0:T(8,128)(2,1)}, bf16[640,768]{1,0:T(8,128)(2,1)}, bf16[768,1280]{1,0:T(8,128)(2,1)}, bf16[768,1280]{1,0:T(8,128)(2,1)}, bf16[896...) custom-call(bf16[192,896]{1,0:T(8,128)(2,1)} %copy-done.30, ...), custom_call_target="tpu_custom_call" | custom-call | tf_op jit(solution)/shard_map/ff_pass/pallas_call | solution.py:667
  167.7 3.1 grad_weight.4
  177.2 3.5 grad_weight.5
  182.1 7.6 %collective-permute-done.22 = bf16[192,896]{1,0:T(8,128)(2,1)} collective-permute-done((bf16[192,896]{1,0:T(8,128)(2,1)}, bf16[192,896]{1,0:T(8,128)(2,1)}, u32[]{:S(2)}, u32[]{:S(2)}) %collective-permute-start.22) | collective-permute-done | bytes 344096 | tf_op jit(solution)/shard_map/ppermute | solution.py:721
  201.8 9.9 %attend_backward.1 = (bf16[192,896]{1,0:T(8,128)(2,1)S(1)}, bf16[4,768,256]{2,1,0:T(8,128)(2,1)S(1)}) custom-call(s32[4]{0:T(128)S(1)} %bitcast.85, bf16[2688,256]{1,0:T(8,128)(2,1)S(1)} %copy-done.34, bf16[192,896]{1,0:T(8,128)(2,1)S(1)} %copy-done.31, bf16[192,896]{1,0:T(8,128)(2,1)S(1)} %copy-done.19, f32[192,128]{1,0:T(8,128)S(1)} %copy.33.refs_5_.cos_ref.refs_4_, ...), custom_call_target="tpu_custom_call" | custom-call | flops 49999998976 | bytes 8388608 | tf_op jit(solution)/shard_map/attend_backward/pallas_call | solution.py:269
  213.1 20.5 %collective-permute-start.31 = (bf16[640,896]{1,0:T(8,128)(2,1)S(1)}, bf16[640,896]{1,0:T(8,128)(2,1)S(1)}, u32[]{:S(2)}, u32[]{:S(2)}) collective-permute-start(bf16[640,896]{1,0:T(8,128)(2,1)S(1)} %grad_weight.6), channel_id=1, source_target_pairs={{0,16},{16,0},{1,17},{17,1},{2,18},{18,2},{3,19},{19,3},{4,20},{20... | collective-permute-start | bytes 3440648 | tf_op jit(solution)/shard_map/ppermute | solution.py:716
  243.4 3.1 collective-permute-done.28
  246.5 8.4 %collective-permute-done.29 = bf16[768,256]{1,0:T(8,128)(2,1)} collective-permute-done((bf16[768,256]{1,0:T(8,128)(2,1)}, bf16[768,256]{1,0:T(8,128)(2,1)}, u32[]{:S(2)}, u32[]{:S(2)}) %collective-permute-start.29) | collective-permute-done | bytes 393248 | tf_op jit(solution)/shard_map/ppermute | solution.py:721
  258.1 3.7 collective-permute-start.32
  266.1 5.2 %collective-permute-done.33.refs_2_ = bf16[192,256]{1,0:T(8,128)(2,1)S(1)} collective-permute-done((bf16[192,256]{1,0:T(8,128)(2,1)}, bf16[192,256]{1,0:T(8,128)(2,1)S(1)}, u32[]{:S(2)}, u32[]{:S(2)}) %collective-permute-start.33) | collective-permute-done | bytes 98336 | tf_op jit(solution)/shard_map/ppermute | solution.py:726
  284.1 7.2 %collective-permute-done.42 = bf16[224,1280]{1,0:T(8,128)(2,1)} collective-permute-done((bf16[224,1280]{1,0:T(8,128)(2,1)}, bf16[224,1280]{1,0:T(8,128)(2,1)}, u32[]{:S(2)}, u32[]{:S(2)}) %collective-permute-start.42) | collective-permute-done | bytes 573472 | tf_op jit(solution)/shard_map/ppermute | solution.py:721
  292.0 10.1 %collective-permute-done.37 = bf16[4,32,2176]{2,1,0:T(8,128)(2,1)S(1)} collective-permute-done((bf16[4,32,2176]{2,1,0:T(8,128)(2,1)}, bf16[4,32,2176]{2,1,0:T(8,128)(2,1)S(1)}, u32[]{:S(2)}, u32[]{:S(2)}) %collective-permute-start.37) | collective-permute-done | bytes 557088 | tf_op jit(solution)/shard_map/ppermute | solution.py:721
  302.2 14.1 %collective-permute-done.38 = bf16[4,32,2176]{2,1,0:T(8,128)(2,1)S(1)} collective-permute-done((bf16[4,32,2176]{2,1,0:T(8,128)(2,1)}, bf16[4,32,2176]{2,1,0:T(8,128)(2,1)S(1)}, u32[]{:S(2)}, u32[]{:S(2)}) %collective-permute-start.38) | collective-permute-done | bytes 557088 | tf_op jit(solution)/shard_map/ppermute | solution.py:721
  325.3 3.5 collective-permute-done.43
  328.7 5.8 %collective-permute-done.44 = bf16[32,2176]{1,0:T(8,128)(2,1)S(1)} collective-permute-done((bf16[32,2176]{1,0:T(8,128)(2,1)S(1)}, bf16[32,2176]{1,0:T(8,128)(2,1)S(1)}, u32[]{:S(2)}, u32[]{:S(2)}) %collective-permute-start.44) | collective-permute-done | bytes 139296 | tf_op jit(solution)/shard_map/ppermute | solution.py:726
  337.3 9.1 %spread_columns.1 = (f32[224,4864]{1,0:T(8,128)}, f32[224,4864]{1,0:T(8,128)}) custom-call(bf16[4,224,1280]{2,1,0:T(8,128)(2,1)} %pad_maximum_fusion.refs_0_, bf16[4,224,1280]{2,1,0:T(8,128)(2,1)} %collective-permute-done.46.refs_1_), custom_call_target="tpu_custom_call" | custom-call | flops 10000000000 | bytes 8388608 | tf_op jit(solution)/shard_map/spread_columns/pallas_call | solution.py:332
  348.4 3.3 collective-permute-start.53
  363.1 3.8 %spread_rows.3 = f32[1216,896]{1,0:T(8,128)} custom-call(bf16[4,160,896]{2,1,0:T(8,128)(2,1)S(1)} %pad_maximum_fusion.4.refs_0_, bf16[4,160,896]{2,1,0:T(8,128)(2,1)S(1)} %collective-permute-done.53.refs_1_), custom_call_target="tpu_custom_call" | custom-call | tf_op jit(solution)/shard_map/spread_rows/pallas_call | solution.py:366
  (295 shorter events, 141.1 us)
Async XLA Ops:
  7.2 89.7 %all-gather.3.cloned.1.call-start = ((), (), s32[]{:S(2)}) async-start(), calls=%async_computation.2 | async-start | bytes 2867200 | tf_op jit(solution)/shard_map/all_gather | solution.py:729
  13.9 14.4 %collective-permute-start = (bf16[464,256]{1,0:T(8,128)(2,1)S(1)}, bf16[464,256]{1,0:T(8,128)(2,1)S(1)}, u32[]{:S(2)}, u32[]{:S(2)}) collective-permute-start(bf16[464,256]{1,0:T(8,128)(2,1)S(1)} %constant_dynamic-update-slice_fusion.refs_0_), channel_id=1, source_target_pairs={{0,1},{1,0},{2,3},{3,2},{4,5},{5,4},{6,7},{7,6},{8,9},{9,8},{10,11... | collective-permute-start | bytes 712712 | tf_op jit(solution)/shard_map/ppermute | solution.py:726
  18.4 15.4 %collective-permute-start.2 = (bf16[464,256]{1,0:T(8,128)(2,1)S(1)}, bf16[464,256]{1,0:T(8,128)(2,1)}, u32[]{:S(2)}, u32[]{:S(2)}) collective-permute-start(bf16[464,256]{1,0:T(8,128)(2,1)S(1)} %constant_dynamic-update-slice_fusion.refs_0_), channel_id=1, source_target_pairs={{0,3},{1,2},{2,1},{3,0},{4,7},{5,6},{6,5},{7,4},{8,11},{9,10},{10,... | collective-permute-start | bytes 712712 | tf_op jit(solution)/shard_map/ppermute | solution.py:726
  33.9 105.2 %all-gather.5.cloned.1.call-start = ((), (), s32[]{:S(2)}) async-start(), calls=%async_computation.3 | async-start | bytes 1433600 | tf_op jit(solution)/shard_map/all_gather | solution.py:729
  37.2 28.6 %collective-permute-start.6 = (bf16[4,64,896]{2,1,0:T(8,128)(2,1)S(1)}, bf16[4,64,896]{2,1,0:T(8,128)(2,1)S(1)}, u32[]{:S(2)}, u32[]{:S(2)}) collective-permute-start(bf16[4,64,896]{2,1,0:T(8,128)(2,1)S(1)} %constant_dynamic-update-slice_fusion.2), channel_id=1, source_target_pairs={{0,4},{4,0},{8,12},{12,8},{1,5},{5,1},{9,13},{13,9},{2,6},{6,2},{1... | collective-permute-start | bytes 1376264 | tf_op jit(solution)/shard_map/ppermute | solution.py:721
  38.4 27.4 %collective-permute-start.7 = (bf16[4,64,896]{2,1,0:T(8,128)(2,1)S(1)}, bf16[4,64,896]{2,1,0:T(8,128)(2,1)S(1)}, u32[]{:S(2)}, u32[]{:S(2)}) collective-permute-start(bf16[4,64,896]{2,1,0:T(8,128)(2,1)S(1)} %constant_dynamic-update-slice_fusion.2), channel_id=1, source_target_pairs={{0,8},{4,12},{8,0},{12,4},{1,9},{5,13},{9,1},{13,5},{2,10},{6,14},... | collective-permute-start | bytes 1376264 | tf_op jit(solution)/shard_map/ppermute | solution.py:721
  39.7 26.2 %collective-permute-start.8 = (bf16[4,64,896]{2,1,0:T(8,128)(2,1)S(1)}, bf16[4,64,896]{2,1,0:T(8,128)(2,1)S(1)}, u32[]{:S(2)}, u32[]{:S(2)}) collective-permute-start(bf16[4,64,896]{2,1,0:T(8,128)(2,1)S(1)} %constant_dynamic-update-slice_fusion.2), channel_id=1, source_target_pairs={{0,12},{4,8},{8,4},{12,0},{1,13},{5,9},{9,5},{13,1},{2,14},{6,10},... | collective-permute-start | bytes 1376264 | tf_op jit(solution)/shard_map/ppermute | solution.py:721
  44.2 13.2 %collective-permute-start.3 = (bf16[192,256]{1,0:T(8,128)(2,1)S(1)}, bf16[192,256]{1,0:T(8,128)(2,1)S(1)}, u32[]{:S(2)}, u32[]{:S(2)}) collective-permute-start(bf16[192,256]{1,0:T(8,128)(2,1)S(1)} %get-tuple-element.176), channel_id=1, source_target_pairs={{0,1},{1,0},{2,3},{3,2},{4,5},{5,4},{6,7},{7,6},{8,9},{9,8},{10,11... | collective-permute-start | bytes 294920 | tf_op jit(solution)/shard_map/ppermute | solution.py:726
  74.1 17.7 %collective-permute-start.11 = (bf16[768,256]{1,0:T(8,128)(2,1)S(1)}, bf16[768,256]{1,0:T(8,128)(2,1)S(1)}, u32[]{:S(2)}, u32[]{:S(2)}) collective-permute-start(bf16[768,256]{1,0:T(8,128)(2,1)S(1)} %constant_dynamic-update-slice_fusion.6), channel_id=1, source_target_pairs={{0,8},{4,12},{8,0},{12,4},{1,9},{5,13},{9,1},{13,5},{2,10},{6,14},... | collective-permute-start | bytes 1179656 | tf_op jit(solution)/shard_map/ppermute | solution.py:721
  75.3 17.8 %collective-permute-start.12 = (bf16[768,256]{1,0:T(8,128)(2,1)S(1)}, bf16[768,256]{1,0:T(8,128)(2,1)}, u32[]{:S(2)}, u32[]{:S(2)}) collective-permute-start(bf16[768,256]{1,0:T(8,128)(2,1)S(1)} %constant_dynamic-update-slice_fusion.6), channel_id=1, source_target_pairs={{0,12},{4,8},{8,4},{12,0},{1,13},{5,9},{9,5},{13,1},{2,14},{6,10},... | collective-permute-start | bytes 1179656 | tf_op jit(solution)/shard_map/ppermute | solution.py:721
  99.3 14.9 %collective-permute-start.15 = (bf16[192,896]{1,0:T(8,128)(2,1)S(1)}, bf16[192,896]{1,0:T(8,128)(2,1)}, u32[]{:S(2)}, u32[]{:S(2)}) collective-permute-start(bf16[192,896]{1,0:T(8,128)(2,1)S(1)} %bitcast.92), channel_id=1, source_target_pairs={{0,12},{4,8},{8,4},{12,0},{1,13},{5,9},{9,5},{13,1},{2,14},{6,10},... | collective-permute-start | bytes 1032200 | tf_op jit(solution)/shard_map/ppermute | solution.py:721
  99.6 155.4 %reduce-scatter.3.cloned.1.call-start = ((), (), s32[]{:S(2)}) async-start(), calls=%async_computation.4 | async-start | bytes 2867200 | tf_op jit(solution)/shard_map/reduce_scatter | solution.py:732
  99.8 40.5 %collective-permute-start.19 = (bf16[896,1280]{1,0:T(8,128)(2,1)}, bf16[896,1280]{1,0:T(8,128)(2,1)}, u32[]{:S(2)}, u32[]{:S(2)}) collective-permute-start(bf16[896,1280]{1,0:T(8,128)(2,1)} %all-gather.3.cloned.1.call-done.refs_8_), channel_id=1, source_target_pairs={{0,16},{16,0},{1,17},{17,1},{2,18},{18,2},{3,19},{19,3},{4,20},{20... | collective-permute-start | bytes 6881288 | tf_op jit(solution)/shard_map/ppermute | solution.py:716
  120.1 19.0 %collective-permute-start.17 = (bf16[192,896]{1,0:T(8,128)(2,1)S(1)}, bf16[192,896]{1,0:T(8,128)(2,1)S(1)}, u32[]{:S(2)}, u32[]{:S(2)}) collective-permute-start(bf16[192,896]{1,0:T(8,128)(2,1)S(1)} %get-tuple-element.199.refs_0_), channel_id=1, source_target_pairs={{0,8},{4,12},{8,0},{12,4},{1,9},{5,13},{9,1},{13,5},{2,10},{6,14},... | collective-permute-start | bytes 1032200 | tf_op jit(solution)/shard_map/ppermute | solution.py:721
  123.8 15.3 %collective-permute-start.18 = (bf16[192,896]{1,0:T(8,128)(2,1)S(1)}, bf16[192,896]{1,0:T(8,128)(2,1)S(1)}, u32[]{:S(2)}, u32[]{:S(2)}) collective-permute-start(bf16[192,896]{1,0:T(8,128)(2,1)S(1)} %get-tuple-element.199.refs_0_), channel_id=1, source_target_pairs={{0,12},{4,8},{8,4},{12,0},{1,13},{5,9},{9,5},{13,1},{2,14},{6,10},... | collective-permute-start | bytes 1032200 | tf_op jit(solution)/shard_map/ppermute | solution.py:721
  172.8 16.9 %collective-permute-start.22 = (bf16[192,896]{1,0:T(8,128)(2,1)}, bf16[192,896]{1,0:T(8,128)(2,1)}, u32[]{:S(2)}, u32[]{:S(2)}) collective-permute-start(bf16[192,896]{1,0:T(8,128)(2,1)} %get-tuple-element.211), channel_id=1, source_target_pairs={{0,8},{4,12},{8,0},{12,4},{1,9},{5,13},{9,1},{13,5},{2,10},{6,14},... | collective-permute-start | bytes 1032200 | tf_op jit(solution)/shard_map/ppermute | solution.py:721
  173.0 16.7 %collective-permute-start.23 = (bf16[192,896]{1,0:T(8,128)(2,1)}, bf16[192,896]{1,0:T(8,128)(2,1)}, u32[]{:S(2)}, u32[]{:S(2)}) collective-permute-start(bf16[192,896]{1,0:T(8,128)(2,1)} %get-tuple-element.212), channel_id=1, source_target_pairs={{0,12},{4,8},{8,4},{12,0},{1,13},{5,9},{9,5},{13,1},{2,14},{6,10},... | collective-permute-start | bytes 1032200 | tf_op jit(solution)/shard_map/ppermute | solution.py:721
  195.2 16.5 %collective-permute-start.25 = (bf16[192,896]{1,0:T(8,128)(2,1)}, bf16[192,896]{1,0:T(8,128)(2,1)}, u32[]{:S(2)}, u32[]{:S(2)}) collective-permute-start(bf16[192,896]{1,0:T(8,128)(2,1)} %get-tuple-element.230), channel_id=1, source_target_pairs={{0,4},{4,0},{8,12},{12,8},{1,5},{5,1},{9,13},{13,9},{2,6},{6,2},{1... | collective-permute-start | bytes 1032200 | tf_op jit(solution)/shard_map/ppermute | solution.py:721
  195.2 16.4 %collective-permute-start.26 = (bf16[192,896]{1,0:T(8,128)(2,1)}, bf16[192,896]{1,0:T(8,128)(2,1)}, u32[]{:S(2)}, u32[]{:S(2)}) collective-permute-start(bf16[192,896]{1,0:T(8,128)(2,1)} %get-tuple-element.231), channel_id=1, source_target_pairs={{0,8},{4,12},{8,0},{12,4},{1,9},{5,13},{9,1},{13,5},{2,10},{6,14},... | collective-permute-start | bytes 1032200 | tf_op jit(solution)/shard_map/ppermute | solution.py:721
  196.7 15.0 %collective-permute-start.27 = (bf16[192,896]{1,0:T(8,128)(2,1)}, bf16[192,896]{1,0:T(8,128)(2,1)}, u32[]{:S(2)}, u32[]{:S(2)}) collective-permute-start(bf16[192,896]{1,0:T(8,128)(2,1)} %get-tuple-element.232), channel_id=1, source_target_pairs={{0,12},{4,8},{8,4},{12,0},{1,13},{5,9},{9,5},{13,1},{2,14},{6,10},... | collective-permute-start | bytes 1032200 | tf_op jit(solution)/shard_map/ppermute | solution.py:721
  197.9 94.2 %reduce-scatter.5.cloned.1.call-start = ((), (), s32[]{:S(2)}) async-start(), calls=%async_computation.5 | async-start | bytes 1433600 | tf_op jit(solution)/shard_map/reduce_scatter | solution.py:732
  213.1 28.1 %collective-permute-start.31 = (bf16[640,896]{1,0:T(8,128)(2,1)S(1)}, bf16[640,896]{1,0:T(8,128)(2,1)S(1)}, u32[]{:S(2)}, u32[]{:S(2)}) collective-permute-start(bf16[640,896]{1,0:T(8,128)(2,1)S(1)} %grad_weight.6), channel_id=1, source_target_pairs={{0,16},{16,0},{1,17},{17,1},{2,18},{18,2},{3,19},{19,3},{4,20},{20... | collective-permute-start | bytes 3440648 | tf_op jit(solution)/shard_map/ppermute | solution.py:716
  235.4 19.5 %collective-permute-start.29 = (bf16[768,256]{1,0:T(8,128)(2,1)}, bf16[768,256]{1,0:T(8,128)(2,1)}, u32[]{:S(2)}, u32[]{:S(2)}) collective-permute-start(bf16[768,256]{1,0:T(8,128)(2,1)} %get-tuple-element.330), channel_id=1, source_target_pairs={{0,8},{4,12},{8,0},{12,4},{1,9},{5,13},{9,1},{13,5},{2,10},{6,14},... | collective-permute-start | bytes 1179656 | tf_op jit(solution)/shard_map/ppermute | solution.py:721
  235.4 19.5 %collective-permute-start.30 = (bf16[768,256]{1,0:T(8,128)(2,1)}, bf16[768,256]{1,0:T(8,128)(2,1)}, u32[]{:S(2)}, u32[]{:S(2)}) collective-permute-start(bf16[768,256]{1,0:T(8,128)(2,1)} %get-tuple-element.329), channel_id=1, source_target_pairs={{0,12},{4,8},{8,4},{12,0},{1,13},{5,9},{9,5},{13,1},{2,14},{6,10},... | collective-permute-start | bytes 1179656 | tf_op jit(solution)/shard_map/ppermute | solution.py:721
  254.9 17.6 %collective-permute-start.35 = (bf16[4,128,1792]{2,1,0:T(8,128)(2,1)}, bf16[4,128,1792]{2,1,0:T(8,128)(2,1)}, u32[]{:S(2)}, u32[]{:S(2)}) collective-permute-start(bf16[4,128,1792]{2,1,0:T(8,128)(2,1)} %get-tuple-element.255), channel_id=1, source_target_pairs={{0,16},{16,0},{1,17},{17,1},{2,18},{18,2},{3,19},{19,3},{4,20},{20... | collective-permute-start | bytes 5505032 | tf_op jit(solution)/shard_map/ppermute | solution.py:716
  263.8 19.1 %collective-permute-start.40 = (bf16[224,1280]{1,0:T(8,128)(2,1)}, bf16[224,1280]{1,0:T(8,128)(2,1)}, u32[]{:S(2)}, u32[]{:S(2)}) collective-permute-start(bf16[224,1280]{1,0:T(8,128)(2,1)} %reduce-scatter.3.cloned.1.call-done), channel_id=1, source_target_pairs={{0,4},{4,0},{8,12},{12,8},{1,5},{5,1},{9,13},{13,9},{2,6},{6,2},{1... | collective-permute-start | bytes 1720328 | tf_op jit(solution)/shard_map/ppermute | solution.py:721
  265.3 18.8 %collective-permute-start.41 = (bf16[224,1280]{1,0:T(8,128)(2,1)}, bf16[224,1280]{1,0:T(8,128)(2,1)}, u32[]{:S(2)}, u32[]{:S(2)}) collective-permute-start(bf16[224,1280]{1,0:T(8,128)(2,1)} %reduce-scatter.3.cloned.1.call-done), channel_id=1, source_target_pairs={{0,8},{4,12},{8,0},{12,4},{1,9},{5,13},{9,1},{13,5},{2,10},{6,14},... | collective-permute-start | bytes 1720328 | tf_op jit(solution)/shard_map/ppermute | solution.py:721
  271.3 19.9 %collective-permute-start.42 = (bf16[224,1280]{1,0:T(8,128)(2,1)}, bf16[224,1280]{1,0:T(8,128)(2,1)}, u32[]{:S(2)}, u32[]{:S(2)}) collective-permute-start(bf16[224,1280]{1,0:T(8,128)(2,1)} %reduce-scatter.3.cloned.1.call-done), channel_id=1, source_target_pairs={{0,12},{4,8},{8,4},{12,0},{1,13},{5,9},{9,5},{13,1},{2,14},{6,10},... | collective-permute-start | bytes 1720328 | tf_op jit(solution)/shard_map/ppermute | solution.py:721
  281.4 20.8 %collective-permute-start.37 = (bf16[4,32,2176]{2,1,0:T(8,128)(2,1)}, bf16[4,32,2176]{2,1,0:T(8,128)(2,1)S(1)}, u32[]{:S(2)}, u32[]{:S(2)}) collective-permute-start(bf16[4,32,2176]{2,1,0:T(8,128)(2,1)} %get-tuple-element.315), channel_id=1, source_target_pairs={{0,4},{4,0},{8,12},{12,8},{1,5},{5,1},{9,13},{13,9},{2,6},{6,2},{1... | collective-permute-start | bytes 1671176 | tf_op jit(solution)/shard_map/ppermute | solution.py:721
  282.6 33.7 %collective-permute-start.38 = (bf16[4,32,2176]{2,1,0:T(8,128)(2,1)}, bf16[4,32,2176]{2,1,0:T(8,128)(2,1)S(1)}, u32[]{:S(2)}, u32[]{:S(2)}) collective-permute-start(bf16[4,32,2176]{2,1,0:T(8,128)(2,1)} %get-tuple-element.314), channel_id=1, source_target_pairs={{0,8},{4,12},{8,0},{12,4},{1,9},{5,13},{9,1},{13,5},{2,10},{6,14},... | collective-permute-start | bytes 1671176 | tf_op jit(solution)/shard_map/ppermute | solution.py:721
  282.9 33.4 %collective-permute-start.39 = (bf16[4,32,2176]{2,1,0:T(8,128)(2,1)}, bf16[4,32,2176]{2,1,0:T(8,128)(2,1)}, u32[]{:S(2)}, u32[]{:S(2)}) collective-permute-start(bf16[4,32,2176]{2,1,0:T(8,128)(2,1)} %get-tuple-element.313), channel_id=1, source_target_pairs={{0,12},{4,8},{8,4},{12,0},{1,13},{5,9},{9,5},{13,1},{2,14},{6,10},... | collective-permute-start | bytes 1671176 | tf_op jit(solution)/shard_map/ppermute | solution.py:721
  319.3 15.2 %collective-permute-start.46 = (bf16[4,224,1280]{2,1,0:T(8,128)(2,1)}, bf16[4,224,1280]{2,1,0:T(8,128)(2,1)}, u32[]{:S(2)}, u32[]{:S(2)}) collective-permute-start(bf16[4,224,1280]{2,1,0:T(8,128)(2,1)} %pad_maximum_fusion.refs_0_), channel_id=1, source_target_pairs={{0,16},{16,0},{1,17},{17,1},{2,18},{18,2},{3,19},{19,3},{4,20},{20... | collective-permute-start | bytes 6881288 | tf_op jit(solution)/shard_map/ppermute | solution.py:716
  (82 other events, 674.8 us)
Sparse Core Ops, SparseCore 0:
  34.0 62.8 all-gather.2
  99.7 30.7 all-gather.4
  198.0 48.5 reduce-scatter.2
  265.4 26.5 reduce-scatter.4

commit v8 on v7

--- a/solution.py
+++ b/solution.py
@@ -878,9 +878,8 @@
     grad_resid = og_here.astype(F32) + grad_norm_two
     grad_proj = grad_resid.astype(BF16)
     grad_att = times_transposed(grad_proj, w_out).astype(BF16)
-    grad_att, d_gu, ff_out = lax.optimization_barrier((grad_att, d_gu, ff_out))
+    grad_att, d_gu = lax.optimization_barrier((grad_att, d_gu))
     d_gu = scatter_z(d_gu)
-    ff_out = [hop(ff_out[k], k) for k in range(tp)]
     grad_q_pre, grad_terms = attend_backward(
         order_row, n_ctx == tp, queries_ext, grad_att, attended, cos_wide, sin_wide, kv_whole
     )
@@ -908,8 +907,6 @@
     d_gu = ctx_groups_sum(d_gu)
     gu_pieces = [hop(d_gu, k) for k in range(tp)]
     qo_sib = swap(qo_oth)
-    result = resid + sum(v.astype(F32) for v in ff_out)
-    layer_out = result.astype(BF16)[None]
     d_down = scatter_z(d_down)
     kv_terms, qo_own, qo_sib = lax.optimization_barrier((kv_terms, qo_own, qo_sib))
 
@@ -932,7 +929,8 @@
     kv_own, kv_sib, last = lax.optimization_barrier((kv_own, swap(kv_oth), last))
 
     last = scatter_parts(jnp.concatenate([last, core_total(kv_own, kv_sib)], 2))
-    last, d_down, gu_pieces = lax.optimization_barrier((last, d_down, gu_pieces))
+    last, d_down, gu_pieces, ff_out = lax.optimization_barrier((last, d_down, gu_pieces, ff_out))
+    ff_out = [hop(ff_out[k], k) for k in range(tp)]
 
     last = sum(v.astype(F32) for v in last).astype(BF16)
     last = [
@@ -944,6 +942,9 @@
     last, d_down, gu_pieces, gu_sib = lax.optimization_barrier(
         (last, d_down, gu_pieces, gu_sib)
     )
+
+    result = resid + sum(v.astype(F32) for v in ff_out)
+    layer_out = result.astype(BF16)[None]
 
     last = ctx_groups_sum(sum(v.astype(F32) for v in last).astype(BF16))
     last = lax.optimization_barrier(last)

time: 386 us -> 396 us (1.026)
  Pallas kernels: 67.1 us -> 76.8 us
  starting transfers between devices: 96.6 us -> 89.3 us
  waiting for transfers between devices: 131 us -> 138 us
    ppermute x10, starting transfers between devices: 35.9 us -> 24.3 us  [swap(): return lax.ppermute(v, 'seq', [(0, 1), (1, 0)])]
    ppermute x33, waiting for transfers between devices: 90.6 us -> 98.1 us  [hop(): return lax.ppermute(v, 'ctx', [(i, i ^ k) for i in range(n_ctx)])]
    pallas_call x1, Pallas kernels: 9.86 us -> 16 us  [attend_backward(): pl.pallas_call(functools.partial(backward_kernel, by_xor), grid_spec=pltp...]
    ppermute x33, starting transfers between devices: 36 us -> 40.4 us  [hop(): return lax.ppermute(v, 'ctx', [(i, i ^ k) for i in range(n_ctx)])]
    unnamed x117 -> x123, local copies, waits for them, and re-layouts: 19.3 us -> 20.1 us
  transfers between devices with their start and end apart: 59 -> 59, of which waited for: 26 -> 29; matrix products, arithmetic and copies ran while one was open for 8% -> 8% of each run, Pallas kernels for 11% -> 13%
where the time goes in v8:
time: 396 us; the launch traced here: 388 us
  waiting for transfers between devices  138 us (35%)
  starting transfers between devices  89.3 us (23%)
  Pallas kernels  76.8 us (19%)
  local copies, waits for them, and re-layouts  45 us (11%)
  other arithmetic  20.3 us (5%)
  between operations  15.6 us (4%)
    ppermute x33, waiting for transfers between devices, hop(): return lax.ppermute(v, 'ctx', [(i, i ^ k) for i in range(n_ctx)])  98.1 us
    ppermute x33, starting transfers between devices, hop(): return lax.ppermute(v, 'ctx', [(i, i ^ k) for i in range(n_ctx)])  40.4 us
    ppermute x12, waiting for transfers between devices, hop_z(): return lax.ppermute(v, 'fsdp', [(i, i ^ k) for i in range(n_z)])  31 us
    ppermute x12, starting transfers between devices, hop_z(): return lax.ppermute(v, 'fsdp', [(i, i ^ k) for i in range(n_z)])  24.3 us
    ppermute x10, starting transfers between devices, swap(): return lax.ppermute(v, 'seq', [(0, 1), (1, 0)])  24.3 us
    pallas_call x1, Pallas kernels, ff_pass(): pl.pallas_call(functools.partial(ff_kernel, tp, n_z), in_specs=[vmem] * (...  20.9 us
    unnamed x123, local copies, waits for them, and re-layouts  20.1 us
    pallas_call x1, Pallas kernels, attend_backward(): pl.pallas_call(functools.partial(backward_kernel, by_xor), grid_spec=pltp...  16 us
  transfers between devices with their start and end apart: 59, of which 29 were waited for; matrix products, arithmetic and copies ran while one was open for 8% of the time, Pallas kernels for 13%

profile of v8, /device:TPU:1, one launch (start us, length us, event | category | flops | bytes accessed | tf_op | source)
XLA Modules:
  0.0 388.2 jit_solution(8275934271100041221)
XLA Ops:
  28.4 5.4 %collective-permute-done.2.refs_3_ = bf16[464,256]{1,0:T(8,128)(2,1)} collective-permute-done((bf16[464,256]{1,0:T(8,128)(2,1)S(1)}, bf16[464,256]{1,0:T(8,128)(2,1)}, u32[]{:S(2)}, u32[]{:S(2)}) %collective-permute-start.2) | collective-permute-done | bytes 237600 | tf_op jit(solution)/shard_map/ppermute | solution.py:726
  44.2 5.3 %collective-permute-start.3 = (bf16[192,256]{1,0:T(8,128)(2,1)S(1)}, bf16[192,256]{1,0:T(8,128)(2,1)S(1)}, u32[]{:S(2)}, u32[]{:S(2)}) collective-permute-start(bf16[192,256]{1,0:T(8,128)(2,1)S(1)} %get-tuple-element.176), channel_id=1, source_target_pairs={{0,1},{1,0},{2,3},{3,2},{4,5},{5,4},{6,7},{7,6},{8,9},{9,8},{10,11... | collective-permute-start | bytes 294920 | tf_op jit(solution)/shard_map/ppermute | solution.py:726
  50.5 6.9 %collective-permute-done.3 = bf16[192,256]{1,0:T(8,128)(2,1)S(1)} collective-permute-done((bf16[192,256]{1,0:T(8,128)(2,1)S(1)}, bf16[192,256]{1,0:T(8,128)(2,1)S(1)}, u32[]{:S(2)}, u32[]{:S(2)}) %collective-permute-start.3) | collective-permute-done | bytes 98336 | tf_op jit(solution)/shard_map/ppermute | solution.py:726
  57.4 4.2 %collective-permute-start.5 = (bf16[192,256]{1,0:T(8,128)(2,1)S(1)}, bf16[192,256]{1,0:T(8,128)(2,1)S(1)}, u32[]{:S(2)}, u32[]{:S(2)}) collective-permute-start(bf16[192,256]{1,0:T(8,128)(2,1)S(1)} %get-tuple-element.176), channel_id=1, source_target_pairs={{0,3},{1,2},{2,1},{3,0},{4,7},{5,6},{6,5},{7,4},{8,11},{9,10},{10,... | collective-permute-start | bytes 294920 | tf_op jit(solution)/shard_map/ppermute | solution.py:726
  61.5 4.3 %collective-permute-done.5 = bf16[192,256]{1,0:T(8,128)(2,1)S(1)} collective-permute-done((bf16[192,256]{1,0:T(8,128)(2,1)S(1)}, bf16[192,256]{1,0:T(8,128)(2,1)S(1)}, u32[]{:S(2)}, u32[]{:S(2)}) %collective-permute-start.5) | collective-permute-done | bytes 98336 | tf_op jit(solution)/shard_map/ppermute | solution.py:726
  68.6 4.1 %collective-permute-start.9 = (bf16[4,4,64,896]{3,2,1,0:T(8,128)(2,1)S(1)}, bf16[4,4,64,896]{3,2,1,0:T(8,128)(2,1)S(1)}, u32[]{:S(2)}, u32[]{:S(2)}) collective-permute-start(bf16[4,4,64,896]{3,2,1,0:T(8,128)(2,1)S(1)} %pad_maximum_fusion.2.own_ref), channel_id=1, source_target_pairs={{0,16},{16,0},{1,17},{17,1},{2,18},{18,2},{3,19},{19,3},{4,20},{20... | collective-permute-start | bytes 5505032 | tf_op jit(solution)/shard_map/ppermute | solution.py:716
  78.5 5.2 %collective-permute-done.10 = bf16[768,256]{1,0:T(8,128)(2,1)S(1)} collective-permute-done((bf16[768,256]{1,0:T(8,128)(2,1)S(1)}, bf16[768,256]{1,0:T(8,128)(2,1)S(1)}, u32[]{:S(2)}, u32[]{:S(2)}) %collective-permute-start.10) | collective-permute-done | bytes 393248 | tf_op jit(solution)/shard_map/ppermute | solution.py:721
  83.7 8.2 %collective-permute-done.11 = bf16[768,256]{1,0:T(8,128)(2,1)S(1)} collective-permute-done((bf16[768,256]{1,0:T(8,128)(2,1)S(1)}, bf16[768,256]{1,0:T(8,128)(2,1)S(1)}, u32[]{:S(2)}, u32[]{:S(2)}) %collective-permute-start.11) | collective-permute-done | bytes 393248 | tf_op jit(solution)/shard_map/ppermute | solution.py:721
  93.2 3.7 all-gather.3.cloned.1.call-done.refs_8_
  103.0 9.7 %attend_forward.1 = (bf16[192,896]{1,0:T(8,128)(2,1)S(1)}, bf16[2688,256]{1,0:T(8,128)(2,1)S(1)}) custom-call(s32[4]{0:T(128)S(1)} %bitcast.84, bf16[192,896]{1,0:T(8,128)(2,1)S(1)} %get-tuple-element.186.q_ref, bf16[4,768,256]{2,1,0:T(8,128)(2,1)S(1)} %pad_maximum_fusion.3.kv_ref), custom_call_target="tpu_custom_call" | custom-call | flops 30000001024 | bytes 8388608 | tf_op jit(solution)/shard_map/attend_forward/pallas_call | solution.py:239
  117.8 6.0 %collective-permute-start.17 = (bf16[192,896]{1,0:T(8,128)(2,1)S(1)}, bf16[192,896]{1,0:T(8,128)(2,1)S(1)}, u32[]{:S(2)}, u32[]{:S(2)}) collective-permute-start(bf16[192,896]{1,0:T(8,128)(2,1)S(1)} %get-tuple-element.199.refs_0_), channel_id=1, source_target_pairs={{0,8},{4,12},{8,0},{12,4},{1,9},{5,13},{9,1},{13,5},{2,10},{6,14},... | collective-permute-start | bytes 1032200 | tf_op jit(solution)/shard_map/ppermute | solution.py:721
  125.0 12.3 %collective-permute-done.17.refs_2_ = bf16[192,896]{1,0:T(8,128)(2,1)S(1)} collective-permute-done((bf16[192,896]{1,0:T(8,128)(2,1)S(1)}, bf16[192,896]{1,0:T(8,128)(2,1)S(1)}, u32[]{:S(2)}, u32[]{:S(2)}) %collective-permute-start.17) | collective-permute-done | bytes 344096 | tf_op jit(solution)/shard_map/ppermute | solution.py:721
  137.3 3.5 collective-permute-done.18.refs_3_
  144.9 20.9 %ff_pass.1 = (bf16[640,768]{1,0:T(8,128)(2,1)}, bf16[640,768]{1,0:T(8,128)(2,1)}, bf16[768,1280]{1,0:T(8,128)(2,1)}, bf16[768,1280]{1,0:T(8,128)(2,1)}, bf16[896...) custom-call(bf16[192,896]{1,0:T(8,128)(2,1)} %copy-done.30, ...), custom_call_target="tpu_custom_call" | custom-call | tf_op jit(solution)/shard_map/ff_pass/pallas_call | solution.py:667
  178.1 3.5 grad_weight.5
  183.0 6.8 %collective-permute-done.23 = bf16[192,896]{1,0:T(8,128)(2,1)} collective-permute-done((bf16[192,896]{1,0:T(8,128)(2,1)}, bf16[192,896]{1,0:T(8,128)(2,1)}, u32[]{:S(2)}, u32[]{:S(2)}) %collective-permute-start.23) | collective-permute-done | bytes 344096 | tf_op jit(solution)/shard_map/ppermute | solution.py:721
  199.9 16.0 %attend_backward.1 = (bf16[192,896]{1,0:T(8,128)(2,1)S(1)}, bf16[4,768,256]{2,1,0:T(8,128)(2,1)S(1)}) custom-call(s32[4]{0:T(128)S(1)} %bitcast.85, bf16[2688,256]{1,0:T(8,128)(2,1)S(1)} %copy-done.34, bf16[192,896]{1,0:T(8,128)(2,1)S(1)} %copy-done.31, bf16[192,896]{1,0:T(8,128)(2,1)S(1)} %copy-done.19, f32[192,128]{1,0:T(8,128)S(1)} %copy.33.refs_5_.cos_ref.refs_4_, ...), custom_call_target="tpu_custom_call" | custom-call | flops 49999998976 | bytes 8388608 | tf_op jit(solution)/shard_map/attend_backward/pallas_call | solution.py:269
  217.3 7.3 %collective-permute-start.28 = (bf16[640,896]{1,0:T(8,128)(2,1)S(1)}, bf16[640,896]{1,0:T(8,128)(2,1)S(1)}, u32[]{:S(2)}, u32[]{:S(2)}) collective-permute-start(bf16[640,896]{1,0:T(8,128)(2,1)S(1)} %grad_weight.6), channel_id=1, source_target_pairs={{0,16},{16,0},{1,17},{17,1},{2,18},{18,2},{3,19},{19,3},{4,20},{20... | collective-permute-start | bytes 3440648 | tf_op jit(solution)/shard_map/ppermute | solution.py:716
  226.5 7.6 %collective-permute-start.26 = (bf16[768,256]{1,0:T(8,128)(2,1)}, bf16[768,256]{1,0:T(8,128)(2,1)}, u32[]{:S(2)}, u32[]{:S(2)}) collective-permute-start(bf16[768,256]{1,0:T(8,128)(2,1)} %get-tuple-element.330), channel_id=1, source_target_pairs={{0,8},{4,12},{8,0},{12,4},{1,9},{5,13},{9,1},{13,5},{2,10},{6,14},... | collective-permute-start | bytes 1179656 | tf_op jit(solution)/shard_map/ppermute | solution.py:721
  239.4 11.7 %collective-permute-done.26 = bf16[768,256]{1,0:T(8,128)(2,1)} collective-permute-done((bf16[768,256]{1,0:T(8,128)(2,1)}, bf16[768,256]{1,0:T(8,128)(2,1)}, u32[]{:S(2)}, u32[]{:S(2)}) %collective-permute-start.26) | collective-permute-done | bytes 393248 | tf_op jit(solution)/shard_map/ppermute | solution.py:721
  255.3 3.6 collective-permute-start.29
  263.6 4.9 %collective-permute-done.30.refs_2_ = bf16[192,256]{1,0:T(8,128)(2,1)S(1)} collective-permute-done((bf16[192,256]{1,0:T(8,128)(2,1)}, bf16[192,256]{1,0:T(8,128)(2,1)S(1)}, u32[]{:S(2)}, u32[]{:S(2)}) %collective-permute-start.30) | collective-permute-done | bytes 98336 | tf_op jit(solution)/shard_map/ppermute | solution.py:726
  281.3 7.5 %collective-permute-done.39 = bf16[224,1280]{1,0:T(8,128)(2,1)} collective-permute-done((bf16[224,1280]{1,0:T(8,128)(2,1)}, bf16[224,1280]{1,0:T(8,128)(2,1)}, u32[]{:S(2)}, u32[]{:S(2)}) %collective-permute-start.39) | collective-permute-done | bytes 573472 | tf_op jit(solution)/shard_map/ppermute | solution.py:721
  289.5 9.8 %collective-permute-done.34 = bf16[4,32,2176]{2,1,0:T(8,128)(2,1)S(1)} collective-permute-done((bf16[4,32,2176]{2,1,0:T(8,128)(2,1)}, bf16[4,32,2176]{2,1,0:T(8,128)(2,1)S(1)}, u32[]{:S(2)}, u32[]{:S(2)}) %collective-permute-start.34) | collective-permute-done | bytes 557088 | tf_op jit(solution)/shard_map/ppermute | solution.py:721
  299.4 3.6 collective-permute-done.35
  302.9 9.7 %collective-permute-done.36 = bf16[4,32,2176]{2,1,0:T(8,128)(2,1)} collective-permute-done((bf16[4,32,2176]{2,1,0:T(8,128)(2,1)}, bf16[4,32,2176]{2,1,0:T(8,128)(2,1)}, u32[]{:S(2)}, u32[]{:S(2)}) %collective-permute-start.36) | collective-permute-done | bytes 557088 | tf_op jit(solution)/shard_map/ppermute | solution.py:721
  322.3 3.4 collective-permute-done.43
  325.7 6.0 %collective-permute-done.44 = bf16[32,2176]{1,0:T(8,128)(2,1)S(1)} collective-permute-done((bf16[32,2176]{1,0:T(8,128)(2,1)S(1)}, bf16[32,2176]{1,0:T(8,128)(2,1)S(1)}, u32[]{:S(2)}, u32[]{:S(2)}) %collective-permute-start.44) | collective-permute-done | bytes 139296 | tf_op jit(solution)/shard_map/ppermute | solution.py:726
  334.5 9.1 %spread_columns.1 = (f32[224,4864]{1,0:T(8,128)}, f32[224,4864]{1,0:T(8,128)}) custom-call(bf16[4,224,1280]{2,1,0:T(8,128)(2,1)} %pad_maximum_fusion.refs_0_, bf16[4,224,1280]{2,1,0:T(8,128)(2,1)} %collective-permute-done.46.refs_1_), custom_call_target="tpu_custom_call" | custom-call | flops 10000000000 | bytes 8388608 | tf_op jit(solution)/shard_map/spread_columns/pallas_call | solution.py:332
  359.9 4.4 %collective-permute-done.40 = bf16[192,896]{1,0:T(8,128)(2,1)S(1)} collective-permute-done((bf16[192,896]{1,0:T(8,128)(2,1)S(1)}, bf16[192,896]{1,0:T(8,128)(2,1)S(1)}, u32[]{:S(2)}, u32[]{:S(2)}) %collective-permute-start.40) | collective-permute-done | bytes 344096 | tf_op jit(solution)/shard_map/ppermute | solution.py:721
  364.3 7.3 %collective-permute-done.42 = bf16[192,896]{1,0:T(8,128)(2,1)S(1)} collective-permute-done((bf16[192,896]{1,0:T(8,128)(2,1)S(1)}, bf16[192,896]{1,0:T(8,128)(2,1)S(1)}, u32[]{:S(2)}, u32[]{:S(2)}) %collective-permute-start.42) | collective-permute-done | bytes 344096 | tf_op jit(solution)/shard_map/ppermute | solution.py:721
  372.5 3.8 spread_rows.3
  (301 shorter events, 147.0 us)
Async XLA Ops:
  7.2 89.7 %all-gather.3.cloned.1.call-start = ((), (), s32[]{:S(2)}) async-start(), calls=%async_computation.2 | async-start | bytes 2867200 | tf_op jit(solution)/shard_map/all_gather | solution.py:729
  13.9 14.4 %collective-permute-start = (bf16[464,256]{1,0:T(8,128)(2,1)S(1)}, bf16[464,256]{1,0:T(8,128)(2,1)S(1)}, u32[]{:S(2)}, u32[]{:S(2)}) collective-permute-start(bf16[464,256]{1,0:T(8,128)(2,1)S(1)} %constant_dynamic-update-slice_fusion.refs_0_), channel_id=1, source_target_pairs={{0,1},{1,0},{2,3},{3,2},{4,5},{5,4},{6,7},{7,6},{8,9},{9,8},{10,11... | collective-permute-start | bytes 712712 | tf_op jit(solution)/shard_map/ppermute | solution.py:726
  18.4 15.4 %collective-permute-start.2 = (bf16[464,256]{1,0:T(8,128)(2,1)S(1)}, bf16[464,256]{1,0:T(8,128)(2,1)}, u32[]{:S(2)}, u32[]{:S(2)}) collective-permute-start(bf16[464,256]{1,0:T(8,128)(2,1)S(1)} %constant_dynamic-update-slice_fusion.refs_0_), channel_id=1, source_target_pairs={{0,3},{1,2},{2,1},{3,0},{4,7},{5,6},{6,5},{7,4},{8,11},{9,10},{10,... | collective-permute-start | bytes 712712 | tf_op jit(solution)/shard_map/ppermute | solution.py:726
  33.9 107.0 %all-gather.5.cloned.1.call-start = ((), (), s32[]{:S(2)}) async-start(), calls=%async_computation.3 | async-start | bytes 1433600 | tf_op jit(solution)/shard_map/all_gather | solution.py:729
  37.2 28.7 %collective-permute-start.6 = (bf16[4,64,896]{2,1,0:T(8,128)(2,1)S(1)}, bf16[4,64,896]{2,1,0:T(8,128)(2,1)S(1)}, u32[]{:S(2)}, u32[]{:S(2)}) collective-permute-start(bf16[4,64,896]{2,1,0:T(8,128)(2,1)S(1)} %constant_dynamic-update-slice_fusion.2), channel_id=1, source_target_pairs={{0,4},{4,0},{8,12},{12,8},{1,5},{5,1},{9,13},{13,9},{2,6},{6,2},{1... | collective-permute-start | bytes 1376264 | tf_op jit(solution)/shard_map/ppermute | solution.py:721
  38.4 27.4 %collective-permute-start.7 = (bf16[4,64,896]{2,1,0:T(8,128)(2,1)S(1)}, bf16[4,64,896]{2,1,0:T(8,128)(2,1)S(1)}, u32[]{:S(2)}, u32[]{:S(2)}) collective-permute-start(bf16[4,64,896]{2,1,0:T(8,128)(2,1)S(1)} %constant_dynamic-update-slice_fusion.2), channel_id=1, source_target_pairs={{0,8},{4,12},{8,0},{12,4},{1,9},{5,13},{9,1},{13,5},{2,10},{6,14},... | collective-permute-start | bytes 1376264 | tf_op jit(solution)/shard_map/ppermute | solution.py:721
  39.7 26.2 %collective-permute-start.8 = (bf16[4,64,896]{2,1,0:T(8,128)(2,1)S(1)}, bf16[4,64,896]{2,1,0:T(8,128)(2,1)S(1)}, u32[]{:S(2)}, u32[]{:S(2)}) collective-permute-start(bf16[4,64,896]{2,1,0:T(8,128)(2,1)S(1)} %constant_dynamic-update-slice_fusion.2), channel_id=1, source_target_pairs={{0,12},{4,8},{8,4},{12,0},{1,13},{5,9},{9,5},{13,1},{2,14},{6,10},... | collective-permute-start | bytes 1376264 | tf_op jit(solution)/shard_map/ppermute | solution.py:721
  44.2 13.2 %collective-permute-start.3 = (bf16[192,256]{1,0:T(8,128)(2,1)S(1)}, bf16[192,256]{1,0:T(8,128)(2,1)S(1)}, u32[]{:S(2)}, u32[]{:S(2)}) collective-permute-start(bf16[192,256]{1,0:T(8,128)(2,1)S(1)} %get-tuple-element.176), channel_id=1, source_target_pairs={{0,1},{1,0},{2,3},{3,2},{4,5},{5,4},{6,7},{7,6},{8,9},{9,8},{10,11... | collective-permute-start | bytes 294920 | tf_op jit(solution)/shard_map/ppermute | solution.py:726
  74.1 17.8 %collective-permute-start.11 = (bf16[768,256]{1,0:T(8,128)(2,1)S(1)}, bf16[768,256]{1,0:T(8,128)(2,1)S(1)}, u32[]{:S(2)}, u32[]{:S(2)}) collective-permute-start(bf16[768,256]{1,0:T(8,128)(2,1)S(1)} %constant_dynamic-update-slice_fusion.6), channel_id=1, source_target_pairs={{0,8},{4,12},{8,0},{12,4},{1,9},{5,13},{9,1},{13,5},{2,10},{6,14},... | collective-permute-start | bytes 1179656 | tf_op jit(solution)/shard_map/ppermute | solution.py:721
  75.4 17.8 %collective-permute-start.12 = (bf16[768,256]{1,0:T(8,128)(2,1)S(1)}, bf16[768,256]{1,0:T(8,128)(2,1)}, u32[]{:S(2)}, u32[]{:S(2)}) collective-permute-start(bf16[768,256]{1,0:T(8,128)(2,1)S(1)} %constant_dynamic-update-slice_fusion.6), channel_id=1, source_target_pairs={{0,12},{4,8},{8,4},{12,0},{1,13},{5,9},{9,5},{13,1},{2,14},{6,10},... | collective-permute-start | bytes 1179656 | tf_op jit(solution)/shard_map/ppermute | solution.py:721
  96.9 15.8 %collective-permute-start.13 = (bf16[192,896]{1,0:T(8,128)(2,1)S(1)}, bf16[192,896]{1,0:T(8,128)(2,1)}, u32[]{:S(2)}, u32[]{:S(2)}) collective-permute-start(bf16[192,896]{1,0:T(8,128)(2,1)S(1)} %bitcast.90), channel_id=1, source_target_pairs={{0,4},{4,0},{8,12},{12,8},{1,5},{5,1},{9,13},{13,9},{2,6},{6,2},{1... | collective-permute-start | bytes 1032200 | tf_op jit(solution)/shard_map/ppermute | solution.py:721
  98.1 14.7 %collective-permute-start.14 = (bf16[192,896]{1,0:T(8,128)(2,1)S(1)}, bf16[192,896]{1,0:T(8,128)(2,1)}, u32[]{:S(2)}, u32[]{:S(2)}) collective-permute-start(bf16[192,896]{1,0:T(8,128)(2,1)S(1)} %bitcast.91), channel_id=1, source_target_pairs={{0,8},{4,12},{8,0},{12,4},{1,9},{5,13},{9,1},{13,5},{2,10},{6,14},... | collective-permute-start | bytes 1032200 | tf_op jit(solution)/shard_map/ppermute | solution.py:721
  99.3 14.9 %collective-permute-start.15 = (bf16[192,896]{1,0:T(8,128)(2,1)S(1)}, bf16[192,896]{1,0:T(8,128)(2,1)}, u32[]{:S(2)}, u32[]{:S(2)}) collective-permute-start(bf16[192,896]{1,0:T(8,128)(2,1)S(1)} %bitcast.92), channel_id=1, source_target_pairs={{0,12},{4,8},{8,4},{12,0},{1,13},{5,9},{9,5},{13,1},{2,14},{6,10},... | collective-permute-start | bytes 1032200 | tf_op jit(solution)/shard_map/ppermute | solution.py:721
  99.6 152.2 %reduce-scatter.3.cloned.1.call-start = ((), (), s32[]{:S(2)}) async-start(), calls=%async_computation.4 | async-start | bytes 2867200 | tf_op jit(solution)/shard_map/reduce_scatter | solution.py:732
  99.8 41.4 %collective-permute-start.19 = (bf16[896,1280]{1,0:T(8,128)(2,1)}, bf16[896,1280]{1,0:T(8,128)(2,1)}, u32[]{:S(2)}, u32[]{:S(2)}) collective-permute-start(bf16[896,1280]{1,0:T(8,128)(2,1)} %all-gather.3.cloned.1.call-done.refs_8_), channel_id=1, source_target_pairs={{0,16},{16,0},{1,17},{17,1},{2,18},{18,2},{3,19},{19,3},{4,20},{20... | collective-permute-start | bytes 6881288 | tf_op jit(solution)/shard_map/ppermute | solution.py:716
  117.8 19.5 %collective-permute-start.17 = (bf16[192,896]{1,0:T(8,128)(2,1)S(1)}, bf16[192,896]{1,0:T(8,128)(2,1)S(1)}, u32[]{:S(2)}, u32[]{:S(2)}) collective-permute-start(bf16[192,896]{1,0:T(8,128)(2,1)S(1)} %get-tuple-element.199.refs_0_), channel_id=1, source_target_pairs={{0,8},{4,12},{8,0},{12,4},{1,9},{5,13},{9,1},{13,5},{2,10},{6,14},... | collective-permute-start | bytes 1032200 | tf_op jit(solution)/shard_map/ppermute | solution.py:721
  123.8 17.0 %collective-permute-start.18 = (bf16[192,896]{1,0:T(8,128)(2,1)S(1)}, bf16[192,896]{1,0:T(8,128)(2,1)S(1)}, u32[]{:S(2)}, u32[]{:S(2)}) collective-permute-start(bf16[192,896]{1,0:T(8,128)(2,1)S(1)} %get-tuple-element.199.refs_0_), channel_id=1, source_target_pairs={{0,12},{4,8},{8,4},{12,0},{1,13},{5,9},{9,5},{13,1},{2,14},{6,10},... | collective-permute-start | bytes 1032200 | tf_op jit(solution)/shard_map/ppermute | solution.py:721
  174.2 15.5 %collective-permute-start.23 = (bf16[192,896]{1,0:T(8,128)(2,1)}, bf16[192,896]{1,0:T(8,128)(2,1)}, u32[]{:S(2)}, u32[]{:S(2)}) collective-permute-start(bf16[192,896]{1,0:T(8,128)(2,1)} %get-tuple-element.212), channel_id=1, source_target_pairs={{0,12},{4,8},{8,4},{12,0},{1,13},{5,9},{9,5},{13,1},{2,14},{6,10},... | collective-permute-start | bytes 1032200 | tf_op jit(solution)/shard_map/ppermute | solution.py:721
  196.0 93.5 %reduce-scatter.5.cloned.1.call-start = ((), (), s32[]{:S(2)}) async-start(), calls=%async_computation.5 | async-start | bytes 1433600 | tf_op jit(solution)/shard_map/reduce_scatter | solution.py:732
  217.3 19.9 %collective-permute-start.28 = (bf16[640,896]{1,0:T(8,128)(2,1)S(1)}, bf16[640,896]{1,0:T(8,128)(2,1)S(1)}, u32[]{:S(2)}, u32[]{:S(2)}) collective-permute-start(bf16[640,896]{1,0:T(8,128)(2,1)S(1)} %grad_weight.6), channel_id=1, source_target_pairs={{0,16},{16,0},{1,17},{17,1},{2,18},{18,2},{3,19},{19,3},{4,20},{20... | collective-permute-start | bytes 3440648 | tf_op jit(solution)/shard_map/ppermute | solution.py:716
  226.5 24.6 %collective-permute-start.26 = (bf16[768,256]{1,0:T(8,128)(2,1)}, bf16[768,256]{1,0:T(8,128)(2,1)}, u32[]{:S(2)}, u32[]{:S(2)}) collective-permute-start(bf16[768,256]{1,0:T(8,128)(2,1)} %get-tuple-element.330), channel_id=1, source_target_pairs={{0,8},{4,12},{8,0},{12,4},{1,9},{5,13},{9,1},{13,5},{2,10},{6,14},... | collective-permute-start | bytes 1179656 | tf_op jit(solution)/shard_map/ppermute | solution.py:721
  234.2 17.6 %collective-permute-start.27 = (bf16[768,256]{1,0:T(8,128)(2,1)}, bf16[768,256]{1,0:T(8,128)(2,1)}, u32[]{:S(2)}, u32[]{:S(2)}) collective-permute-start(bf16[768,256]{1,0:T(8,128)(2,1)} %get-tuple-element.329), channel_id=1, source_target_pairs={{0,12},{4,8},{8,4},{12,0},{1,13},{5,9},{9,5},{13,1},{2,14},{6,10},... | collective-permute-start | bytes 1179656 | tf_op jit(solution)/shard_map/ppermute | solution.py:721
  251.8 18.0 %collective-permute-start.32 = (bf16[4,128,1792]{2,1,0:T(8,128)(2,1)}, bf16[4,128,1792]{2,1,0:T(8,128)(2,1)}, u32[]{:S(2)}, u32[]{:S(2)}) collective-permute-start(bf16[4,128,1792]{2,1,0:T(8,128)(2,1)} %get-tuple-element.247), channel_id=1, source_target_pairs={{0,16},{16,0},{1,17},{17,1},{2,18},{18,2},{3,19},{19,3},{4,20},{20... | collective-permute-start | bytes 5505032 | tf_op jit(solution)/shard_map/ppermute | solution.py:716
  261.0 19.1 %collective-permute-start.37 = (bf16[224,1280]{1,0:T(8,128)(2,1)}, bf16[224,1280]{1,0:T(8,128)(2,1)}, u32[]{:S(2)}, u32[]{:S(2)}) collective-permute-start(bf16[224,1280]{1,0:T(8,128)(2,1)} %reduce-scatter.3.cloned.1.call-done), channel_id=1, source_target_pairs={{0,4},{4,0},{8,12},{12,8},{1,5},{5,1},{9,13},{13,9},{2,6},{6,2},{1... | collective-permute-start | bytes 1720328 | tf_op jit(solution)/shard_map/ppermute | solution.py:721
  262.2 19.0 %collective-permute-start.38 = (bf16[224,1280]{1,0:T(8,128)(2,1)}, bf16[224,1280]{1,0:T(8,128)(2,1)}, u32[]{:S(2)}, u32[]{:S(2)}) collective-permute-start(bf16[224,1280]{1,0:T(8,128)(2,1)} %reduce-scatter.3.cloned.1.call-done), channel_id=1, source_target_pairs={{0,8},{4,12},{8,0},{12,4},{1,9},{5,13},{9,1},{13,5},{2,10},{6,14},... | collective-permute-start | bytes 1720328 | tf_op jit(solution)/shard_map/ppermute | solution.py:721
  268.6 20.2 %collective-permute-start.39 = (bf16[224,1280]{1,0:T(8,128)(2,1)}, bf16[224,1280]{1,0:T(8,128)(2,1)}, u32[]{:S(2)}, u32[]{:S(2)}) collective-permute-start(bf16[224,1280]{1,0:T(8,128)(2,1)} %reduce-scatter.3.cloned.1.call-done), channel_id=1, source_target_pairs={{0,12},{4,8},{8,4},{12,0},{1,13},{5,9},{9,5},{13,1},{2,14},{6,10},... | collective-permute-start | bytes 1720328 | tf_op jit(solution)/shard_map/ppermute | solution.py:721
  278.6 20.8 %collective-permute-start.34 = (bf16[4,32,2176]{2,1,0:T(8,128)(2,1)}, bf16[4,32,2176]{2,1,0:T(8,128)(2,1)S(1)}, u32[]{:S(2)}, u32[]{:S(2)}) collective-permute-start(bf16[4,32,2176]{2,1,0:T(8,128)(2,1)} %get-tuple-element.315), channel_id=1, source_target_pairs={{0,4},{4,0},{8,12},{12,8},{1,5},{5,1},{9,13},{13,9},{2,6},{6,2},{1... | collective-permute-start | bytes 1671176 | tf_op jit(solution)/shard_map/ppermute | solution.py:721
  280.1 22.9 %collective-permute-start.35 = (bf16[4,32,2176]{2,1,0:T(8,128)(2,1)}, bf16[4,32,2176]{2,1,0:T(8,128)(2,1)S(1)}, u32[]{:S(2)}, u32[]{:S(2)}) collective-permute-start(bf16[4,32,2176]{2,1,0:T(8,128)(2,1)} %get-tuple-element.314), channel_id=1, source_target_pairs={{0,8},{4,12},{8,0},{12,4},{1,9},{5,13},{9,1},{13,5},{2,10},{6,14},... | collective-permute-start | bytes 1671176 | tf_op jit(solution)/shard_map/ppermute | solution.py:721
  280.1 32.5 %collective-permute-start.36 = (bf16[4,32,2176]{2,1,0:T(8,128)(2,1)}, bf16[4,32,2176]{2,1,0:T(8,128)(2,1)}, u32[]{:S(2)}, u32[]{:S(2)}) collective-permute-start(bf16[4,32,2176]{2,1,0:T(8,128)(2,1)} %get-tuple-element.313), channel_id=1, source_target_pairs={{0,12},{4,8},{8,4},{12,0},{1,13},{5,9},{9,5},{13,1},{2,14},{6,10},... | collective-permute-start | bytes 1671176 | tf_op jit(solution)/shard_map/ppermute | solution.py:721
  315.7 16.0 %collective-permute-start.46 = (bf16[4,224,1280]{2,1,0:T(8,128)(2,1)}, bf16[4,224,1280]{2,1,0:T(8,128)(2,1)}, u32[]{:S(2)}, u32[]{:S(2)}) collective-permute-start(bf16[4,224,1280]{2,1,0:T(8,128)(2,1)} %pad_maximum_fusion.refs_0_), channel_id=1, source_target_pairs={{0,16},{16,0},{1,17},{17,1},{2,18},{18,2},{3,19},{19,3},{4,20},{20... | collective-permute-start | bytes 6881288 | tf_op jit(solution)/shard_map/ppermute | solution.py:716
  354.3 17.3 %collective-permute-start.42 = (bf16[192,896]{1,0:T(8,128)(2,1)S(1)}, bf16[192,896]{1,0:T(8,128)(2,1)S(1)}, u32[]{:S(2)}, u32[]{:S(2)}) collective-permute-start(bf16[192,896]{1,0:T(8,128)(2,1)S(1)} %copy-done.55), channel_id=1, source_target_pairs={{0,12},{4,8},{8,4},{12,0},{1,13},{5,9},{9,5},{13,1},{2,14},{6,10},... | collective-permute-start | bytes 1032200 | tf_op jit(solution)/shard_map/ppermute | solution.py:721
  356.9 19.5 %collective-permute-start.54 = (bf16[4,32,2176]{2,1,0:T(8,128)(2,1)S(1)}, bf16[4,32,2176]{2,1,0:T(8,128)(2,1)S(1)}, u32[]{:S(2)}, u32[]{:S(2)}) collective-permute-start(bf16[4,32,2176]{2,1,0:T(8,128)(2,1)S(1)} %pad_maximum_fusion.5.refs_0_), channel_id=1, source_target_pairs={{0,16},{16,0},{1,17},{17,1},{2,18},{18,2},{3,19},{19,3},{4,20},{20... | collective-permute-start | bytes 1671176 | tf_op jit(solution)/shard_map/ppermute | solution.py:716
  (85 other events, 720.3 us)
Sparse Core Ops, SparseCore 0:
  34.0 62.8 all-gather.2
  99.7 30.8 all-gather.4
  196.1 47.9 reduce-scatter.2
  262.3 27.1 reduce-scatter.4
